TPU v7x, 32 devices: a whole 2x2x4 slice. The times are simulated.
32 devices in a mesh: wide: 8 (over y, x, core), narrow: 4 (over z).
Axes of the slice: x: 2, y: 2, z: 4, core: 2. Of those that a mesh axis runs over, the one named last changes fastest.
Arguments:
- text_in: bfloat16 [8, 4, 512, 768], P(None, 'narrow', 'wide'), may hold values from -6 to 6
- patch_in: bfloat16 [8, 4, 576, 768], P('wide', None, 'narrow'), may hold values from -6 to 6
- res_class: int32 [8, 4], P('wide', 'narrow'), may hold values from 0 to 1, as said below
- text_len: int32 [8, 4], P('wide', 'narrow'), may hold values from 128 to 512, as said below
- pos_line: int32 [8, 4, 1088], P('wide', 'narrow'), may hold values from 0 to 63
- pos_x: int32 [8, 4, 1088], P('wide', 'narrow'), may hold values from 0 to 127
- pos_y: int32 [8, 4, 1088], P('wide', 'narrow'), may hold values from 0 to 127
- query_weight: bfloat16 [768, 768], replicated, may hold values from -0.21875 to 0.21875
- query_bias: float32 [768], replicated, may hold values from -1.8 to 1.8
- key_weight: bfloat16 [768, 768], replicated, may hold values from -0.21875 to 0.21875
- value_weight: bfloat16 [768, 768], replicated, may hold values from -0.21875 to 0.21875
- value_bias: float32 [768], replicated, may hold values from -1.8 to 1.8
- output_weight: bfloat16 [768, 768], replicated, may hold values from -0.875 to 0.875
- output_bias: float32 [768], replicated, may hold values from -3 to 3
- norm_gain: float32 [768], replicated, may hold values from 0.5 to 1.5
- norm_shift: float32 [768], replicated, may hold values from -1.8 to 1.8
- up_weight: bfloat16 [768, 3072], replicated, may hold values from -0.21875 to 0.21875
- up_bias: float32 [3072], replicated, may hold values from -3 to 3
- down_weight: bfloat16 [3072, 768], replicated, may hold values from -0.21875 to 0.21875
- down_bias: float32 [768], replicated, may hold values from -3 to 3
- final_gain: float32 [768], replicated, may hold values from 0.5 to 1.5
- final_shift: float32 [768], replicated, may hold values from -1.8 to 1.8
- line_table: float32 [33, 12], replicated, may hold values from -3 to 3
- width_table: float32 [65, 12], replicated, may hold values from -3 to 3
- height_table: float32 [65, 12], replicated, may hold values from -3 to 3
- cot_text: bfloat16 [8, 4, 512, 768], P(None, 'narrow', 'wide'), may hold values from -6 to 6
- cot_patch: bfloat16 [8, 4, 576, 768], P('wide', None, 'narrow'), may hold values from -6 to 6
Outputs:
- text_out: bfloat16 [8, 4, 512, 768], P(None, 'narrow', 'wide')
- patch_out: bfloat16 [8, 4, 576, 768], P('wide', None, 'narrow')
- text_grad: bfloat16 [8, 4, 512, 768], P(None, 'narrow', 'wide')
- patch_grad: bfloat16 [8, 4, 576, 768], P('wide', None, 'narrow')
- query_weight_grad: float32 [768, 768], replicated
- query_bias_grad: float32 [768], replicated
- key_weight_grad: float32 [768, 768], replicated
- value_weight_grad: float32 [768, 768], replicated
- value_bias_grad: float32 [768], replicated
- output_weight_grad: float32 [768, 768], replicated
- output_bias_grad: float32 [768], replicated
- norm_gain_grad: float32 [768], replicated
- norm_shift_grad: float32 [768], replicated
- up_weight_grad: float32 [768, 3072], replicated
- up_bias_grad: float32 [3072], replicated
- down_weight_grad: float32 [3072, 768], replicated
- down_bias_grad: float32 [768], replicated
- final_gain_grad: float32 [768], replicated
- final_shift_grad: float32 [768], replicated
- line_table_grad: float32 [33, 12], replicated
- width_table_grad: float32 [65, 12], replicated
- height_table_grad: float32 [65, 12], replicated
Inputs may be any that keep to these rules, and one draw needn't show every extreme that they name: `res_class`: 0 for a page of 196 patches, 1 for one of 576; some page is of class 1 in every draw. `text_len`: the CLS row is always live; some page has all 512 text rows live in every draw.
All inputs are finite; a program needn't handle non-finite values.
Results may differ from a plain program's by a relative error of at most 0.018.
Values may be sent and summed in bfloat16 or wider, within the bound.
No kernel may reach another device: no remote copies, remote signals or barrier semaphores. Data moves between devices by JAX's collectives and lax.ppermute only.
A program may use at most 384 MiB of HBM per device.

v0:
```python
from functools import partial

import jax
import jax.numpy as jnp
from jax import lax
from jax.sharding import PartitionSpec as P

HEADS = 12
TEXT = 512
PATCH = 576
SMALL_PATCH = 196


HIGH = lax.Precision.HIGHEST


def layer_norm(rows, gain, shift):
    mean = jnp.mean(rows, axis=-1, keepdims=True)
    centred = rows - mean
    spread = jnp.mean(centred * centred, axis=-1, keepdims=True)
    return centred * lax.rsqrt(spread + 1e-05) * gain + shift


def inner(left, right):
    return lax.dot_general(
        left, right, (((0,), (0,)), ((), ())), preferred_element_type=jnp.float32
    )


def against(left, right):
    return lax.dot_general(
        left, right, (((1,), (1,)), ((), ())), preferred_element_type=jnp.float32
    )


def key_onehot(positions, tables):
    columns = []
    for spots, table in zip(positions, tables):
        span = 2 * (table.shape[0] - 1)
        columns.append(
            (spots[:, None] == jnp.arange(span, dtype=jnp.int32)[None, :]).astype(jnp.bfloat16)
        )
    return jnp.concatenate(columns, axis=1)


def bucket_bias(query_spots, key_hot, tables):
    selects = []
    nearby = []
    for spots, table in zip(query_spots, tables):
        reach = (table.shape[0] - 1) // 2
        span = 4 * reach
        offsets = (
            jnp.clip(spots[:, None] - jnp.arange(span, dtype=jnp.int32)[None, :], -reach, reach)
            + reach
        )
        select = (offsets[:, :, None] == jnp.arange(2 * reach + 1, dtype=jnp.int32)).astype(
            jnp.float32
        )
        selects.append(select)
        nearby.append(jnp.einsum("qub,bh->hqu", select, table, precision=HIGH))
    joined = jnp.concatenate(nearby, axis=2)
    high_part = joined.astype(jnp.bfloat16)
    low_part = (joined - high_part.astype(jnp.float32)).astype(jnp.bfloat16)
    bias = jnp.einsum(
        "hqu,ku->hqk", high_part, key_hot, preferred_element_type=jnp.float32
    ) + jnp.einsum("hqu,ku->hqk", low_part, key_hot, preferred_element_type=jnp.float32)
    return (bias, selects)


def block_scores(query, keys, bias, key_valid):
    scaled = (
        jnp.einsum("qhd,khd->hqk", query, keys, preferred_element_type=jnp.float32)
        * query.shape[-1] ** (-0.5)
        + bias
    )
    return jnp.where(key_valid[None, None, :], scaled, -1e30)


def split_heads(page_qkv):
    seq = page_qkv.shape[0]
    dim = page_qkv.shape[1] // 3
    query = page_qkv[:, :dim].reshape(seq, HEADS, -1)
    keys = page_qkv[:, dim : 2 * dim].reshape(seq, HEADS, -1)
    values = page_qkv[:, 2 * dim :].reshape(seq, HEADS, -1)
    return (query, keys, values)


def page_attend(page, tables):
    page_qkv, key_valid, line_pos, width_pos, height_pos = page
    query, keys, values = split_heads(page_qkv)
    seq = query.shape[0]
    half = seq // 2
    dim = page_qkv.shape[1] // 3
    key_hot = key_onehot((line_pos, width_pos, height_pos), tables)

    def one_block(inputs):
        q_blk, line_q, width_q, height_q = inputs
        bias, unused = bucket_bias((line_q, width_q, height_q), key_hot, tables)
        scores = block_scores(q_blk, keys, bias, key_valid)
        peak = jnp.max(scores, axis=-1, keepdims=True)
        total = jnp.sum(jnp.exp(scores - peak), axis=-1, keepdims=True)
        log_total = peak + jnp.log(total)
        probs = jnp.exp(scores - log_total).astype(jnp.bfloat16)
        context = jnp.einsum("hqk,khd->qhd", probs, values, preferred_element_type=jnp.float32)
        return (context.reshape(q_blk.shape[0], dim).astype(jnp.bfloat16), log_total[..., 0])

    blocks = (
        query.reshape(2, half, HEADS, -1),
        line_pos.reshape(2, half),
        width_pos.reshape(2, half),
        height_pos.reshape(2, half),
    )
    context, log_total = lax.map(one_block, blocks)
    return (context.reshape(seq, dim), log_total)


def page_back(page, tables):
    page_qkv, key_valid, line_pos, width_pos, height_pos, log_total, d_context = page
    query, keys, values = split_heads(page_qkv)
    seq = query.shape[0]
    half = seq // 2
    dim = page_qkv.shape[1] // 3
    scale = query.shape[-1] ** (-0.5)
    key_hot = key_onehot((line_pos, width_pos, height_pos), tables)
    spans = [2 * (table.shape[0] - 1) for table in tables]

    def one_block(carry, inputs):
        d_keys, d_values, g_line, g_width, g_height = carry
        q_blk, dc_blk, total_blk, line_q, width_q, height_q = inputs
        bias, selects = bucket_bias((line_q, width_q, height_q), key_hot, tables)
        scores = block_scores(q_blk, keys, bias, key_valid)
        probs = jnp.exp(scores - total_blk[..., None])
        d_out = dc_blk.reshape(half, HEADS, -1)
        d_probs = jnp.einsum("qhd,khd->hqk", d_out, values, preferred_element_type=jnp.float32)
        delta = jnp.sum(probs * d_probs, axis=-1, keepdims=True)
        d_scores = (probs * (d_probs - delta)).astype(jnp.bfloat16)
        d_query = (
            jnp.einsum("hqk,khd->qhd", d_scores, keys, preferred_element_type=jnp.float32) * scale
        )
        d_keys = (
            d_keys
            + jnp.einsum("hqk,qhd->khd", d_scores, q_blk, preferred_element_type=jnp.float32)
            * scale
        )
        d_values = d_values + jnp.einsum(
            "hqk,qhd->khd", probs.astype(jnp.bfloat16), d_out, preferred_element_type=jnp.float32
        )
        spread = jnp.einsum("hqk,ku->hqu", d_scores, key_hot, preferred_element_type=jnp.float32)
        first = spans[0]
        second = spans[0] + spans[1]
        g_line = g_line + jnp.einsum(
            "hqu,qub->bh", spread[:, :, :first], selects[0], precision=HIGH
        )
        g_width = g_width + jnp.einsum(
            "hqu,qub->bh", spread[:, :, first:second], selects[1], precision=HIGH
        )
        g_height = g_height + jnp.einsum(
            "hqu,qub->bh", spread[:, :, second:], selects[2], precision=HIGH
        )
        return (
            (d_keys, d_values, g_line, g_width, g_height),
            d_query.reshape(half, dim).astype(jnp.bfloat16),
        )

    start = (
        jnp.zeros(keys.shape, jnp.float32),
        jnp.zeros(values.shape, jnp.float32),
        jnp.zeros(tables[0].shape, jnp.float32),
        jnp.zeros(tables[1].shape, jnp.float32),
        jnp.zeros(tables[2].shape, jnp.float32),
    )
    blocks = (
        query.reshape(2, half, HEADS, -1),
        d_context.reshape(2, half, dim),
        log_total,
        line_pos.reshape(2, half),
        width_pos.reshape(2, half),
        height_pos.reshape(2, half),
    )
    (d_keys, d_values, g_line, g_width, g_height), d_query = lax.scan(one_block, start, blocks)
    d_qkv = jnp.concatenate(
        [
            d_query.reshape(seq, dim),
            d_keys.reshape(seq, dim).astype(jnp.bfloat16),
            d_values.reshape(seq, dim).astype(jnp.bfloat16),
        ],
        axis=1,
    )
    return (d_qkv, g_line, g_width, g_height)


def row_pass(rows_in, ctx_rows, cot, weights):
    (
        output_weight,
        output_bias,
        norm_gain,
        norm_shift,
        up_weight,
        up_bias,
        down_weight,
        down_bias,
        final_gain,
        final_shift,
    ) = weights
    attn = jnp.dot(ctx_rows, output_weight, preferred_element_type=jnp.float32) + output_bias
    mid = rows_in.astype(jnp.float32) + attn
    normed, norm_back = jax.vjp(layer_norm, mid, norm_gain, norm_shift)
    normed_low = normed.astype(jnp.bfloat16)
    pre = jnp.dot(normed_low, up_weight, preferred_element_type=jnp.float32) + up_bias
    act, gelu_back = jax.vjp(partial(jax.nn.gelu, approximate=False), pre)
    act_low = act.astype(jnp.bfloat16)
    branch = jnp.dot(act_low, down_weight, preferred_element_type=jnp.float32) + down_bias
    final, final_back = jax.vjp(layer_norm, normed + branch, final_gain, final_shift)
    final_low = final.astype(jnp.bfloat16)
    d_sum, final_gain_grad, final_shift_grad = final_back(cot)
    d_branch = d_sum.astype(jnp.bfloat16)
    down_weight_grad = inner(act_low, d_branch)
    down_bias_grad = jnp.sum(d_branch.astype(jnp.float32), axis=0)
    d_act = against(d_branch, down_weight)
    (d_pre,) = gelu_back(d_act)
    d_pre_low = d_pre.astype(jnp.bfloat16)
    up_weight_grad = inner(normed_low, d_pre_low)
    up_bias_grad = jnp.sum(d_pre_low.astype(jnp.float32), axis=0)
    d_normed = d_sum + against(d_pre_low, up_weight)
    d_mid, norm_gain_grad, norm_shift_grad = norm_back(d_normed)
    d_attn = d_mid.astype(jnp.bfloat16)
    output_weight_grad = inner(ctx_rows, d_attn)
    output_bias_grad = jnp.sum(d_attn.astype(jnp.float32), axis=0)
    d_ctx = against(d_attn, output_weight).astype(jnp.bfloat16)
    grads = (
        output_weight_grad,
        output_bias_grad,
        norm_gain_grad,
        norm_shift_grad,
        up_weight_grad,
        up_bias_grad,
        down_weight_grad,
        down_bias_grad,
        final_gain_grad,
        final_shift_grad,
    )
    return (final_low, d_mid, d_ctx, grads)


def body(
    text_in,
    patch_in,
    res_class,
    text_len,
    pos_line,
    pos_x,
    pos_y,
    query_weight,
    query_bias,
    key_weight,
    value_weight,
    value_bias,
    output_weight,
    output_bias,
    norm_gain,
    norm_shift,
    up_weight,
    up_bias,
    down_weight,
    down_bias,
    final_gain,
    final_shift,
    line_table,
    width_table,
    height_table,
    cot_text,
    cot_patch,
):
    text_shape = text_in.shape
    patch_shape = patch_in.shape
    dim = text_shape[3]
    home_pages = patch_shape[0]
    seq = TEXT + PATCH
    tables = (line_table, width_table, height_table)
    weights = (
        output_weight,
        output_bias,
        norm_gain,
        norm_shift,
        up_weight,
        up_bias,
        down_weight,
        down_bias,
        final_gain,
        final_shift,
    )
    joined_weight = jnp.concatenate([query_weight, key_weight, value_weight], axis=1)
    joined_bias = jnp.concatenate([query_bias, jnp.zeros_like(query_bias), value_bias])
    text_flat = text_in.reshape(-1, dim)
    patch_flat = patch_in.reshape(-1, dim)
    n_text = text_flat.shape[0]
    rows_in = jnp.concatenate([text_flat, patch_flat], axis=0)
    cot = jnp.concatenate([cot_text.reshape(-1, dim), cot_patch.reshape(-1, dim)], axis=0).astype(
        jnp.float32
    )
    qkv_rows = (
        jnp.dot(rows_in, joined_weight, preferred_element_type=jnp.float32) + joined_bias
    ).astype(jnp.bfloat16)
    text_qkv = qkv_rows[:n_text].reshape(text_shape[0], text_shape[1], text_shape[2], 3 * dim)
    patch_qkv = qkv_rows[n_text:].reshape(patch_shape[0], patch_shape[1], patch_shape[2], 3 * dim)
    home_text = lax.all_to_all(text_qkv, "wide", split_axis=0, concat_axis=2, tiled=True)
    home_patch = lax.all_to_all(patch_qkv, "narrow", split_axis=1, concat_axis=2, tiled=True)
    home_qkv = jnp.concatenate([home_text, home_patch], axis=2).reshape(home_pages, seq, 3 * dim)
    live_patch = jnp.where(res_class.reshape(-1) == 1, PATCH, SMALL_PATCH)
    text_live = jnp.arange(TEXT, dtype=jnp.int32)[None, :] < text_len.reshape(-1)[:, None]
    patch_live = jnp.arange(PATCH, dtype=jnp.int32)[None, :] < live_patch[:, None]
    key_valid = jnp.concatenate([text_live, patch_live], axis=1)
    line_home = pos_line.reshape(home_pages, seq)
    width_home = pos_x.reshape(home_pages, seq)
    height_home = pos_y.reshape(home_pages, seq)
    context, log_total = lax.map(
        partial(page_attend, tables=tables),
        (home_qkv, key_valid, line_home, width_home, height_home),
    )
    context = context.reshape(home_pages, 1, seq, dim)
    ctx_text = lax.all_to_all(context[:, :, :TEXT], "wide", split_axis=2, concat_axis=0, tiled=True)
    ctx_patch = lax.all_to_all(
        context[:, :, TEXT:], "narrow", split_axis=2, concat_axis=1, tiled=True
    )
    ctx_rows = jnp.concatenate([ctx_text.reshape(-1, dim), ctx_patch.reshape(-1, dim)], axis=0)
    final_low, d_mid, d_ctx, row_grads = row_pass(rows_in, ctx_rows, cot, weights)
    (
        output_weight_grad,
        output_bias_grad,
        norm_gain_grad,
        norm_shift_grad,
        up_weight_grad,
        up_bias_grad,
        down_weight_grad,
        down_bias_grad,
        final_gain_grad,
        final_shift_grad,
    ) = row_grads
    d_text = d_ctx[:n_text].reshape(text_shape)
    d_patch = d_ctx[n_text:].reshape(patch_shape)
    home_d_text = lax.all_to_all(d_text, "wide", split_axis=0, concat_axis=2, tiled=True)
    home_d_patch = lax.all_to_all(d_patch, "narrow", split_axis=1, concat_axis=2, tiled=True)
    home_d_ctx = jnp.concatenate([home_d_text, home_d_patch], axis=2).reshape(home_pages, seq, dim)
    d_qkv, g_line, g_width, g_height = lax.map(
        partial(page_back, tables=tables),
        (home_qkv, key_valid, line_home, width_home, height_home, log_total, home_d_ctx),
    )
    line_table_grad = jnp.sum(g_line, axis=0)
    width_table_grad = jnp.sum(g_width, axis=0)
    height_table_grad = jnp.sum(g_height, axis=0)
    d_qkv = d_qkv.reshape(home_pages, 1, seq, 3 * dim)
    back_text = lax.all_to_all(d_qkv[:, :, :TEXT], "wide", split_axis=2, concat_axis=0, tiled=True)
    back_patch = lax.all_to_all(
        d_qkv[:, :, TEXT:], "narrow", split_axis=2, concat_axis=1, tiled=True
    )
    dqkv_rows = jnp.concatenate(
        [back_text.reshape(-1, 3 * dim), back_patch.reshape(-1, 3 * dim)], axis=0
    )
    joined_grad = inner(rows_in, dqkv_rows)
    query_weight_grad = joined_grad[:, :dim]
    key_weight_grad = joined_grad[:, dim : 2 * dim]
    value_weight_grad = joined_grad[:, 2 * dim :]
    qkv_sums = jnp.sum(dqkv_rows.astype(jnp.float32), axis=0)
    query_bias_grad = qkv_sums[:dim]
    value_bias_grad = qkv_sums[2 * dim :]
    d_rows = (d_mid + against(dqkv_rows, joined_weight)).astype(jnp.bfloat16)
    text_out = final_low[:n_text].reshape(text_shape)
    patch_out = final_low[n_text:].reshape(patch_shape)
    text_grad = d_rows[:n_text].reshape(text_shape)
    patch_grad = d_rows[n_text:].reshape(patch_shape)
    (
        query_weight_grad,
        query_bias_grad,
        key_weight_grad,
        value_weight_grad,
        value_bias_grad,
        output_weight_grad,
        output_bias_grad,
        norm_gain_grad,
        norm_shift_grad,
        up_weight_grad,
        up_bias_grad,
        down_weight_grad,
        down_bias_grad,
        final_gain_grad,
        final_shift_grad,
        line_table_grad,
        width_table_grad,
        height_table_grad,
    ) = lax.psum(
        (
            query_weight_grad,
            query_bias_grad,
            key_weight_grad,
            value_weight_grad,
            value_bias_grad,
            output_weight_grad,
            output_bias_grad,
            norm_gain_grad,
            norm_shift_grad,
            up_weight_grad,
            up_bias_grad,
            down_weight_grad,
            down_bias_grad,
            final_gain_grad,
            final_shift_grad,
            line_table_grad,
            width_table_grad,
            height_table_grad,
        ),
        ("wide", "narrow"),
    )
    return (
        text_out,
        patch_out,
        text_grad,
        patch_grad,
        query_weight_grad,
        query_bias_grad,
        key_weight_grad,
        value_weight_grad,
        value_bias_grad,
        output_weight_grad,
        output_bias_grad,
        norm_gain_grad,
        norm_shift_grad,
        up_weight_grad,
        up_bias_grad,
        down_weight_grad,
        down_bias_grad,
        final_gain_grad,
        final_shift_grad,
        line_table_grad,
        width_table_grad,
        height_table_grad,
    )


def solution(mesh):
    in_specs = (
        P(None, "narrow", "wide", None),
        P("wide", None, "narrow", None),
        P("wide", "narrow"),
        P("wide", "narrow"),
        P("wide", "narrow", None),
        P("wide", "narrow", None),
        P("wide", "narrow", None),
        P(),
        P(),
        P(),
        P(),
        P(),
        P(),
        P(),
        P(),
        P(),
        P(),
        P(),
        P(),
        P(),
        P(),
        P(),
        P(),
        P(),
        P(),
        P(None, "narrow", "wide", None),
        P("wide", None, "narrow", None),
    )
    out_specs = (
        P(None, "narrow", "wide", None),
        P("wide", None, "narrow", None),
        P(None, "narrow", "wide", None),
        P("wide", None, "narrow", None),
        P(),
        P(),
        P(),
        P(),
        P(),
        P(),
        P(),
        P(),
        P(),
        P(),
        P(),
        P(),
        P(),
        P(),
        P(),
        P(),
        P(),
        P(),
    )
    return jax.shard_map(body, mesh=mesh, in_specs=in_specs, out_specs=out_specs, check_vma=False)
```

profile of v0, /device:TPU:0, one launch (start us, length us, event | category | flops | bytes accessed | tf_op | source)
XLA Modules:
  0.0 1759.5 jit_solution(11683179011082448149)
XLA Ops:
  27.8 26.0 %all-to-all-done = bf16[8,1,64,2304]{3,2,1,0:T(8,128)(2,1)S(1)} async-done(((bf16[8,1,64,2304]{3,2,1,0:T(8,128)(2,1)}), bf16[8,1,64,2304]{3,2,1,0:T(8,128)(2,1)S(1)}, u32[]{:S(2)}, u32[]{:S(2)}) %all-to-all-start) | async-done | bytes 2359328 | tf_op jit(solution)/shard_map/all_to_all | solution.py:306
  68.7 47.5 %all-to-all-done.1 = bf16[1,4,144,2304]{3,2,0,1:T(8,128)(2,1)} async-done(((bf16[1,4,144,2304]{3,2,0,1:T(8,128)(2,1)}), bf16[1,4,144,2304]{3,2,0,1:T(8,128)(2,1)}, u32[]{:S(2)}, u32[]{:S(2)}) %all-to-all-start.1) | async-done | bytes 2654240 | tf_op jit(solution)/shard_map/all_to_all | solution.py:307
  136.1 273.0 %while.57 = (s32[]{:T(128)}, bf16[2,544,768]{2,1,0:T(8,128)(2,1)}, f32[2,12,544]{2,1,0:T(8,128)}, pred[1088]{0:T(1024)(128)(4,1)S(1)}, bf16[2,544,12,64]{1,3,2,0...) while((s32[]{:T(128)}, bf16[2,544,768]{2,1,0:T(8,128)(2,1)}, ...), condition=%wide.region_3.4_spmd, body=%wide.region_0.3_spmd.sunk | while | flops 12478466048 | bytes 276147296 | solution.py:113
  188.5 16.3 fusion.205
  204.7 16.3 fusion.204
  221.0 32.2 %fusion.206 = (f32[12,544]{1,0:T(8,128)S(1)}, f32[12,544,1088]{2,1,0:T(8,128)}) fusion(f32[12,544,1088]{2,1,0:T(8,128)} %fusion.204, f32[12,544,1088]{2,1,0:T(8,128)} %fusion.205, bf16[1088,12,64]{0,2,1:T(8,128)(2,1)} %get-tuple-element.1107, bf16[2,544,12,64]{1,3,2,0:T(8,128)(2,1)} %get-tuple-element.1106, s32[]{:T(128)} %get-tuple-element.1087, ...), kind=kOutput, calls=%fused_computation.196.clone.1 | convolution fusion | flops 944621184 | bytes 91352128 | tf_op jit(solution)/shard_map/while/body/eval_jaxpr/while/body/eval_jaxpr/qhd,khd->hqk/dot_general | solution.py:72
  253.2 12.1 exponential_reduce_fusion.2
  265.3 13.1 fusion.207
  316.3 16.2 fusion.205
  332.6 16.3 fusion.204
  348.8 32.2 %fusion.206 = (f32[12,544]{1,0:T(8,128)S(1)}, f32[12,544,1088]{2,1,0:T(8,128)}) fusion(f32[12,544,1088]{2,1,0:T(8,128)} %fusion.204, f32[12,544,1088]{2,1,0:T(8,128)} %fusion.205, bf16[1088,12,64]{0,2,1:T(8,128)(2,1)} %get-tuple-element.1107, bf16[2,544,12,64]{1,3,2,0:T(8,128)(2,1)} %get-tuple-element.1106, s32[]{:T(128)} %get-tuple-element.1087, ...), kind=kOutput, calls=%fused_computation.196.clone.1 | convolution fusion | flops 944621184 | bytes 91352128 | tf_op jit(solution)/shard_map/while/body/eval_jaxpr/while/body/eval_jaxpr/qhd,khd->hqk/dot_general | solution.py:72
  381.0 12.1 exponential_reduce_fusion.2
  393.2 13.1 fusion.207
  450.7 17.2 all-to-all-done.3
  476.2 36.9 %multiply_convert_fusion.2 = (bf16[1088,3072]{1,0:T(8,128)(2,1)S(1)}, f32[1088,3072]{1,0:T(8,128)}, f32[1088,3072]{1,0:T(8,128)}) fusion(f32[3072]{0:T(1024)S(1)} %copy-done.79, bf16[768,3072]{1,0:T(8,128)(2,1)S(1)} %bitcast.334, f32[1088,768]{1,0:T(8,128)S(1)} %get-tuple-element.833, f32[768]{0:T(1024)S(1)} %copy-done.55, f32[768]{0:T(1024)S(1)} %copy-done.53, ...), kind=kOutput, calls=%fused_computation.109 | convolution fusion | flops 5358600192 | bytes 41511424 | tf_op jit(solution)/shard_map/dot_general | solution.py:209
  529.9 19.8 %convert_reduce_fusion = (f32[3072]{0:T(1024)}, bf16[1088,3072]{1,0:T(8,128)(2,1)}) fusion(f32[1088,3072]{1,0:T(8,128)} %get-tuple-element.812, f32[1088,3072]{1,0:T(8,128)} %get-tuple-element.834, bf16[1088,768]{1,0:T(8,128)(2,1)} %get-tuple-element.804, bf16[3072,768]{1,0:T(8,128)(2,1)} %param.49), kind=kOutput, calls=%fused_computation.107 | convolution fusion | flops 5187302400 | bytes 39825408 | tf_op jit(solution)/shard_map/dot_general | solution.py:31
  549.7 12.4 multiply_reduce_fusion.1
  573.7 10.5 all-to-all-done.4
  587.7 19.6 %all-to-all-done.5 = bf16[1,4,144,768]{3,2,0,1:T(8,128)(2,1)S(1)} async-done(((bf16[1,4,144,768]{3,2,0,1:T(8,128)(2,1)}), bf16[1,4,144,768]{3,2,0,1:T(8,128)(2,1)S(1)}, u32[]{:S(2)}, u32[]{:S(2)}) %all-to-all-start.5) | async-done | bytes 884768 | tf_op jit(solution)/shard_map/all_to_all | solution.py:342
  609.9 484.1 %while.58 = (s32[]{:T(128)}, f32[1088,12,64]{0,2,1:T(8,128)}, f32[1088,12,64]{0,2,1:T(8,128)}, f32[33,12]{0,1:T(8,128)}, f32[65,12]{0,1:T(8,128)S(1)}, /*index=5...) while((s32[]{:T(128)}, f32[1088,12,64]{0,2,1:T(8,128)}, ...), condition=%wide.region_14.15_spmd.clone, body=%wide.region_12.14_spmd.clone.sunk | while | flops 21249351680 | bytes 609365952 | solution.py:180
  647.4 16.5 fusion.232
  663.9 16.2 fusion.233
  682.4 15.6 fusion.228
  698.1 40.2 %multiply_reduce_fusion.6 = (f32[12,544]{1,0:T(8,128)S(1)}, f32[12,544,1088]{2,1,0:T(8,128)}) fusion(f32[12,544,1088]{2,1,0:T(8,128)} %fusion.228, f32[12,544]{1,0:T(8,128)S(1)} %dynamic-slice_bitcast_fusion.2, f32[12,544,1088]{2,1,0:T(8,128)} %fusion.232, f32[12,544,1088]{2,1,0:T(8,128)} %fusion.233, bf16[1088,12,64]{0,2,1:T(8,128)(2,1)S(1)} %copy-done.4, ...), kind=kOutput, calls=%fused_computation.41.clone.2 | convolution fusion | flops 958826112 | bytes 116461056 | tf_op jit(solution)/shard_map/while/body/eval_jaxpr/while/body/eval_jaxpr/qhd,khd->hqk/dot_general | solution.py:72
  738.3 24.8 %multiply_convert_fusion.5 = bf16[12,544,1088]{2,1,0:T(8,128)(2,1)} fusion(f32[12,544,1088]{2,1,0:T(8,128)} %get-tuple-element.1068, f32[12,544,1088]{2,1,0:T(8,128)} %fusion.228, f32[12,544]{1,0:T(8,128)S(1)} %get-tuple-element.1069), kind=kLoop, calls=%fused_computation.40.clone.1 | loop fusion | flops 21307392 | bytes 71050752 | tf_op jit(solution)/shard_map/while/body/eval_jaxpr/while/body/eval_jaxpr/convert_element_type | solution.py:136
  763.0 9.7 fusion.236
  784.7 11.6 fusion.239
  802.1 11.6 fusion.240
  834.5 14.0 fusion.235
  865.0 9.0 fusion.230
  886.3 16.4 fusion.232
  902.7 16.2 fusion.233
  921.0 15.6 fusion.228
  936.7 40.2 %multiply_reduce_fusion.6 = (f32[12,544]{1,0:T(8,128)S(1)}, f32[12,544,1088]{2,1,0:T(8,128)}) fusion(f32[12,544,1088]{2,1,0:T(8,128)} %fusion.228, f32[12,544]{1,0:T(8,128)S(1)} %dynamic-slice_bitcast_fusion.2, f32[12,544,1088]{2,1,0:T(8,128)} %fusion.232, f32[12,544,1088]{2,1,0:T(8,128)} %fusion.233, bf16[1088,12,64]{0,2,1:T(8,128)(2,1)S(1)} %copy-done.4, ...), kind=kOutput, calls=%fused_computation.41.clone.2 | convolution fusion | flops 958826112 | bytes 116461056 | tf_op jit(solution)/shard_map/while/body/eval_jaxpr/while/body/eval_jaxpr/qhd,khd->hqk/dot_general | solution.py:72
  976.9 24.8 %multiply_convert_fusion.5 = bf16[12,544,1088]{2,1,0:T(8,128)(2,1)} fusion(f32[12,544,1088]{2,1,0:T(8,128)} %get-tuple-element.1068, f32[12,544,1088]{2,1,0:T(8,128)} %fusion.228, f32[12,544]{1,0:T(8,128)S(1)} %get-tuple-element.1069), kind=kLoop, calls=%fused_computation.40.clone.1 | loop fusion | flops 21307392 | bytes 71050752 | tf_op jit(solution)/shard_map/while/body/eval_jaxpr/while/body/eval_jaxpr/convert_element_type | solution.py:136
  1001.7 9.7 fusion.236
  1023.3 11.6 fusion.239
  1040.8 11.6 fusion.240
  1073.2 15.1 fusion.235
  1114.2 14.9 reduce.23
  1149.3 58.3 %reduce.22 = bf16[576,2304]{1,0:T(8,128)(2,1)} reduce(bf16[576,1,1,2304]{3,2,1,0:T(2,128)(2,1)} %bitcast.290, bf16[]{:T(256)} %broadcast.395), dimensions={1,2}, to_apply=%bitcast.181.reduce_sub_computation | reduce | bytes 5308418
  1221.7 11.0 fusion.115
  1232.8 9.6 fusion.101
  1249.7 28.1 %all-to-all-done.7 = bf16[4,2,165888]{2,1,0:T(2,128)(2,1)} async-done(((bf16[4,2,165888]{2,1,0:T(2,128)(2,1)}), bf16[4,2,165888]{2,1,0:T(2,128)(2,1)}, u32[]{:S(2)}, u32[]{:S(2)}) %all-to-all-start.7) | async-done | bytes 2654240 | tf_op jit(solution)/shard_map/all_to_all | solution.py:353
  1300.4 9.0 fusion.88
  1312.5 42.0 %all-reduce = (f32[768]{0:T(1024)}, f32[768]{0:T(1024)}, f32[768]{0:T(1024)}, f32[768]{0:T(1024)}, f32[768]{0:T(1024)}, /*index=5*/f32[3072]{0:T(1024)}, f32[768...) all-reduce(f32[768]{0:T(1024)S(1)} %get-tuple-element.831, ...), channel_id=1, replica_groups=mesh['wide'=8,'narrow'=4] {'wide','narrow'}, use_global_device_ids=true, to_apply=%region_17.18 | all-reduce | flops 11172 | bytes 89376 | tf_op jit(solution)/shard_map/psum | solution.py:390
  1354.6 377.1 %all-reduce.4.cloned.1.call-done = (f32[768,768]{1,0:T(8,128)}, f32[768,768]{1,0:T(8,128)}, f32[768,768]{1,0:T(8,128)}, f32[768,768]{1,0:T(8,128)}, f32[768,3072]{1,0:T(8,128)}, /*index=5*/f32[3072,768]{1,0:T(8,128)}) async-done(((f32[768,768]{1,0:T(8,128)}, f32[768,768]{1,0:T(8,128)}, f32[768,768]{1,0:T(8,128)}, f32[768,768]{1,0:T(8,128)}, f32[768,3072]{1,0:T(8,128)}, /*index=5*/f32[3072,768]{1,0:T(8,128)}), ...) | async-done | bytes 28311568 | tf_op jit(solution)/shard_map/psum | solution.py:390
  1739.4 9.3 copy.319
  (431 shorter events, 459.0 us)
Async XLA Ops:
  7.2 463.4 %copy-start = (bf16[768,768]{1,0:T(8,128)(2,1)S(1)}, bf16[768,768]{1,0:T(8,128)(2,1)}, u32[]{:S(2)}) copy-start(bf16[768,768]{1,0:T(8,128)(2,1)} %param.43) | copy-start | bytes 3538948
  19.2 34.6 %all-to-all-start = ((bf16[8,1,64,2304]{3,2,1,0:T(8,128)(2,1)}), bf16[8,1,64,2304]{3,2,1,0:T(8,128)(2,1)S(1)}, u32[]{:S(2)}, u32[]{:S(2)}) async-start(bf16[8,1,64,2304]{3,2,1,0:T(8,128)(2,1)} %bitcast.305), calls=%async_computation | async-start | bytes 4718592 | tf_op jit(solution)/shard_map/all_to_all | solution.py:306
  27.8 30.9 %copy-start.68 = (s32[1,1,1088]{2,1,0:T(1,128)S(1)}, s32[1,1,1088]{2,1,0:T(1,128)}, u32[]{:S(2)}) copy-start(s32[1,1,1088]{2,1,0:T(1,128)} %param.36) | copy-start | bytes 13060
  27.8 31.5 %copy-start.69 = (s32[1,1,1088]{2,1,0:T(1,128)S(1)}, s32[1,1,1088]{2,1,0:T(1,128)}, u32[]{:S(2)}) copy-start(s32[1,1,1088]{2,1,0:T(1,128)} %param.37) | copy-start | bytes 13060
  53.9 62.3 %all-to-all-start.1 = ((bf16[1,4,144,2304]{3,2,0,1:T(8,128)(2,1)}), bf16[1,4,144,2304]{3,2,0,1:T(8,128)(2,1)}, u32[]{:S(2)}, u32[]{:S(2)}) async-start(bf16[1,4,144,2304]{3,2,0,1:T(8,128)(2,1)} %bitcast.295), calls=%async_computation.1 | async-start | bytes 5308416 | tf_op jit(solution)/shard_map/all_to_all | solution.py:307
  253.2 12.1 copy-start.39
  253.2 12.1 copy-start.5
  265.3 13.1 copy-start.40
  381.0 12.1 copy-start.39
  381.0 12.1 copy-start.5
  393.1 13.1 copy-start.40
  409.1 14.3 copy-start.34
  409.1 14.3 copy-start.50
  410.3 18.2 %copy-start.23 = (bf16[2,544,768]{2,1,0:T(8,128)(2,1)S(1)}, bf16[2,544,768]{2,1,0:T(8,128)(2,1)}, u32[]{:S(2)}) copy-start(bf16[2,544,768]{2,1,0:T(8,128)(2,1)} %get-tuple-element.280) | copy-start | bytes 5013508
  423.4 17.7 %all-to-all-start.2 = ((bf16[8,2,24576]{2,1,0:T(2,128)(2,1)}), bf16[8,2,24576]{2,1,0:T(2,128)(2,1)}, u32[]{:S(2)}, u32[]{:S(2)}) async-start(bf16[8,2,24576]{2,1,0:T(2,128)(2,1)} %reshape.579), calls=%async_computation.2 | async-start | bytes 1572864 | tf_op jit(solution)/shard_map/all_to_all | solution.py:321
  441.1 26.8 %all-to-all-start.3 = ((bf16[4,2,55296]{2,1,0:T(2,128)(2,1)}), bf16[4,2,55296]{2,1,0:T(2,128)(2,1)}, u32[]{:S(2)}, u32[]{:S(2)}) async-start(bf16[4,2,55296]{2,1,0:T(2,128)(2,1)} %reshape.577), calls=%async_computation.3 | async-start | bytes 1769472 | tf_op jit(solution)/shard_map/all_to_all | solution.py:322
  449.7 20.9 %copy-start.80 = (f32[768]{0:T(1024)S(1)}, f32[768]{0:T(1024)}, u32[]{:S(2)}) copy-start(f32[768]{0:T(1024)} %param.44) | copy-start | bytes 9220
  470.7 42.4 %slice-start.10 = ((s8[4718592]{0:T(1024)(128)(4,1)}), s8[4194304]{0:T(1024)(128)(4,1)S(1)}, s32[]{:S(2)}) async-start(s8[4718592]{0:T(1024)(128)(4,1)} %bitcast.331), calls=%async_computation.19 | async-start | bytes 8388608
  474.5 87.7 %copy-start.11 = (f32[1088,768]{1,0:T(8,128)}, f32[1088,768]{1,0:T(8,128)S(1)}, u32[]{:S(2)}) copy-start(f32[1088,768]{1,0:T(8,128)S(1)} %get-tuple-element.833) | copy-start | bytes 10027012
  474.5 87.6 %copy-start.43 = (f32[1088]{0:T(1024)}, f32[1088]{0:T(1024)S(1)}, u32[]{:S(2)}) copy-start(f32[1088]{0:T(1024)S(1)} %broadcast_multiply_fusion.1) | copy-start | bytes 13060
  476.1 86.0 %copy-start.48 = (f32[1088]{0:T(1024)}, f32[1088]{0:T(1024)S(1)}, u32[]{:S(2)}) copy-start(f32[1088]{0:T(1024)S(1)} %fusion.94) | copy-start | bytes 13060
  476.1 36.9 %slice-start.11 = ((s8[4718592]{0:T(1024)(128)(4,1)}), s8[524288]{0:T(1024)(128)(4,1)S(1)}, s32[]{:S(2)}) async-start(s8[4718592]{0:T(1024)(128)(4,1)} %bitcast.331), calls=%async_computation.20 | async-start | bytes 1048576
  476.2 36.9 %copy-start.81 = (f32[768]{0:T(1024)S(1)}, f32[768]{0:T(1024)}, u32[]{:S(2)}) copy-start(f32[768]{0:T(1024)} %param.50) | copy-start | bytes 9220
  549.7 12.4 copy-start.52
  567.7 16.4 all-to-all-start.4
  571.6 38.3 %copy-start.35 = (pred[1088]{0:T(1024)(128)(4,1)S(1)}, pred[1088]{0:T(1024)(128)(4,1)}, u32[]{:S(2)}) copy-start(pred[1088]{0:T(1024)(128)(4,1)} %copy-done.34) | copy-start | bytes 3268
  584.2 23.2 %all-to-all-start.5 = ((bf16[1,4,144,768]{3,2,0,1:T(8,128)(2,1)}), bf16[1,4,144,768]{3,2,0,1:T(8,128)(2,1)S(1)}, u32[]{:S(2)}, u32[]{:S(2)}) async-start(bf16[1,4,144,768]{3,2,0,1:T(8,128)(2,1)} %bitcast.34), calls=%async_computation.5 | async-start | bytes 1769472 | tf_op jit(solution)/shard_map/all_to_all | solution.py:342
  682.4 15.7 copy-start.41
  682.4 15.7 copy-start.4
  682.4 15.7 copy-start.9
  802.1 11.6 slice-start.4
  802.1 11.6 copy-start.45
  813.7 11.5 copy-start.66
  813.8 11.5 slice-start
  921.0 15.7 copy-start.41
  921.0 15.7 copy-start.4
  921.0 15.7 copy-start.9
  1040.8 11.6 slice-start.4
  1040.8 11.6 copy-start.45
  1052.4 11.9 copy-start.66
  1052.5 11.8 slice-start
  1132.4 79.5 %all-to-all-start.6 = ((bf16[8,2,73728]{2,1,0:T(2,128)(2,1)}), bf16[8,2,73728]{2,1,0:T(2,128)(2,1)S(1)}, u32[]{:S(2)}, u32[]{:S(2)}) async-start(bf16[8,2,73728]{2,1,0:T(2,128)(2,1)} %reshape.583), calls=%async_computation.6 | async-start | bytes 4718592 | tf_op jit(solution)/shard_map/all_to_all | solution.py:352
  1211.9 65.9 %all-to-all-start.7 = ((bf16[4,2,165888]{2,1,0:T(2,128)(2,1)}), bf16[4,2,165888]{2,1,0:T(2,128)(2,1)}, u32[]{:S(2)}, u32[]{:S(2)}) async-start(bf16[4,2,165888]{2,1,0:T(2,128)(2,1)} %reshape.581), calls=%async_computation.7 | async-start | bytes 5308416 | tf_op jit(solution)/shard_map/all_to_all | solution.py:353
  1216.6 515.1 %all-reduce.4.cloned.1.call-start = ((), (), s32[]{:S(2)}) async-start(), calls=%async_computation.8 | async-start | bytes 56623104 | tf_op jit(solution)/shard_map/psum | solution.py:390
  1216.7 16.1 slice-start.8
  1221.7 11.1 copy-start.49
  1221.7 11.1 copy-start.54
  1221.7 11.1 copy-start.56
  (83 other events, 423.7 us)
Sparse Core Ops, SparseCore 0:
  1296.3 435.3 all-reduce.3
where the time goes:
time: 1770 us; the launch traced here: 1760 us
  matrix products  670 us (38%)
  waiting for transfers between devices  527 us (30%)
  local copies, waits for them, and re-layouts  252 us (14%)
  other arithmetic  191 us (11%)
  blocking collectives  42 us (2%)
  starting transfers between devices  36.9 us (2%)
  loops' own time  24.3 us (1%)
    psum x1, waiting for transfers between devices, body(): lax.psum((query_weight_grad, query_bias_grad, key_weight_grad, value_weig...  377 us
    dot_general x4, matrix products, block_scores(): jnp.einsum('qhd,khd->hqk', query, keys, preferred_element_type=jnp.float32)  145 us
    unnamed x16, other arithmetic  90 us
    dot_general x12, matrix products, bucket_bias(): nearby.append(jnp.einsum('qub,bh->hqu', select, table, precision=HIGH))  83.4 us
    unnamed x165, local copies, waits for them, and re-layouts  72.3 us
    dot_general x4, matrix products, bucket_bias(): jnp.einsum('hqu,ku->hqk', high_part, key_hot, preferred_element_type=jnp....  65.4 us
    dot_general x4, matrix products, bucket_bias(): jnp.einsum('hqu,ku->hqk', low_part, key_hot, preferred_element_type=jnp.f...  65 us
    dot_general x12, local copies, waits for them, and re-layouts, bucket_bias(): nearby.append(jnp.einsum('qub,bh->hqu', select, table, precision=HIGH))  56.1 us
  transfers between devices with their start and end apart: 9, of which 8 were waited for; matrix products, arithmetic and copies ran while one was open for 9% of the time, Pallas kernels for 0%

commit v1 on v0

v1 whole, which is shorter than its diff:
```python
from functools import partial

import jax
import jax.numpy as jnp
from jax import lax
from jax.experimental import pallas as pl
from jax.experimental.pallas import tpu as pltpu
from jax.sharding import PartitionSpec as P

HEADS = 12
TEXT = 512
PATCH = 576
SMALL_PATCH = 196
BF = jnp.bfloat16
F32 = jnp.float32
VMEM_BYTES = 60 * 2**20


def mm(left, right):
    return lax.dot_general(left, right, (((1,), (0,)), ((), ())), preferred_element_type=F32)


def inner(left, right):
    return lax.dot_general(left, right, (((0,), (0,)), ((), ())), preferred_element_type=F32)


def against(left, right):
    return lax.dot_general(left, right, (((1,), (1,)), ((), ())), preferred_element_type=F32)


def layer_norm(rows, gain, shift):
    mean = jnp.mean(rows, axis=-1, keepdims=True)
    centred = rows - mean
    spread = jnp.mean(centred * centred, axis=-1, keepdims=True)
    return centred * lax.rsqrt(spread + 1e-05) * gain + shift


def attend_kernel(
    k_ref, qt_ref, vt_ref, hot_ref, mask_ref, hott_ref, line_ref, width_ref, height_ref,
    exp_ref, ctx_ref, inv_ref, keys, queries, values,
):
    seq = k_ref.shape[0]
    lanes = qt_ref.shape[1]

    @pl.when(pl.program_id(0) == 0)
    def _():
        keys[:, 0:320] = hot_ref[0:seq, :]
        keys[:, 320:640] = hot_ref[0:seq, :]
        values[64:80, :] = jnp.ones((16, seq), BF)

    lane = lax.broadcasted_iota(jnp.int32, (seq, 128), 1)
    for h in range(2):
        mine = (lane < 64) if h == 0 else (lane >= 64)
        own, other = (640, 704) if h == 0 else (704, 640)
        keys[:, 640:768] = jnp.where(
            mine, k_ref[...].astype(F32), mask_ref[...].astype(F32)
        ).astype(BF)
        queries[own : own + 64, :] = qt_ref[h * 64 : h * 64 + 64, :]
        queries[other : other + 64, :] = jnp.ones((64, lanes), BF)
        values[0:64, :] = vt_ref[h * 64 : h * 64 + 64, :]
        near = mm(line_ref[h], hott_ref[0:64, :]).astype(BF)
        queries[0:64, :] = near[0:64]
        queries[320:384, :] = near[64:128]
        near = mm(width_ref[h], hott_ref[64:192, :]).astype(BF)
        queries[64:192, :] = near[0:128]
        queries[384:512, :] = near[128:256]
        near = mm(height_ref[h], hott_ref[192:320, :]).astype(BF)
        queries[192:320, :] = near[0:128]
        queries[512:640, :] = near[128:256]
        scores = mm(keys[...], queries[...])
        peak = jnp.max(scores, axis=0, keepdims=True)
        weights = jnp.exp(scores - peak).astype(BF)
        exp_ref[h] = weights
        ctx = mm(values[...], weights)
        inverse = 1.0 / ctx[64:65]
        inv_ref[h] = inverse
        ctx_ref[h * 64 : h * 64 + 64, :] = (ctx[0:64] * inverse).astype(BF)


def attend(k, q_t, v_t, hot, mask, hot_t, line, width, height):
    seq = k.shape[0]
    dim, lanes = q_t.shape

    def whole(a):
        return pl.BlockSpec(a.shape, lambda p: (0,) * a.ndim)

    def pair(a):
        return pl.BlockSpec((2,) + a.shape[1:], lambda p: (p, 0, 0))

    return pl.pallas_call(
        attend_kernel,
        grid=(HEADS // 2,),
        in_specs=[
            pl.BlockSpec((seq, 128), lambda p: (0, p)),
            pl.BlockSpec((128, lanes), lambda p: (p, 0)),
            pl.BlockSpec((128, seq), lambda p: (p, 0)),
            whole(hot),
            whole(mask),
            whole(hot_t),
            pair(line),
            pair(width),
            pair(height),
        ],
        out_specs=[
            pl.BlockSpec((2, seq, lanes), lambda p: (p, 0, 0)),
            pl.BlockSpec((128, lanes), lambda p: (p, 0)),
            pl.BlockSpec((2, 1, lanes), lambda p: (p, 0, 0)),
        ],
        out_shape=[
            jax.ShapeDtypeStruct((HEADS, seq, lanes), BF),
            jax.ShapeDtypeStruct((dim, lanes), BF),
            jax.ShapeDtypeStruct((HEADS, 1, lanes), F32),
        ],
        scratch_shapes=[
            pltpu.VMEM((seq, 768), BF),
            pltpu.VMEM((768, lanes), BF),
            pltpu.VMEM((80, seq), BF),
        ],
        compiler_params=pltpu.CompilerParams(vmem_limit_bytes=VMEM_BYTES),
    )(k, q_t, v_t, hot, mask, hot_t, line, width, height)


def attend_back_kernel(
    exp_ref, ctx_ref, v_ref, kt_ref, q_ref, dc_ref, dct_ref, hot_ref, hott_ref,
    dqt_ref, dk_ref, dv_ref, gwidth_ref, gheight_ref, gline_ref, values, dctx, lefts, rights, ds,
):
    seq = v_ref.shape[0]
    lanes = dct_ref.shape[1]

    @pl.when(pl.program_id(0) == 0)
    def _():
        for h in range(2):
            lefts[h, 64:192, :] = hott_ref[64:192, 0:seq]
            rights[h, :, 128:256] = hot_ref[:, 192:320]

    lane = lax.broadcasted_iota(jnp.int32, (seq, 128), 1)
    query_lane = lax.broadcasted_iota(jnp.int32, (lanes, 128), 1)
    row = lax.broadcasted_iota(jnp.int32, (64, lanes), 0)
    line_hot = jnp.concatenate([hot_ref[:, 0:64], hot_ref[:, 0:64]], axis=1).astype(F32)
    results = []
    for h in range(2):
        mine = (lane < 64) if h == 0 else (lane >= 64)
        query_mine = (query_lane < 64) if h == 0 else (query_lane >= 64)
        own, other = (0, 64) if h == 0 else (64, 0)
        part = slice(h * 64, h * 64 + 64)
        values[h] = jnp.where(mine, v_ref[...].astype(F32), 1.0).astype(BF)
        d_rows = dct_ref[part, :]
        delta = -jnp.sum(
            d_rows.astype(F32) * ctx_ref[part, :].astype(F32), axis=0, keepdims=True
        )
        high = delta.astype(BF).astype(F32)
        extra = jnp.where(row == 0, high, jnp.where(row == 1, delta - high, 0.0))
        dctx[h, own : own + 64, :] = d_rows
        dctx[h, other : other + 64, :] = extra.astype(BF)
        lefts[h, 0:64, :] = kt_ref[part, :]
        rights[h, :, 0:128] = jnp.where(query_mine, q_ref[...].astype(F32), line_hot).astype(BF)
        d_scores = mm(values[h], dctx[h])
        ds[h] = (exp_ref[h].astype(F32) * d_scores).astype(BF)
        by_query = mm(lefts[h], ds[h])
        dqt_ref[part, :] = (by_query[0:64] * 0.125).astype(BF)
        gwidth_ref[h] = mm(by_query[64:192].astype(BF), hot_ref[:, 64:192])
        by_key = mm(ds[h], rights[h])
        near = mm(hott_ref[0:64, 0:seq], by_key[:, 0:128].astype(BF))
        gline_ref[h] = near[:, 64:128] if h == 0 else near[:, 0:64]
        gheight_ref[h] = mm(hott_ref[192:320, 0:seq], by_key[:, 128:256].astype(BF))
        results.append((by_key[:, 0:128], mm(exp_ref[h], dc_ref[...])))
    dk_ref[...] = jnp.where(lane < 64, results[0][0], results[1][0]).astype(BF)
    dv_ref[...] = jnp.where(lane < 64, results[0][1], results[1][1]).astype(BF)


def attend_back(exps, ctx_t, v, k_t, q, d_ctx, d_ctx_t, hot, hot_t):
    seq, dim = v.shape
    lanes = d_ctx_t.shape[1]

    def whole(a):
        return pl.BlockSpec(a.shape, lambda p: (0,) * a.ndim)

    def columns(rows):
        return pl.BlockSpec((rows, 128), lambda p: (0, p))

    def rows(length):
        return pl.BlockSpec((128, length), lambda p: (p, 0))

    def pair(*shape):
        return pl.BlockSpec((2,) + shape, lambda p: (p, 0, 0))

    shape = jax.ShapeDtypeStruct
    return pl.pallas_call(
        attend_back_kernel,
        grid=(HEADS // 2,),
        in_specs=[
            pair(seq, lanes),
            rows(lanes),
            columns(seq),
            rows(seq),
            columns(lanes),
            columns(lanes),
            rows(lanes),
            whole(hot),
            whole(hot_t),
        ],
        out_specs=[
            rows(lanes),
            columns(seq),
            columns(seq),
            pair(128, 128),
            pair(128, 128),
            pair(64, 64),
        ],
        out_shape=[
            shape((dim, lanes), BF),
            shape((seq, dim), BF),
            shape((seq, dim), BF),
            shape((HEADS, 128, 128), F32),
            shape((HEADS, 128, 128), F32),
            shape((HEADS, 64, 64), F32),
        ],
        scratch_shapes=[
            pltpu.VMEM((2, seq, 128), BF),
            pltpu.VMEM((2, 128, lanes), BF),
            pltpu.VMEM((2, 192, seq), BF),
            pltpu.VMEM((2, lanes, 256), BF),
            pltpu.VMEM((2, seq, lanes), BF),
        ],
        compiler_params=pltpu.CompilerParams(vmem_limit_bytes=VMEM_BYTES),
    )(exps, ctx_t, v, k_t, q, d_ctx, d_ctx_t, hot, hot_t)


def bucket_select(table):
    reach = (table.shape[0] - 1) // 2
    spots = jnp.arange(4 * reach, dtype=jnp.int32)
    bucket = jnp.clip(spots[None, :] - spots[:, None], -reach, reach) + reach
    return bucket[None] == jnp.arange(2 * reach + 1, dtype=jnp.int32)[:, None, None]


def spread_table(table):
    span = 2 * (table.shape[0] - 1)
    high = table.astype(BF)
    low = (table - high.astype(F32)).astype(BF)
    both = jnp.stack([high, low], axis=2).reshape(table.shape[0], -1)
    spread = lax.dot_general(
        both,
        bucket_select(table).astype(BF).reshape(table.shape[0], -1),
        (((0,), (0,)), ((), ())),
        preferred_element_type=F32,
    )
    return spread.astype(BF).reshape(HEADS, 2 * span, span)


def gather_table(grads, table):
    select = bucket_select(table).astype(F32).reshape(table.shape[0], -1)
    return lax.dot_general(
        select,
        grads.reshape(HEADS, -1),
        (((1,), (1,)), ((), ())),
        precision=lax.Precision.HIGHEST,
        preferred_element_type=F32,
    )


def row_pass(rows_in, ctx_t, cot, inverse, weights):
    (
        output_weight,
        output_bias,
        norm_gain,
        norm_shift,
        up_weight,
        up_bias,
        down_weight,
        down_bias,
        final_gain,
        final_shift,
    ) = weights
    seq = rows_in.shape[0]
    lanes = inverse.shape[2]
    attn = inner(ctx_t, output_weight)[:seq] + output_bias
    mid = rows_in.astype(F32) + attn
    normed, norm_back = jax.vjp(layer_norm, mid, norm_gain, norm_shift)
    normed_low = normed.astype(BF)
    pre = mm(normed_low, up_weight) + up_bias
    act, gelu_back = jax.vjp(partial(jax.nn.gelu, approximate=False), pre)
    act_low = act.astype(BF)
    branch = mm(act_low, down_weight) + down_bias
    final, final_back = jax.vjp(layer_norm, normed + branch, final_gain, final_shift)
    final_low = final.astype(BF)
    d_sum, final_gain_grad, final_shift_grad = final_back(cot)
    d_branch = d_sum.astype(BF)
    down_weight_grad = inner(act_low, d_branch)
    down_bias_grad = jnp.sum(d_branch.astype(F32), axis=0)
    d_act = against(d_branch, down_weight)
    (d_pre,) = gelu_back(d_act)
    d_pre_low = d_pre.astype(BF)
    up_weight_grad = inner(normed_low, d_pre_low)
    up_bias_grad = jnp.sum(d_pre_low.astype(F32), axis=0)
    d_normed = d_sum + against(d_pre_low, up_weight)
    d_mid, norm_gain_grad, norm_shift_grad = norm_back(d_normed)
    d_attn = d_mid.astype(BF)
    output_weight_grad = mm(ctx_t[:, :seq], d_attn)
    output_bias_grad = jnp.sum(d_attn.astype(F32), axis=0)
    d_attn_long = jnp.pad(d_attn, ((0, lanes - seq), (0, 0)))
    d_ctx_t = against(output_weight, d_attn_long).reshape(HEADS, -1, lanes) * inverse
    d_ctx_t = d_ctx_t.astype(BF).reshape(-1, lanes)
    grads = (
        output_weight_grad,
        output_bias_grad,
        norm_gain_grad,
        norm_shift_grad,
        up_weight_grad,
        up_bias_grad,
        down_weight_grad,
        down_bias_grad,
        final_gain_grad,
        final_shift_grad,
    )
    return (final_low, d_mid, d_ctx_t, grads)


def text_home(rows):
    pages, _, part, dim = rows.shape
    moved = lax.all_to_all(
        rows.reshape(pages, part, dim), "wide", split_axis=0, concat_axis=0, tiled=True
    )
    return moved.reshape(-1, dim)


def patch_home(rows):
    _, pages, part, dim = rows.shape
    moved = lax.all_to_all(
        rows.reshape(pages, part, dim), "narrow", split_axis=0, concat_axis=0, tiled=True
    )
    return moved.reshape(-1, dim)


def text_away(rows, shape):
    pages, _, part, dim = shape
    moved = lax.all_to_all(
        rows.reshape(pages, part, dim), "wide", split_axis=0, concat_axis=0, tiled=True
    )
    return moved.reshape(shape)


def patch_away(rows, shape):
    _, pages, part, dim = shape
    moved = lax.all_to_all(
        rows.reshape(pages, part, dim), "narrow", split_axis=0, concat_axis=0, tiled=True
    )
    return moved.reshape(shape)


def body(
    text_in,
    patch_in,
    res_class,
    text_len,
    pos_line,
    pos_x,
    pos_y,
    query_weight,
    query_bias,
    key_weight,
    value_weight,
    value_bias,
    output_weight,
    output_bias,
    norm_gain,
    norm_shift,
    up_weight,
    up_bias,
    down_weight,
    down_bias,
    final_gain,
    final_shift,
    line_table,
    width_table,
    height_table,
    cot_text,
    cot_patch,
):
    text_shape = text_in.shape
    patch_shape = patch_in.shape
    dim = text_shape[3]
    seq = TEXT + PATCH
    lanes = -(-seq // 128) * 128
    weights = (
        output_weight,
        output_bias,
        norm_gain,
        norm_shift,
        up_weight,
        up_bias,
        down_weight,
        down_bias,
        final_gain,
        final_shift,
    )
    rows_in = jnp.concatenate([text_home(text_in), patch_home(patch_in)], axis=0)
    cot = jnp.concatenate([text_home(cot_text), patch_home(cot_patch)], axis=0).astype(F32)

    line = spread_table(line_table)
    width = spread_table(width_table)
    height = spread_table(height_table)
    hots = []
    hots_t = []
    for spots, table in ((pos_line, line_table), (pos_x, width_table), (pos_y, height_table)):
        span = jnp.arange(2 * (table.shape[0] - 1), dtype=jnp.int32)
        long = jnp.pad(spots.reshape(-1), (0, lanes - seq), constant_values=-1)
        hots.append((long[:, None] == span[None, :]).astype(BF))
        hots_t.append((long[None, :] == span[:, None]).astype(BF))
    hot = jnp.concatenate(hots, axis=1)
    hot_t = jnp.concatenate(hots_t, axis=0)
    index = jnp.arange(seq, dtype=jnp.int32)
    live_patch = jnp.where(res_class.reshape(()) == 1, PATCH, SMALL_PATCH)
    valid = jnp.where(index < TEXT, index < text_len.reshape(()), index - TEXT < live_patch)
    column = jnp.arange(128, dtype=jnp.int32)
    mask = jnp.where((column[None, :] % 64 == 0) & ~valid[:, None], -1e30, 0.0).astype(BF)

    rows_long = jnp.pad(rows_in, ((0, lanes - seq), (0, 0)))
    q = ((mm(rows_long, query_weight) + query_bias) * 0.125).astype(BF)
    q_t = (
        (lax.dot_general(query_weight, rows_long, (((0,), (1,)), ((), ())), preferred_element_type=F32)
         + query_bias[:, None]) * 0.125
    ).astype(BF)
    k = mm(rows_in, key_weight).astype(BF)
    k_t = k.T
    v = (mm(rows_in, value_weight) + value_bias).astype(BF)
    v_t = v.T
    exps, ctx_t, inverse = attend(k, q_t, v_t, hot, mask, hot_t, line, width, height)
    final_low, d_mid, d_ctx_t, row_grads = row_pass(rows_in, ctx_t, cot, inverse, weights)
    d_q_t, d_k, d_v, g_width, g_height, g_line = attend_back(
        exps, ctx_t, v, k_t, q, d_ctx_t.T, d_ctx_t, hot, hot_t
    )
    d_q = d_q_t[:, :seq].T
    line_table_grad = gather_table(g_line, line_table)
    width_table_grad = gather_table(g_width, width_table)
    height_table_grad = gather_table(g_height, height_table)
    query_weight_grad = inner(rows_in, d_q)
    key_weight_grad = inner(rows_in, d_k)
    value_weight_grad = inner(rows_in, d_v)
    query_bias_grad = jnp.sum(d_q.astype(F32), axis=0)
    value_bias_grad = jnp.sum(d_v.astype(F32), axis=0)
    d_rows = (
        d_mid + against(d_q, query_weight) + against(d_k, key_weight) + against(d_v, value_weight)
    ).astype(BF)
    text_out = text_away(final_low[:TEXT], text_shape)
    patch_out = patch_away(final_low[TEXT:], patch_shape)
    text_grad = text_away(d_rows[:TEXT], text_shape)
    patch_grad = patch_away(d_rows[TEXT:], patch_shape)
    (
        output_weight_grad,
        output_bias_grad,
        norm_gain_grad,
        norm_shift_grad,
        up_weight_grad,
        up_bias_grad,
        down_weight_grad,
        down_bias_grad,
        final_gain_grad,
        final_shift_grad,
    ) = row_grads
    both = ("wide", "narrow")

    def total(grad):
        return lax.psum(grad.astype(BF), both).astype(F32)

    down_weight_grad, up_weight_grad, output_weight_grad = (
        total(down_weight_grad), total(up_weight_grad), total(output_weight_grad)
    )
    query_weight_grad, key_weight_grad, value_weight_grad = (
        total(query_weight_grad), total(key_weight_grad), total(value_weight_grad)
    )
    (
        query_bias_grad,
        value_bias_grad,
        output_bias_grad,
        norm_gain_grad,
        norm_shift_grad,
        up_bias_grad,
        down_bias_grad,
        final_gain_grad,
        final_shift_grad,
        line_table_grad,
        width_table_grad,
        height_table_grad,
    ) = lax.psum(
        (
            query_bias_grad,
            value_bias_grad,
            output_bias_grad,
            norm_gain_grad,
            norm_shift_grad,
            up_bias_grad,
            down_bias_grad,
            final_gain_grad,
            final_shift_grad,
            line_table_grad,
            width_table_grad,
            height_table_grad,
        ),
        both,
    )
    return (
        text_out,
        patch_out,
        text_grad,
        patch_grad,
        query_weight_grad,
        query_bias_grad,
        key_weight_grad,
        value_weight_grad,
        value_bias_grad,
        output_weight_grad,
        output_bias_grad,
        norm_gain_grad,
        norm_shift_grad,
        up_weight_grad,
        up_bias_grad,
        down_weight_grad,
        down_bias_grad,
        final_gain_grad,
        final_shift_grad,
        line_table_grad,
        width_table_grad,
        height_table_grad,
    )


def solution(mesh):
    text = P(None, "narrow", "wide", None)
    patch = P("wide", None, "narrow", None)
    page = P("wide", "narrow")
    spots = P("wide", "narrow", None)
    in_specs = (text, patch, page, page, spots, spots, spots) + (P(),) * 18 + (text, patch)
    out_specs = (text, patch, text, patch) + (P(),) * 18
    return jax.shard_map(body, mesh=mesh, in_specs=in_specs, out_specs=out_specs, check_vma=False)
```

time: 1770 us -> 667 us (0.38)
  matrix products: 670 us -> 146 us
  waiting for transfers between devices: 527 us -> 226 us
  local copies, waits for them, and re-layouts: 252 us -> 39.7 us
  other arithmetic: 191 us -> 42.1 us
  Pallas kernels: 0 us -> 111 us
  loops' own time: 24.3 us -> 0 us
    dot_general x46 -> x12, matrix products: 597 us -> 74 us  [the longest x5 59.1 us: mm(): lax.dot_general(left, right, (((1,), (0,)), ((), ())), preferred_element_...]
    psum x1, waiting for transfers between devices: 377 us -> 140 us  [total(): return lax.psum(grad.astype(BF), both).astype(F32)]
    pallas_call x0 -> x2, Pallas kernels: none -> 111 us  [the longest x1 58.4 us: attend_back(): pl.pallas_call(attend_back_kernel, grid=(HEADS // 2,), in_specs=[pair(seq...]
    unnamed x16 -> x5, other arithmetic: 90 us -> 2.14 us
    slice x32 -> x4, local copies, waits for them, and re-layouts: 81.4 us -> 5.03 us  [the longest x1 2.2 us: body(): patch_grad = patch_away(d_rows[TEXT:], patch_shape)]
    all_to_all x8, waiting for transfers between devices: 150 us -> 86.3 us  [the longest x2 34.3 us: text_away(): lax.all_to_all(rows.reshape(pages, part, dim), 'wide', split_axis=0, conc...]
    unnamed x165 -> x109, local copies, waits for them, and re-layouts: 72.3 us -> 15 us
    dot_general x12 -> x0, local copies, waits for them, and re-layouts: 56.1 us -> none  [bucket_bias(): nearby.append(jnp.einsum('qub,bh->hqu', select, table, precision=HIGH))]
  transfers between devices with their start and end apart: 9 -> 9, of which waited for: 8 -> 7; matrix products, arithmetic and copies ran while one was open for 9% -> 17% of each run, Pallas kernels for 0% -> 8%
where the time goes in v1:
time: 667 us; the launch traced here: 661 us
  waiting for transfers between devices  226 us (34%)
  matrix products  146 us (22%)
  Pallas kernels  111 us (17%)
  blocking collectives  43.2 us (6%)
  other arithmetic  42.1 us (6%)
  local copies, waits for them, and re-layouts  39.7 us (6%)
  starting transfers between devices  35.7 us (5%)
  between operations  16.6 us (2%)
    psum x1, waiting for transfers between devices, total(): return lax.psum(grad.astype(BF), both).astype(F32)  140 us
    dot_general x5, matrix products, mm(): lax.dot_general(left, right, (((1,), (0,)), ((), ())), preferred_element_...  59.1 us
    pallas_call x1, Pallas kernels, attend_back(): pl.pallas_call(attend_back_kernel, grid=(HEADS // 2,), in_specs=[pair(seq...  58.4 us
    pallas_call x1, Pallas kernels, attend(): pl.pallas_call(attend_kernel, grid=(HEADS // 2,), in_specs=[pl.BlockSpec(...  52.8 us
    psum x1, blocking collectives, body(): lax.psum((query_bias_grad, value_bias_grad, output_bias_grad, norm_gain_g...  43.2 us
    dot_general x6, matrix products, against(): lax.dot_general(left, right, (((1,), (1,)), ((), ())), preferred_element_...  38.5 us
    all_to_all x2, waiting for transfers between devices, text_away(): lax.all_to_all(rows.reshape(pages, part, dim), 'wide', split_axis=0, conc...  34.3 us
    dot_general x6, matrix products, inner(): lax.dot_general(left, right, (((0,), (0,)), ((), ())), preferred_element_...  33.8 us
  transfers between devices with their start and end apart: 9, of which 7 were waited for; matrix products, arithmetic and copies ran while one was open for 17% of the time, Pallas kernels for 8%

profile of v1, /device:TPU:0, one launch (start us, length us, event | category | flops | bytes accessed | tf_op | source)
XLA Modules:
  0.0 661.0 jit_solution(923233729194130905)
XLA Ops:
  7.2 5.3 all-to-all-start
  21.7 3.4 all-to-all-done
  25.1 4.9 all-to-all-start.1
  30.0 2.2 reshape.304.width_ref
  32.2 2.2 reshape.306.height_ref
  40.1 9.4 %all-to-all-done.1 = bf16[4,144,768]{2,1,0:T(8,128)(2,1)S(1)} async-done(((bf16[4,144,768]{2,1,0:T(8,128)(2,1)}), bf16[4,144,768]{2,1,0:T(8,128)(2,1)S(1)}, u32[]{:S(2)}, u32[]{:S(2)}) %all-to-all-start.1) | async-done | bytes 884768 | tf_op jit(solution)/shard_map/all_to_all | solution.py:328
  49.5 5.0 all-to-all-start.4
  56.0 2.8 fusion.15.q_ref
  58.7 3.9 copy.73.qt_ref
  62.6 4.2 fusion.16.v_ref
  66.8 3.8 copy.74.vt_ref
  70.6 4.2 convolution_convert_fusion.5.k_ref
  74.8 52.8 %shard_map.426 = (bf16[12,1088,1152]{2,1,0:T(8,128)(2,1)}, bf16[768,1152]{1,0:T(8,128)(2,1)}, f32[12,1,1152]{2,1,0:T(1,128)}) custom-call(bf16[1088,768]{1,0:T(8,128)(2,1)} %convolution_convert_fusion.5.k_ref, bf16[768,1152]{1,0:T(8,128)(2,1)} %copy.73.qt_ref, bf16[768,1088]{1,0:T(8,128)(2,1)} %copy.74.vt_ref, bf16[1152,320]{1,0:T(8,128)(2,1)} %add_convert_fusion.4.hot_ref, ...), custom_call_target="tpu_custom_call" | custom-call | tf_op jit(solution)/shard_map/pallas_call | solution.py:90
  127.6 3.6 fusion.60
  133.1 36.9 %multiply_convert_fusion = (bf16[1088,3072]{1,0:T(8,128)(2,1)}, f32[1088,3072]{1,0:T(8,128)}, f32[1088,3072]{1,0:T(8,128)}) fusion(f32[3072]{0:T(1024)S(1)} %copy-done.41, bf16[768,3072]{1,0:T(8,128)(2,1)S(1)} %bitcast.119, f32[1088,768]{1,0:T(8,128)S(1)} %get-tuple-element.82, f32[768]{0:T(1024)S(1)} %copy-done.46, f32[768]{0:T(1024)S(1)} %copy-done.35, ...), kind=kOutput, calls=%fused_computation.7 | convolution fusion | flops 5358600192 | bytes 41511424 | tf_op jit(solution)/shard_map/dot_general | solution.py:20
  170.0 3.5 all-to-all-start.5
  173.5 11.1 %fusion.61 = (f32[1088]{0:T(1024)S(1)}, f32[1088,768]{1,0:T(8,128)S(1)}) fusion(f32[768]{0:T(1024)S(1)} %copy-done.45, bf16[1088,3072]{1,0:T(8,128)(2,1)} %get-tuple-element.72, bf16[3072,768]{1,0:T(8,128)(2,1)} %param.45, f32[768]{0:T(1024)S(1)} %copy-done.46, f32[768]{0:T(1024)S(1)} %copy-done.35, f32[1088]{0:T(1024)S(1)} %fusion.47, ...), kind=kOutput, calls=%fused_computation.143 | convolution fusion | flops 5139676160 | bytes 18110208 | tf_op jit(solution)/shard_map/dot_general | solution.py:20
  187.0 9.6 %all-to-all-done.5 = bf16[4,144,768]{2,1,0:T(8,128)(2,1)S(1)} async-done(((bf16[4,144,768]{2,1,0:T(8,128)(2,1)}), bf16[4,144,768]{2,1,0:T(8,128)(2,1)S(1)}, u32[]{:S(2)}, u32[]{:S(2)}) %all-to-all-start.5) | async-done | bytes 884768 | tf_op jit(solution)/shard_map/all_to_all | solution.py:328
  196.6 3.5 fusion.19
  200.1 4.0 fusion.58
  204.5 8.2 %convolution_convert_fusion.2 = bf16[3072,768]{1,0:T(8,128)(2,1)} fusion(bf16[1088,3072]{1,0:T(8,128)(2,1)S(1)} %bitcast.121, bf16[1088,768]{1,0:T(8,128)(2,1)S(1)} %get-tuple-element.65), kind=kOutput, calls=%fused_computation.21 | convolution fusion | flops 5136187392 | bytes 13074432 | tf_op jit(solution)/shard_map/dot_general | solution.py:24
  212.7 18.9 %convert_reduce_fusion = (f32[3072]{0:T(1024)S(1)}, bf16[1088,3072]{1,0:T(8,128)(2,1)}) fusion(f32[1088,3072]{1,0:T(8,128)} %get-tuple-element.73, f32[1088,3072]{1,0:T(8,128)} %get-tuple-element.83, bf16[1088,768]{1,0:T(8,128)(2,1)} %copy-done.21, bf16[3072,768]{1,0:T(8,128)(2,1)} %param.45), kind=kOutput, calls=%fused_computation.5 | convolution fusion | flops 5187302400 | bytes 39825408 | tf_op jit(solution)/shard_map/dot_general | solution.py:28
  231.6 11.6 %convolution_convert_fusion.3 = bf16[768,3072]{1,0:T(8,128)(2,1)} fusion(bf16[1088,3072]{1,0:T(8,128)(2,1)} %get-tuple-element.88, f32[1088,768]{1,0:T(8,128)S(1)} %copy-done.4, f32[768]{0:T(1024)S(1)} %copy-done.46, f32[768]{0:T(1024)S(1)} %copy-done.35, f32[1088]{0:T(1024)S(1)} %fusion.47, f32[1088]{0:T(1024)S(1)} %broadcast_multiply_fusion.1), kind=kOutput, calls=%fused_computation.22 | convolution fusion | flops 5140365312 | bytes 14760448 | tf_op jit(solution)/shard_map/dot_general | solution.py:24
  243.3 10.5 %multiply_reduce_fusion = (f32[768]{0:T(1024)S(1)}, f32[1088]{0:T(1024)S(1)}, f32[768]{0:T(1024)S(1)}, f32[1088,768]{1,0:T(8,128)}) fusion(f32[1088,768]{1,0:T(8,128)S(1)} %copy-done.4, f32[1088]{0:T(1024)S(1)} %fusion.47, f32[1088]{0:T(1024)S(1)} %broadcast_multiply_fusion.1, f32[768]{0:T(1024)S(1)} %copy-done.35, bf16[1088,3072]{1,0:T(8,128)(2,1)S(1)} %copy-done.47, ...), kind=kOutput, calls=%fused_computation.57 | convolution fusion | flops 5142180864 | bytes 21456896 | tf_op jit(solution)/shard_map/dot_general | solution.py:28
  253.8 3.8 copy.75
  257.7 4.1 fusion.57
  262.2 2.3 copy-done.17
  264.5 2.7 fusion.30
  269.2 2.4 copy.77.dc_ref
  271.7 58.4 %shard_map.427 = (bf16[768,1152]{1,0:T(8,128)(2,1)}, bf16[1088,768]{1,0:T(8,128)(2,1)}, bf16[1088,768]{1,0:T(8,128)(2,1)}, f32[12,128,128]{2,1,0:T(8,128)}, f32[...) custom-call(bf16[12,1088,1152]{2,1,0:T(8,128)(2,1)} %get-tuple-element.32.exp_ref, ...), custom_call_target="tpu_custom_call" | custom-call | tf_op jit(solution)/shard_map/pallas_call | solution.py:188
  330.1 4.9 convolution_convert_fusion.6
  335.0 2.8 convolution_convert_fusion.7
  337.8 2.8 convolution_convert_fusion.8
  340.6 4.3 convolution_add_fusion.6
  351.1 4.2 all-to-all-start.6
  356.3 16.4 %all-to-all-done.6 = bf16[8,64,768]{2,1,0:T(8,128)(2,1)} async-done(((bf16[8,64,768]{2,1,0:T(8,128)(2,1)}), bf16[8,64,768]{2,1,0:T(8,128)(2,1)}, u32[]{:S(2)}, u32[]{:S(2)}) %all-to-all-start.6) | async-done | bytes 786464 | tf_op jit(solution)/shard_map/all_to_all | solution.py:336
  372.7 4.2 all-to-all-start.2
  376.9 2.2 slice.32
  379.1 17.9 %all-to-all-done.2 = bf16[8,64,768]{2,1,0:T(8,128)(2,1)} async-done(((bf16[8,64,768]{2,1,0:T(8,128)(2,1)}), bf16[8,64,768]{2,1,0:T(8,128)(2,1)}, u32[]{:S(2)}, u32[]{:S(2)}) %all-to-all-start.2) | async-done | bytes 786464 | tf_op jit(solution)/shard_map/all_to_all | solution.py:336
  397.0 4.2 all-to-all-start.7
  402.2 29.6 %all-to-all-done.7 = bf16[4,144,768]{2,1,0:T(8,128)(2,1)} async-done(((bf16[4,144,768]{2,1,0:T(8,128)(2,1)}), bf16[4,144,768]{2,1,0:T(8,128)(2,1)}, u32[]{:S(2)}, u32[]{:S(2)}) %all-to-all-start.7) | async-done | bytes 884768 | tf_op jit(solution)/shard_map/all_to_all | solution.py:344
  431.8 4.3 all-to-all-start.3
  437.1 3.7 fusion.37
  440.7 3.7 fusion.38
  445.0 43.2 %all-reduce.5 = (f32[768]{0:T(1024)}, f32[768]{0:T(1024)}, f32[768]{0:T(1024)}, f32[768]{0:T(1024)}, f32[768]{0:T(1024)}, /*index=5*/f32[3072]{0:T(1024)}, f32[7...) all-reduce(f32[768]{0:T(1024)S(1)} %convert_reduce_fusion.2, ...), channel_id=1, replica_groups=mesh['wide'=8,'narrow'=4] {'wide','narrow'}, use_global_device_ids=true, to_apply=%region_10.11 | all-reduce | flops 11172 | bytes 89376 | tf_op jit(solution)/shard_map/psum | solution.py:484
  488.2 139.9 %all-reduce.9.cloned.1.call-done = (bf16[768,768]{1,0:T(8,128)(2,1)}, bf16[768,768]{1,0:T(8,128)(2,1)}, bf16[768,768]{1,0:T(8,128)(2,1)}, bf16[768,768]{1,0:T(8,...) async-done(((bf16[768,768]{1,0:T(8,128)(2,1)}, bf16[768,768]{1,0:T(8,128)(2,1)}, bf16[768,768]{1,0:T(8,128)(2,1)}, bf16[768,768]{1,0:T(8,128)(2,1)}, ...) | async-done | bytes 14155792 | tf_op jit(solution)/shard_map/psum | solution.py:463
  628.1 7.5 %convert_element_type.194 = f32[768,3072]{1,0:T(8,128)} convert(bf16[768,3072]{1,0:T(8,128)(2,1)} %get-tuple-element.62) | non-fusion elementwise | flops 2359296 | bytes 14155776 | tf_op jit(solution)/shard_map/convert_element_type | solution.py:463
  635.6 4.5 convert_element_type.197
  (173 shorter events, 45.1 us)
Async XLA Ops:
  7.2 120.4 %copy-start = (bf16[768,768]{1,0:T(8,128)(2,1)S(1)}, bf16[768,768]{1,0:T(8,128)(2,1)}, u32[]{:S(2)}) copy-start(bf16[768,768]{1,0:T(8,128)(2,1)} %param.39) | copy-start | bytes 3538948
  7.2 12.8 %copy-start.33 = (f32[33,12]{0,1:T(8,128)S(1)}, f32[33,12]{0,1:T(8,128)}, u32[]{:S(2)}) copy-start(f32[33,12]{0,1:T(8,128)} %param.49) | copy-start | bytes 4756
  7.2 17.9 %all-to-all-start = ((bf16[8,64,768]{2,1,0:T(8,128)(2,1)}), bf16[8,64,768]{2,1,0:T(8,128)(2,1)S(1)}, u32[]{:S(2)}, u32[]{:S(2)}) async-start(bf16[8,64,768]{2,1,0:T(8,128)(2,1)} %bitcast.112), calls=%async_computation | async-start | bytes 1572864 | tf_op jit(solution)/shard_map/all_to_all | solution.py:320
  12.6 12.6 %copy-start.27 = (s32[64,64]{1,0:T(8,128)}, s32[64,64]{1,0:T(8,128)S(1)}, u32[]{:S(2)}) copy-start(s32[64,64]{1,0:T(8,128)S(1)} %clamp_add_fusion.1) | copy-start | bytes 49156
  25.1 14.0 %copy-start.13 = (bf16[8,64,768]{2,1,0:T(8,128)(2,1)}, bf16[8,64,768]{2,1,0:T(8,128)(2,1)S(1)}, u32[]{:S(2)}) copy-start(bf16[8,64,768]{2,1,0:T(8,128)(2,1)S(1)} %all-to-all-done) | copy-start | bytes 2359300
  25.1 24.3 %all-to-all-start.1 = ((bf16[4,144,768]{2,1,0:T(8,128)(2,1)}), bf16[4,144,768]{2,1,0:T(8,128)(2,1)S(1)}, u32[]{:S(2)}, u32[]{:S(2)}) async-start(bf16[4,144,768]{2,1,0:T(8,128)(2,1)} %bitcast.110), calls=%async_computation.1 | async-start | bytes 1769472 | tf_op jit(solution)/shard_map/all_to_all | solution.py:328
  37.5 18.3 %copy-start.42 = (f32[768]{0:T(1024)S(1)}, f32[768]{0:T(1024)}, u32[]{:S(2)}) copy-start(f32[768]{0:T(1024)} %param.35) | copy-start | bytes 9220
  49.5 78.1 %copy-start.11 = (bf16[4,144,768]{2,1,0:T(8,128)(2,1)}, bf16[4,144,768]{2,1,0:T(8,128)(2,1)S(1)}, u32[]{:S(2)}) copy-start(bf16[4,144,768]{2,1,0:T(8,128)(2,1)S(1)} %all-to-all-done.1) | copy-start | bytes 2654212
  49.5 120.5 %all-to-all-start.4 = ((bf16[8,64,768]{2,1,0:T(8,128)(2,1)}), bf16[8,64,768]{2,1,0:T(8,128)(2,1)S(1)}, u32[]{:S(2)}, u32[]{:S(2)}) async-start(bf16[8,64,768]{2,1,0:T(8,128)(2,1)} %bitcast.113), calls=%async_computation.4 | async-start | bytes 1572864 | tf_op jit(solution)/shard_map/all_to_all | solution.py:320
  58.7 3.9 copy-start.43
  74.8 52.8 %copy-start.44 = (f32[768]{0:T(1024)S(1)}, f32[768]{0:T(1024)}, u32[]{:S(2)}) copy-start(f32[768]{0:T(1024)} %param.40) | copy-start | bytes 9220
  127.6 5.4 slice-start
  127.6 5.4 slice-start.1
  131.8 38.1 %copy-start.29 = (f32[1088]{0:T(1024)}, f32[1088]{0:T(1024)S(1)}, u32[]{:S(2)}) copy-start(f32[1088]{0:T(1024)S(1)} %multiply_reduce_fusion.3) | copy-start | bytes 13060
  133.0 40.5 %copy-start.45 = (f32[768]{0:T(1024)S(1)}, f32[768]{0:T(1024)}, u32[]{:S(2)}) copy-start(f32[768]{0:T(1024)} %param.46) | copy-start | bytes 9220
  170.0 26.6 %all-to-all-start.5 = ((bf16[4,144,768]{2,1,0:T(8,128)(2,1)}), bf16[4,144,768]{2,1,0:T(8,128)(2,1)S(1)}, u32[]{:S(2)}, u32[]{:S(2)}) async-start(bf16[4,144,768]{2,1,0:T(8,128)(2,1)} %bitcast.111), calls=%async_computation.5 | async-start | bytes 1769472 | tf_op jit(solution)/shard_map/all_to_all | solution.py:328
  173.5 454.6 %all-reduce.9.cloned.1.call-start = ((), (), s32[]{:S(2)}) async-start(), calls=%async_computation.8 | async-start | bytes 28311552 | tf_op jit(solution)/shard_map/psum | solution.py:463
  184.7 11.9 %copy-start.32 = (f32[768]{0:T(1024)S(1)}, f32[768]{0:T(1024)}, u32[]{:S(2)}) copy-start(f32[768]{0:T(1024)} %param.47) | copy-start | bytes 9220
  187.0 13.1 %copy-start.34 = (f32[768]{0:T(1024)S(1)}, f32[768]{0:T(1024)}, u32[]{:S(2)}) copy-start(f32[768]{0:T(1024)} %param.48) | copy-start | bytes 9220
  196.6 3.5 copy-start.2
  200.1 4.5 slice-start.2
  200.1 4.4 slice-start.3
  204.1 8.6 %copy-start.6 = (f32[1088,768]{1,0:T(8,128)}, f32[1088,768]{1,0:T(8,128)S(1)}, u32[]{:S(2)}) copy-start(f32[1088,768]{1,0:T(8,128)S(1)} %get-tuple-element.71) | copy-start | bytes 10027012
  204.5 8.2 %copy-start.21 = (bf16[1088,768]{1,0:T(8,128)(2,1)}, bf16[1088,768]{1,0:T(8,128)(2,1)S(1)}, u32[]{:S(2)}) copy-start(bf16[1088,768]{1,0:T(8,128)(2,1)S(1)} %get-tuple-element.65) | copy-start | bytes 5013508
  212.7 18.9 %copy-start.4 = (f32[1088,768]{1,0:T(8,128)S(1)}, f32[1088,768]{1,0:T(8,128)}, u32[]{:S(2)}) copy-start(f32[1088,768]{1,0:T(8,128)} %copy-done.3) | copy-start | bytes 10027012
  231.6 11.6 %copy-start.7 = (f32[1088,768]{1,0:T(8,128)S(1)}, f32[1088,768]{1,0:T(8,128)}, u32[]{:S(2)}) copy-start(f32[1088,768]{1,0:T(8,128)} %copy-done.6) | copy-start | bytes 10027012
  231.6 11.7 %copy-start.47 = (bf16[1088,3072]{1,0:T(8,128)(2,1)S(1)}, bf16[1088,3072]{1,0:T(8,128)(2,1)}, u32[]{:S(2)}) copy-start(bf16[1088,3072]{1,0:T(8,128)(2,1)} %get-tuple-element.88) | copy-start | bytes 20054020
  253.8 3.8 copy-start.30
  261.8 5.4 copy-start.5
  330.1 4.9 copy-start.12
  330.1 4.9 copy-start.14
  330.1 4.9 copy-start.36
  335.0 2.8 copy-start.15
  340.6 4.4 copy-start.37
  340.6 4.4 copy-start.39
  350.2 5.2 copy-start.9
  351.1 21.5 %all-to-all-start.6 = ((bf16[8,64,768]{2,1,0:T(8,128)(2,1)}), bf16[8,64,768]{2,1,0:T(8,128)(2,1)}, u32[]{:S(2)}, u32[]{:S(2)}) async-start(bf16[8,64,768]{2,1,0:T(8,128)(2,1)} %bitcast.102), calls=%async_computation.6 | async-start | bytes 1572864 | tf_op jit(solution)/shard_map/all_to_all | solution.py:336
  372.7 24.3 %all-to-all-start.2 = ((bf16[8,64,768]{2,1,0:T(8,128)(2,1)}), bf16[8,64,768]{2,1,0:T(8,128)(2,1)}, u32[]{:S(2)}, u32[]{:S(2)}) async-start(bf16[8,64,768]{2,1,0:T(8,128)(2,1)} %bitcast.101), calls=%async_computation.2 | async-start | bytes 1572864 | tf_op jit(solution)/shard_map/all_to_all | solution.py:336
  376.9 59.2 %copy-start.26 = (f32[12,64,64]{2,1,0:T(8,128)S(1)}, f32[12,64,64]{2,1,0:T(8,128)}, u32[]{:S(2)}) copy-start(f32[12,64,64]{2,1,0:T(8,128)} %get-tuple-element.37) | copy-start | bytes 589828
  376.9 59.2 %copy-start.28 = (s32[64,64]{1,0:T(8,128)S(1)}, s32[64,64]{1,0:T(8,128)}, u32[]{:S(2)}) copy-start(s32[64,64]{1,0:T(8,128)} %copy-done.27) | copy-start | bytes 49156
  397.0 34.8 %all-to-all-start.7 = ((bf16[4,144,768]{2,1,0:T(8,128)(2,1)}), bf16[4,144,768]{2,1,0:T(8,128)(2,1)}, u32[]{:S(2)}, u32[]{:S(2)}) async-start(bf16[4,144,768]{2,1,0:T(8,128)(2,1)} %bitcast.100), calls=%async_computation.7 | async-start | bytes 1769472 | tf_op jit(solution)/shard_map/all_to_all | solution.py:344
  431.8 56.4 %all-to-all-start.3 = ((bf16[4,144,768]{2,1,0:T(8,128)(2,1)}), bf16[4,144,768]{2,1,0:T(8,128)(2,1)S(1)}, u32[]{:S(2)}, u32[]{:S(2)}) async-start(bf16[4,144,768]{2,1,0:T(8,128)(2,1)} %bitcast.99), calls=%async_computation.3 | async-start | bytes 1769472 | tf_op jit(solution)/shard_map/all_to_all | solution.py:344
  436.1 8.3 %copy-start.20 = (bf16[1088,768]{1,0:T(8,128)(2,1)S(1)}, bf16[1088,768]{1,0:T(8,128)(2,1)}, u32[]{:S(2)}) copy-start(bf16[1088,768]{1,0:T(8,128)(2,1)} %get-tuple-element.36) | copy-start | bytes 5013508
  436.1 8.6 %copy-start.16 = (bf16[768,1152]{1,0:T(8,128)(2,1)S(1)}, bf16[768,1152]{1,0:T(8,128)(2,1)}, u32[]{:S(2)}) copy-start(bf16[768,1152]{1,0:T(8,128)(2,1)} %get-tuple-element.34) | copy-start | bytes 5308420
  628.1 7.5 %copy-start.10 = (bf16[3072,768]{1,0:T(8,128)(2,1)S(1)}, bf16[3072,768]{1,0:T(8,128)(2,1)}, u32[]{:S(2)}) copy-start(bf16[3072,768]{1,0:T(8,128)(2,1)} %get-tuple-element.63) | copy-start | bytes 14155780
  635.6 4.5 copy-start.25
  640.1 3.2 copy-start.23
  641.8 3.2 copy-start.22
  (13 other events, 25.5 us)
Sparse Core Ops, SparseCore 0:
  340.7 287.3 all-reduce.8

commit v2 on v1

--- a/solution.py
+++ b/solution.py
@@ -117,13 +117,18 @@
             pltpu.VMEM((80, seq), BF),
         ],
         compiler_params=pltpu.CompilerParams(vmem_limit_bytes=VMEM_BYTES),
+        cost_estimate=pl.CostEstimate(
+            flops=HEADS * seq * lanes * 4096, bytes_accessed=HEADS * seq * lanes * 2,
+            transcendentals=HEADS * seq * lanes,
+        ),
     )(k, q_t, v_t, hot, mask, hot_t, line, width, height)
 
 
-def attend_back_kernel(
-    exp_ref, ctx_ref, v_ref, kt_ref, q_ref, dc_ref, dct_ref, hot_ref, hott_ref,
-    dqt_ref, dk_ref, dv_ref, gwidth_ref, gheight_ref, gline_ref, values, dctx, lefts, rights, ds,
-):
+def attend_back_kernel(held, *refs):
+    (
+        exp_ref, ctx_ref, v_ref, kt_ref, q_ref, dc_ref, dct_ref, hot_ref, hott_ref,
+        dqt_ref, dk_ref, dv_ref, gwidth_ref, gheight_ref, gline_ref, values, dctx, lefts, rights, ds,
+    ) = refs[:9] + refs[9 + held :]
     seq = v_ref.shape[0]
     lanes = dct_ref.shape[1]
 
@@ -168,26 +173,26 @@
     dv_ref[...] = jnp.where(lane < 64, results[0][1], results[1][1]).astype(BF)
 
 
-def attend_back(exps, ctx_t, v, k_t, q, d_ctx, d_ctx_t, hot, hot_t):
+def attend_back(first, pairs, held, exps, ctx_t, v, k_t, q, d_ctx, d_ctx_t, hot, hot_t):
     seq, dim = v.shape
     lanes = d_ctx_t.shape[1]
 
     def whole(a):
         return pl.BlockSpec(a.shape, lambda p: (0,) * a.ndim)
 
-    def columns(rows):
-        return pl.BlockSpec((rows, 128), lambda p: (0, p))
-
-    def rows(length):
-        return pl.BlockSpec((128, length), lambda p: (p, 0))
-
-    def pair(*shape):
-        return pl.BlockSpec((2,) + shape, lambda p: (p, 0, 0))
+    def columns(rows, start=first):
+        return pl.BlockSpec((rows, 128), lambda p: (0, p + start))
+
+    def rows(length, start=first):
+        return pl.BlockSpec((128, length), lambda p: (p + start, 0))
+
+    def pair(*shape, start=first):
+        return pl.BlockSpec((2,) + shape, lambda p: (p + start, 0, 0))
 
     shape = jax.ShapeDtypeStruct
     return pl.pallas_call(
-        attend_back_kernel,
-        grid=(HEADS // 2,),
+        partial(attend_back_kernel, len(held)),
+        grid=(pairs,),
         in_specs=[
             pair(seq, lanes),
             rows(lanes),
@@ -198,22 +203,23 @@
             rows(lanes),
             whole(hot),
             whole(hot_t),
-        ],
+        ]
+        + [pl.BlockSpec(memory_space=pl.ANY)] * len(held),
         out_specs=[
-            rows(lanes),
-            columns(seq),
-            columns(seq),
-            pair(128, 128),
-            pair(128, 128),
-            pair(64, 64),
+            rows(lanes, 0),
+            columns(seq, 0),
+            columns(seq, 0),
+            pair(128, 128, start=0),
+            pair(128, 128, start=0),
+            pair(64, 64, start=0),
         ],
         out_shape=[
-            shape((dim, lanes), BF),
-            shape((seq, dim), BF),
-            shape((seq, dim), BF),
-            shape((HEADS, 128, 128), F32),
-            shape((HEADS, 128, 128), F32),
-            shape((HEADS, 64, 64), F32),
+            shape((128 * pairs, lanes), BF),
+            shape((seq, 128 * pairs), BF),
+            shape((seq, 128 * pairs), BF),
+            shape((2 * pairs, 128, 128), F32),
+            shape((2 * pairs, 128, 128), F32),
+            shape((2 * pairs, 64, 64), F32),
         ],
         scratch_shapes=[
             pltpu.VMEM((2, seq, 128), BF),
@@ -223,7 +229,11 @@
             pltpu.VMEM((2, seq, lanes), BF),
         ],
         compiler_params=pltpu.CompilerParams(vmem_limit_bytes=VMEM_BYTES),
-    )(exps, ctx_t, v, k_t, q, d_ctx, d_ctx_t, hot, hot_t)
+        cost_estimate=pl.CostEstimate(
+            flops=2 * pairs * seq * lanes * 4096, bytes_accessed=2 * pairs * seq * lanes * 2,
+            transcendentals=0,
+        ),
+    )(exps, ctx_t, v, k_t, q, d_ctx, d_ctx_t, hot, hot_t, *held)
 
 
 def bucket_select(table):
@@ -315,36 +325,131 @@
     return (final_low, d_mid, d_ctx_t, grads)
 
 
-def text_home(rows):
-    pages, _, part, dim = rows.shape
-    moved = lax.all_to_all(
-        rows.reshape(pages, part, dim), "wide", split_axis=0, concat_axis=0, tiled=True
-    )
-    return moved.reshape(-1, dim)
-
-
-def patch_home(rows):
-    _, pages, part, dim = rows.shape
-    moved = lax.all_to_all(
-        rows.reshape(pages, part, dim), "narrow", split_axis=0, concat_axis=0, tiled=True
-    )
-    return moved.reshape(-1, dim)
-
-
-def text_away(rows, shape):
-    pages, _, part, dim = shape
-    moved = lax.all_to_all(
-        rows.reshape(pages, part, dim), "wide", split_axis=0, concat_axis=0, tiled=True
-    )
-    return moved.reshape(shape)
-
-
-def patch_away(rows, shape):
-    _, pages, part, dim = shape
-    moved = lax.all_to_all(
-        rows.reshape(pages, part, dim), "narrow", split_axis=0, concat_axis=0, tiled=True
-    )
-    return moved.reshape(shape)
+def shift_pairs(size, step):
+    return [(i, (i + step) % size) for i in range(size)]
+
+
+def flip_pairs(size, step):
+    return [(i, i ^ step) for i in range(size)]
+
+
+def pick(array, index):
+    return lax.dynamic_index_in_dim(array, index, 0, keepdims=False)
+
+
+def swap_text(parts):
+    return lax.all_to_all(parts, "wide", split_axis=0, concat_axis=0, tiled=True)
+
+
+def patch_order(size):
+    me = lax.axis_index("narrow")
+    return [me ^ k for k in range(size)]
+
+
+def swap_patch(parts):
+    size = parts.shape[0]
+    me = lax.axis_index("narrow")
+    return [pick(parts, me)] + [
+        lax.ppermute(pick(parts, me ^ k), "narrow", flip_pairs(size, k)) for k in range(1, size)
+    ]
+
+
+def flip_axis(array, axis, bit):
+    return jnp.where(bit == 1, jnp.flip(array, axis), array)
+
+
+def from_flipped(parts, me):
+    size = parts.shape[0]
+    bits = size.bit_length() - 1
+    parts = parts.reshape((2,) * bits + parts.shape[1:])
+    for b in range(bits):
+        parts = flip_axis(parts, bits - 1 - b, (me >> b) & 1)
+    return parts.reshape((size,) + parts.shape[bits:])
+
+
+def patch_away(rows, size):
+    me = lax.axis_index("narrow")
+    parts = rows.reshape(size, -1, rows.shape[1])
+    arrived = [parts[0]] + [
+        lax.ppermute(parts[k], "narrow", flip_pairs(size, k)) for k in range(1, size)
+    ]
+    return from_flipped(jnp.stack(arrived), me)
+
+
+def add(*terms):
+    total = terms[0].astype(F32)
+    for term in terms[1:]:
+        total = total + term.astype(F32)
+    return total.astype(BF)
+
+
+def stages(wide, order):
+    bits = list(range(1, wide.bit_length() - 1))
+    return [0] + bits[:: 1 if order == 0 else -1] + [None]
+
+
+def scatter_step(grad, wide, narrow, bit):
+    columns = grad.shape[1]
+    if bit is None:
+        me = lax.axis_index("narrow")
+        return add(*swap_patch(grad.reshape(narrow, -1, columns)))
+    me = (lax.axis_index("wide") >> bit) & 1
+    parts = grad.reshape(2, -1, columns)
+    arrived = lax.ppermute(pick(parts, 1 - me), "wide", flip_pairs(wide, 1 << bit))
+    return add(pick(parts, me), arrived)
+
+
+def scatter_sum(grad, wide, narrow, order):
+    steps = []
+    for bit in stages(wide, order):
+        grad = scatter_step(grad, wide, narrow, bit)
+        steps.append(grad)
+    return steps
+
+
+def gather_all(part, wide, narrow, order):
+    rows, columns = part.shape
+    order = stages(wide, order)
+    part = part[None]
+    for bit in order[::-1]:
+        if bit is None:
+            parts = [part] + [
+                lax.ppermute(part, "narrow", flip_pairs(narrow, k)) for k in range(1, narrow)
+            ]
+        else:
+            parts = [part, lax.ppermute(part, "wide", flip_pairs(wide, 1 << bit))]
+        part = jnp.concatenate(parts, axis=0)
+    bits = []
+    for bit in order:
+        if bit is None:
+            me = lax.axis_index("narrow")
+            bits += [(me >> b) & 1 for b in range(narrow.bit_length() - 2, -1, -1)]
+        else:
+            bits.append((lax.axis_index("wide") >> bit) & 1)
+    part = part.reshape((2,) * len(bits) + (rows, columns))
+    for axis, bit in enumerate(bits):
+        part = flip_axis(part, axis, bit)
+    return part.reshape(-1, columns)
+
+
+def pack(grads, columns, rows):
+    lines = []
+    for grad in grads:
+        flat = grad.reshape(-1)
+        lines.append(jnp.pad(flat, (0, -flat.shape[0] % columns)).reshape(-1, columns))
+    lines = jnp.concatenate(lines, axis=0)
+    return jnp.pad(lines, ((0, -lines.shape[0] % rows), (0, 0)))
+
+
+def unpack(lines, grads):
+    columns = lines.shape[1]
+    at = 0
+    out = []
+    for grad in grads:
+        count = -(-grad.size // columns)
+        out.append(lines[at : at + count].reshape(-1)[: grad.size].reshape(grad.shape))
+        at += count
+    return out
 
 
 def body(
@@ -393,24 +498,46 @@
         final_gain,
         final_shift,
     )
-    rows_in = jnp.concatenate([text_home(text_in), patch_home(patch_in)], axis=0)
-    cot = jnp.concatenate([text_home(cot_text), patch_home(cot_patch)], axis=0).astype(F32)
+    wide = text_shape[0]
+    narrow = patch_shape[1]
+    rows_in = jnp.concatenate(
+        [swap_text(text_in.reshape(wide, -1, dim)).reshape(-1, dim)]
+        + swap_patch(patch_in.reshape(narrow, -1, dim)),
+        axis=0,
+    )
+    cot = [swap_text(cot_text.reshape(wide, -1, dim)).reshape(-1, dim)] + swap_patch(
+        cot_patch.reshape(narrow, -1, dim)
+    )
+    index = jnp.arange(seq, dtype=jnp.int32)
+    live_patch = jnp.where(res_class.reshape(()) == 1, PATCH, SMALL_PATCH)
+    valid = jnp.where(index < TEXT, index < text_len.reshape(()), index - TEXT < live_patch)
+    facts = jnp.concatenate(
+        [pos_line.reshape(1, -1), pos_x.reshape(1, -1), pos_y.reshape(1, -1), valid.astype(jnp.int32)[None]]
+    )
+    patch_facts = facts[:, TEXT:].reshape(4, narrow, -1)
+    facts = jnp.concatenate(
+        [facts[:, :TEXT]]
+        + [
+            lax.dynamic_index_in_dim(patch_facts, i, 1, keepdims=False)
+            for i in patch_order(narrow)
+        ],
+        axis=1,
+    )
+    line_spots, x_spots, y_spots = facts[0], facts[1], facts[2]
+    valid = facts[3] == 1
 
     line = spread_table(line_table)
     width = spread_table(width_table)
     height = spread_table(height_table)
     hots = []
     hots_t = []
-    for spots, table in ((pos_line, line_table), (pos_x, width_table), (pos_y, height_table)):
+    for spots, table in ((line_spots, line_table), (x_spots, width_table), (y_spots, height_table)):
         span = jnp.arange(2 * (table.shape[0] - 1), dtype=jnp.int32)
-        long = jnp.pad(spots.reshape(-1), (0, lanes - seq), constant_values=-1)
+        long = jnp.pad(spots, (0, lanes - seq), constant_values=-1)
         hots.append((long[:, None] == span[None, :]).astype(BF))
         hots_t.append((long[None, :] == span[:, None]).astype(BF))
     hot = jnp.concatenate(hots, axis=1)
     hot_t = jnp.concatenate(hots_t, axis=0)
-    index = jnp.arange(seq, dtype=jnp.int32)
-    live_patch = jnp.where(res_class.reshape(()) == 1, PATCH, SMALL_PATCH)
-    valid = jnp.where(index < TEXT, index < text_len.reshape(()), index - TEXT < live_patch)
     column = jnp.arange(128, dtype=jnp.int32)
     mask = jnp.where((column[None, :] % 64 == 0) & ~valid[:, None], -1e30, 0.0).astype(BF)
 
@@ -425,26 +552,9 @@
     v = (mm(rows_in, value_weight) + value_bias).astype(BF)
     v_t = v.T
     exps, ctx_t, inverse = attend(k, q_t, v_t, hot, mask, hot_t, line, width, height)
+    ctx_t, cot = lax.optimization_barrier((ctx_t, cot))
+    cot = jnp.concatenate(cot, axis=0).astype(F32)
     final_low, d_mid, d_ctx_t, row_grads = row_pass(rows_in, ctx_t, cot, inverse, weights)
-    d_q_t, d_k, d_v, g_width, g_height, g_line = attend_back(
-        exps, ctx_t, v, k_t, q, d_ctx_t.T, d_ctx_t, hot, hot_t
-    )
-    d_q = d_q_t[:, :seq].T
-    line_table_grad = gather_table(g_line, line_table)
-    width_table_grad = gather_table(g_width, width_table)
-    height_table_grad = gather_table(g_height, height_table)
-    query_weight_grad = inner(rows_in, d_q)
-    key_weight_grad = inner(rows_in, d_k)
-    value_weight_grad = inner(rows_in, d_v)
-    query_bias_grad = jnp.sum(d_q.astype(F32), axis=0)
-    value_bias_grad = jnp.sum(d_v.astype(F32), axis=0)
-    d_rows = (
-        d_mid + against(d_q, query_weight) + against(d_k, key_weight) + against(d_v, value_weight)
-    ).astype(BF)
-    text_out = text_away(final_low[:TEXT], text_shape)
-    patch_out = patch_away(final_low[TEXT:], patch_shape)
-    text_grad = text_away(d_rows[:TEXT], text_shape)
-    patch_grad = patch_away(d_rows[TEXT:], patch_shape)
     (
         output_weight_grad,
         output_bias_grad,
@@ -457,20 +567,20 @@
         final_gain_grad,
         final_shift_grad,
     ) = row_grads
-    both = ("wide", "narrow")
-
-    def total(grad):
-        return lax.psum(grad.astype(BF), both).astype(F32)
-
-    down_weight_grad, up_weight_grad, output_weight_grad = (
-        total(down_weight_grad), total(up_weight_grad), total(output_weight_grad)
-    )
-    query_weight_grad, key_weight_grad, value_weight_grad = (
-        total(query_weight_grad), total(key_weight_grad), total(value_weight_grad)
-    )
+    early = (
+        output_bias_grad, norm_gain_grad, norm_shift_grad, up_bias_grad, down_bias_grad,
+        final_gain_grad, final_shift_grad,
+    )
+    sums = lax.psum(
+        (
+            down_weight_grad.astype(BF),
+            up_weight_grad.astype(BF),
+            jnp.concatenate([output_weight_grad, pack(early, dim, 16)], axis=0).astype(BF),
+        ),
+        ("wide", "narrow"),
+    )
+    down_weight_grad, up_weight_grad, output_weight_grad = (a.astype(F32) for a in sums)
     (
-        query_bias_grad,
-        value_bias_grad,
         output_bias_grad,
         norm_gain_grad,
         norm_shift_grad,
@@ -478,26 +588,69 @@
         down_bias_grad,
         final_gain_grad,
         final_shift_grad,
-        line_table_grad,
-        width_table_grad,
-        height_table_grad,
-    ) = lax.psum(
-        (
-            query_bias_grad,
-            value_bias_grad,
-            output_bias_grad,
-            norm_gain_grad,
-            norm_shift_grad,
-            up_bias_grad,
-            down_bias_grad,
-            final_gain_grad,
-            final_shift_grad,
-            line_table_grad,
-            width_table_grad,
-            height_table_grad,
-        ),
-        both,
-    )
+    ) = unpack(output_weight_grad[dim:], early)
+    output_weight_grad = output_weight_grad[:dim]
+    def backward():
+        text_out = swap_text(final_low[:TEXT].reshape(wide, -1, dim)).reshape(text_shape)
+        patch_out = patch_away(final_low[TEXT:], narrow).reshape(patch_shape)
+        pairs = HEADS // 4
+        held = [[], [text_out, patch_out]]
+        d_ctx = d_ctx_t.T
+        backs = [
+            attend_back(i * pairs, pairs, held[i], exps, ctx_t, v, k_t, q, d_ctx, d_ctx_t, hot, hot_t)
+            for i in range(2)
+        ]
+        d_q = jnp.concatenate([b[0] for b in backs], axis=0)[:, :seq].T
+        d_k = jnp.concatenate([b[1] for b in backs], axis=1)
+        d_v = jnp.concatenate([b[2] for b in backs], axis=1)
+        g_width = jnp.concatenate([b[3] for b in backs], axis=0)
+        g_height = jnp.concatenate([b[4] for b in backs], axis=0)
+        g_line = jnp.concatenate([b[5] for b in backs], axis=0)
+        d_rows = (
+            d_mid + against(d_q, query_weight) + against(d_k, key_weight) + against(d_v, value_weight)
+        ).astype(BF)
+        text_grad = swap_text(d_rows[:TEXT].reshape(wide, -1, dim)).reshape(text_shape)
+        patch_grad = patch_away(d_rows[TEXT:], narrow).reshape(patch_shape)
+        late = (
+            jnp.sum(d_q.astype(F32), axis=0),
+            jnp.sum(d_v.astype(F32), axis=0),
+            gather_table(g_line, line_table),
+            gather_table(g_width, width_table),
+            gather_table(g_height, height_table),
+        )
+        tail = jnp.concatenate(
+            [
+                inner(rows_in, d_q),
+                inner(rows_in, d_k),
+                inner(rows_in, d_v),
+                pack(late, dim, 8 * wide * narrow),
+            ],
+            axis=0,
+        ).astype(BF)
+        half = tail.shape[0] // 2
+        tail = jnp.concatenate(
+            [
+                gather_all(
+                    scatter_sum(tail[order * half : (order + 1) * half], wide, narrow, order)[-1],
+                    wide,
+                    narrow,
+                    order,
+                )
+                for order in range(2)
+            ],
+            axis=0,
+        ).astype(F32)
+        return (text_out, patch_out, text_grad, patch_grad) + tuple(
+            tail[i * dim : (i + 1) * dim] for i in range(3)
+        ) + tuple(unpack(tail[3 * dim :], late))
+
+    def never():
+        return jax.tree.map(lambda a: jnp.zeros(a.shape, a.dtype), jax.eval_shape(backward))
+
+    (
+        text_out, patch_out, text_grad, patch_grad, query_weight_grad, key_weight_grad, value_weight_grad,
+        query_bias_grad, value_bias_grad, line_table_grad, width_table_grad, height_table_grad,
+    ) = lax.cond(text_len.reshape(()) >= 0, backward, never)
     return (
         text_out,
         patch_out,

time: 667 us -> 530 us (0.79)
  waiting for transfers between devices: 226 us -> 67.9 us
  blocking collectives: 43.2 us -> 0 us
  starting transfers between devices: 35.7 us -> 67.6 us
  local copies, waits for them, and re-layouts: 39.7 us -> 63.4 us
  other arithmetic: 42.1 us -> 54.2 us
  matrix products: 146 us -> 135 us
    psum x1, waiting for transfers between devices: 140 us -> 0.02 us  [body(): lax.psum((down_weight_grad.astype(BF), up_weight_grad.astype(BF), jnp.con...]
    all_to_all x8 -> x4, waiting for transfers between devices: 86.3 us -> 0.01 us  [swap_text(): lax.all_to_all(parts, 'wide', split_axis=0, concat_axis=0, tiled=True)]
    ppermute x0 -> x36, waiting for transfers between devices: none -> 67.8 us  [the longest x6 24.8 us: gather_all(): parts = [part, lax.ppermute(part, 'wide', flip_pairs(wide, 1 << bit))]]
    ppermute x0 -> x36, starting transfers between devices: none -> 51.1 us  [the longest x12 19.7 us: swap_patch(): lax.ppermute(pick(parts, me ^ k), 'narrow', flip_pairs(size, k))]
    psum x1 -> x0, blocking collectives: 43.2 us -> none  [body(): lax.psum((query_bias_grad, value_bias_grad, output_bias_grad, norm_gain_g...]
    all_to_all x8 -> x4, starting transfers between devices: 35.6 us -> 16.5 us  [swap_text(): lax.all_to_all(parts, 'wide', split_axis=0, concat_axis=0, tiled=True)]
    another operation x0 -> x7, local copies, waits for them, and re-layouts: none -> 14.2 us
    convert_element_type x3 -> x0, local copies, waits for them, and re-layouts: 11.5 us -> none  [the longest x1 3.86 us: body(): q_t = ((lax.dot_general(query_weight, rows_long, (((0,), (1,)), ((), ()))...]
  transfers between devices with their start and end apart: 9 -> 41, of which waited for: 7 -> 17; matrix products, arithmetic and copies ran while one was open for 17% -> 23% of each run, Pallas kernels for 8% -> 22%
where the time goes in v2:
time: 530 us; the launch traced here: 521 us
  matrix products  135 us (25%)
  Pallas kernels  115 us (22%)
  waiting for transfers between devices  67.9 us (13%)
  starting transfers between devices  67.6 us (13%)
  local copies, waits for them, and re-layouts  63.4 us (12%)
  other arithmetic  54.2 us (10%)
  between operations  16.5 us (3%)
    pallas_call x2, Pallas kernels, attend_back(): pl.pallas_call(partial(attend_back_kernel, len(held)), grid=(pairs,), in_...  62.9 us
    pallas_call x1, Pallas kernels, attend(): pl.pallas_call(attend_kernel, grid=(HEADS // 2,), in_specs=[pl.BlockSpec(...  52.5 us
    dot_general x5, matrix products, mm(): lax.dot_general(left, right, (((1,), (0,)), ((), ())), preferred_element_...  49.7 us
    dot_general x6, matrix products, against(): lax.dot_general(left, right, (((1,), (1,)), ((), ())), preferred_element_...  38.1 us
    dot_general x6, matrix products, inner(): lax.dot_general(left, right, (((0,), (0,)), ((), ())), preferred_element_...  36.2 us
    ppermute x6, waiting for transfers between devices, gather_all(): parts = [part, lax.ppermute(part, 'wide', flip_pairs(wide, 1 << bit))]  24.8 us
    ppermute x12, starting transfers between devices, swap_patch(): lax.ppermute(pick(parts, me ^ k), 'narrow', flip_pairs(size, k))  19.7 us
    all_to_all x4, starting transfers between devices, swap_text(): lax.all_to_all(parts, 'wide', split_axis=0, concat_axis=0, tiled=True)  16.5 us
  transfers between devices with their start and end apart: 41, of which 17 were waited for; matrix products, arithmetic and copies ran while one was open for 23% of the time, Pallas kernels for 22%

profile of v2, /device:TPU:0, one launch (start us, length us, event | category | flops | bytes accessed | tf_op | source)
XLA Modules:
  0.0 520.8 jit_solution(3632850273607653613)
XLA Ops:
  9.4 3.0 collective-permute-start.30
  12.4 3.7 all-to-all-start.2
  16.2 2.7 collective-permute-start.31
  20.7 3.5 collective-permute-start.34
  38.3 4.1 all-to-all-start.3
  46.8 2.7 convolution_convert_fusion.8.k_ref
  49.5 3.0 fusion.50
  52.5 3.0 fusion.51
  55.5 52.5 %shard_map.426 = (bf16[12,1088,1152]{2,1,0:T(8,128)(2,1)}, bf16[768,1152]{1,0:T(8,128)(2,1)}, f32[12,1,1152]{2,1,0:T(1,128)}) custom-call(bf16[1088,768]{1,0:T(8,128)(2,1)} %convolution_convert_fusion.8.k_ref, bf16[768,1152]{1,0:T(8,128)(2,1)} %bitcast.234, bf16[768,1088]{1,0:T(8,128)(2,1)} %bitcast.237, bf16[1152,320]{1,0:T(8,128)(2,1)S(1)} %copy-done.18, ...), custom_call_target="tpu_custom_call" | custom-call | flops 61605937152 | bytes 30081024 | tf_op jit(solution)/shard_map/pallas_call | solution.py:90
  109.0 3.9 fusion.91
  114.2 36.4 %multiply_convert_fusion = (bf16[1088,3072]{1,0:T(8,128)(2,1)S(1)}, f32[1088,3072]{1,0:T(8,128)}, f32[1088,3072]{1,0:T(8,128)}) fusion(f32[3072]{0:T(1024)S(1)} %copy-done.58, bf16[768,3072]{1,0:T(8,128)(2,1)S(1)} %bitcast.258, f32[1088,768]{1,0:T(8,128)S(1)} %get-tuple-element.337, f32[768]{0:T(1024)S(1)} %copy-done.63, f32[768]{0:T(1024)S(1)} %copy-done.49, ...), kind=kOutput, calls=%fused_computation.147 | convolution fusion | flops 5358600192 | bytes 41511424 | tf_op jit(solution)/shard_map/dot_general | solution.py:20
  150.7 5.9 %fusion.92 = (f32[1088]{0:T(1024)S(1)}, f32[1088,768]{1,0:T(8,128)S(1)}) fusion(f32[768]{0:T(1024)S(1)} %copy-done.62, bf16[1088,3072]{1,0:T(8,128)(2,1)S(1)} %get-tuple-element.249, bf16[3072,768]{1,0:T(8,128)(2,1)S(1)} %bitcast.256, f32[768]{0:T(1024)S(1)} %copy-done.63, f32[768]{0:T(1024)S(1)} %copy-done.49, f32[1088]{0:T(1024)S(1)} %fusion.68, ...), kind=kOutput, calls=%fused_computation.299 | convolution fusion | flops 5139676160 | bytes 18110208 | tf_op jit(solution)/shard_map/dot_general | solution.py:20
  161.6 2.6 fusion.83
  164.6 8.0 %convolution_convert_fusion.5 = bf16[3072,768]{1,0:T(8,128)(2,1)} fusion(bf16[1088,3072]{1,0:T(8,128)(2,1)S(1)} %get-tuple-element.249, bf16[1088,768]{1,0:T(8,128)(2,1)S(1)} %get-tuple-element.241), kind=kOutput, calls=%fused_computation.161 | convolution fusion | flops 5136187392 | bytes 13074432 | tf_op jit(solution)/shard_map/dot_general | solution.py:24
  172.6 19.0 %fusion.93 = (bf16[3072]{0:T(1024)(128)(2,1)S(1)}, bf16[1088,3072]{1,0:T(8,128)(2,1)}) fusion(f32[1088,3072]{1,0:T(8,128)} %get-tuple-element.250, f32[1088,3072]{1,0:T(8,128)} %get-tuple-element.338, bf16[1088,768]{1,0:T(8,128)(2,1)} %copy-done.15, bf16[3072,768]{1,0:T(8,128)(2,1)} %param.47), kind=kOutput, calls=%fused_computation.300 | convolution fusion | flops 5183960064 | bytes 39819264 | tf_op jit(solution)/shard_map/dot_general | solution.py:28
  191.6 11.9 %convolution_convert_fusion.6 = bf16[768,3072]{1,0:T(8,128)(2,1)} fusion(bf16[1088,3072]{1,0:T(8,128)(2,1)} %get-tuple-element.343, f32[1088,768]{1,0:T(8,128)S(1)} %get-tuple-element.337, f32[768]{0:T(1024)S(1)} %copy-done.63, f32[768]{0:T(1024)S(1)} %copy-done.49, f32[1088]{0:T(1024)S(1)} %fusion.68, f32[1088]{0:T(1024)S(1)} %broadcast_multiply_fusion.1), kind=kOutput, calls=%fused_computation.162 | convolution fusion | flops 5140365312 | bytes 14760448 | tf_op jit(solution)/shard_map/dot_general | solution.py:24
  203.5 9.0 %multiply_reduce_fusion = (bf16[768]{0:T(1024)(128)(2,1)S(1)}, f32[1088]{0:T(1024)S(1)}, bf16[768]{0:T(1024)(128)(2,1)S(1)}, f32[1088,768]{1,0:T(8,128)S(1)}) fusion(f32[1088,768]{1,0:T(8,128)S(1)} %get-tuple-element.337, f32[1088]{0:T(1024)S(1)} %fusion.68, f32[1088]{0:T(1024)S(1)} %broadcast_multiply_fusion.1, f32[768]{0:T(1024)S(1)} %copy-done.49, ...), kind=kOutput, calls=%fused_computation.186 | convolution fusion | flops 5142180864 | bytes 21453824 | tf_op jit(solution)/shard_map/dot_general | solution.py:28
  221.9 5.2 %copy.78 = f32[768,1152]{0,1:T(8,128)} copy(f32[768,1152]{1,0:T(8,128)} %bitcast.212) | data formatting | bytes 7077888 | tf_op jit(solution)/shard_map/mul | solution.py:311
  227.2 5.5 %fusion.49 = bf16[768,1152]{0,1:T(8,128)(2,1)} fusion(f32[768,1152]{0,1:T(8,128)} %copy.78, bf16[768,768]{1,0:T(8,128)(2,1)S(1)} %copy-done, bf16[1088,768]{1,0:T(8,128)(2,1)} %copy-done.16), kind=kOutput, calls=%fused_computation.180 | convolution fusion | flops 1360723968 | bytes 8159232 | tf_op jit(solution)/shard_map/dot_general | solution.py:28
  232.6 262.4 %conditional.1 = (bf16[8,1,64,768]{3,2,1,0:T(8,128)(2,1)}, bf16[1,4,144,768]{3,2,1,0:T(8,128)(2,1)}, bf16[8,1,64,768]{3,2,0,1:T(8,128)(2,1)}, bf16[1,4,144,768]{...) conditional(s32[]{:T(128)} %convert_element_type.269, () %tuple.17, ...), branch_computations={%region_8.9_spmd, %region_9.12_spmd} | conditional | flops 69695455232 | bytes 379628256 | solution.py:653
  234.4 3.2 collective-permute-start.1
  238.8 4.4 all-to-all-start
  243.2 3.9 copy.79.refs_6_
  247.1 3.8 copy.81.refs_3_
  253.1 3.9 copy.80.refs_2_
  257.1 31.0 %branch_1_fun.2 = (bf16[384,1152]{1,0:T(8,128)(2,1)}, bf16[1088,384]{1,0:T(8,128)(2,1)}, bf16[1088,384]{1,0:T(8,128)(2,1)}, f32[6,128,128]{2,1,0:T(8,128)}, f32[...) custom-call(bf16[12,1088,1152]{2,1,0:T(8,128)(2,1)} %get-tuple-element.30.refs_0_, bf16[768,1152]{1,0:T(8,128)(2,1)} %get-tuple-element.31.refs_1_, ...), custom_call_target="tpu_custom_call" | custom-call | flops 30802968576 | bytes 15040512 | tf_op jit(solution)/shard_map/cond/branch_1_fun/pallas_call | solution.py:193
  294.0 31.9 %branch_1_fun.3 = (bf16[384,1152]{1,0:T(8,128)(2,1)}, bf16[1088,384]{1,0:T(8,128)(2,1)}, bf16[1088,384]{1,0:T(8,128)(2,1)}, f32[6,128,128]{2,1,0:T(8,128)}, f32[...) custom-call(bf16[12,1088,1152]{2,1,0:T(8,128)(2,1)} %get-tuple-element.30.refs_0_, bf16[768,1152]{1,0:T(8,128)(2,1)} %get-tuple-element.31.refs_1_, ...), custom_call_target="tpu_custom_call" | custom-call | flops 30802968576 | bytes 15040512 | tf_op jit(solution)/shard_map/cond/branch_1_fun/pallas_call | solution.py:193
  327.6 4.9 fusion.9
  334.3 2.8 fusion.11
  338.8 2.5 fusion.16
  341.6 2.5 fusion.17
  345.7 4.7 fusion.10
  350.5 2.7 pad_maximum_fusion.1
  364.6 3.6 collective-permute-start.4
  368.4 4.2 all-to-all-start.1
  381.8 6.8 %collective-permute-done.5 = bf16[144,768]{1,0:T(8,128)(2,1)} collective-permute-done((bf16[144,768]{1,0:T(8,128)(2,1)}, bf16[144,768]{1,0:T(8,128)(2,1)}, u32[]{:S(2)}, u32[]{:S(2)}) %collective-permute-start.5) | collective-permute-done | bytes 221216 | tf_op jit(solution)/shard_map/cond/branch_1_fun/ppermute | solution.py:374
  389.9 10.6 %collective-permute-done.7 = bf16[320,768]{1,0:T(8,128)(2,1)S(1)} collective-permute-done((bf16[320,768]{1,0:T(8,128)(2,1)S(1)}, bf16[320,768]{1,0:T(8,128)(2,1)S(1)}, u32[]{:S(2)}, u32[]{:S(2)}) %collective-permute-start.7) | collective-permute-done | bytes 491552 | tf_op jit(solution)/shard_map/cond/branch_1_fun/ppermute | solution.py:398
  402.9 5.8 %collective-permute-done.8 = bf16[160,768]{1,0:T(8,128)(2,1)S(1)} collective-permute-done((bf16[160,768]{1,0:T(8,128)(2,1)S(1)}, bf16[160,768]{1,0:T(8,128)(2,1)S(1)}, u32[]{:S(2)}, u32[]{:S(2)}) %collective-permute-start.8) | collective-permute-done | bytes 245792 | tf_op jit(solution)/shard_map/cond/branch_1_fun/ppermute | solution.py:398
  430.0 5.2 collective-permute-done.14
  437.3 4.2 collective-permute-done.15
  448.0 2.8 collective-permute-done.25
  453.6 8.0 %collective-permute-done.27 = bf16[4,40,768]{2,1,0:T(8,128)(2,1)S(1)} collective-permute-done((bf16[4,40,768]{2,1,0:T(8,128)(2,1)S(1)}, bf16[4,40,768]{2,1,0:T(8,128)(2,1)S(1)}, u32[]{:S(2)}, u32[]{:S(2)}) %collective-permute-start.27) | collective-permute-done | bytes 245792 | tf_op jit(solution)/shard_map/cond/branch_1_fun/ppermute | solution.py:420
  461.6 3.2 collective-permute-start.28
  466.1 11.9 %collective-permute-done.28 = bf16[8,40,768]{2,1,0:T(8,128)(2,1)S(1)} collective-permute-done((bf16[8,40,768]{2,1,0:T(8,128)(2,1)S(1)}, bf16[8,40,768]{2,1,0:T(8,128)(2,1)S(1)}, u32[]{:S(2)}, u32[]{:S(2)}) %collective-permute-start.28) | collective-permute-done | bytes 491552 | tf_op jit(solution)/shard_map/cond/branch_1_fun/ppermute | solution.py:420
  482.6 3.9 maximum_convert_fusion
  488.6 6.2 %fusion.85 = (f32[768,768]{1,0:T(8,128)}, f32[768,768]{1,0:T(8,128)}, f32[768,768]{1,0:T(8,128)}) fusion(f32[2560,768]{1,0:T(8,128)} %maximum_convert_fusion), kind=kLoop, calls=%fused_computation.292 | loop fusion | bytes 14155776 | tf_op jit(solution)/shard_map/cond/branch_1_fun/slice | solution.py:644
  498.8 5.0 convert_element_type.304
  503.9 4.5 convert_element_type.306
  (391 shorter events, 129.6 us)
Async XLA Ops:
  7.2 101.8 %copy-start = (bf16[768,768]{1,0:T(8,128)(2,1)S(1)}, bf16[768,768]{1,0:T(8,128)(2,1)}, u32[]{:S(2)}) copy-start(bf16[768,768]{1,0:T(8,128)(2,1)} %param.41) | copy-start | bytes 3538948
  7.2 18.2 %copy-start.40 = (s32[1,1,1088]{2,1,0:T(1,128)S(1)}, s32[1,1,1088]{2,1,0:T(1,128)}, u32[]{:S(2)}) copy-start(s32[1,1,1088]{2,1,0:T(1,128)} %param.33) | copy-start | bytes 13060
  7.2 21.5 %copy-start.42 = (f32[65,12]{0,1:T(8,128)S(1)}, f32[65,12]{0,1:T(8,128)}, u32[]{:S(2)}) copy-start(f32[65,12]{0,1:T(8,128)} %param.52) | copy-start | bytes 9364
  9.4 34.2 %collective-permute-start.30 = (bf16[144,768]{1,0:T(8,128)(2,1)}, bf16[144,768]{1,0:T(8,128)(2,1)}, u32[]{:S(2)}, u32[]{:S(2)}) collective-permute-start(bf16[144,768]{1,0:T(8,128)(2,1)} %get-tuple-element.314), channel_id=1, source_target_pairs={{0,1},{1,0},{2,3},{3,2},{4,5},{5,4},{6,7},{7,6},{8,9},{9,8},{10,11... | collective-permute-start | bytes 663560 | tf_op jit(solution)/shard_map/ppermute | solution.py:353
  12.4 25.8 %all-to-all-start.2 = ((bf16[8,64,768]{2,1,0:T(8,128)(2,1)}), bf16[8,64,768]{2,1,0:T(8,128)(2,1)S(1)}, u32[]{:S(2)}, u32[]{:S(2)}) async-start(bf16[8,64,768]{2,1,0:T(8,128)(2,1)} %bitcast.243), calls=%async_computation.2 | async-start | bytes 1572864 | tf_op jit(solution)/shard_map/all_to_all | solution.py:341
  16.2 28.7 %collective-permute-start.31 = (bf16[144,768]{1,0:T(8,128)(2,1)}, bf16[144,768]{1,0:T(8,128)(2,1)}, u32[]{:S(2)}, u32[]{:S(2)}) collective-permute-start(bf16[144,768]{1,0:T(8,128)(2,1)} %get-tuple-element.315), channel_id=1, source_target_pairs={{0,2},{1,3},{2,0},{3,1},{4,6},{5,7},{6,4},{7,5},{8,10},{9,11},{10,... | collective-permute-start | bytes 663560 | tf_op jit(solution)/shard_map/ppermute | solution.py:353
  18.8 27.0 %collective-permute-start.32 = (bf16[144,768]{1,0:T(8,128)(2,1)}, bf16[144,768]{1,0:T(8,128)(2,1)}, u32[]{:S(2)}, u32[]{:S(2)}) collective-permute-start(bf16[144,768]{1,0:T(8,128)(2,1)} %get-tuple-element.313), channel_id=1, source_target_pairs={{0,3},{1,2},{2,1},{3,0},{4,7},{5,6},{6,5},{7,4},{8,11},{9,10},{10,... | collective-permute-start | bytes 663560 | tf_op jit(solution)/shard_map/ppermute | solution.py:353
  20.0 88.0 %collective-permute-start.33 = (bf16[144,768]{1,0:T(8,128)(2,1)}, bf16[144,768]{1,0:T(8,128)(2,1)}, u32[]{:S(2)}, u32[]{:S(2)}) collective-permute-start(bf16[144,768]{1,0:T(8,128)(2,1)} %get-tuple-element.310), channel_id=1, source_target_pairs={{0,1},{1,0},{2,3},{3,2},{4,5},{5,4},{6,7},{7,6},{8,9},{9,8},{10,11... | collective-permute-start | bytes 663560 | tf_op jit(solution)/shard_map/ppermute | solution.py:353
  20.7 87.4 %collective-permute-start.34 = (bf16[144,768]{1,0:T(8,128)(2,1)}, bf16[144,768]{1,0:T(8,128)(2,1)}, u32[]{:S(2)}, u32[]{:S(2)}) collective-permute-start(bf16[144,768]{1,0:T(8,128)(2,1)} %get-tuple-element.312), channel_id=1, source_target_pairs={{0,2},{1,3},{2,0},{3,1},{4,6},{5,7},{6,4},{7,5},{8,10},{9,11},{10,... | collective-permute-start | bytes 663560 | tf_op jit(solution)/shard_map/ppermute | solution.py:353
  38.3 69.8 %all-to-all-start.3 = ((bf16[8,64,768]{2,1,0:T(8,128)(2,1)}), bf16[8,64,768]{2,1,0:T(8,128)(2,1)S(1)}, u32[]{:S(2)}, u32[]{:S(2)}) async-start(bf16[8,64,768]{2,1,0:T(8,128)(2,1)} %bitcast.81), calls=%async_computation.3 | async-start | bytes 1572864 | tf_op jit(solution)/shard_map/all_to_all | solution.py:341
  42.4 452.7 %all-reduce.13.cloned.1.call-start = ((), (), s32[]{:S(2)}) async-start(), calls=%async_computation.4 | async-start | bytes 21282816 | tf_op jit(solution)/shard_map/psum | solution.py:574
  43.6 64.4 %collective-permute-start.35 = (bf16[144,768]{1,0:T(8,128)(2,1)}, bf16[144,768]{1,0:T(8,128)(2,1)S(1)}, u32[]{:S(2)}, u32[]{:S(2)}) collective-permute-start(bf16[144,768]{1,0:T(8,128)(2,1)} %get-tuple-element.309), channel_id=1, source_target_pairs={{0,3},{1,2},{2,1},{3,0},{4,7},{5,6},{6,5},{7,4},{8,11},{9,10},{10,... | collective-permute-start | bytes 663560 | tf_op jit(solution)/shard_map/ppermute | solution.py:353
  55.5 53.5 %copy-start.61 = (f32[768]{0:T(1024)S(1)}, f32[768]{0:T(1024)}, u32[]{:S(2)}) copy-start(f32[768]{0:T(1024)} %param.42) | copy-start | bytes 9220
  109.0 41.6 %slice-start.2 = ((s8[4718592]{0:T(1024)(128)(4,1)}), s8[4194304]{0:T(1024)(128)(4,1)S(1)}, s32[]{:S(2)}) async-start(s8[4718592]{0:T(1024)(128)(4,1)} %bitcast.255), calls=%async_computation.7 | async-start | bytes 8388608
  114.2 36.5 %slice-start.3 = ((s8[4718592]{0:T(1024)(128)(4,1)}), s8[524288]{0:T(1024)(128)(4,1)S(1)}, s32[]{:S(2)}) async-start(s8[4718592]{0:T(1024)(128)(4,1)} %bitcast.255), calls=%async_computation.8 | async-start | bytes 1048576
  114.2 36.5 %copy-start.62 = (f32[768]{0:T(1024)S(1)}, f32[768]{0:T(1024)}, u32[]{:S(2)}) copy-start(f32[768]{0:T(1024)} %param.48) | copy-start | bytes 9220
  233.5 58.1 %collective-permute-start = (bf16[144,768]{1,0:T(8,128)(2,1)}, bf16[144,768]{1,0:T(8,128)(2,1)S(1)}, u32[]{:S(2)}, u32[]{:S(2)}) collective-permute-start(bf16[144,768]{1,0:T(8,128)(2,1)} %get-tuple-element.262), channel_id=1, source_target_pairs={{0,1},{1,0},{2,3},{3,2},{4,5},{5,4},{6,7},{7,6},{8,9},{9,8},{10,11... | collective-permute-start | bytes 663560 | tf_op jit(solution)/shard_map/cond/branch_1_fun/ppermute | solution.py:374
  234.4 57.1 %collective-permute-start.1 = (bf16[144,768]{1,0:T(8,128)(2,1)}, bf16[144,768]{1,0:T(8,128)(2,1)}, u32[]{:S(2)}, u32[]{:S(2)}) collective-permute-start(bf16[144,768]{1,0:T(8,128)(2,1)} %get-tuple-element.261), channel_id=1, source_target_pairs={{0,2},{1,3},{2,0},{3,1},{4,6},{5,7},{6,4},{7,5},{8,10},{9,11},{10,... | collective-permute-start | bytes 663560 | tf_op jit(solution)/shard_map/cond/branch_1_fun/ppermute | solution.py:374
  237.7 53.9 %collective-permute-start.2 = (bf16[144,768]{1,0:T(8,128)(2,1)}, bf16[144,768]{1,0:T(8,128)(2,1)}, u32[]{:S(2)}, u32[]{:S(2)}) collective-permute-start(bf16[144,768]{1,0:T(8,128)(2,1)} %get-tuple-element.263), channel_id=1, source_target_pairs={{0,3},{1,2},{2,1},{3,0},{4,7},{5,6},{6,5},{7,4},{8,11},{9,10},{10,... | collective-permute-start | bytes 663560 | tf_op jit(solution)/shard_map/cond/branch_1_fun/ppermute | solution.py:374
  238.8 55.2 %all-to-all-start = ((bf16[8,64,768]{2,1,0:T(8,128)(2,1)}), bf16[8,64,768]{2,1,0:T(8,128)(2,1)}, u32[]{:S(2)}, u32[]{:S(2)}) async-start(bf16[8,64,768]{2,1,0:T(8,128)(2,1)} %bitcast.1), calls=%async_computation | async-start | bytes 1572864 | tf_op jit(solution)/shard_map/cond/branch_1_fun/all_to_all | solution.py:341
  355.5 17.2 %collective-permute-start.6 = (bf16[640,768]{1,0:T(8,128)(2,1)}, bf16[640,768]{1,0:T(8,128)(2,1)}, u32[]{:S(2)}, u32[]{:S(2)}) collective-permute-start(bf16[640,768]{1,0:T(8,128)(2,1)} %dynamic-slice_bitcast_fusion.1), channel_id=1, source_target_pairs={{0,4},{4,0},{8,12},{12,8},{16,20},{20,16},{24,28},{28,24},{1,5},{5... | collective-permute-start | bytes 2949128 | tf_op jit(solution)/shard_map/cond/branch_1_fun/ppermute | solution.py:398
  357.1 19.4 %collective-permute-start.18 = (bf16[640,768]{1,0:T(8,128)(2,1)}, bf16[640,768]{1,0:T(8,128)(2,1)}, u32[]{:S(2)}, u32[]{:S(2)}) collective-permute-start(bf16[640,768]{1,0:T(8,128)(2,1)} %dynamic-slice_bitcast_fusion), channel_id=1, source_target_pairs={{0,4},{4,0},{8,12},{12,8},{16,20},{20,16},{24,28},{28,24},{1,5},{5... | collective-permute-start | bytes 2949128 | tf_op jit(solution)/shard_map/cond/branch_1_fun/ppermute | solution.py:398
  364.0 15.6 %collective-permute-start.3 = (bf16[144,768]{1,0:T(8,128)(2,1)}, bf16[144,768]{1,0:T(8,128)(2,1)}, u32[]{:S(2)}, u32[]{:S(2)}) collective-permute-start(bf16[144,768]{1,0:T(8,128)(2,1)} %get-tuple-element.259), channel_id=1, source_target_pairs={{0,1},{1,0},{2,3},{3,2},{4,5},{5,4},{6,7},{7,6},{8,9},{9,8},{10,11... | collective-permute-start | bytes 663560 | tf_op jit(solution)/shard_map/cond/branch_1_fun/ppermute | solution.py:374
  364.6 17.2 %collective-permute-start.4 = (bf16[144,768]{1,0:T(8,128)(2,1)}, bf16[144,768]{1,0:T(8,128)(2,1)}, u32[]{:S(2)}, u32[]{:S(2)}) collective-permute-start(bf16[144,768]{1,0:T(8,128)(2,1)} %get-tuple-element.258), channel_id=1, source_target_pairs={{0,2},{1,3},{2,0},{3,1},{4,6},{5,7},{6,4},{7,5},{8,10},{9,11},{10,... | collective-permute-start | bytes 663560 | tf_op jit(solution)/shard_map/cond/branch_1_fun/ppermute | solution.py:374
  368.1 20.5 %collective-permute-start.5 = (bf16[144,768]{1,0:T(8,128)(2,1)}, bf16[144,768]{1,0:T(8,128)(2,1)}, u32[]{:S(2)}, u32[]{:S(2)}) collective-permute-start(bf16[144,768]{1,0:T(8,128)(2,1)} %get-tuple-element.257), channel_id=1, source_target_pairs={{0,3},{1,2},{2,1},{3,0},{4,7},{5,6},{6,5},{7,4},{8,11},{9,10},{10,... | collective-permute-start | bytes 663560 | tf_op jit(solution)/shard_map/cond/branch_1_fun/ppermute | solution.py:374
  368.4 126.4 %all-to-all-start.1 = ((bf16[8,64,768]{2,1,0:T(8,128)(2,1)}), bf16[8,64,768]{2,1,0:T(8,128)(2,1)}, u32[]{:S(2)}, u32[]{:S(2)}) async-start(bf16[8,64,768]{2,1,0:T(8,128)(2,1)} %bitcast.225), calls=%async_computation.1 | async-start | bytes 1572864 | tf_op jit(solution)/shard_map/cond/branch_1_fun/all_to_all | solution.py:341
  374.6 25.8 %collective-permute-start.7 = (bf16[320,768]{1,0:T(8,128)(2,1)S(1)}, bf16[320,768]{1,0:T(8,128)(2,1)S(1)}, u32[]{:S(2)}, u32[]{:S(2)}) collective-permute-start(bf16[320,768]{1,0:T(8,128)(2,1)S(1)} %dynamic-slice_bitcast_fusion.3), channel_id=1, source_target_pairs={{0,8},{4,12},{8,0},{12,4},{16,24},{20,28},{24,16},{28,20},{1,9},{5... | collective-permute-start | bytes 1474568 | tf_op jit(solution)/shard_map/cond/branch_1_fun/ppermute | solution.py:398
  378.1 24.1 %collective-permute-start.19 = (bf16[320,768]{1,0:T(8,128)(2,1)S(1)}, bf16[320,768]{1,0:T(8,128)(2,1)S(1)}, u32[]{:S(2)}, u32[]{:S(2)}) collective-permute-start(bf16[320,768]{1,0:T(8,128)(2,1)S(1)} %dynamic-slice_bitcast_fusion.2), channel_id=1, source_target_pairs={{0,16},{4,20},{8,24},{12,28},{16,0},{20,4},{24,8},{28,12},{1,17},{... | collective-permute-start | bytes 1474568 | tf_op jit(solution)/shard_map/cond/branch_1_fun/ppermute | solution.py:398
  400.6 8.1 %collective-permute-start.8 = (bf16[160,768]{1,0:T(8,128)(2,1)S(1)}, bf16[160,768]{1,0:T(8,128)(2,1)S(1)}, u32[]{:S(2)}, u32[]{:S(2)}) collective-permute-start(bf16[160,768]{1,0:T(8,128)(2,1)S(1)} %dynamic-slice_bitcast_fusion.5), channel_id=1, source_target_pairs={{0,16},{4,20},{8,24},{12,28},{16,0},{20,4},{24,8},{28,12},{1,17},{... | collective-permute-start | bytes 737288 | tf_op jit(solution)/shard_map/cond/branch_1_fun/ppermute | solution.py:398
  402.4 10.2 %collective-permute-start.20 = (bf16[160,768]{1,0:T(8,128)(2,1)S(1)}, bf16[160,768]{1,0:T(8,128)(2,1)S(1)}, u32[]{:S(2)}, u32[]{:S(2)}) collective-permute-start(bf16[160,768]{1,0:T(8,128)(2,1)S(1)} %dynamic-slice_bitcast_fusion.4), channel_id=1, source_target_pairs={{0,8},{4,12},{8,0},{12,4},{16,24},{20,28},{24,16},{28,20},{1,9},{5... | collective-permute-start | bytes 737288 | tf_op jit(solution)/shard_map/cond/branch_1_fun/ppermute | solution.py:398
  408.9 9.0 %collective-permute-start.10 = (bf16[40,768]{1,0:T(8,128)(2,1)S(1)}, bf16[40,768]{1,0:T(8,128)(2,1)S(1)}, u32[]{:S(2)}, u32[]{:S(2)}) collective-permute-start(bf16[40,768]{1,0:T(8,128)(2,1)S(1)} %get-tuple-element.275), channel_id=1, source_target_pairs={{0,2},{1,3},{2,0},{3,1},{4,6},{5,7},{6,4},{7,5},{8,10},{9,11},{10,... | collective-permute-start | bytes 184328 | tf_op jit(solution)/shard_map/cond/branch_1_fun/ppermute | solution.py:353
  411.2 8.2 %collective-permute-start.11 = (bf16[40,768]{1,0:T(8,128)(2,1)S(1)}, bf16[40,768]{1,0:T(8,128)(2,1)S(1)}, u32[]{:S(2)}, u32[]{:S(2)}) collective-permute-start(bf16[40,768]{1,0:T(8,128)(2,1)S(1)} %get-tuple-element.274), channel_id=1, source_target_pairs={{0,3},{1,2},{2,1},{3,0},{4,7},{5,6},{6,5},{7,4},{8,11},{9,10},{10,... | collective-permute-start | bytes 184328 | tf_op jit(solution)/shard_map/cond/branch_1_fun/ppermute | solution.py:353
  412.6 7.8 %collective-permute-start.9 = (bf16[40,768]{1,0:T(8,128)(2,1)S(1)}, bf16[40,768]{1,0:T(8,128)(2,1)S(1)}, u32[]{:S(2)}, u32[]{:S(2)}) collective-permute-start(bf16[40,768]{1,0:T(8,128)(2,1)S(1)} %get-tuple-element.273), channel_id=1, source_target_pairs={{0,1},{1,0},{2,3},{3,2},{4,5},{5,4},{6,7},{7,6},{8,9},{9,8},{10,11... | collective-permute-start | bytes 184328 | tf_op jit(solution)/shard_map/cond/branch_1_fun/ppermute | solution.py:353
  412.7 29.3 %collective-permute-start.21 = (bf16[40,768]{1,0:T(8,128)(2,1)S(1)}, bf16[40,768]{1,0:T(8,128)(2,1)S(1)}, u32[]{:S(2)}, u32[]{:S(2)}) collective-permute-start(bf16[40,768]{1,0:T(8,128)(2,1)S(1)} %get-tuple-element.279), channel_id=1, source_target_pairs={{0,1},{1,0},{2,3},{3,2},{4,5},{5,4},{6,7},{7,6},{8,9},{9,8},{10,11... | collective-permute-start | bytes 184328 | tf_op jit(solution)/shard_map/cond/branch_1_fun/ppermute | solution.py:353
  414.8 27.3 %collective-permute-start.22 = (bf16[40,768]{1,0:T(8,128)(2,1)S(1)}, bf16[40,768]{1,0:T(8,128)(2,1)S(1)}, u32[]{:S(2)}, u32[]{:S(2)}) collective-permute-start(bf16[40,768]{1,0:T(8,128)(2,1)S(1)} %get-tuple-element.281), channel_id=1, source_target_pairs={{0,2},{1,3},{2,0},{3,1},{4,6},{5,7},{6,4},{7,5},{8,10},{9,11},{10,... | collective-permute-start | bytes 184328 | tf_op jit(solution)/shard_map/cond/branch_1_fun/ppermute | solution.py:353
  420.4 7.0 %collective-permute-start.12 = (bf16[1,40,768]{2,1,0:T(8,128)(2,1)S(1)}, bf16[1,40,768]{2,1,0:T(8,128)(2,1)S(1)}, u32[]{:S(2)}, u32[]{:S(2)}) collective-permute-start(bf16[1,40,768]{2,1,0:T(8,128)(2,1)S(1)} %get-tuple-element.237), channel_id=1, source_target_pairs={{0,1},{1,0},{2,3},{3,2},{4,5},{5,4},{6,7},{7,6},{8,9},{9,8},{10,11... | collective-permute-start | bytes 184328 | tf_op jit(solution)/shard_map/cond/branch_1_fun/ppermute | solution.py:417
  422.2 7.8 %collective-permute-start.13 = (bf16[1,40,768]{2,1,0:T(8,128)(2,1)S(1)}, bf16[1,40,768]{2,1,0:T(8,128)(2,1)S(1)}, u32[]{:S(2)}, u32[]{:S(2)}) collective-permute-start(bf16[1,40,768]{2,1,0:T(8,128)(2,1)S(1)} %get-tuple-element.237), channel_id=1, source_target_pairs={{0,2},{1,3},{2,0},{3,1},{4,6},{5,7},{6,4},{7,5},{8,10},{9,11},{10,... | collective-permute-start | bytes 184328 | tf_op jit(solution)/shard_map/cond/branch_1_fun/ppermute | solution.py:417
  423.2 12.0 %collective-permute-start.14 = (bf16[1,40,768]{2,1,0:T(8,128)(2,1)S(1)}, bf16[1,40,768]{2,1,0:T(8,128)(2,1)S(1)}, u32[]{:S(2)}, u32[]{:S(2)}) collective-permute-start(bf16[1,40,768]{2,1,0:T(8,128)(2,1)S(1)} %get-tuple-element.237), channel_id=1, source_target_pairs={{0,3},{1,2},{2,1},{3,0},{4,7},{5,6},{6,5},{7,4},{8,11},{9,10},{10,... | collective-permute-start | bytes 184328 | tf_op jit(solution)/shard_map/cond/branch_1_fun/ppermute | solution.py:417
  427.4 14.7 %collective-permute-start.23 = (bf16[40,768]{1,0:T(8,128)(2,1)S(1)}, bf16[40,768]{1,0:T(8,128)(2,1)S(1)}, u32[]{:S(2)}, u32[]{:S(2)}) collective-permute-start(bf16[40,768]{1,0:T(8,128)(2,1)S(1)} %get-tuple-element.280), channel_id=1, source_target_pairs={{0,3},{1,2},{2,1},{3,0},{4,7},{5,6},{6,5},{7,4},{8,11},{9,10},{10,... | collective-permute-start | bytes 184328 | tf_op jit(solution)/shard_map/cond/branch_1_fun/ppermute | solution.py:353
  435.2 6.3 %collective-permute-start.15 = (bf16[4,40,768]{2,1,0:T(8,128)(2,1)S(1)}, bf16[4,40,768]{2,1,0:T(8,128)(2,1)S(1)}, u32[]{:S(2)}, u32[]{:S(2)}) collective-permute-start(bf16[4,40,768]{2,1,0:T(8,128)(2,1)S(1)} %pad_maximum_fusion.10), channel_id=1, source_target_pairs={{0,16},{4,20},{8,24},{12,28},{16,0},{20,4},{24,8},{28,12},{1,17},{... | collective-permute-start | bytes 737288 | tf_op jit(solution)/shard_map/cond/branch_1_fun/ppermute | solution.py:420
  441.5 11.8 %collective-permute-start.16 = (bf16[8,40,768]{2,1,0:T(8,128)(2,1)S(1)}, bf16[8,40,768]{2,1,0:T(8,128)(2,1)S(1)}, u32[]{:S(2)}, u32[]{:S(2)}) collective-permute-start(bf16[8,40,768]{2,1,0:T(8,128)(2,1)S(1)} %get-tuple-element.272), channel_id=1, source_target_pairs={{0,8},{4,12},{8,0},{12,4},{16,24},{20,28},{24,16},{28,20},{1,9},{5... | collective-permute-start | bytes 1474568 | tf_op jit(solution)/shard_map/cond/branch_1_fun/ppermute | solution.py:420
  442.1 5.9 %collective-permute-start.24 = (bf16[1,40,768]{2,1,0:T(8,128)(2,1)S(1)}, bf16[1,40,768]{2,1,0:T(8,128)(2,1)S(1)}, u32[]{:S(2)}, u32[]{:S(2)}) collective-permute-start(bf16[1,40,768]{2,1,0:T(8,128)(2,1)S(1)} %get-tuple-element.239), channel_id=1, source_target_pairs={{0,1},{1,0},{2,3},{3,2},{4,5},{5,4},{6,7},{7,6},{8,9},{9,8},{10,11... | collective-permute-start | bytes 184328 | tf_op jit(solution)/shard_map/cond/branch_1_fun/ppermute | solution.py:417
  443.9 6.9 %collective-permute-start.25 = (bf16[1,40,768]{2,1,0:T(8,128)(2,1)S(1)}, bf16[1,40,768]{2,1,0:T(8,128)(2,1)S(1)}, u32[]{:S(2)}, u32[]{:S(2)}) collective-permute-start(bf16[1,40,768]{2,1,0:T(8,128)(2,1)S(1)} %get-tuple-element.239), channel_id=1, source_target_pairs={{0,2},{1,3},{2,0},{3,1},{4,6},{5,7},{6,4},{7,5},{8,10},{9,11},{10,... | collective-permute-start | bytes 184328 | tf_op jit(solution)/shard_map/cond/branch_1_fun/ppermute | solution.py:417
  445.3 6.5 %collective-permute-start.26 = (bf16[1,40,768]{2,1,0:T(8,128)(2,1)S(1)}, bf16[1,40,768]{2,1,0:T(8,128)(2,1)S(1)}, u32[]{:S(2)}, u32[]{:S(2)}) collective-permute-start(bf16[1,40,768]{2,1,0:T(8,128)(2,1)S(1)} %get-tuple-element.239), channel_id=1, source_target_pairs={{0,3},{1,2},{2,1},{3,0},{4,7},{5,6},{6,5},{7,4},{8,11},{9,10},{10,... | collective-permute-start | bytes 184328 | tf_op jit(solution)/shard_map/cond/branch_1_fun/ppermute | solution.py:417
  451.9 9.7 %collective-permute-start.27 = (bf16[4,40,768]{2,1,0:T(8,128)(2,1)S(1)}, bf16[4,40,768]{2,1,0:T(8,128)(2,1)S(1)}, u32[]{:S(2)}, u32[]{:S(2)}) collective-permute-start(bf16[4,40,768]{2,1,0:T(8,128)(2,1)S(1)} %pad_maximum_fusion.11), channel_id=1, source_target_pairs={{0,8},{4,12},{8,0},{12,4},{16,24},{20,28},{24,16},{28,20},{1,9},{5... | collective-permute-start | bytes 737288 | tf_op jit(solution)/shard_map/cond/branch_1_fun/ppermute | solution.py:420
  453.4 24.7 %collective-permute-start.17 = (bf16[16,40,768]{2,1,0:T(8,128)(2,1)S(1)}, bf16[16,40,768]{2,1,0:T(8,128)(2,1)S(1)}, u32[]{:S(2)}, u32[]{:S(2)}) collective-permute-start(bf16[16,40,768]{2,1,0:T(8,128)(2,1)S(1)} %get-tuple-element.266), channel_id=1, source_target_pairs={{0,4},{4,0},{8,12},{12,8},{16,20},{20,16},{24,28},{28,24},{1,5},{5... | collective-permute-start | bytes 2949128 | tf_op jit(solution)/shard_map/cond/branch_1_fun/ppermute | solution.py:420
  461.6 16.3 %collective-permute-start.28 = (bf16[8,40,768]{2,1,0:T(8,128)(2,1)S(1)}, bf16[8,40,768]{2,1,0:T(8,128)(2,1)S(1)}, u32[]{:S(2)}, u32[]{:S(2)}) collective-permute-start(bf16[8,40,768]{2,1,0:T(8,128)(2,1)S(1)} %get-tuple-element.278), channel_id=1, source_target_pairs={{0,16},{4,20},{8,24},{12,28},{16,0},{20,4},{24,8},{28,12},{1,17},{... | collective-permute-start | bytes 1474568 | tf_op jit(solution)/shard_map/cond/branch_1_fun/ppermute | solution.py:420
  478.0 2.6 collective-permute-start.29
  (65 other events, 318.6 us)
Sparse Core Ops, SparseCore 0:
  219.2 266.9 all-reduce.12

commit v3 on v2

v3 whole, which is shorter than its diff:
```python
from functools import partial

import jax
import jax.numpy as jnp
from jax import lax
from jax.experimental import pallas as pl
from jax.experimental.pallas import tpu as pltpu
from jax.sharding import PartitionSpec as P

HEADS = 12
TEXT = 512
PATCH = 576
SMALL_PATCH = 196
BF = jnp.bfloat16
F32 = jnp.float32
VMEM_BYTES = 60 * 2**20


def mm(left, right):
    return lax.dot_general(left, right, (((1,), (0,)), ((), ())), preferred_element_type=F32)


def inner(left, right):
    return lax.dot_general(left, right, (((0,), (0,)), ((), ())), preferred_element_type=F32)


def against(left, right):
    return lax.dot_general(left, right, (((1,), (1,)), ((), ())), preferred_element_type=F32)


def assemble(pieces, rows):
    at = 0
    for piece in pieces:
        rows[at : at + piece.shape[0], :] = piece[...]
        at += piece.shape[0]


def attend_kernel(count, *refs):
    pieces = refs[:count]
    (
        qw_ref, kw_ref, vw_ref, bias_ref, hot_ref, mask_ref, hott_ref, line_ref, width_ref,
        height_ref, exp_ref, ctxt_ref, ctx_ref, inv_ref, q_ref, kt_ref, v_ref, x_ref,
        keys, queries, values, rows,
    ) = refs[count:]
    seq = v_ref.shape[0]
    lanes = rows.shape[0]

    @pl.when(pl.program_id(0) == 0)
    def _():
        keys[:, 0:320] = hot_ref[0:seq, :]
        keys[:, 320:640] = hot_ref[0:seq, :]
        values[64:80, :] = jnp.ones((16, seq), BF)
        assemble(pieces, rows)
        rows[seq:lanes, :] = jnp.zeros((lanes - seq, rows.shape[1]), BF)
        x_ref[...] = rows[0:seq, :]

    both = mm(rows[...], jnp.concatenate([qw_ref[...], kw_ref[...]], axis=1))
    q = ((both[:, 0:128] + bias_ref[0]) * 0.125).astype(BF)
    k = both[:, 128:256].astype(BF)
    v = (mm(rows[...], vw_ref[...]) + bias_ref[1]).astype(BF)
    q_ref[...] = q
    v_ref[...] = v[0:seq]
    q_t = q.astype(F32).T.astype(BF)
    k = k.astype(F32)
    kt_ref[...] = k.T[:, 0:seq].astype(BF)
    v_t = v.astype(F32).T[:, 0:seq].astype(BF)
    lane = lax.broadcasted_iota(jnp.int32, (seq, 128), 1)
    contexts = []
    for h in range(2):
        mine = (lane < 64) if h == 0 else (lane >= 64)
        own, other = (640, 704) if h == 0 else (704, 640)
        keys[:, 640:768] = jnp.where(mine, k[0:seq], mask_ref[...].astype(F32)).astype(BF)
        queries[own : own + 64, :] = q_t[h * 64 : h * 64 + 64, :]
        queries[other : other + 64, :] = jnp.ones((64, lanes), BF)
        values[0:64, :] = v_t[h * 64 : h * 64 + 64, :]
        near = mm(line_ref[h], hott_ref[0:64, :]).astype(BF)
        queries[0:64, :] = near[0:64]
        queries[320:384, :] = near[64:128]
        near = mm(width_ref[h], hott_ref[64:192, :]).astype(BF)
        queries[64:192, :] = near[0:128]
        queries[384:512, :] = near[128:256]
        near = mm(height_ref[h], hott_ref[192:320, :]).astype(BF)
        queries[192:320, :] = near[0:128]
        queries[512:640, :] = near[128:256]
        scores = mm(keys[...], queries[...])
        peak = jnp.max(scores, axis=0, keepdims=True)
        weights = jnp.exp(scores - peak).astype(BF)
        exp_ref[h] = weights
        ctx = mm(values[...], weights)
        inverse = 1.0 / ctx[64:65]
        inv_ref[h] = inverse
        contexts.append(ctx[0:64] * inverse)
    ctx = jnp.concatenate(contexts, axis=0)
    ctxt_ref[...] = ctx.astype(BF)
    ctx_ref[...] = ctx.T[0:seq].astype(BF)


def attend(pieces, q_weight, k_weight, v_weight, bias, hot, mask, hot_t, line, width, height):
    seq = mask.shape[0]
    lanes, dim = hot.shape[0], q_weight.shape[0]

    def whole(a):
        return pl.BlockSpec(a.shape, lambda p: (0,) * a.ndim, pipeline_mode=pl.Buffered(1))

    def pair(a):
        return pl.BlockSpec((2,) + a.shape[1:], lambda p: (p, 0, 0))

    def columns(rows):
        return pl.BlockSpec((rows, 128), lambda p: (0, p))

    def rows(length):
        return pl.BlockSpec((128, length), lambda p: (p, 0))

    shape = jax.ShapeDtypeStruct
    return pl.pallas_call(
        partial(attend_kernel, len(pieces)),
        grid=(HEADS // 2,),
        in_specs=[whole(a) for a in pieces]
        + [
            columns(dim),
            columns(dim),
            columns(dim),
            pl.BlockSpec((2, 1, 128), lambda p: (0, 0, p)),
            whole(hot),
            whole(mask),
            whole(hot_t),
            pair(line),
            pair(width),
            pair(height),
        ],
        out_specs=[
            pl.BlockSpec((2, seq, lanes), lambda p: (p, 0, 0)),
            rows(lanes),
            columns(seq),
            pl.BlockSpec((2, 1, lanes), lambda p: (p, 0, 0)),
            columns(lanes),
            rows(seq),
            columns(seq),
            pl.BlockSpec((seq, dim), lambda p: (0, 0)),
        ],
        out_shape=[
            shape((HEADS, seq, lanes), BF),
            shape((dim, lanes), BF),
            shape((seq, dim), BF),
            shape((HEADS, 1, lanes), F32),
            shape((lanes, dim), BF),
            shape((dim, seq), BF),
            shape((seq, dim), BF),
            shape((seq, dim), BF),
        ],
        scratch_shapes=[
            pltpu.VMEM((seq, 768), BF),
            pltpu.VMEM((768, lanes), BF),
            pltpu.VMEM((80, seq), BF),
            pltpu.VMEM((lanes, dim), BF),
        ],
        compiler_params=pltpu.CompilerParams(vmem_limit_bytes=VMEM_BYTES),
        cost_estimate=pl.CostEstimate(
            flops=HEADS * seq * lanes * 4096, bytes_accessed=HEADS * seq * lanes * 2,
            transcendentals=HEADS * seq * lanes,
        ),
    )(*pieces, q_weight, k_weight, v_weight, bias, hot, mask, hot_t, line, width, height)


def attend_back_kernel(held, *refs):
    (
        exp_ref, ctxt_ref, inv_ref, v_ref, kt_ref, q_ref, dattn_ref, outw_ref, hot_ref, hott_ref,
        dqkv_ref, gwidth_ref, gheight_ref, gline_ref, values, dctx, lefts, rights, ds, dattn,
    ) = refs[:10] + refs[10 + held :]
    seq = v_ref.shape[0]
    lanes = q_ref.shape[0]

    @pl.when(pl.program_id(0) == 0)
    def _():
        for h in range(2):
            lefts[h, 64:192, :] = hott_ref[64:192, 0:seq]
            rights[h, :, 128:256] = hot_ref[:, 192:320]
        dattn[0:seq, :] = dattn_ref[...]
        dattn[seq:lanes, :] = jnp.zeros((lanes - seq, dattn.shape[1]), BF)

    lane = lax.broadcasted_iota(jnp.int32, (seq, 128), 1)
    query_lane = lax.broadcasted_iota(jnp.int32, (lanes, 128), 1)
    row = lax.broadcasted_iota(jnp.int32, (64, lanes), 0)
    line_hot = jnp.concatenate([hot_ref[:, 0:64], hot_ref[:, 0:64]], axis=1).astype(F32)
    d_rows_t = against(outw_ref[...], dattn[...])
    d_rows_t = [d_rows_t[h * 64 : h * 64 + 64] * inv_ref[h] for h in range(2)]
    d_rows = jnp.concatenate(d_rows_t, axis=0).T.astype(BF)
    results = []
    by_queries = []
    for h in range(2):
        mine = (lane < 64) if h == 0 else (lane >= 64)
        query_mine = (query_lane < 64) if h == 0 else (query_lane >= 64)
        own, other = (0, 64) if h == 0 else (64, 0)
        part = slice(h * 64, h * 64 + 64)
        values[h] = jnp.where(mine, v_ref[...].astype(F32), 1.0).astype(BF)
        delta = -jnp.sum(d_rows_t[h] * ctxt_ref[part, :].astype(F32), axis=0, keepdims=True)
        high = delta.astype(BF).astype(F32)
        extra = jnp.where(row == 0, high, jnp.where(row == 1, delta - high, 0.0))
        dctx[h, own : own + 64, :] = d_rows_t[h].astype(BF)
        dctx[h, other : other + 64, :] = extra.astype(BF)
        lefts[h, 0:64, :] = kt_ref[part, :]
        rights[h, :, 0:128] = jnp.where(query_mine, q_ref[...].astype(F32), line_hot).astype(BF)
        d_scores = mm(values[h], dctx[h])
        ds[h] = (exp_ref[h].astype(F32) * d_scores).astype(BF)
        by_query = mm(lefts[h], ds[h])
        by_queries.append(by_query[0:64] * 0.125)
        gwidth_ref[h] = mm(by_query[64:192].astype(BF), hot_ref[:, 64:192])
        by_key = mm(ds[h], rights[h])
        near = mm(hott_ref[0:64, 0:seq], by_key[:, 0:128].astype(BF))
        gline_ref[h] = near[:, 64:128] if h == 0 else near[:, 0:64]
        gheight_ref[h] = mm(hott_ref[192:320, 0:seq], by_key[:, 128:256].astype(BF))
        results.append((by_key[:, 0:128], mm(exp_ref[h], d_rows)))
    dqkv_ref[0] = jnp.concatenate(by_queries, axis=0).T[0:seq].astype(BF)
    dqkv_ref[1] = jnp.where(lane < 64, results[0][0], results[1][0]).astype(BF)
    dqkv_ref[2] = jnp.where(lane < 64, results[0][1], results[1][1]).astype(BF)


def attend_back(first, pairs, held, exps, ctx_t, inverse, v, k_t, q, d_attn, out_weight, hot, hot_t):
    seq, dim = v.shape
    lanes = q.shape[0]

    def whole(a):
        return pl.BlockSpec(a.shape, lambda p: (0,) * a.ndim, pipeline_mode=pl.Buffered(1))

    def columns(rows):
        return pl.BlockSpec((rows, 128), lambda p: (0, p + first))

    def rows(length):
        return pl.BlockSpec((128, length), lambda p: (p + first, 0))

    def pair(*shape, start=first):
        return pl.BlockSpec((2,) + shape, lambda p: (p + start, 0, 0))

    shape = jax.ShapeDtypeStruct
    return pl.pallas_call(
        partial(attend_back_kernel, len(held)),
        grid=(pairs,),
        in_specs=[
            pair(seq, lanes),
            rows(lanes),
            pair(1, lanes),
            columns(seq),
            rows(seq),
            columns(lanes),
            whole(d_attn),
            rows(dim),
            whole(hot),
            whole(hot_t),
        ]
        + [pl.BlockSpec(memory_space=pl.ANY)] * len(held),
        out_specs=[
            pl.BlockSpec((3, seq, 128), lambda p: (0, 0, p)),
            pair(128, 128, start=0),
            pair(128, 128, start=0),
            pair(64, 64, start=0),
        ],
        out_shape=[
            shape((3, seq, 128 * pairs), BF),
            shape((2 * pairs, 128, 128), F32),
            shape((2 * pairs, 128, 128), F32),
            shape((2 * pairs, 64, 64), F32),
        ],
        scratch_shapes=[
            pltpu.VMEM((2, seq, 128), BF),
            pltpu.VMEM((2, 128, lanes), BF),
            pltpu.VMEM((2, 192, seq), BF),
            pltpu.VMEM((2, lanes, 256), BF),
            pltpu.VMEM((2, seq, lanes), BF),
            pltpu.VMEM((lanes, dim), BF),
        ],
        compiler_params=pltpu.CompilerParams(vmem_limit_bytes=VMEM_BYTES),
        cost_estimate=pl.CostEstimate(
            flops=2 * pairs * seq * lanes * 4096, bytes_accessed=4 * pairs * seq * lanes,
            transcendentals=0,
        ),
    )(exps, ctx_t, inverse, v, k_t, q, d_attn, out_weight, hot, hot_t, *held)


def gelu_pair(x):
    bell = jnp.exp(x * x * -0.5)
    t = 1.0 / (1.0 + 0.23164189 * jnp.abs(x))
    poly = t * (0.127414796 + t * (-0.142248368 + t * (0.7107068705 + t * (-0.7265760135 + t * 0.5307027145))))
    upper = poly * bell
    phi = jnp.where(x < 0, upper, 1.0 - upper)
    return x * phi, phi + x * bell * 0.3989422804014327

def normalise(rows):
    mean = jnp.mean(rows, axis=-1, keepdims=True)
    centred = rows - mean
    scale = lax.rsqrt(jnp.mean(centred * centred, axis=-1, keepdims=True) + 1e-05)
    return centred * scale, scale

def normalise_back(hat, scale, d_hat):
    return scale * (d_hat - jnp.mean(d_hat, axis=-1, keepdims=True) - hat * jnp.mean(d_hat * hat, axis=-1, keepdims=True))

def rows_kernel(count, *refs):
    pieces = refs[:count]
    (
        x_ref, ctx_ref, out_w, up_w, down_w, bias_ref, up_b, final_ref, dmid_ref, dattn_ref,
        normed_ref, act_ref, dbranch_ref, dpre_ref, sums_ref, upsum_ref, slope, cots,
    ) = refs[count:]
    step = pl.program_id(0)
    block = x_ref.shape[0]

    @pl.when(pl.program_id(0)==0)
    def _():
        sums_ref[...] = jnp.zeros_like(sums_ref)
        upsum_ref[...] = jnp.zeros_like(upsum_ref)
        assemble(pieces, cots)

    ff = up_w.shape[1]
    attn = mm(ctx_ref[...], out_w[...]) + bias_ref[0:1]
    hat, scale = normalise(x_ref[...].astype(F32) + attn)
    normed = hat * bias_ref[1:2] + bias_ref[2:3]
    low = normed.astype(BF)
    normed_ref[...] = low
    branch = bias_ref[3:4]
    for f in range(0, ff, 768):
        part = slice(f, f+768)
        act, grad = gelu_pair(mm(low, up_w[:, part]) + up_b[:, part])
        slope[:, part] = grad
        act = act.astype(BF)
        act_ref[:, part] = act
        branch = branch + mm(act, down_w[part, :])
    final_hat, final_scale = normalise(normed + branch)
    final_ref[...] = (final_hat * bias_ref[4:5] + bias_ref[5:6]).astype(BF)
    cot = cots[pl.ds(pl.multiple_of(step * block, 16), block), :].astype(F32)
    d_sum = normalise_back(final_hat, final_scale, cot * bias_ref[4:5])
    d_branch = d_sum.astype(BF)
    dbranch_ref[...] = d_branch
    total = lambda a: jnp.sum(a, axis=0, keepdims=True)
    d_normed = d_sum
    for f in range(0, ff, 768):
        part = slice(f, f+768)
        d_pre = (against(d_branch, down_w[part, :]) * slope[:, part]).astype(BF)
        dpre_ref[:, part] = d_pre
        upsum_ref[:, part] += total(d_pre.astype(F32))
        d_normed = d_normed + against(d_pre, up_w[:, part])
    d_mid = normalise_back(hat, scale, d_normed * bias_ref[1:2])
    dmid_ref[...] = d_mid
    d_attn = d_mid.astype(BF)
    dattn_ref[...] = d_attn
    sums_ref[...] += jnp.concatenate([total(d_attn.astype(F32)), total(d_normed*hat), total(d_normed), total(d_branch.astype(F32)), total(cot*final_hat), total(cot), jnp.zeros((2,cot.shape[1]),F32)], axis=0)

def rows_pass(pieces, x, ctx, out_w, up_w, down_w, bias, up_b):
    seq, dim = ctx.shape
    ff = up_w.shape[1]
    block = seq // 4
    row = lambda w: pl.BlockSpec((block, w), lambda i: (i,0))
    whole = lambda a: pl.BlockSpec(a.shape, lambda i: (0,)*a.ndim, pipeline_mode=pl.Buffered(1))
    sd = jax.ShapeDtypeStruct
    return pl.pallas_call(partial(rows_kernel, len(pieces)), grid=(seq//block,),
        in_specs=[whole(a) for a in pieces] + [row(dim),row(dim),whole(out_w),whole(up_w),whole(down_w),whole(bias),whole(up_b)],
        out_specs=[row(dim),row(dim),row(dim),row(dim),row(ff),row(dim),row(ff),pl.BlockSpec((8,dim),lambda i:(0,0)),pl.BlockSpec((1,ff),lambda i:(0,0))],
        out_shape=[sd((seq,dim),BF),sd((seq,dim),F32),sd((seq,dim),BF),sd((seq,dim),BF),sd((seq,ff),BF),sd((seq,dim),BF),sd((seq,ff),BF),sd((8,dim),F32),sd((1,ff),F32)],
        scratch_shapes=[pltpu.VMEM((block, ff), F32), pltpu.VMEM((seq, dim), BF)],
        compiler_params=pltpu.CompilerParams(vmem_limit_bytes=VMEM_BYTES),
        cost_estimate=pl.CostEstimate(
            flops=34 * seq * dim * dim, bytes_accessed=64 * seq * dim, transcendentals=seq * ff
        ),
    )(*pieces,x,ctx,out_w,up_w,down_w,bias,up_b)


def down_kernel(act_ref, dbranch_ref, ctxt_ref, dattn_ref, down_ref, out_ref):
    step = pl.program_id(0)
    last = pl.num_programs(0) - 1
    seq = act_ref.shape[0]

    @pl.when(step < last)
    def _():
        down_ref[...] = inner(act_ref[...], dbranch_ref[...]).astype(BF)

    @pl.when(step == last)
    def _():
        out_ref[...] = mm(ctxt_ref[:, 0:seq], dattn_ref[...]).astype(BF)


def down_sums(room, act, d_branch, ctx_t, d_attn):
    seq, ff = act.shape
    dim = d_branch.shape[1]
    steps = ff // dim

    def whole(a):
        return pl.BlockSpec(a.shape, lambda p: (0,) * a.ndim, pipeline_mode=pl.Buffered(1))

    shape = jax.ShapeDtypeStruct
    return pl.pallas_call(
        down_kernel,
        grid=(steps + 1,),
        in_specs=[
            pl.BlockSpec((seq, dim), lambda p: (0, jnp.minimum(p, steps - 1))),
            whole(d_branch),
            whole(ctx_t),
            whole(d_attn),
        ],
        out_specs=[
            pl.BlockSpec((dim, dim), lambda p: (jnp.minimum(p, steps - 1), 0)),
            pl.BlockSpec((dim, dim), lambda p: (0, 0)),
        ],
        out_shape=[shape((ff, dim), BF), shape((dim + room, dim), BF)],
        compiler_params=pltpu.CompilerParams(vmem_limit_bytes=VMEM_BYTES),
        cost_estimate=pl.CostEstimate(
            flops=10 * seq * dim * dim, bytes_accessed=32 * seq * dim, transcendentals=0
        ),
    )(act, d_branch, ctx_t, d_attn)


def up_kernel(normed_ref, dpre_ref, grad_ref, normed_t):
    @pl.when(pl.program_id(0) == 0)
    def _():
        normed_t[...] = normed_ref[...].astype(F32).T.astype(BF)

    grad_ref[...] = mm(normed_t[...], dpre_ref[...]).astype(BF)


def up_sums(normed, d_pre):
    seq, dim = normed.shape
    ff = d_pre.shape[1]
    return pl.pallas_call(
        up_kernel,
        grid=(ff // dim,),
        in_specs=[
            pl.BlockSpec((seq, dim), lambda p: (0, 0), pipeline_mode=pl.Buffered(1)),
            pl.BlockSpec((seq, dim), lambda p: (0, p)),
        ],
        out_specs=pl.BlockSpec((dim, dim), lambda p: (0, p)),
        out_shape=jax.ShapeDtypeStruct((dim, ff), BF),
        scratch_shapes=[pltpu.VMEM((dim, seq), BF)],
        compiler_params=pltpu.CompilerParams(vmem_limit_bytes=VMEM_BYTES),
        cost_estimate=pl.CostEstimate(
            flops=8 * seq * dim * dim, bytes_accessed=24 * seq * dim, transcendentals=0
        ),
    )(normed, d_pre)


def last_kernel(count, held, *refs):
    parts = refs[:count]
    x_ref, weight_ref, dmid_ref = refs[count : count + 3]
    grad_ref, drows_ref, sums_ref, x_t, total = refs[count + 3 + held :]
    step = pl.program_id(0)
    d_qkv = jnp.concatenate([part[0] for part in parts], axis=1)

    @pl.when(step == 0)
    def _():
        x_t[...] = x_ref[...].astype(F32).T.astype(BF)
        total[...] = dmid_ref[...]

    grad_ref[...] = mm(x_t[...], d_qkv).astype(BF)
    total[...] += against(d_qkv, weight_ref[0])
    sums_ref[0] = jnp.broadcast_to(
        jnp.sum(d_qkv.astype(F32), axis=0, keepdims=True), sums_ref.shape[1:]
    )

    @pl.when(step == 2)
    def _():
        drows_ref[...] = total[...].astype(BF)


def last_products(rows, held, x, d_qkv, weights, d_mid):
    seq, dim = d_mid.shape

    def whole(a):
        return pl.BlockSpec(a.shape, lambda p: (0,) * a.ndim, pipeline_mode=pl.Buffered(1))

    shape = jax.ShapeDtypeStruct
    return pl.pallas_call(
        partial(last_kernel, len(d_qkv), len(held)),
        grid=(3,),
        in_specs=[pl.BlockSpec((1,) + a.shape[1:], lambda p: (p, 0, 0)) for a in d_qkv]
        + [
            whole(x),
            pl.BlockSpec((1, dim, dim), lambda p: (p, 0, 0)),
            whole(d_mid),
        ]
        + [pl.BlockSpec(memory_space=pl.ANY)] * len(held),
        out_specs=[
            pl.BlockSpec((dim, dim), lambda p: (p, 0)),
            pl.BlockSpec((seq, dim), lambda p: (0, 0)),
            pl.BlockSpec((1, 8, dim), lambda p: (p, 0, 0)),
        ],
        out_shape=[shape((rows, dim), BF), shape((seq, dim), BF), shape((3, 8, dim), F32)],
        scratch_shapes=[pltpu.VMEM((dim, seq), BF), pltpu.VMEM((seq, dim), F32)],
        compiler_params=pltpu.CompilerParams(vmem_limit_bytes=VMEM_BYTES),
        cost_estimate=pl.CostEstimate(
            flops=12 * seq * dim * dim, bytes_accessed=32 * seq * dim, transcendentals=0
        ),
    )(*d_qkv, x, weights, d_mid, *held)


def bucket_select(table):
    reach = (table.shape[0] - 1) // 2
    spots = jnp.arange(4 * reach, dtype=jnp.int32)
    bucket = jnp.clip(spots[None, :] - spots[:, None], -reach, reach) + reach
    return bucket[None] == jnp.arange(2 * reach + 1, dtype=jnp.int32)[:, None, None]


def spread_table(table):
    span = 2 * (table.shape[0] - 1)
    high = table.astype(BF)
    low = (table - high.astype(F32)).astype(BF)
    both = jnp.stack([high, low], axis=2).reshape(table.shape[0], -1)
    spread = lax.dot_general(
        both,
        bucket_select(table).astype(BF).reshape(table.shape[0], -1),
        (((0,), (0,)), ((), ())),
        preferred_element_type=F32,
    )
    return spread.astype(BF).reshape(HEADS, 2 * span, span)


def gather_table(parts, table):
    select = bucket_select(table).astype(F32).reshape(table.shape[0], -1)
    return jnp.concatenate(
        [
            lax.dot_general(
                select,
                grads.reshape(grads.shape[0], -1),
                (((1,), (1,)), ((), ())),
                precision=lax.Precision.HIGHEST,
                preferred_element_type=F32,
            )
            for grads in parts
        ],
        axis=1,
    )


def shift_pairs(size, step):
    return [(i, (i + step) % size) for i in range(size)]


def flip_pairs(size, step):
    return [(i, i ^ step) for i in range(size)]


def pick(array, index):
    return lax.dynamic_index_in_dim(array, index, 0, keepdims=False)


def swap_text(parts):
    return lax.all_to_all(parts, "wide", split_axis=0, concat_axis=0, tiled=True)


def patch_order(size):
    me = lax.axis_index("narrow")
    return [me ^ k for k in range(size)]


def swap_patch(parts):
    size = parts.shape[0]
    me = lax.axis_index("narrow")
    return [pick(parts, me)] + [
        lax.ppermute(pick(parts, me ^ k), "narrow", flip_pairs(size, k)) for k in range(1, size)
    ]


def flip_axis(array, axis, bit):
    return jnp.where(bit == 1, jnp.flip(array, axis), array)


def from_flipped(parts, me):
    size = parts.shape[0]
    bits = size.bit_length() - 1
    parts = parts.reshape((2,) * bits + parts.shape[1:])
    for b in range(bits):
        parts = flip_axis(parts, bits - 1 - b, (me >> b) & 1)
    return parts.reshape((size,) + parts.shape[bits:])


def patch_away(rows, size):
    me = lax.axis_index("narrow")
    parts = rows.reshape(size, -1, rows.shape[1])
    arrived = [parts[0]] + [
        lax.ppermute(parts[k], "narrow", flip_pairs(size, k)) for k in range(1, size)
    ]
    return from_flipped(jnp.stack(arrived), me)


def add(*terms):
    total = terms[0].astype(F32)
    for term in terms[1:]:
        total = total + term.astype(F32)
    return total.astype(BF)


def wide_orders(wide, ways):
    bits = list(range(1, wide.bit_length() - 1))
    return [bits, bits[::-1]][:ways]


def wide_bit(bit):
    return (lax.axis_index("wide") >> bit) & 1


def add_kernel(me_ref, own_ref, arrived_ref, *refs):
    refs[-1][...] = (own_ref[0].astype(F32) + arrived_ref[...].astype(F32)).astype(BF)


def add_own(parts, me, arrived, held):
    rows, columns = arrived.shape
    steps = 2 if rows % 32 == 0 else 1
    block = rows // steps
    return pl.pallas_call(
        add_kernel,
        grid_spec=pltpu.PrefetchScalarGridSpec(
            num_scalar_prefetch=1,
            grid=(steps,),
            in_specs=[
                pl.BlockSpec((1, block, columns), lambda i, me_ref: (me_ref[0], i, 0)),
                pl.BlockSpec((block, columns), lambda i, me_ref: (i, 0)),
            ]
            + [pl.BlockSpec(memory_space=pl.ANY)] * len(held),
            out_specs=pl.BlockSpec((block, columns), lambda i, me_ref: (i, 0)),
        ),
        out_shape=jax.ShapeDtypeStruct((rows, columns), BF),
        compiler_params=pltpu.CompilerParams(vmem_limit_bytes=VMEM_BYTES),
        cost_estimate=pl.CostEstimate(flops=0, bytes_accessed=6 * rows * columns, transcendentals=0),
    )(me.reshape(1), parts, arrived, *held)


def wide_step(grad, wide, bit, held=()):
    parts = grad.reshape(2, -1, grad.shape[1])
    me = wide_bit(bit)
    arrived = lax.ppermute(pick(parts, 1 - me), "wide", flip_pairs(wide, 1 << bit))
    return add_own(parts, me, arrived, held) if held else add(pick(parts, me), arrived)


def cut(grad, ways):
    part = grad.shape[0] // ways
    return [grad[i * part : (i + 1) * part] for i in range(ways)]


def wide_steps(shares, wide, i, held=()):
    orders = wide_orders(wide, len(shares))
    return [
        wide_step(a, wide, order[i], held if n == 0 else ())
        for n, (a, order) in enumerate(zip(shares, orders))
    ]


def narrow_step(shares, narrow):
    me = lax.axis_index("narrow")
    parts = [a.reshape(narrow, -1, a.shape[1]) for a in shares]

    def picked(index):
        return jnp.stack([pick(a, index) for a in parts])

    arrived = [
        lax.ppermute(picked(me ^ k), "narrow", flip_pairs(narrow, k)) for k in range(1, narrow)
    ]
    return add(picked(me), *arrived)


def gather_narrow(part, narrow):
    parts = [part] + [
        lax.ppermute(part, "narrow", flip_pairs(narrow, k)) for k in range(1, narrow)
    ]
    return [jnp.stack([p[n] for p in parts]) for n in range(part.shape[0])]


def gather_wide(shares, wide, i):
    return [
        jnp.concatenate([a, lax.ppermute(a, "wide", flip_pairs(wide, 1 << order[i]))], axis=0)
        for a, order in zip(shares, wide_orders(wide, len(shares)))
    ]


def gather_core(shares, wide):
    return shares + [lax.ppermute(a, "wide", flip_pairs(wide, 1)) for a in shares]


def convert_kernel(up_ref, down_ref, out_ref, after_ref, up_out, down_out, out_out):
    step = pl.program_id(0)
    parts = (pl.num_programs(0) - 1) // 2

    @pl.when(step < parts)
    def _():
        up_out[...] = up_ref[...].astype(F32)

    @pl.when((step >= parts) & (step < 2 * parts))
    def _():
        down_out[...] = down_ref[...].astype(F32)

    @pl.when(step == 2 * parts)
    def _():
        out_out[...] = out_ref[...].astype(F32)


def convert(up_total, down_total, out_total, after):
    dim, ff = up_total.shape
    parts = ff // dim

    def block(index):
        return pl.BlockSpec((dim, dim), index)

    up_block = block(lambda p: (0, jnp.minimum(p, parts - 1)))
    down_block = block(lambda p: (jnp.clip(p - parts, 0, parts - 1), 0))
    out_block = block(lambda p: (0, 0))
    shape = jax.ShapeDtypeStruct
    return pl.pallas_call(
        convert_kernel,
        grid=(2 * parts + 1,),
        in_specs=[up_block, down_block, out_block, pl.BlockSpec(memory_space=pl.ANY)],
        out_specs=[up_block, down_block, out_block],
        out_shape=[shape((dim, ff), F32), shape((ff, dim), F32), shape((dim, dim), F32)],
        compiler_params=pltpu.CompilerParams(vmem_limit_bytes=VMEM_BYTES),
        cost_estimate=pl.CostEstimate(flops=0, bytes_accessed=13 * dim * ff, transcendentals=0),
    )(up_total, down_total, out_total, after)


def finish_kernel(places, ways, cuts, index_ref, *refs):
    pieces, outs = refs[: 2 * ways], refs[2 * ways :]
    rows = pieces[0].shape[1]
    for core in range(2):
        for way in range(ways):
            for place in range(places):
                at = ((core * ways + way) * places + place) * rows
                if at >= cuts[-1][1]:
                    continue
                here = index_ref[way, place]
                same = pieces[way][here].astype(F32)
                other = pieces[ways + way][here].astype(F32)
                block = jnp.where(index_ref[2, 0] == core, same, other)
                for (start, stop), out in zip(cuts, outs):
                    low, high = max(at, start), min(at + rows, stop)
                    if low < high:
                        out[low - start : high - start, :] = block[low - at : high - at]


def finish(pieces, wide, narrow, lengths):
    places, _, columns = pieces[0].shape
    ways = len(pieces) // 2
    index = []
    for order in wide_orders(wide, 2):
        me = jnp.int32(0)
        for bit in order:
            me = me * 2 + wide_bit(bit)
        me = me * narrow + lax.axis_index("narrow")
        index.append(jnp.arange(places, dtype=jnp.int32) ^ me)
    index.append(jnp.full((places,), wide_bit(0), jnp.int32))
    cuts = []
    for length in lengths:
        start = cuts[-1][1] if cuts else 0
        cuts.append((start, start + length))
    return pl.pallas_call(
        partial(finish_kernel, places, ways, cuts),
        in_specs=[pl.BlockSpec(memory_space=pltpu.SMEM)]
        + [pl.BlockSpec(memory_space=pltpu.VMEM)] * len(pieces),
        out_specs=[pl.BlockSpec(memory_space=pltpu.VMEM)] * len(lengths),
        out_shape=[jax.ShapeDtypeStruct((length, columns), F32) for length in lengths],
        compiler_params=pltpu.CompilerParams(vmem_limit_bytes=VMEM_BYTES),
        cost_estimate=pl.CostEstimate(
            flops=0, bytes_accessed=8 * sum(lengths) * columns, transcendentals=0
        ),
    )(jnp.stack(index), *pieces)


def room_for(rows, wide, narrow):
    return 16 + -(rows + 16) % (8 * wide * narrow)


def pack(grads, columns, rows):
    lines = []
    for grad in grads:
        flat = grad.reshape(-1)
        lines.append(jnp.pad(flat, (0, -flat.shape[0] % columns)).reshape(-1, columns))
    lines = jnp.concatenate(lines, axis=0)
    return jnp.pad(lines, ((0, -lines.shape[0] % rows), (0, 0)))


def unpack(lines, grads):
    columns = lines.shape[1]
    at = 0
    out = []
    for grad in grads:
        count = -(-grad.size // columns)
        out.append(lines[at : at + count].reshape(-1)[: grad.size].reshape(grad.shape))
        at += count
    return out


def body(
    text_in,
    patch_in,
    res_class,
    text_len,
    pos_line,
    pos_x,
    pos_y,
    query_weight,
    query_bias,
    key_weight,
    value_weight,
    value_bias,
    output_weight,
    output_bias,
    norm_gain,
    norm_shift,
    up_weight,
    up_bias,
    down_weight,
    down_bias,
    final_gain,
    final_shift,
    line_table,
    width_table,
    height_table,
    cot_text,
    cot_patch,
):
    text_shape = text_in.shape
    patch_shape = patch_in.shape
    dim = text_shape[3]
    seq = TEXT + PATCH
    lanes = -(-seq // 128) * 128
    wide = text_shape[0]
    narrow = patch_shape[1]
    pieces = [swap_text(text_in.reshape(wide, -1, dim)).reshape(-1, dim)]
    pieces += swap_patch(patch_in.reshape(narrow, -1, dim))
    cot_text, cot_patch, pieces = lax.optimization_barrier((cot_text, cot_patch, pieces))
    cots = [swap_text(cot_text.reshape(wide, -1, dim)).reshape(-1, dim)]
    cots += swap_patch(cot_patch.reshape(narrow, -1, dim))
    index = jnp.arange(seq, dtype=jnp.int32)
    live_patch = jnp.where(res_class.reshape(()) == 1, PATCH, SMALL_PATCH)
    valid = jnp.where(index < TEXT, index < text_len.reshape(()), index - TEXT < live_patch)
    facts = jnp.concatenate(
        [pos_line.reshape(1, -1), pos_x.reshape(1, -1), pos_y.reshape(1, -1), valid.astype(jnp.int32)[None]]
    )
    patch_facts = facts[:, TEXT:].reshape(4, narrow, -1)
    facts = jnp.concatenate(
        [facts[:, :TEXT]]
        + [
            lax.dynamic_index_in_dim(patch_facts, i, 1, keepdims=False)
            for i in patch_order(narrow)
        ],
        axis=1,
    )
    line_spots, x_spots, y_spots = facts[0], facts[1], facts[2]
    valid = facts[3] == 1

    line = spread_table(line_table)
    width = spread_table(width_table)
    height = spread_table(height_table)
    hots = []
    hots_t = []
    for spots, table in ((line_spots, line_table), (x_spots, width_table), (y_spots, height_table)):
        span = jnp.arange(2 * (table.shape[0] - 1), dtype=jnp.int32)
        long = jnp.pad(spots, (0, lanes - seq), constant_values=-1)
        hots.append((long[:, None] == span[None, :]).astype(BF))
        hots_t.append((long[None, :] == span[:, None]).astype(BF))
    hot = jnp.concatenate(hots, axis=1)
    hot_t = jnp.concatenate(hots_t, axis=0)
    column = jnp.arange(128, dtype=jnp.int32)
    mask = jnp.where((column[None, :] % 64 == 0) & ~valid[:, None], -1e30, 0.0).astype(BF)

    exps, ctx_t, ctx, inverse, q, k_t, v, rows_in = attend(
        pieces,
        query_weight,
        key_weight,
        value_weight,
        jnp.stack([query_bias, value_bias])[:, None],
        hot,
        mask,
        hot_t,
        line,
        width,
        height,
    )
    vectors = jnp.stack(
        [output_bias, norm_gain, norm_shift, down_bias, final_gain, final_shift] + [final_shift] * 2
    )
    final_low, d_mid, d_attn, normed, act, d_branch, d_pre, sums, up_sum = rows_pass(
        cots, rows_in, ctx, output_weight, up_weight, down_weight, vectors, up_bias[None]
    )
    early = (sums[0], sums[1], sums[2], up_sum, sums[3], sums[4], sums[5])
    small = pack(early, dim, 16).astype(BF)
    down_low, out_low = down_sums(small.shape[0], act, d_branch, ctx_t, d_attn)
    out_low = lax.dynamic_update_slice(out_low, small, (dim, 0))
    up_low = up_sums(normed, d_pre)
    down_total, up_total, out_total = lax.psum((down_low, up_low, out_low), ("wide", "narrow"))
    qkv_weight = jnp.stack([query_weight, key_weight, value_weight])

    def backward():
        text_out = swap_text(final_low[:TEXT].reshape(wide, -1, dim)).reshape(text_shape)
        patch_out = patch_away(final_low[TEXT:], narrow).reshape(patch_shape)
        levels = wide.bit_length() - 2
        d_qkv, g_width, g_height, g_line = attend_back(
            0, HEADS // 2, [], exps, ctx_t, inverse, v, k_t, q, d_attn, output_weight, hot, hot_t
        )
        late_room = room_for(3 * dim, wide, narrow)
        tail, d_rows, qkv_sums = last_products(
            3 * dim + late_room, [text_out, patch_out], rows_in, [d_qkv], qkv_weight, d_mid
        )
        text_grad = swap_text(d_rows[:TEXT].reshape(wide, -1, dim)).reshape(text_shape)
        patch_grad = patch_away(d_rows[TEXT:], narrow).reshape(patch_shape)
        late = (
            qkv_sums[0, 0],
            qkv_sums[2, 0],
            gather_table([g_line], line_table),
            gather_table([g_width], width_table),
            gather_table([g_height], height_table),
        )
        small = pack(late, dim, late_room).astype(BF)
        tail = lax.dynamic_update_slice(tail, small, (3 * dim, 0))
        halves = cut(wide_step(tail, wide, 0), 2)
        for i in range(levels):
            moved = [text_grad, patch_grad] if i == levels - 1 else []
            halves = wide_steps(halves, wide, i, moved)
        halves = gather_narrow(narrow_step(halves, narrow), narrow)
        for i in range(levels - 1, -1, -1):
            halves = gather_wide(halves, wide, i)
        *large, late_small = finish(gather_core(halves, wide), wide, narrow, (dim,) * 3 + (16,))
        return (
            text_out, patch_out, text_grad, patch_grad, *large, *unpack(late_small, late),
        )

    def never():
        return jax.tree.map(lambda a: jnp.zeros(a.shape, a.dtype), jax.eval_shape(backward))

    (
        text_out, patch_out, text_grad, patch_grad, query_weight_grad, key_weight_grad,
        value_weight_grad, query_bias_grad, value_bias_grad, line_table_grad, width_table_grad,
        height_table_grad,
    ) = lax.cond(text_len.reshape(()) >= 0, backward, never)
    up_weight_grad, down_weight_grad, output_weight_grad = convert(
        up_total, down_total, out_total, value_weight_grad
    )
    (
        output_bias_grad,
        norm_gain_grad,
        norm_shift_grad,
        up_bias_grad,
        down_bias_grad,
        final_gain_grad,
        final_shift_grad,
    ) = unpack(out_total[dim:].astype(F32), early)
    up_bias_grad = up_bias_grad.reshape(-1)
    return (
        text_out,
        patch_out,
        text_grad,
        patch_grad,
        query_weight_grad,
        query_bias_grad,
        key_weight_grad,
        value_weight_grad,
        value_bias_grad,
        output_weight_grad,
        output_bias_grad,
        norm_gain_grad,
        norm_shift_grad,
        up_weight_grad,
        up_bias_grad,
        down_weight_grad,
        down_bias_grad,
        final_gain_grad,
        final_shift_grad,
        line_table_grad,
        width_table_grad,
        height_table_grad,
    )


def solution(mesh):
    text = P(None, "narrow", "wide", None)
    patch = P("wide", None, "narrow", None)
    page = P("wide", "narrow")
    spots = P("wide", "narrow", None)
    in_specs = (text, patch, page, page, spots, spots, spots) + (P(),) * 18 + (text, patch)
    out_specs = (text, patch, text, patch) + (P(),) * 18
    return jax.shard_map(body, mesh=mesh, in_specs=in_specs, out_specs=out_specs, check_vma=False)
```

time: 530 us -> 463 us (0.87)
  matrix products: 135 us -> 10.4 us
  Pallas kernels: 115 us -> 224 us
  other arithmetic: 54.2 us -> 20.3 us
  local copies, waits for them, and re-layouts: 63.4 us -> 30.9 us
  waiting for transfers between devices: 67.9 us -> 95.2 us
  starting transfers between devices: 67.6 us -> 59.3 us
    dot_general x21 -> x3, matrix products: 133 us -> 8.29 us  [gather_table(): lax.dot_general(select, grads.reshape(grads.shape[0], -1), (((1,), (1,)),...]
    pallas_call x1 -> x8, Pallas kernels: 52.5 us -> 163 us  [the longest x1 60.9 us: attend(): pl.pallas_call(partial(attend_kernel, len(pieces)), grid=(HEADS // 2,), i...]
    psum x1, waiting for transfers between devices: 0.02 us -> 19.7 us  [body(): lax.psum((down_low, up_low, out_low), ('wide', 'narrow'))]
    convert_element_type x4 -> x1, other arithmetic: 15 us -> 0.74 us  [body(): out_total[dim:].astype(F32)]
    reduce_sum x15 -> x0, other arithmetic: 13.5 us -> none  [the longest x2 3.95 us: layer_norm(): centred = rows - mean]
    another operation x7 -> x14, local copies, waits for them, and re-layouts: 14.2 us -> 1.79 us  [the longest x7 0.73 us: body(): jnp.stack([output_bias, norm_gain, norm_shift, down_bias, final_gain, fin...]
    ppermute x18 -> x17, waiting for transfers between devices: 54.7 us -> 64.7 us  [the longest x5 18.3 us: wide_step(): lax.ppermute(pick(parts, 1 - me), 'wide', flip_pairs(wide, 1 << bit))]
    ppermute x12 -> x6, starting transfers between devices: 19.7 us -> 10.2 us  [swap_patch(): lax.ppermute(pick(parts, me ^ k), 'narrow', flip_pairs(size, k))]
  transfers between devices with their start and end apart: 41 -> 34, of which waited for: 17 -> 15; matrix products, arithmetic and copies ran while one was open for 23% -> 11% of each run, Pallas kernels for 22% -> 32%
where the time goes in v3:
time: 463 us; the launch traced here: 457 us
  Pallas kernels  224 us (48%)
  waiting for transfers between devices  95.2 us (21%)
  starting transfers between devices  59.3 us (13%)
  local copies, waits for them, and re-layouts  30.9 us (7%)
  other arithmetic  20.3 us (4%)
  between operations  16.2 us (3%)
  matrix products  10.4 us (2%)
    pallas_call x1, Pallas kernels, attend_back(): pl.pallas_call(partial(attend_back_kernel, len(held)), grid=(pairs,), in_...  61.5 us
    pallas_call x1, Pallas kernels, attend(): pl.pallas_call(partial(attend_kernel, len(pieces)), grid=(HEADS // 2,), i...  60.9 us
    pallas_call x1, Pallas kernels, rows_pass(): pl.pallas_call(partial(rows_kernel, len(pieces)), grid=(seq // block,), i...  41.7 us
    psum x1, waiting for transfers between devices, body(): lax.psum((down_low, up_low, out_low), ('wide', 'narrow'))  19.7 us
    ppermute x5, waiting for transfers between devices, wide_step(): lax.ppermute(pick(parts, 1 - me), 'wide', flip_pairs(wide, 1 << bit))  18.3 us
    ppermute x4, waiting for transfers between devices, gather_wide(): lax.ppermute(a, 'wide', flip_pairs(wide, 1 << order[i]))  18.1 us
    all_to_all x4, starting transfers between devices, swap_text(): lax.all_to_all(parts, 'wide', split_axis=0, concat_axis=0, tiled=True)  16.6 us
    pallas_call x1, Pallas kernels, last_products(): pl.pallas_call(partial(last_kernel, len(d_qkv), len(held)), grid=(3,), in...  16.2 us
  transfers between devices with their start and end apart: 34, of which 15 were waited for; matrix products, arithmetic and copies ran while one was open for 11% of the time, Pallas kernels for 32%

profile of v3, /device:TPU:0, one launch (start us, length us, event | category | flops | bytes accessed | tf_op | source)
XLA Modules:
  0.0 456.9 jit_solution(7284039955681144186)
XLA Ops:
  7.3 2.2 dynamic-slice_bitcast_fusion.9
  9.4 3.0 collective-permute-start.23
  12.5 2.6 collective-permute-start.24
  15.1 3.9 all-to-all-start.2
  30.0 1.6 add_convert_fusion.1.refs_9_
  34.2 2.1 collective-permute-start.26
  36.3 2.1 collective-permute-start.27
  38.8 4.0 all-to-all-start.3
  43.5 60.9 %shard_map.426 = (bf16[12,1088,1152]{2,1,0:T(8,128)(2,1)}, bf16[768,1152]{1,0:T(8,128)(2,1)}, bf16[1088,768]{1,0:T(8,128)(2,1)}, f32[12,1,1152]{2,1,0:T(1,128)S(...) custom-call(bf16[512,768]{1,0:T(8,128)(2,1)} %bitcast.144, ...), custom_call_target="tpu_custom_call" | custom-call | flops 61605937152 | bytes 30081024 | tf_op jit(solution)/shard_map/pallas_call | solution.py:115
  105.3 41.7 %shard_map.427 = (bf16[1088,768]{1,0:T(8,128)(2,1)}, f32[1088,768]{1,0:T(8,128)}, bf16[1088,768]{1,0:T(8,128)(2,1)}, bf16[1088,768]{1,0:T(8,128)(2,1)}, bf16[108...) custom-call(bf16[512,768]{1,0:T(8,128)(2,1)} %bitcast.145, ...), custom_call_target="tpu_custom_call" | custom-call | flops 21818769408 | bytes 53477376 | tf_op jit(solution)/shard_map/pallas_call | solution.py:352
  148.5 10.7 %shard_map.428 = bf16[768,3072]{1,0:T(8,128)(2,1)} custom-call(bf16[1088,768]{1,0:T(8,128)(2,1)} %get-tuple-element.143.normed_ref, bf16[1088,3072]{1,0:T(8,128)(2,1)} %get-tuple-element.144.dpre_ref), custom_call_target="tpu_custom_call" | custom-call | flops 5133828096 | bytes 20054016 | tf_op jit(solution)/shard_map/pallas_call | solution.py:419
  159.2 13.0 %shard_map.429 = (bf16[3072,768]{1,0:T(8,128)(2,1)}, bf16[784,768]{1,0:T(8,128)(2,1)}) custom-call(bf16[1088,3072]{1,0:T(8,128)(2,1)} %get-tuple-element.145.act_ref, bf16[1088,768]{1,0:T(8,128)(2,1)} %get-tuple-element.146.dbranch_ref, bf16[768,1152]{1,0:T(8,128)(2,1)S(1)} %copy-done.34, bf16[1088,768]{1,0:T(8,128)(2,1)} %get-tuple-element.132.dattn_ref), custom_call_target="tpu_custom_call" | custom-call | flops 6417285120 | bytes 26738688 | tf_op jit(solution)/shard_map/pallas_call | solution.py:387
  174.1 3.3 pad_maximum_fusion.7
  177.5 234.2 %conditional.1 = (bf16[8,1,64,768]{3,2,1,0:T(8,128)(2,1)}, bf16[1,4,144,768]{3,2,1,0:T(8,128)(2,1)}, bf16[8,1,64,768]{3,2,1,0:T(8,128)(2,1)S(1)}, bf16[1,4,144,7...) conditional(s32[]{:T(128)} %convert_element_type.141, () %tuple.17, ...), branch_computations={%region_0.1_spmd, %region_1.2_spmd} | conditional | flops 69647499264 | bytes 182262816 | solution.py:924
  179.1 3.5 collective-permute-start.1
  183.6 4.2 all-to-all-start
  187.9 61.5 %branch_1_fun.4 = (bf16[3,1088,768]{2,1,0:T(8,128)(2,1)}, f32[12,128,128]{2,1,0:T(8,128)}, f32[12,128,128]{2,1,0:T(8,128)}, f32[12,64,64]{2,1,0:T(8,128)}) custom-call(bf16[12,1088,1152]{2,1,0:T(8,128)(2,1)} %get-tuple-element.29.refs_0_, bf16[768,1152]{1,0:T(8,128)(2,1)} %get-tuple-element.30.refs_1_, f32[12,1,1152]{2,1,0:T(1,128)S(1)} %get-tuple-element.31.refs_2_, ...), custom_call_target="tpu_custom_call" | custom-call | flops 61605937152 | bytes 30081024 | tf_op jit(solution)/shard_map/cond/branch_1_fun/pallas_call | solution.py:235
  249.5 3.7 fusion.10
  253.2 3.7 fusion.9
  261.0 16.2 %branch_1_fun.5 = (bf16[2560,768]{1,0:T(8,128)(2,1)}, bf16[1088,768]{1,0:T(8,128)(2,1)}, f32[3,8,768]{2,1,0:T(8,128)}) custom-call(bf16[3,1088,768]{2,1,0:T(8,128)(2,1)} %get-tuple-element.39.refs_0_, bf16[1088,768]{1,0:T(8,128)(2,1)} %get-tuple-element.40.refs_1_, bf16[3,768,768]{2,1,0:T(8,128)(2,1)} %get-tuple-element.41.refs_2_, ...), custom_call_target="tpu_custom_call" | custom-call | flops 7700742144 | bytes 26738688 | tf_op jit(solution)/shard_map/cond/branch_1_fun/pallas_call | solution.py:466
  279.0 3.0 dynamic-slice_bitcast_fusion
  282.3 2.1 slice.133
  284.4 2.2 slice_bitcast_fusion
  286.9 3.9 collective-permute-start.4
  291.0 4.4 all-to-all-start.1
  295.4 2.1 fusion.2
  297.6 2.1 collective-permute-start.7
  299.7 2.8 collective-permute-done.3
  302.6 8.0 %collective-permute-done.4 = bf16[144,768]{1,0:T(8,128)(2,1)} collective-permute-done((bf16[144,768]{1,0:T(8,128)(2,1)}, bf16[144,768]{1,0:T(8,128)(2,1)}, u32[]{:S(2)}, u32[]{:S(2)}) %collective-permute-start.4) | collective-permute-done | bytes 221216 | tf_op jit(solution)/shard_map/cond/branch_1_fun/ppermute | solution.py:574
  313.2 4.4 collective-permute-done.7
  319.3 10.3 %collective-permute-done.9 = bf16[320,768]{1,0:T(8,128)(2,1)S(1)} collective-permute-done((bf16[320,768]{1,0:T(8,128)(2,1)S(1)}, bf16[320,768]{1,0:T(8,128)(2,1)S(1)}, u32[]{:S(2)}, u32[]{:S(2)}) %collective-permute-start.9) | collective-permute-done | bytes 491552 | tf_op jit(solution)/shard_map/cond/branch_1_fun/ppermute | solution.py:624
  332.4 3.7 collective-permute-done.10
  336.9 1.8 branch_1_fun.6
  339.7 4.4 collective-permute-start.11
  344.9 1.7 collective-permute-start.13
  346.6 6.6 %collective-permute-done.11 = bf16[2,40,768]{2,1,0:T(8,128)(2,1)S(1)} collective-permute-done((bf16[2,40,768]{2,1,0:T(8,128)(2,1)S(1)}, bf16[2,40,768]{2,1,0:T(8,128)(2,1)S(1)}, u32[]{:S(2)}, u32[]{:S(2)}) %collective-permute-start.11) | collective-permute-done | bytes 122912 | tf_op jit(solution)/shard_map/cond/branch_1_fun/ppermute | solution.py:649
  353.2 8.4 %collective-permute-done.12 = bf16[2,40,768]{2,1,0:T(8,128)(2,1)S(1)} collective-permute-done((bf16[2,40,768]{2,1,0:T(8,128)(2,1)S(1)}, bf16[2,40,768]{2,1,0:T(8,128)(2,1)S(1)}, u32[]{:S(2)}, u32[]{:S(2)}) %collective-permute-start.12) | collective-permute-done | bytes 122912 | tf_op jit(solution)/shard_map/cond/branch_1_fun/ppermute | solution.py:649
  361.7 2.2 collective-permute-start.14
  364.0 2.4 collective-permute-start.16
  368.0 8.7 %collective-permute-done.15 = bf16[2,40,768]{2,1,0:T(8,128)(2,1)S(1)} collective-permute-done((bf16[2,40,768]{2,1,0:T(8,128)(2,1)S(1)}, bf16[2,40,768]{2,1,0:T(8,128)(2,1)S(1)}, u32[]{:S(2)}, u32[]{:S(2)}) %collective-permute-start.15) | collective-permute-done | bytes 122912 | tf_op jit(solution)/shard_map/cond/branch_1_fun/ppermute | solution.py:656
  376.8 2.0 collective-permute-start.19
  379.7 3.4 collective-permute-done.19
  384.4 5.0 %collective-permute-done.17 = bf16[4,40,768]{2,1,0:T(8,128)(2,1)S(1)} collective-permute-done((bf16[4,40,768]{2,1,0:T(8,128)(2,1)S(1)}, bf16[4,40,768]{2,1,0:T(8,128)(2,1)S(1)}, u32[]{:S(2)}, u32[]{:S(2)}) %collective-permute-start.17) | collective-permute-done | bytes 245792 | tf_op jit(solution)/shard_map/cond/branch_1_fun/ppermute | solution.py:663
  389.5 9.8 %collective-permute-done.20 = bf16[8,40,768]{2,1,0:T(8,128)(2,1)S(1)} collective-permute-done((bf16[8,40,768]{2,1,0:T(8,128)(2,1)S(1)}, bf16[8,40,768]{2,1,0:T(8,128)(2,1)S(1)}, u32[]{:S(2)}, u32[]{:S(2)}) %collective-permute-start.20) | collective-permute-done | bytes 491552 | tf_op jit(solution)/shard_map/cond/branch_1_fun/ppermute | solution.py:663
  403.7 4.8 %branch_1_fun.7 = (f32[768,768]{1,0:T(8,128)}, f32[768,768]{1,0:T(8,128)}, f32[768,768]{1,0:T(8,128)S(1)}, f32[16,768]{1,0:T(8,128)}) custom-call(s32[3,16]{1,0:T(4,128)} %add_add_fusion.index_ref, bf16[16,40,768]{2,1,0:T(8,128)(2,1)} %copy-done.6, bf16[16,40,768]{2,1,0:T(8,128)(2,1)} %copy-done.7, bf16[16,40,768]{2,1,0:T(8,128)(2,1)} %collective-permute-done.21.refs_2_, ...), custom_call_target="tpu_custom_call" | custom-call | bytes 14254080 | tf_op jit(solution)/shard_map/cond/branch_1_fun/pallas_call | solution.py:745
  411.8 19.7 %all-reduce.11.cloned.1.call-done = (bf16[768,3072]{1,0:T(8,128)(2,1)}, bf16[3072,768]{1,0:T(8,128)(2,1)}, bf16[784,768]{1,0:T(8,128)(2,1)}) async-done(((bf16[768,3072]{1,0:T(8,128)(2,1)}, bf16[3072,768]{1,0:T(8,128)(2,1)}, bf16[784,768]{1,0:T(8,128)(2,1)}), (bf16[768,3072]{1,0:T(8,128)(2,1)}, bf16[3072,768]{1,0:T(8,128)(2,1)}, bf16[784,768]{1,0:T(8,128)(2,1)})) %all-reduce.11.cloned.1.call-update) | async-done | bytes 10641424 | tf_op jit(solution)/shard_map/psum | solution.py:880
  433.5 13.5 %shard_map.430 = (f32[768,3072]{1,0:T(8,128)}, f32[3072,768]{1,0:T(8,128)}, f32[768,768]{1,0:T(8,128)}) custom-call(bf16[768,3072]{1,0:T(8,128)(2,1)} %get-tuple-element.215.up_ref, bf16[3072,768]{1,0:T(8,128)(2,1)} %get-tuple-element.216.down_ref, bf16[784,768]{1,0:T(8,128)(2,1)} %get-tuple-element.217.out_ref, f32[768,768]{1,0:T(8,128)S(1)} %get-tuple-element.351.after_ref), custom_call_target="tpu_custom_call" | custom-call | bytes 30670848 | tf_op jit(solution)/shard_map/pallas_call | solution.py:700
  447.0 2.1 copy.138
  (237 shorter events, 50.9 us)
Async XLA Ops:
  7.2 13.2 %copy-start.17 = (s32[1,1,1088]{2,1,0:T(1,128)S(1)}, s32[1,1,1088]{2,1,0:T(1,128)}, u32[]{:S(2)}) copy-start(s32[1,1,1088]{2,1,0:T(1,128)} %param.33) | copy-start | bytes 13060
  7.2 13.2 %copy-start.16 = (s32[1,1,1088]{2,1,0:T(1,128)S(1)}, s32[1,1,1088]{2,1,0:T(1,128)}, u32[]{:S(2)}) copy-start(s32[1,1,1088]{2,1,0:T(1,128)} %param.34) | copy-start | bytes 13060
  7.2 13.2 %copy-start.15 = (s32[1,1,1088]{2,1,0:T(1,128)S(1)}, s32[1,1,1088]{2,1,0:T(1,128)}, u32[]{:S(2)}) copy-start(s32[1,1,1088]{2,1,0:T(1,128)} %param.35) | copy-start | bytes 13060
  7.2 15.1 %copy-start.18 = (f32[65,12]{0,1:T(8,128)S(1)}, f32[65,12]{0,1:T(8,128)}, u32[]{:S(2)}) copy-start(f32[65,12]{0,1:T(8,128)} %param.52) | copy-start | bytes 9364
  9.4 23.8 %collective-permute-start.23 = (bf16[144,768]{1,0:T(8,128)(2,1)}, bf16[144,768]{1,0:T(8,128)(2,1)}, u32[]{:S(2)}, u32[]{:S(2)}) collective-permute-start(bf16[144,768]{1,0:T(8,128)(2,1)} %get-tuple-element.279), channel_id=1, source_target_pairs={{0,1},{1,0},{2,3},{3,2},{4,5},{5,4},{6,7},{7,6},{8,9},{9,8},{10,11... | collective-permute-start | bytes 663560 | tf_op jit(solution)/shard_map/ppermute | solution.py:553
  12.5 20.8 %collective-permute-start.24 = (bf16[144,768]{1,0:T(8,128)(2,1)}, bf16[144,768]{1,0:T(8,128)(2,1)}, u32[]{:S(2)}, u32[]{:S(2)}) collective-permute-start(bf16[144,768]{1,0:T(8,128)(2,1)} %get-tuple-element.281), channel_id=1, source_target_pairs={{0,2},{1,3},{2,0},{3,1},{4,6},{5,7},{6,4},{7,5},{8,10},{9,11},{10,... | collective-permute-start | bytes 663560 | tf_op jit(solution)/shard_map/ppermute | solution.py:553
  15.1 18.2 %collective-permute-start.25 = (bf16[144,768]{1,0:T(8,128)(2,1)}, bf16[144,768]{1,0:T(8,128)(2,1)}, u32[]{:S(2)}, u32[]{:S(2)}) collective-permute-start(bf16[144,768]{1,0:T(8,128)(2,1)} %get-tuple-element.278), channel_id=1, source_target_pairs={{0,3},{1,2},{2,1},{3,0},{4,7},{5,6},{6,5},{7,4},{8,11},{9,10},{10,... | collective-permute-start | bytes 663560 | tf_op jit(solution)/shard_map/ppermute | solution.py:553
  15.1 18.2 %all-to-all-start.2 = ((bf16[8,64,768]{2,1,0:T(8,128)(2,1)}), bf16[8,64,768]{2,1,0:T(8,128)(2,1)S(1)}, u32[]{:S(2)}, u32[]{:S(2)}) async-start(bf16[8,64,768]{2,1,0:T(8,128)(2,1)} %bitcast.143), calls=%async_computation.2 | async-start | bytes 1572864 | tf_op jit(solution)/shard_map/all_to_all | solution.py:541
  31.6 72.8 %copy-start.9 = (bf16[1152,320]{1,0:T(8,128)(2,1)}, bf16[1152,320]{1,0:T(8,128)(2,1)S(1)}, u32[]{:S(2)}) copy-start(bf16[1152,320]{1,0:T(8,128)(2,1)S(1)} %add_convert_fusion.1.refs_9_) | copy-start | bytes 2211844
  34.2 70.1 %collective-permute-start.26 = (bf16[144,768]{1,0:T(8,128)(2,1)S(1)}, bf16[144,768]{1,0:T(8,128)(2,1)}, u32[]{:S(2)}, u32[]{:S(2)}) collective-permute-start(bf16[144,768]{1,0:T(8,128)(2,1)S(1)} %get-tuple-element.276), channel_id=1, source_target_pairs={{0,1},{1,0},{2,3},{3,2},{4,5},{5,4},{6,7},{7,6},{8,9},{9,8},{10,11... | collective-permute-start | bytes 663560 | tf_op jit(solution)/shard_map/ppermute | solution.py:553
  36.3 68.1 %collective-permute-start.27 = (bf16[144,768]{1,0:T(8,128)(2,1)S(1)}, bf16[144,768]{1,0:T(8,128)(2,1)}, u32[]{:S(2)}, u32[]{:S(2)}) collective-permute-start(bf16[144,768]{1,0:T(8,128)(2,1)S(1)} %get-tuple-element.275), channel_id=1, source_target_pairs={{0,2},{1,3},{2,0},{3,1},{4,6},{5,7},{6,4},{7,5},{8,10},{9,11},{10,... | collective-permute-start | bytes 663560 | tf_op jit(solution)/shard_map/ppermute | solution.py:553
  38.4 66.0 %collective-permute-start.28 = (bf16[144,768]{1,0:T(8,128)(2,1)S(1)}, bf16[144,768]{1,0:T(8,128)(2,1)}, u32[]{:S(2)}, u32[]{:S(2)}) collective-permute-start(bf16[144,768]{1,0:T(8,128)(2,1)S(1)} %get-tuple-element.274), channel_id=1, source_target_pairs={{0,3},{1,2},{2,1},{3,0},{4,7},{5,6},{6,5},{7,4},{8,11},{9,10},{10,... | collective-permute-start | bytes 663560 | tf_op jit(solution)/shard_map/ppermute | solution.py:553
  38.8 65.6 %all-to-all-start.3 = ((bf16[8,64,768]{2,1,0:T(8,128)(2,1)}), bf16[8,64,768]{2,1,0:T(8,128)(2,1)S(1)}, u32[]{:S(2)}, u32[]{:S(2)}) async-start(bf16[8,64,768]{2,1,0:T(8,128)(2,1)} %bitcast.45), calls=%async_computation.3 | async-start | bytes 1572864 | tf_op jit(solution)/shard_map/all_to_all | solution.py:541
  42.8 388.6 %all-reduce.11.cloned.1.call-start = ((), (), s32[]{:S(2)}) async-start(), calls=%async_computation.4 | async-start | bytes 21282816 | tf_op jit(solution)/shard_map/psum | solution.py:880
  178.3 80.3 %collective-permute-start = (bf16[144,768]{1,0:T(8,128)(2,1)}, bf16[144,768]{1,0:T(8,128)(2,1)S(1)}, u32[]{:S(2)}, u32[]{:S(2)}) collective-permute-start(bf16[144,768]{1,0:T(8,128)(2,1)} %get-tuple-element.227), channel_id=1, source_target_pairs={{0,1},{1,0},{2,3},{3,2},{4,5},{5,4},{6,7},{7,6},{8,9},{9,8},{10,11... | collective-permute-start | bytes 663560 | tf_op jit(solution)/shard_map/cond/branch_1_fun/ppermute | solution.py:574
  179.1 79.5 %collective-permute-start.1 = (bf16[144,768]{1,0:T(8,128)(2,1)}, bf16[144,768]{1,0:T(8,128)(2,1)}, u32[]{:S(2)}, u32[]{:S(2)}) collective-permute-start(bf16[144,768]{1,0:T(8,128)(2,1)} %get-tuple-element.226), channel_id=1, source_target_pairs={{0,2},{1,3},{2,0},{3,1},{4,6},{5,7},{6,4},{7,5},{8,10},{9,11},{10,... | collective-permute-start | bytes 663560 | tf_op jit(solution)/shard_map/cond/branch_1_fun/ppermute | solution.py:574
  182.5 76.1 %collective-permute-start.2 = (bf16[144,768]{1,0:T(8,128)(2,1)S(1)}, bf16[144,768]{1,0:T(8,128)(2,1)}, u32[]{:S(2)}, u32[]{:S(2)}) collective-permute-start(bf16[144,768]{1,0:T(8,128)(2,1)S(1)} %get-tuple-element.225), channel_id=1, source_target_pairs={{0,3},{1,2},{2,1},{3,0},{4,7},{5,6},{6,5},{7,4},{8,11},{9,10},{10,... | collective-permute-start | bytes 663560 | tf_op jit(solution)/shard_map/cond/branch_1_fun/ppermute | solution.py:574
  183.6 77.4 %all-to-all-start = ((bf16[8,64,768]{2,1,0:T(8,128)(2,1)}), bf16[8,64,768]{2,1,0:T(8,128)(2,1)}, u32[]{:S(2)}, u32[]{:S(2)}) async-start(bf16[8,64,768]{2,1,0:T(8,128)(2,1)} %bitcast), calls=%async_computation | async-start | bytes 1572864 | tf_op jit(solution)/shard_map/cond/branch_1_fun/all_to_all | solution.py:541
  281.9 13.4 %collective-permute-start.6 = (bf16[1280,768]{1,0:T(8,128)(2,1)}, bf16[1280,768]{1,0:T(8,128)(2,1)S(1)}, u32[]{:S(2)}, u32[]{:S(2)}) collective-permute-start(bf16[1280,768]{1,0:T(8,128)(2,1)} %dynamic-slice_bitcast_fusion), channel_id=1, source_target_pairs={{0,4},{4,0},{8,12},{12,8},{16,20},{20,16},{24,28},{28,24},{1,5},{5... | collective-permute-start | bytes 5898248 | tf_op jit(solution)/shard_map/cond/branch_1_fun/ppermute | solution.py:624
  286.6 15.9 %collective-permute-start.3 = (bf16[144,768]{1,0:T(8,128)(2,1)}, bf16[144,768]{1,0:T(8,128)(2,1)}, u32[]{:S(2)}, u32[]{:S(2)}) collective-permute-start(bf16[144,768]{1,0:T(8,128)(2,1)} %get-tuple-element.223), channel_id=1, source_target_pairs={{0,1},{1,0},{2,3},{3,2},{4,5},{5,4},{6,7},{7,6},{8,9},{9,8},{10,11... | collective-permute-start | bytes 663560 | tf_op jit(solution)/shard_map/cond/branch_1_fun/ppermute | solution.py:574
  286.9 23.6 %collective-permute-start.4 = (bf16[144,768]{1,0:T(8,128)(2,1)}, bf16[144,768]{1,0:T(8,128)(2,1)}, u32[]{:S(2)}, u32[]{:S(2)}) collective-permute-start(bf16[144,768]{1,0:T(8,128)(2,1)} %get-tuple-element.222), channel_id=1, source_target_pairs={{0,2},{1,3},{2,0},{3,1},{4,6},{5,7},{6,4},{7,5},{8,10},{9,11},{10,... | collective-permute-start | bytes 663560 | tf_op jit(solution)/shard_map/cond/branch_1_fun/ppermute | solution.py:574
  290.8 19.8 %collective-permute-start.5 = (bf16[144,768]{1,0:T(8,128)(2,1)S(1)}, bf16[144,768]{1,0:T(8,128)(2,1)}, u32[]{:S(2)}, u32[]{:S(2)}) collective-permute-start(bf16[144,768]{1,0:T(8,128)(2,1)S(1)} %get-tuple-element.221), channel_id=1, source_target_pairs={{0,3},{1,2},{2,1},{3,0},{4,7},{5,6},{6,5},{7,4},{8,11},{9,10},{10,... | collective-permute-start | bytes 663560 | tf_op jit(solution)/shard_map/cond/branch_1_fun/ppermute | solution.py:574
  291.0 45.1 %all-to-all-start.1 = ((bf16[8,64,768]{2,1,0:T(8,128)(2,1)}), bf16[8,64,768]{2,1,0:T(8,128)(2,1)S(1)}, u32[]{:S(2)}, u32[]{:S(2)}) async-start(bf16[8,64,768]{2,1,0:T(8,128)(2,1)} %bitcast.8), calls=%async_computation.1 | async-start | bytes 1572864 | tf_op jit(solution)/shard_map/cond/branch_1_fun/all_to_all | solution.py:541
  297.6 19.9 %collective-permute-start.7 = (bf16[320,768]{1,0:T(8,128)(2,1)S(1)}, bf16[320,768]{1,0:T(8,128)(2,1)S(1)}, u32[]{:S(2)}, u32[]{:S(2)}) collective-permute-start(bf16[320,768]{1,0:T(8,128)(2,1)S(1)} %dynamic-slice_bitcast_fusion.2), channel_id=1, source_target_pairs={{0,8},{4,12},{8,0},{12,4},{16,24},{20,28},{24,16},{28,20},{1,9},{5... | collective-permute-start | bytes 1474568 | tf_op jit(solution)/shard_map/cond/branch_1_fun/ppermute | solution.py:624
  311.9 17.7 %collective-permute-start.9 = (bf16[320,768]{1,0:T(8,128)(2,1)S(1)}, bf16[320,768]{1,0:T(8,128)(2,1)S(1)}, u32[]{:S(2)}, u32[]{:S(2)}) collective-permute-start(bf16[320,768]{1,0:T(8,128)(2,1)S(1)} %dynamic-slice_bitcast_fusion.1), channel_id=1, source_target_pairs={{0,16},{4,20},{8,24},{12,28},{16,0},{20,4},{24,8},{28,12},{1,17},{... | collective-permute-start | bytes 1474568 | tf_op jit(solution)/shard_map/cond/branch_1_fun/ppermute | solution.py:624
  317.7 12.0 %copy-start.3 = (bf16[320,768]{1,0:T(8,128)(2,1)}, bf16[320,768]{1,0:T(8,128)(2,1)S(1)}, u32[]{:S(2)}) copy-start(bf16[320,768]{1,0:T(8,128)(2,1)S(1)} %fusion.15) | copy-start | bytes 1474564 | tf_op jit(solution)/shard_map/cond
  317.7 18.4 %collective-permute-start.8 = (bf16[160,768]{1,0:T(8,128)(2,1)S(1)}, bf16[160,768]{1,0:T(8,128)(2,1)S(1)}, u32[]{:S(2)}, u32[]{:S(2)}) collective-permute-start(bf16[160,768]{1,0:T(8,128)(2,1)S(1)} %dynamic-slice_bitcast_fusion.4), channel_id=1, source_target_pairs={{0,16},{4,20},{8,24},{12,28},{16,0},{20,4},{24,8},{28,12},{1,17},{... | collective-permute-start | bytes 737288 | tf_op jit(solution)/shard_map/cond/branch_1_fun/ppermute | solution.py:624
  329.8 6.3 %collective-permute-start.10 = (bf16[160,768]{1,0:T(8,128)(2,1)S(1)}, bf16[160,768]{1,0:T(8,128)(2,1)S(1)}, u32[]{:S(2)}, u32[]{:S(2)}) collective-permute-start(bf16[160,768]{1,0:T(8,128)(2,1)S(1)} %dynamic-slice_bitcast_fusion.3), channel_id=1, source_target_pairs={{0,8},{4,12},{8,0},{12,4},{16,24},{20,28},{24,16},{28,20},{1,9},{5... | collective-permute-start | bytes 737288 | tf_op jit(solution)/shard_map/cond/branch_1_fun/ppermute | solution.py:624
  336.1 25.6 %copy-start.1 = (bf16[8,64,768]{2,1,0:T(8,128)(2,1)}, bf16[8,64,768]{2,1,0:T(8,128)(2,1)S(1)}, u32[]{:S(2)}) copy-start(bf16[8,64,768]{2,1,0:T(8,128)(2,1)S(1)} %all-to-all-done.1) | copy-start | bytes 2359300 | tf_op jit(solution)/shard_map/cond
  339.7 13.6 %collective-permute-start.11 = (bf16[2,40,768]{2,1,0:T(8,128)(2,1)S(1)}, bf16[2,40,768]{2,1,0:T(8,128)(2,1)S(1)}, u32[]{:S(2)}, u32[]{:S(2)}) collective-permute-start(bf16[2,40,768]{2,1,0:T(8,128)(2,1)S(1)} %pad_maximum_fusion.4), channel_id=1, source_target_pairs={{0,1},{1,0},{2,3},{3,2},{4,5},{5,4},{6,7},{7,6},{8,9},{9,8},{10,11... | collective-permute-start | bytes 368648 | tf_op jit(solution)/shard_map/cond/branch_1_fun/ppermute | solution.py:649
  344.1 17.6 %collective-permute-start.12 = (bf16[2,40,768]{2,1,0:T(8,128)(2,1)S(1)}, bf16[2,40,768]{2,1,0:T(8,128)(2,1)S(1)}, u32[]{:S(2)}, u32[]{:S(2)}) collective-permute-start(bf16[2,40,768]{2,1,0:T(8,128)(2,1)S(1)} %pad_maximum_fusion.5), channel_id=1, source_target_pairs={{0,2},{1,3},{2,0},{3,1},{4,6},{5,7},{6,4},{7,5},{8,10},{9,11},{10,... | collective-permute-start | bytes 368648 | tf_op jit(solution)/shard_map/cond/branch_1_fun/ppermute | solution.py:649
  344.9 16.8 %collective-permute-start.13 = (bf16[2,40,768]{2,1,0:T(8,128)(2,1)S(1)}, bf16[2,40,768]{2,1,0:T(8,128)(2,1)S(1)}, u32[]{:S(2)}, u32[]{:S(2)}) collective-permute-start(bf16[2,40,768]{2,1,0:T(8,128)(2,1)S(1)} %pad_maximum_fusion.6), channel_id=1, source_target_pairs={{0,3},{1,2},{2,1},{3,0},{4,7},{5,6},{6,5},{7,4},{8,11},{9,10},{10,... | collective-permute-start | bytes 368648 | tf_op jit(solution)/shard_map/cond/branch_1_fun/ppermute | solution.py:649
  361.7 6.2 %collective-permute-start.14 = (bf16[2,40,768]{2,1,0:T(8,128)(2,1)S(1)}, bf16[2,40,768]{2,1,0:T(8,128)(2,1)S(1)}, u32[]{:S(2)}, u32[]{:S(2)}) collective-permute-start(bf16[2,40,768]{2,1,0:T(8,128)(2,1)S(1)} %add_convert_fusion), channel_id=1, source_target_pairs={{0,1},{1,0},{2,3},{3,2},{4,5},{5,4},{6,7},{7,6},{8,9},{9,8},{10,11... | collective-permute-start | bytes 368648 | tf_op jit(solution)/shard_map/cond/branch_1_fun/ppermute | solution.py:656
  364.0 12.7 %collective-permute-start.15 = (bf16[2,40,768]{2,1,0:T(8,128)(2,1)S(1)}, bf16[2,40,768]{2,1,0:T(8,128)(2,1)S(1)}, u32[]{:S(2)}, u32[]{:S(2)}) collective-permute-start(bf16[2,40,768]{2,1,0:T(8,128)(2,1)S(1)} %add_convert_fusion), channel_id=1, source_target_pairs={{0,2},{1,3},{2,0},{3,1},{4,6},{5,7},{6,4},{7,5},{8,10},{9,11},{10,... | collective-permute-start | bytes 368648 | tf_op jit(solution)/shard_map/cond/branch_1_fun/ppermute | solution.py:656
  364.0 12.7 %collective-permute-start.16 = (bf16[2,40,768]{2,1,0:T(8,128)(2,1)S(1)}, bf16[2,40,768]{2,1,0:T(8,128)(2,1)S(1)}, u32[]{:S(2)}, u32[]{:S(2)}) collective-permute-start(bf16[2,40,768]{2,1,0:T(8,128)(2,1)S(1)} %add_convert_fusion), channel_id=1, source_target_pairs={{0,3},{1,2},{2,1},{3,0},{4,7},{5,6},{6,5},{7,4},{8,11},{9,10},{10,... | collective-permute-start | bytes 368648 | tf_op jit(solution)/shard_map/cond/branch_1_fun/ppermute | solution.py:656
  376.8 6.3 %collective-permute-start.19 = (bf16[4,40,768]{2,1,0:T(8,128)(2,1)S(1)}, bf16[4,40,768]{2,1,0:T(8,128)(2,1)S(1)}, u32[]{:S(2)}, u32[]{:S(2)}) collective-permute-start(bf16[4,40,768]{2,1,0:T(8,128)(2,1)S(1)} %pad_maximum_fusion.3), channel_id=1, source_target_pairs={{0,8},{4,12},{8,0},{12,4},{16,24},{20,28},{24,16},{28,20},{1,9},{5... | collective-permute-start | bytes 737288 | tf_op jit(solution)/shard_map/cond/branch_1_fun/ppermute | solution.py:663
  378.8 10.6 %collective-permute-start.17 = (bf16[4,40,768]{2,1,0:T(8,128)(2,1)S(1)}, bf16[4,40,768]{2,1,0:T(8,128)(2,1)S(1)}, u32[]{:S(2)}, u32[]{:S(2)}) collective-permute-start(bf16[4,40,768]{2,1,0:T(8,128)(2,1)S(1)} %pad_maximum_fusion.2), channel_id=1, source_target_pairs={{0,16},{4,20},{8,24},{12,28},{16,0},{20,4},{24,8},{28,12},{1,17},{... | collective-permute-start | bytes 737288 | tf_op jit(solution)/shard_map/cond/branch_1_fun/ppermute | solution.py:663
  383.1 16.2 %collective-permute-start.20 = (bf16[8,40,768]{2,1,0:T(8,128)(2,1)S(1)}, bf16[8,40,768]{2,1,0:T(8,128)(2,1)S(1)}, u32[]{:S(2)}, u32[]{:S(2)}) collective-permute-start(bf16[8,40,768]{2,1,0:T(8,128)(2,1)S(1)} %get-tuple-element.228), channel_id=1, source_target_pairs={{0,16},{4,20},{8,24},{12,28},{16,0},{20,4},{24,8},{28,12},{1,17},{... | collective-permute-start | bytes 1474568 | tf_op jit(solution)/shard_map/cond/branch_1_fun/ppermute | solution.py:663
  389.4 10.0 %collective-permute-start.18 = (bf16[8,40,768]{2,1,0:T(8,128)(2,1)S(1)}, bf16[8,40,768]{2,1,0:T(8,128)(2,1)S(1)}, u32[]{:S(2)}, u32[]{:S(2)}) collective-permute-start(bf16[8,40,768]{2,1,0:T(8,128)(2,1)S(1)} %get-tuple-element.230), channel_id=1, source_target_pairs={{0,8},{4,12},{8,0},{12,4},{16,24},{20,28},{24,16},{28,20},{1,9},{5... | collective-permute-start | bytes 1474568 | tf_op jit(solution)/shard_map/cond/branch_1_fun/ppermute | solution.py:663
  399.3 2.8 collective-permute-start.22
  399.5 12.0 %copy-start.2 = (bf16[8,64,768]{2,1,0:T(8,128)(2,1)S(1)}, bf16[8,64,768]{2,1,0:T(8,128)(2,1)}, u32[]{:S(2)}) copy-start(bf16[8,64,768]{2,1,0:T(8,128)(2,1)} %copy-done.1) | copy-start | bytes 2359300 | tf_op jit(solution)/shard_map/cond
  399.5 4.2 collective-permute-start.21
  411.7 35.2 %copy-start = (f32[768,768]{1,0:T(8,128)}, f32[768,768]{1,0:T(8,128)S(1)}, u32[]{:S(2)}) copy-start(f32[768,768]{1,0:T(8,128)S(1)} %get-tuple-element.351.after_ref) | copy-start | bytes 7077892
  411.7 35.2 %copy-start.21 = (f32[33,12]{0,1:T(8,128)}, f32[33,12]{0,1:T(8,128)S(1)}, u32[]{:S(2)}) copy-start(f32[33,12]{0,1:T(8,128)S(1)} %get-tuple-element.363) | copy-start | bytes 4756
  411.7 35.2 %copy-start.22 = (f32[65,12]{0,1:T(8,128)}, f32[65,12]{0,1:T(8,128)S(1)}, u32[]{:S(2)}) copy-start(f32[65,12]{0,1:T(8,128)S(1)} %get-tuple-element.364) | copy-start | bytes 9364
  411.7 35.2 %copy-start.23 = (f32[65,12]{0,1:T(8,128)}, f32[65,12]{0,1:T(8,128)S(1)}, u32[]{:S(2)}) copy-start(f32[65,12]{0,1:T(8,128)S(1)} %get-tuple-element.365) | copy-start | bytes 9364
  411.7 35.2 %copy-start.32 = (f32[768]{0:T(1024)}, f32[768]{0:T(1024)S(1)}, u32[]{:S(2)}) copy-start(f32[768]{0:T(1024)S(1)} %get-tuple-element.349) | copy-start | bytes 9220
  411.7 35.2 %copy-start.33 = (f32[768]{0:T(1024)}, f32[768]{0:T(1024)S(1)}, u32[]{:S(2)}) copy-start(f32[768]{0:T(1024)S(1)} %get-tuple-element.352) | copy-start | bytes 9220
  (21 other events, 111.0 us)
Sparse Core Ops, SparseCore 0:
  173.0 258.3 all-reduce.10

commit v4 on v3

--- a/solution.py
+++ b/solution.py
@@ -48,7 +48,6 @@
     @pl.when(pl.program_id(0) == 0)
     def _():
         keys[:, 0:320] = hot_ref[0:seq, :]
-        keys[:, 320:640] = hot_ref[0:seq, :]
         values[64:80, :] = jnp.ones((16, seq), BF)
         assemble(pieces, rows)
         rows[seq:lanes, :] = jnp.zeros((lanes - seq, rows.shape[1]), BF)
@@ -68,20 +67,14 @@
     contexts = []
     for h in range(2):
         mine = (lane < 64) if h == 0 else (lane >= 64)
-        own, other = (640, 704) if h == 0 else (704, 640)
-        keys[:, 640:768] = jnp.where(mine, k[0:seq], mask_ref[...].astype(F32)).astype(BF)
+        own, other = (320, 384) if h == 0 else (384, 320)
+        keys[:, 320:448] = jnp.where(mine, k[0:seq], mask_ref[...].astype(F32)).astype(BF)
         queries[own : own + 64, :] = q_t[h * 64 : h * 64 + 64, :]
         queries[other : other + 64, :] = jnp.ones((64, lanes), BF)
         values[0:64, :] = v_t[h * 64 : h * 64 + 64, :]
-        near = mm(line_ref[h], hott_ref[0:64, :]).astype(BF)
-        queries[0:64, :] = near[0:64]
-        queries[320:384, :] = near[64:128]
-        near = mm(width_ref[h], hott_ref[64:192, :]).astype(BF)
-        queries[64:192, :] = near[0:128]
-        queries[384:512, :] = near[128:256]
-        near = mm(height_ref[h], hott_ref[192:320, :]).astype(BF)
-        queries[192:320, :] = near[0:128]
-        queries[512:640, :] = near[128:256]
+        queries[0:64, :] = mm(line_ref[h], hott_ref[0:64, :]).astype(BF)
+        queries[64:192, :] = mm(width_ref[h], hott_ref[64:192, :]).astype(BF)
+        queries[192:320, :] = mm(height_ref[h], hott_ref[192:320, :]).astype(BF)
         scores = mm(keys[...], queries[...])
         peak = jnp.max(scores, axis=0, keepdims=True)
         weights = jnp.exp(scores - peak).astype(BF)
@@ -149,8 +142,8 @@
             shape((seq, dim), BF),
         ],
         scratch_shapes=[
-            pltpu.VMEM((seq, 768), BF),
-            pltpu.VMEM((768, lanes), BF),
+            pltpu.VMEM((seq, 448), BF),
+            pltpu.VMEM((448, lanes), BF),
             pltpu.VMEM((80, seq), BF),
             pltpu.VMEM((lanes, dim), BF),
         ],
@@ -293,144 +286,148 @@
 def normalise_back(hat, scale, d_hat):
     return scale * (d_hat - jnp.mean(d_hat, axis=-1, keepdims=True) - hat * jnp.mean(d_hat * hat, axis=-1, keepdims=True))
 
-def rows_kernel(count, *refs):
+def total(rows):
+    return jnp.sum(rows, axis=0, keepdims=True)
+
+
+def rows_kernel(count, blocks, *refs):
     pieces = refs[:count]
     (
-        x_ref, ctx_ref, out_w, up_w, down_w, bias_ref, up_b, final_ref, dmid_ref, dattn_ref,
-        normed_ref, act_ref, dbranch_ref, dpre_ref, sums_ref, upsum_ref, slope, cots,
+        x_ref, ctx_ref, ctxt_ref, out_w, up_w, down_w, bias_ref, up_b,
+        final_ref, dmid_ref, dattn_ref, up_ref, down_ref, out_ref, sums_ref, upsum_ref,
+        slope, cots, lows, acts, d_branches, d_pres, lows_t, d_attns,
     ) = refs[count:]
     step = pl.program_id(0)
     block = x_ref.shape[0]
-
-    @pl.when(pl.program_id(0)==0)
+    seq, dim = cots.shape
+    parts = acts.shape[0]
+
+    @pl.when(step == 0)
     def _():
         sums_ref[...] = jnp.zeros_like(sums_ref)
         upsum_ref[...] = jnp.zeros_like(upsum_ref)
         assemble(pieces, cots)
 
-    ff = up_w.shape[1]
-    attn = mm(ctx_ref[...], out_w[...]) + bias_ref[0:1]
-    hat, scale = normalise(x_ref[...].astype(F32) + attn)
-    normed = hat * bias_ref[1:2] + bias_ref[2:3]
-    low = normed.astype(BF)
-    normed_ref[...] = low
-    branch = bias_ref[3:4]
-    for f in range(0, ff, 768):
-        part = slice(f, f+768)
-        act, grad = gelu_pair(mm(low, up_w[:, part]) + up_b[:, part])
-        slope[:, part] = grad
-        act = act.astype(BF)
-        act_ref[:, part] = act
-        branch = branch + mm(act, down_w[part, :])
-    final_hat, final_scale = normalise(normed + branch)
-    final_ref[...] = (final_hat * bias_ref[4:5] + bias_ref[5:6]).astype(BF)
-    cot = cots[pl.ds(pl.multiple_of(step * block, 16), block), :].astype(F32)
-    d_sum = normalise_back(final_hat, final_scale, cot * bias_ref[4:5])
-    d_branch = d_sum.astype(BF)
-    dbranch_ref[...] = d_branch
-    total = lambda a: jnp.sum(a, axis=0, keepdims=True)
-    d_normed = d_sum
-    for f in range(0, ff, 768):
-        part = slice(f, f+768)
-        d_pre = (against(d_branch, down_w[part, :]) * slope[:, part]).astype(BF)
-        dpre_ref[:, part] = d_pre
-        upsum_ref[:, part] += total(d_pre.astype(F32))
-        d_normed = d_normed + against(d_pre, up_w[:, part])
-    d_mid = normalise_back(hat, scale, d_normed * bias_ref[1:2])
-    dmid_ref[...] = d_mid
-    d_attn = d_mid.astype(BF)
-    dattn_ref[...] = d_attn
-    sums_ref[...] += jnp.concatenate([total(d_attn.astype(F32)), total(d_normed*hat), total(d_normed), total(d_branch.astype(F32)), total(cot*final_hat), total(cot), jnp.zeros((2,cot.shape[1]),F32)], axis=0)
-
-def rows_pass(pieces, x, ctx, out_w, up_w, down_w, bias, up_b):
+    @pl.when(step < blocks)
+    def _():
+        here = pl.ds(pl.multiple_of(step * block, 16), block)
+        attn = mm(ctx_ref[...], out_w[...]) + bias_ref[0:1]
+        hat, scale = normalise(x_ref[...].astype(F32) + attn)
+        normed = hat * bias_ref[1:2] + bias_ref[2:3]
+        low = normed.astype(BF)
+        lows[here, :] = low
+        branch = bias_ref[3:4]
+        for n in range(parts):
+            part = slice(n * dim, (n + 1) * dim)
+            act, grad = gelu_pair(mm(low, up_w[:, part]) + up_b[:, part])
+            slope[:, part] = grad
+            act = act.astype(BF)
+            acts[n, here, :] = act
+            branch = branch + mm(act, down_w[part, :])
+        final_hat, final_scale = normalise(normed + branch)
+        final_ref[...] = (final_hat * bias_ref[4:5] + bias_ref[5:6]).astype(BF)
+        cot = cots[here, :].astype(F32)
+        d_sum = normalise_back(final_hat, final_scale, cot * bias_ref[4:5])
+        d_branch = d_sum.astype(BF)
+        d_branches[here, :] = d_branch
+        d_normed = d_sum
+        for n in range(parts):
+            part = slice(n * dim, (n + 1) * dim)
+            d_pre = (against(d_branch, down_w[part, :]) * slope[:, part]).astype(BF)
+            d_pres[n, here, :] = d_pre
+            upsum_ref[:, part] += total(d_pre.astype(F32))
+            d_normed = d_normed + against(d_pre, up_w[:, part])
+        d_mid = normalise_back(hat, scale, d_normed * bias_ref[1:2])
+        dmid_ref[...] = d_mid
+        d_attn = d_mid.astype(BF)
+        dattn_ref[...] = d_attn
+        d_attns[here, :] = d_attn
+        sums_ref[...] += jnp.concatenate(
+            [
+                total(d_attn.astype(F32)),
+                total(d_normed * hat),
+                total(d_normed),
+                total(d_branch.astype(F32)),
+                total(cot * final_hat),
+                total(cot),
+                jnp.zeros((2, dim), F32),
+            ],
+            axis=0,
+        )
+
+    @pl.when(step == blocks)
+    def _():
+        lows_t[...] = lows[...].astype(F32).T.astype(BF)
+
+    @pl.when((step >= blocks) & (step < blocks + parts))
+    def _():
+        n = step - blocks
+        down_ref[...] = inner(acts[n], d_branches[...]).astype(BF)
+        up_ref[...] = mm(lows_t[...], d_pres[n]).astype(BF)
+
+    @pl.when(step == blocks + parts)
+    def _():
+        out_ref[...] = mm(ctxt_ref[:, 0:seq], d_attns[...]).astype(BF)
+
+
+def rows_pass(room, pieces, x, ctx, ctx_t, out_w, up_w, down_w, bias, up_b):
     seq, dim = ctx.shape
     ff = up_w.shape[1]
-    block = seq // 4
-    row = lambda w: pl.BlockSpec((block, w), lambda i: (i,0))
-    whole = lambda a: pl.BlockSpec(a.shape, lambda i: (0,)*a.ndim, pipeline_mode=pl.Buffered(1))
-    sd = jax.ShapeDtypeStruct
-    return pl.pallas_call(partial(rows_kernel, len(pieces)), grid=(seq//block,),
-        in_specs=[whole(a) for a in pieces] + [row(dim),row(dim),whole(out_w),whole(up_w),whole(down_w),whole(bias),whole(up_b)],
-        out_specs=[row(dim),row(dim),row(dim),row(dim),row(ff),row(dim),row(ff),pl.BlockSpec((8,dim),lambda i:(0,0)),pl.BlockSpec((1,ff),lambda i:(0,0))],
-        out_shape=[sd((seq,dim),BF),sd((seq,dim),F32),sd((seq,dim),BF),sd((seq,dim),BF),sd((seq,ff),BF),sd((seq,dim),BF),sd((seq,ff),BF),sd((8,dim),F32),sd((1,ff),F32)],
-        scratch_shapes=[pltpu.VMEM((block, ff), F32), pltpu.VMEM((seq, dim), BF)],
+    blocks = 4
+    block = seq // blocks
+    parts = ff // dim
+
+    def row(width):
+        return pl.BlockSpec((block, width), lambda p: (jnp.minimum(p, blocks - 1), 0))
+
+    def whole(a):
+        return pl.BlockSpec(a.shape, lambda p: (0,) * a.ndim, pipeline_mode=pl.Buffered(1))
+
+    def part(p):
+        return jnp.clip(p - blocks, 0, parts - 1)
+
+    shape = jax.ShapeDtypeStruct
+    return pl.pallas_call(
+        partial(rows_kernel, len(pieces), blocks),
+        grid=(blocks + parts + 1,),
+        in_specs=[whole(a) for a in pieces]
+        + [row(dim), row(dim)]
+        + [whole(a) for a in (ctx_t, out_w, up_w, down_w, bias, up_b)],
+        out_specs=[
+            row(dim),
+            row(dim),
+            row(dim),
+            pl.BlockSpec((dim, dim), lambda p: (0, part(p))),
+            pl.BlockSpec((dim, dim), lambda p: (part(p), 0)),
+            pl.BlockSpec((dim, dim), lambda p: (0, 0)),
+            pl.BlockSpec((8, dim), lambda p: (0, 0)),
+            pl.BlockSpec((1, ff), lambda p: (0, 0)),
+        ],
+        out_shape=[
+            shape((seq, dim), BF),
+            shape((seq, dim), F32),
+            shape((seq, dim), BF),
+            shape((dim, ff), BF),
+            shape((ff, dim), BF),
+            shape((dim + room, dim), BF),
+            shape((8, dim), F32),
+            shape((1, ff), F32),
+        ],
+        scratch_shapes=[
+            pltpu.VMEM((block, ff), F32),
+            pltpu.VMEM((seq, dim), BF),
+            pltpu.VMEM((seq, dim), BF),
+            pltpu.VMEM((parts, seq, dim), BF),
+            pltpu.VMEM((seq, dim), BF),
+            pltpu.VMEM((parts, seq, dim), BF),
+            pltpu.VMEM((dim, seq), BF),
+            pltpu.VMEM((seq, dim), BF),
+        ],
         compiler_params=pltpu.CompilerParams(vmem_limit_bytes=VMEM_BYTES),
         cost_estimate=pl.CostEstimate(
-            flops=34 * seq * dim * dim, bytes_accessed=64 * seq * dim, transcendentals=seq * ff
+            flops=56 * seq * dim * dim, bytes_accessed=64 * seq * dim, transcendentals=seq * ff
         ),
-    )(*pieces,x,ctx,out_w,up_w,down_w,bias,up_b)
-
-
-def down_kernel(act_ref, dbranch_ref, ctxt_ref, dattn_ref, down_ref, out_ref):
-    step = pl.program_id(0)
-    last = pl.num_programs(0) - 1
-    seq = act_ref.shape[0]
-
-    @pl.when(step < last)
-    def _():
-        down_ref[...] = inner(act_ref[...], dbranch_ref[...]).astype(BF)
-
-    @pl.when(step == last)
-    def _():
-        out_ref[...] = mm(ctxt_ref[:, 0:seq], dattn_ref[...]).astype(BF)
-
-
-def down_sums(room, act, d_branch, ctx_t, d_attn):
-    seq, ff = act.shape
-    dim = d_branch.shape[1]
-    steps = ff // dim
-
-    def whole(a):
-        return pl.BlockSpec(a.shape, lambda p: (0,) * a.ndim, pipeline_mode=pl.Buffered(1))
-
-    shape = jax.ShapeDtypeStruct
-    return pl.pallas_call(
-        down_kernel,
-        grid=(steps + 1,),
-        in_specs=[
-            pl.BlockSpec((seq, dim), lambda p: (0, jnp.minimum(p, steps - 1))),
-            whole(d_branch),
-            whole(ctx_t),
-            whole(d_attn),
-        ],
-        out_specs=[
-            pl.BlockSpec((dim, dim), lambda p: (jnp.minimum(p, steps - 1), 0)),
-            pl.BlockSpec((dim, dim), lambda p: (0, 0)),
-        ],
-        out_shape=[shape((ff, dim), BF), shape((dim + room, dim), BF)],
-        compiler_params=pltpu.CompilerParams(vmem_limit_bytes=VMEM_BYTES),
-        cost_estimate=pl.CostEstimate(
-            flops=10 * seq * dim * dim, bytes_accessed=32 * seq * dim, transcendentals=0
-        ),
-    )(act, d_branch, ctx_t, d_attn)
-
-
-def up_kernel(normed_ref, dpre_ref, grad_ref, normed_t):
-    @pl.when(pl.program_id(0) == 0)
-    def _():
-        normed_t[...] = normed_ref[...].astype(F32).T.astype(BF)
-
-    grad_ref[...] = mm(normed_t[...], dpre_ref[...]).astype(BF)
-
-
-def up_sums(normed, d_pre):
-    seq, dim = normed.shape
-    ff = d_pre.shape[1]
-    return pl.pallas_call(
-        up_kernel,
-        grid=(ff // dim,),
-        in_specs=[
-            pl.BlockSpec((seq, dim), lambda p: (0, 0), pipeline_mode=pl.Buffered(1)),
-            pl.BlockSpec((seq, dim), lambda p: (0, p)),
-        ],
-        out_specs=pl.BlockSpec((dim, dim), lambda p: (0, p)),
-        out_shape=jax.ShapeDtypeStruct((dim, ff), BF),
-        scratch_shapes=[pltpu.VMEM((dim, seq), BF)],
-        compiler_params=pltpu.CompilerParams(vmem_limit_bytes=VMEM_BYTES),
-        cost_estimate=pl.CostEstimate(
-            flops=8 * seq * dim * dim, bytes_accessed=24 * seq * dim, transcendentals=0
-        ),
-    )(normed, d_pre)
+    )(*pieces, x, ctx, ctx_t, out_w, up_w, down_w, bias, up_b)
 
 
 def last_kernel(count, held, *refs):
@@ -496,16 +493,13 @@
 
 def spread_table(table):
     span = 2 * (table.shape[0] - 1)
-    high = table.astype(BF)
-    low = (table - high.astype(F32)).astype(BF)
-    both = jnp.stack([high, low], axis=2).reshape(table.shape[0], -1)
     spread = lax.dot_general(
-        both,
+        table.astype(BF),
         bucket_select(table).astype(BF).reshape(table.shape[0], -1),
         (((0,), (0,)), ((), ())),
         preferred_element_type=F32,
     )
-    return spread.astype(BF).reshape(HEADS, 2 * span, span)
+    return spread.astype(BF).reshape(HEADS, span, span)
 
 
 def gather_table(parts, table):
@@ -817,7 +811,8 @@
     narrow = patch_shape[1]
     pieces = [swap_text(text_in.reshape(wide, -1, dim)).reshape(-1, dim)]
     pieces += swap_patch(patch_in.reshape(narrow, -1, dim))
-    cot_text, cot_patch, pieces = lax.optimization_barrier((cot_text, cot_patch, pieces))
+    cot_text, pieces[0] = lax.optimization_barrier((cot_text, pieces[0]))
+    cot_patch, pieces = lax.optimization_barrier((cot_patch, pieces))
     cots = [swap_text(cot_text.reshape(wide, -1, dim)).reshape(-1, dim)]
     cots += swap_patch(cot_patch.reshape(narrow, -1, dim))
     index = jnp.arange(seq, dtype=jnp.int32)
@@ -869,14 +864,12 @@
     vectors = jnp.stack(
         [output_bias, norm_gain, norm_shift, down_bias, final_gain, final_shift] + [final_shift] * 2
     )
-    final_low, d_mid, d_attn, normed, act, d_branch, d_pre, sums, up_sum = rows_pass(
-        cots, rows_in, ctx, output_weight, up_weight, down_weight, vectors, up_bias[None]
+    room = 16
+    final_low, d_mid, d_attn, up_low, down_low, out_low, sums, up_sum = rows_pass(
+        room, cots, rows_in, ctx, ctx_t, output_weight, up_weight, down_weight, vectors, up_bias[None]
     )
     early = (sums[0], sums[1], sums[2], up_sum, sums[3], sums[4], sums[5])
-    small = pack(early, dim, 16).astype(BF)
-    down_low, out_low = down_sums(small.shape[0], act, d_branch, ctx_t, d_attn)
-    out_low = lax.dynamic_update_slice(out_low, small, (dim, 0))
-    up_low = up_sums(normed, d_pre)
+    out_low = lax.dynamic_update_slice(out_low, pack(early, dim, room).astype(BF), (dim, 0))
     down_total, up_total, out_total = lax.psum((down_low, up_low, out_low), ("wide", "narrow"))
     qkv_weight = jnp.stack([query_weight, key_weight, value_weight])
 

time: 463 us -> 443 us (0.957)
  Pallas kernels: 224 us -> 204 us
    pallas_call x1, Pallas kernels: 60.9 us -> 46.4 us  [attend(): pl.pallas_call(partial(attend_kernel, len(pieces)), grid=(HEADS // 2,), i...]
    pallas_call x3 -> x1, Pallas kernels: 65.4 us -> 60.2 us  [rows_pass(): pl.pallas_call(partial(rows_kernel, len(pieces), blocks), grid=(blocks +...]
  transfers between devices with their start and end apart: 34 -> 34, of which waited for: 15 -> 15; matrix products, arithmetic and copies ran while one was open for 11% -> 11% of each run, Pallas kernels for 32% -> 30%
where the time goes in v4:
time: 443 us; the launch traced here: 437 us
  Pallas kernels  204 us (46%)
  waiting for transfers between devices  94.3 us (21%)
  starting transfers between devices  59.7 us (13%)
  local copies, waits for them, and re-layouts  30 us (7%)
  other arithmetic  21.7 us (5%)
  between operations  16.2 us (4%)
  matrix products  10.4 us (2%)
    pallas_call x1, Pallas kernels, attend_back(): pl.pallas_call(partial(attend_back_kernel, len(held)), grid=(pairs,), in_...  61.4 us
    pallas_call x1, Pallas kernels, rows_pass(): pl.pallas_call(partial(rows_kernel, len(pieces), blocks), grid=(blocks +...  60.2 us
    pallas_call x1, Pallas kernels, attend(): pl.pallas_call(partial(attend_kernel, len(pieces)), grid=(HEADS // 2,), i...  46.4 us
    psum x1, waiting for transfers between devices, body(): lax.psum((down_low, up_low, out_low), ('wide', 'narrow'))  19.8 us
    ppermute x5, waiting for transfers between devices, wide_step(): lax.ppermute(pick(parts, 1 - me), 'wide', flip_pairs(wide, 1 << bit))  18.3 us
    ppermute x4, waiting for transfers between devices, gather_wide(): lax.ppermute(a, 'wide', flip_pairs(wide, 1 << order[i]))  17 us
    all_to_all x4, starting transfers between devices, swap_text(): lax.all_to_all(parts, 'wide', split_axis=0, concat_axis=0, tiled=True)  16.4 us
    pallas_call x1, Pallas kernels, last_products(): pl.pallas_call(partial(last_kernel, len(d_qkv), len(held)), grid=(3,), in...  16.2 us
  transfers between devices with their start and end apart: 34, of which 15 were waited for; matrix products, arithmetic and copies ran while one was open for 11% of the time, Pallas kernels for 30%

profile of v4, /device:TPU:0, one launch (start us, length us, event | category | flops | bytes accessed | tf_op | source)
XLA Modules:
  0.0 437.5 jit_solution(5460556206184275470)
XLA Ops:
  7.3 2.2 dynamic-slice_bitcast_fusion.9
  9.4 3.0 collective-permute-start.23
  12.5 2.6 collective-permute-start.24
  15.1 3.9 all-to-all-start.2
  30.2 1.7 add_convert_fusion.1.refs_9_
  34.7 1.6 collective-permute-start.26
  36.3 2.6 collective-permute-start.27
  39.1 4.2 all-to-all-start.3
  43.6 46.4 %shard_map.426 = (bf16[12,1088,1152]{2,1,0:T(8,128)(2,1)}, bf16[768,1152]{1,0:T(8,128)(2,1)}, bf16[1088,768]{1,0:T(8,128)(2,1)}, f32[12,1,1152]{2,1,0:T(1,128)S(...) custom-call(bf16[512,768]{1,0:T(8,128)(2,1)} %bitcast.138, ...), custom_call_target="tpu_custom_call" | custom-call | flops 61605937152 | bytes 30081024 | tf_op jit(solution)/shard_map/pallas_call | solution.py:108
  91.1 60.2 %shard_map.427 = (bf16[1088,768]{1,0:T(8,128)(2,1)}, f32[1088,768]{1,0:T(8,128)}, bf16[1088,768]{1,0:T(8,128)(2,1)}, bf16[768,3072]{1,0:T(8,128)(2,1)}, bf16[307...) custom-call(bf16[512,768]{1,0:T(8,128)(2,1)} %bitcast.139, ...), custom_call_target="tpu_custom_call" | custom-call | flops 35936796672 | bytes 53477376 | tf_op jit(solution)/shard_map/pallas_call | solution.py:390
  154.7 3.3 pad_maximum_fusion.7
  158.1 234.0 %conditional.1 = (bf16[8,1,64,768]{3,2,1,0:T(8,128)(2,1)}, bf16[1,4,144,768]{3,2,1,0:T(8,128)(2,1)}, bf16[8,1,64,768]{3,2,1,0:T(8,128)(2,1)S(1)}, bf16[1,4,144,7...) conditional(s32[]{:T(128)} %convert_element_type.132, () %tuple.18, ...), branch_computations={%region_0.1_spmd, %region_1.2_spmd} | conditional | flops 69647499264 | bytes 182262816 | solution.py:917
  159.2 3.8 collective-permute-start.1
  164.2 4.2 all-to-all-start
  168.5 61.4 %branch_1_fun.4 = (bf16[3,1088,768]{2,1,0:T(8,128)(2,1)}, f32[12,128,128]{2,1,0:T(8,128)}, f32[12,128,128]{2,1,0:T(8,128)}, f32[12,64,64]{2,1,0:T(8,128)}) custom-call(bf16[12,1088,1152]{2,1,0:T(8,128)(2,1)} %get-tuple-element.29.refs_0_, bf16[768,1152]{1,0:T(8,128)(2,1)} %get-tuple-element.30.refs_1_, f32[12,1,1152]{2,1,0:T(1,128)S(1)} %get-tuple-element.31.refs_2_, ...), custom_call_target="tpu_custom_call" | custom-call | flops 61605937152 | bytes 30081024 | tf_op jit(solution)/shard_map/cond/branch_1_fun/pallas_call | solution.py:228
  230.0 3.7 fusion.10
  233.7 3.7 fusion.9
  241.5 16.2 %branch_1_fun.5 = (bf16[2560,768]{1,0:T(8,128)(2,1)}, bf16[1088,768]{1,0:T(8,128)(2,1)}, f32[3,8,768]{2,1,0:T(8,128)}) custom-call(bf16[3,1088,768]{2,1,0:T(8,128)(2,1)} %get-tuple-element.39.refs_0_, bf16[1088,768]{1,0:T(8,128)(2,1)} %get-tuple-element.40.refs_1_, bf16[3,768,768]{2,1,0:T(8,128)(2,1)} %get-tuple-element.41.refs_2_, ...), custom_call_target="tpu_custom_call" | custom-call | flops 7700742144 | bytes 26738688 | tf_op jit(solution)/shard_map/cond/branch_1_fun/pallas_call | solution.py:463
  259.5 3.0 dynamic-slice_bitcast_fusion
  262.8 2.1 slice.133
  264.9 2.3 slice_bitcast_fusion
  267.4 3.9 collective-permute-start.4
  271.5 4.1 all-to-all-start.1
  275.6 2.1 fusion.2
  277.9 2.1 collective-permute-start.7
  280.0 3.0 collective-permute-done.3
  283.0 8.1 %collective-permute-done.4 = bf16[144,768]{1,0:T(8,128)(2,1)} collective-permute-done((bf16[144,768]{1,0:T(8,128)(2,1)}, bf16[144,768]{1,0:T(8,128)(2,1)}, u32[]{:S(2)}, u32[]{:S(2)}) %collective-permute-start.4) | collective-permute-done | bytes 221216 | tf_op jit(solution)/shard_map/cond/branch_1_fun/ppermute | solution.py:568
  293.7 4.1 collective-permute-done.7
  298.0 1.5 collective-permute-start.8
  299.5 10.6 %collective-permute-done.9 = bf16[320,768]{1,0:T(8,128)(2,1)S(1)} collective-permute-done((bf16[320,768]{1,0:T(8,128)(2,1)S(1)}, bf16[320,768]{1,0:T(8,128)(2,1)S(1)}, u32[]{:S(2)}, u32[]{:S(2)}) %collective-permute-start.9) | collective-permute-done | bytes 491552 | tf_op jit(solution)/shard_map/cond/branch_1_fun/ppermute | solution.py:618
  310.3 1.6 collective-permute-start.10
  312.9 3.6 collective-permute-done.10
  317.4 1.8 branch_1_fun.6
  320.2 4.7 %collective-permute-start.11 = (bf16[2,40,768]{2,1,0:T(8,128)(2,1)S(1)}, bf16[2,40,768]{2,1,0:T(8,128)(2,1)S(1)}, u32[]{:S(2)}, u32[]{:S(2)}) collective-permute-start(bf16[2,40,768]{2,1,0:T(8,128)(2,1)S(1)} %pad_maximum_fusion.4), channel_id=1, source_target_pairs={{0,1},{1,0},{2,3},{3,2},{4,5},{5,4},{6,7},{7,6},{8,9},{9,8},{10,11... | collective-permute-start | bytes 368648 | tf_op jit(solution)/shard_map/cond/branch_1_fun/ppermute | solution.py:643
  325.5 1.9 collective-permute-start.13
  327.4 6.6 %collective-permute-done.11 = bf16[2,40,768]{2,1,0:T(8,128)(2,1)S(1)} collective-permute-done((bf16[2,40,768]{2,1,0:T(8,128)(2,1)S(1)}, bf16[2,40,768]{2,1,0:T(8,128)(2,1)S(1)}, u32[]{:S(2)}, u32[]{:S(2)}) %collective-permute-start.11) | collective-permute-done | bytes 122912 | tf_op jit(solution)/shard_map/cond/branch_1_fun/ppermute | solution.py:643
  334.0 8.3 %collective-permute-done.12 = bf16[2,40,768]{2,1,0:T(8,128)(2,1)S(1)} collective-permute-done((bf16[2,40,768]{2,1,0:T(8,128)(2,1)S(1)}, bf16[2,40,768]{2,1,0:T(8,128)(2,1)S(1)}, u32[]{:S(2)}, u32[]{:S(2)}) %collective-permute-start.12) | collective-permute-done | bytes 122912 | tf_op jit(solution)/shard_map/cond/branch_1_fun/ppermute | solution.py:643
  342.3 2.2 collective-permute-start.14
  344.6 2.4 collective-permute-start.16
  348.4 9.1 %collective-permute-done.15 = bf16[2,40,768]{2,1,0:T(8,128)(2,1)S(1)} collective-permute-done((bf16[2,40,768]{2,1,0:T(8,128)(2,1)S(1)}, bf16[2,40,768]{2,1,0:T(8,128)(2,1)S(1)}, u32[]{:S(2)}, u32[]{:S(2)}) %collective-permute-start.15) | collective-permute-done | bytes 122912 | tf_op jit(solution)/shard_map/cond/branch_1_fun/ppermute | solution.py:650
  360.3 3.6 collective-permute-done.19
  365.3 2.1 collective-permute-done.17
  368.2 11.3 %collective-permute-done.20 = bf16[8,40,768]{2,1,0:T(8,128)(2,1)S(1)} collective-permute-done((bf16[8,40,768]{2,1,0:T(8,128)(2,1)S(1)}, bf16[8,40,768]{2,1,0:T(8,128)(2,1)S(1)}, u32[]{:S(2)}, u32[]{:S(2)}) %collective-permute-start.20) | collective-permute-done | bytes 491552 | tf_op jit(solution)/shard_map/cond/branch_1_fun/ppermute | solution.py:657
  382.3 1.6 collective-permute-done.21.refs_2_
  383.9 4.9 %branch_1_fun.7 = (f32[768,768]{1,0:T(8,128)}, f32[768,768]{1,0:T(8,128)}, f32[768,768]{1,0:T(8,128)S(1)}, f32[16,768]{1,0:T(8,128)}) custom-call(s32[3,16]{1,0:T(4,128)} %add_add_fusion.index_ref, bf16[16,40,768]{2,1,0:T(8,128)(2,1)} %copy-done.6, bf16[16,40,768]{2,1,0:T(8,128)(2,1)} %copy-done.7, bf16[16,40,768]{2,1,0:T(8,128)(2,1)} %collective-permute-done.21.refs_2_, ...), custom_call_target="tpu_custom_call" | custom-call | bytes 14254080 | tf_op jit(solution)/shard_map/cond/branch_1_fun/pallas_call | solution.py:739
  392.1 19.8 %all-reduce.11.cloned.1.call-done = (bf16[768,3072]{1,0:T(8,128)(2,1)}, bf16[3072,768]{1,0:T(8,128)(2,1)}, bf16[784,768]{1,0:T(8,128)(2,1)}) async-done(((bf16[768,3072]{1,0:T(8,128)(2,1)}, bf16[3072,768]{1,0:T(8,128)(2,1)}, bf16[784,768]{1,0:T(8,128)(2,1)}), (bf16[768,3072]{1,0:T(8,128)(2,1)}, bf16[3072,768]{1,0:T(8,128)(2,1)}, bf16[784,768]{1,0:T(8,128)(2,1)})) %all-reduce.11.cloned.1.call-update) | async-done | bytes 10641424 | tf_op jit(solution)/shard_map/psum | solution.py:873
  413.9 13.5 %shard_map.428 = (f32[768,3072]{1,0:T(8,128)}, f32[3072,768]{1,0:T(8,128)}, f32[768,768]{1,0:T(8,128)}) custom-call(bf16[768,3072]{1,0:T(8,128)(2,1)} %get-tuple-element.211.up_ref, bf16[3072,768]{1,0:T(8,128)(2,1)} %get-tuple-element.212.down_ref, bf16[784,768]{1,0:T(8,128)(2,1)} %get-tuple-element.213.out_ref, f32[768,768]{1,0:T(8,128)S(1)} %get-tuple-element.341.after_ref), custom_call_target="tpu_custom_call" | custom-call | bytes 30670848 | tf_op jit(solution)/shard_map/pallas_call | solution.py:694
  427.4 2.1 copy.137
  (230 shorter events, 48.0 us)
Async XLA Ops:
  7.2 13.2 %copy-start.17 = (s32[1,1,1088]{2,1,0:T(1,128)S(1)}, s32[1,1,1088]{2,1,0:T(1,128)}, u32[]{:S(2)}) copy-start(s32[1,1,1088]{2,1,0:T(1,128)} %param.33) | copy-start | bytes 13060
  7.2 13.2 %copy-start.16 = (s32[1,1,1088]{2,1,0:T(1,128)S(1)}, s32[1,1,1088]{2,1,0:T(1,128)}, u32[]{:S(2)}) copy-start(s32[1,1,1088]{2,1,0:T(1,128)} %param.34) | copy-start | bytes 13060
  7.2 13.2 %copy-start.15 = (s32[1,1,1088]{2,1,0:T(1,128)S(1)}, s32[1,1,1088]{2,1,0:T(1,128)}, u32[]{:S(2)}) copy-start(s32[1,1,1088]{2,1,0:T(1,128)} %param.35) | copy-start | bytes 13060
  7.2 16.4 %copy-start.33 = (f32[65,12]{0,1:T(8,128)S(1)}, f32[65,12]{0,1:T(8,128)}, u32[]{:S(2)}) copy-start(f32[65,12]{0,1:T(8,128)} %param.52) | copy-start | bytes 9364
  9.4 24.2 %collective-permute-start.23 = (bf16[144,768]{1,0:T(8,128)(2,1)}, bf16[144,768]{1,0:T(8,128)(2,1)}, u32[]{:S(2)}, u32[]{:S(2)}) collective-permute-start(bf16[144,768]{1,0:T(8,128)(2,1)} %get-tuple-element.275), channel_id=1, source_target_pairs={{0,1},{1,0},{2,3},{3,2},{4,5},{5,4},{6,7},{7,6},{8,9},{9,8},{10,11... | collective-permute-start | bytes 663560 | tf_op jit(solution)/shard_map/ppermute | solution.py:547
  12.5 21.2 %collective-permute-start.24 = (bf16[144,768]{1,0:T(8,128)(2,1)}, bf16[144,768]{1,0:T(8,128)(2,1)}, u32[]{:S(2)}, u32[]{:S(2)}) collective-permute-start(bf16[144,768]{1,0:T(8,128)(2,1)} %get-tuple-element.277), channel_id=1, source_target_pairs={{0,2},{1,3},{2,0},{3,1},{4,6},{5,7},{6,4},{7,5},{8,10},{9,11},{10,... | collective-permute-start | bytes 663560 | tf_op jit(solution)/shard_map/ppermute | solution.py:547
  15.1 18.6 %collective-permute-start.25 = (bf16[144,768]{1,0:T(8,128)(2,1)}, bf16[144,768]{1,0:T(8,128)(2,1)}, u32[]{:S(2)}, u32[]{:S(2)}) collective-permute-start(bf16[144,768]{1,0:T(8,128)(2,1)} %get-tuple-element.274), channel_id=1, source_target_pairs={{0,3},{1,2},{2,1},{3,0},{4,7},{5,6},{6,5},{7,4},{8,11},{9,10},{10,... | collective-permute-start | bytes 663560 | tf_op jit(solution)/shard_map/ppermute | solution.py:547
  15.1 18.6 %all-to-all-start.2 = ((bf16[8,64,768]{2,1,0:T(8,128)(2,1)}), bf16[8,64,768]{2,1,0:T(8,128)(2,1)S(1)}, u32[]{:S(2)}, u32[]{:S(2)}) async-start(bf16[8,64,768]{2,1,0:T(8,128)(2,1)} %bitcast.137), calls=%async_computation.2 | async-start | bytes 1572864 | tf_op jit(solution)/shard_map/all_to_all | solution.py:535
  32.0 58.1 %copy-start.9 = (bf16[1152,320]{1,0:T(8,128)(2,1)}, bf16[1152,320]{1,0:T(8,128)(2,1)S(1)}, u32[]{:S(2)}) copy-start(bf16[1152,320]{1,0:T(8,128)(2,1)S(1)} %add_convert_fusion.1.refs_9_) | copy-start | bytes 2211844
  34.7 55.4 %collective-permute-start.26 = (bf16[144,768]{1,0:T(8,128)(2,1)}, bf16[144,768]{1,0:T(8,128)(2,1)S(1)}, u32[]{:S(2)}, u32[]{:S(2)}) collective-permute-start(bf16[144,768]{1,0:T(8,128)(2,1)} %get-tuple-element.272), channel_id=1, source_target_pairs={{0,1},{1,0},{2,3},{3,2},{4,5},{5,4},{6,7},{7,6},{8,9},{9,8},{10,11... | collective-permute-start | bytes 663560 | tf_op jit(solution)/shard_map/ppermute | solution.py:547
  36.3 53.8 %collective-permute-start.27 = (bf16[144,768]{1,0:T(8,128)(2,1)}, bf16[144,768]{1,0:T(8,128)(2,1)S(1)}, u32[]{:S(2)}, u32[]{:S(2)}) collective-permute-start(bf16[144,768]{1,0:T(8,128)(2,1)} %get-tuple-element.271), channel_id=1, source_target_pairs={{0,2},{1,3},{2,0},{3,1},{4,6},{5,7},{6,4},{7,5},{8,10},{9,11},{10,... | collective-permute-start | bytes 663560 | tf_op jit(solution)/shard_map/ppermute | solution.py:547
  38.8 51.2 %collective-permute-start.28 = (bf16[144,768]{1,0:T(8,128)(2,1)S(1)}, bf16[144,768]{1,0:T(8,128)(2,1)}, u32[]{:S(2)}, u32[]{:S(2)}) collective-permute-start(bf16[144,768]{1,0:T(8,128)(2,1)S(1)} %get-tuple-element.270), channel_id=1, source_target_pairs={{0,3},{1,2},{2,1},{3,0},{4,7},{5,6},{6,5},{7,4},{8,11},{9,10},{10,... | collective-permute-start | bytes 663560 | tf_op jit(solution)/shard_map/ppermute | solution.py:547
  39.1 51.0 %all-to-all-start.3 = ((bf16[8,64,768]{2,1,0:T(8,128)(2,1)}), bf16[8,64,768]{2,1,0:T(8,128)(2,1)S(1)}, u32[]{:S(2)}, u32[]{:S(2)}) async-start(bf16[8,64,768]{2,1,0:T(8,128)(2,1)} %bitcast.41), calls=%async_computation.3 | async-start | bytes 1572864 | tf_op jit(solution)/shard_map/all_to_all | solution.py:535
  43.3 368.6 %all-reduce.11.cloned.1.call-start = ((), (), s32[]{:S(2)}) async-start(), calls=%async_computation.4 | async-start | bytes 21282816 | tf_op jit(solution)/shard_map/psum | solution.py:873
  158.9 80.2 %collective-permute-start = (bf16[144,768]{1,0:T(8,128)(2,1)}, bf16[144,768]{1,0:T(8,128)(2,1)S(1)}, u32[]{:S(2)}, u32[]{:S(2)}) collective-permute-start(bf16[144,768]{1,0:T(8,128)(2,1)} %get-tuple-element.223), channel_id=1, source_target_pairs={{0,1},{1,0},{2,3},{3,2},{4,5},{5,4},{6,7},{7,6},{8,9},{9,8},{10,11... | collective-permute-start | bytes 663560 | tf_op jit(solution)/shard_map/cond/branch_1_fun/ppermute | solution.py:568
  159.2 79.9 %collective-permute-start.1 = (bf16[144,768]{1,0:T(8,128)(2,1)}, bf16[144,768]{1,0:T(8,128)(2,1)}, u32[]{:S(2)}, u32[]{:S(2)}) collective-permute-start(bf16[144,768]{1,0:T(8,128)(2,1)} %get-tuple-element.222), channel_id=1, source_target_pairs={{0,2},{1,3},{2,0},{3,1},{4,6},{5,7},{6,4},{7,5},{8,10},{9,11},{10,... | collective-permute-start | bytes 663560 | tf_op jit(solution)/shard_map/cond/branch_1_fun/ppermute | solution.py:568
  163.1 76.1 %collective-permute-start.2 = (bf16[144,768]{1,0:T(8,128)(2,1)S(1)}, bf16[144,768]{1,0:T(8,128)(2,1)}, u32[]{:S(2)}, u32[]{:S(2)}) collective-permute-start(bf16[144,768]{1,0:T(8,128)(2,1)S(1)} %get-tuple-element.221), channel_id=1, source_target_pairs={{0,3},{1,2},{2,1},{3,0},{4,7},{5,6},{6,5},{7,4},{8,11},{9,10},{10,... | collective-permute-start | bytes 663560 | tf_op jit(solution)/shard_map/cond/branch_1_fun/ppermute | solution.py:568
  164.2 77.3 %all-to-all-start = ((bf16[8,64,768]{2,1,0:T(8,128)(2,1)}), bf16[8,64,768]{2,1,0:T(8,128)(2,1)}, u32[]{:S(2)}, u32[]{:S(2)}) async-start(bf16[8,64,768]{2,1,0:T(8,128)(2,1)} %bitcast), calls=%async_computation | async-start | bytes 1572864 | tf_op jit(solution)/shard_map/cond/branch_1_fun/all_to_all | solution.py:535
  262.4 13.2 %collective-permute-start.6 = (bf16[1280,768]{1,0:T(8,128)(2,1)}, bf16[1280,768]{1,0:T(8,128)(2,1)S(1)}, u32[]{:S(2)}, u32[]{:S(2)}) collective-permute-start(bf16[1280,768]{1,0:T(8,128)(2,1)} %dynamic-slice_bitcast_fusion), channel_id=1, source_target_pairs={{0,4},{4,0},{8,12},{12,8},{16,20},{20,16},{24,28},{28,24},{1,5},{5... | collective-permute-start | bytes 5898248 | tf_op jit(solution)/shard_map/cond/branch_1_fun/ppermute | solution.py:618
  267.1 15.8 %collective-permute-start.3 = (bf16[144,768]{1,0:T(8,128)(2,1)}, bf16[144,768]{1,0:T(8,128)(2,1)}, u32[]{:S(2)}, u32[]{:S(2)}) collective-permute-start(bf16[144,768]{1,0:T(8,128)(2,1)} %get-tuple-element.219), channel_id=1, source_target_pairs={{0,1},{1,0},{2,3},{3,2},{4,5},{5,4},{6,7},{7,6},{8,9},{9,8},{10,11... | collective-permute-start | bytes 663560 | tf_op jit(solution)/shard_map/cond/branch_1_fun/ppermute | solution.py:568
  267.4 23.7 %collective-permute-start.4 = (bf16[144,768]{1,0:T(8,128)(2,1)}, bf16[144,768]{1,0:T(8,128)(2,1)}, u32[]{:S(2)}, u32[]{:S(2)}) collective-permute-start(bf16[144,768]{1,0:T(8,128)(2,1)} %get-tuple-element.218), channel_id=1, source_target_pairs={{0,2},{1,3},{2,0},{3,1},{4,6},{5,7},{6,4},{7,5},{8,10},{9,11},{10,... | collective-permute-start | bytes 663560 | tf_op jit(solution)/shard_map/cond/branch_1_fun/ppermute | solution.py:568
  271.3 19.8 %collective-permute-start.5 = (bf16[144,768]{1,0:T(8,128)(2,1)S(1)}, bf16[144,768]{1,0:T(8,128)(2,1)}, u32[]{:S(2)}, u32[]{:S(2)}) collective-permute-start(bf16[144,768]{1,0:T(8,128)(2,1)S(1)} %get-tuple-element.217), channel_id=1, source_target_pairs={{0,3},{1,2},{2,1},{3,0},{4,7},{5,6},{6,5},{7,4},{8,11},{9,10},{10,... | collective-permute-start | bytes 663560 | tf_op jit(solution)/shard_map/cond/branch_1_fun/ppermute | solution.py:568
  271.5 45.1 %all-to-all-start.1 = ((bf16[8,64,768]{2,1,0:T(8,128)(2,1)}), bf16[8,64,768]{2,1,0:T(8,128)(2,1)S(1)}, u32[]{:S(2)}, u32[]{:S(2)}) async-start(bf16[8,64,768]{2,1,0:T(8,128)(2,1)} %bitcast.8), calls=%async_computation.1 | async-start | bytes 1572864 | tf_op jit(solution)/shard_map/cond/branch_1_fun/all_to_all | solution.py:535
  277.9 19.9 %collective-permute-start.7 = (bf16[320,768]{1,0:T(8,128)(2,1)S(1)}, bf16[320,768]{1,0:T(8,128)(2,1)S(1)}, u32[]{:S(2)}, u32[]{:S(2)}) collective-permute-start(bf16[320,768]{1,0:T(8,128)(2,1)S(1)} %dynamic-slice_bitcast_fusion.2), channel_id=1, source_target_pairs={{0,8},{4,12},{8,0},{12,4},{16,24},{20,28},{24,16},{28,20},{1,9},{5... | collective-permute-start | bytes 1474568 | tf_op jit(solution)/shard_map/cond/branch_1_fun/ppermute | solution.py:618
  292.4 17.7 %collective-permute-start.9 = (bf16[320,768]{1,0:T(8,128)(2,1)S(1)}, bf16[320,768]{1,0:T(8,128)(2,1)S(1)}, u32[]{:S(2)}, u32[]{:S(2)}) collective-permute-start(bf16[320,768]{1,0:T(8,128)(2,1)S(1)} %dynamic-slice_bitcast_fusion.1), channel_id=1, source_target_pairs={{0,16},{4,20},{8,24},{12,28},{16,0},{20,4},{24,8},{28,12},{1,17},{... | collective-permute-start | bytes 1474568 | tf_op jit(solution)/shard_map/cond/branch_1_fun/ppermute | solution.py:618
  298.0 12.3 %copy-start.3 = (bf16[320,768]{1,0:T(8,128)(2,1)}, bf16[320,768]{1,0:T(8,128)(2,1)S(1)}, u32[]{:S(2)}) copy-start(bf16[320,768]{1,0:T(8,128)(2,1)S(1)} %fusion.15) | copy-start | bytes 1474564 | tf_op jit(solution)/shard_map/cond
  298.0 18.6 %collective-permute-start.8 = (bf16[160,768]{1,0:T(8,128)(2,1)S(1)}, bf16[160,768]{1,0:T(8,128)(2,1)S(1)}, u32[]{:S(2)}, u32[]{:S(2)}) collective-permute-start(bf16[160,768]{1,0:T(8,128)(2,1)S(1)} %dynamic-slice_bitcast_fusion.4), channel_id=1, source_target_pairs={{0,16},{4,20},{8,24},{12,28},{16,0},{20,4},{24,8},{28,12},{1,17},{... | collective-permute-start | bytes 737288 | tf_op jit(solution)/shard_map/cond/branch_1_fun/ppermute | solution.py:618
  310.3 6.3 %collective-permute-start.10 = (bf16[160,768]{1,0:T(8,128)(2,1)S(1)}, bf16[160,768]{1,0:T(8,128)(2,1)S(1)}, u32[]{:S(2)}, u32[]{:S(2)}) collective-permute-start(bf16[160,768]{1,0:T(8,128)(2,1)S(1)} %dynamic-slice_bitcast_fusion.3), channel_id=1, source_target_pairs={{0,8},{4,12},{8,0},{12,4},{16,24},{20,28},{24,16},{28,20},{1,9},{5... | collective-permute-start | bytes 737288 | tf_op jit(solution)/shard_map/cond/branch_1_fun/ppermute | solution.py:618
  316.6 25.7 %copy-start.1 = (bf16[8,64,768]{2,1,0:T(8,128)(2,1)}, bf16[8,64,768]{2,1,0:T(8,128)(2,1)S(1)}, u32[]{:S(2)}) copy-start(bf16[8,64,768]{2,1,0:T(8,128)(2,1)S(1)} %all-to-all-done.1) | copy-start | bytes 2359300 | tf_op jit(solution)/shard_map/cond
  320.2 13.8 %collective-permute-start.11 = (bf16[2,40,768]{2,1,0:T(8,128)(2,1)S(1)}, bf16[2,40,768]{2,1,0:T(8,128)(2,1)S(1)}, u32[]{:S(2)}, u32[]{:S(2)}) collective-permute-start(bf16[2,40,768]{2,1,0:T(8,128)(2,1)S(1)} %pad_maximum_fusion.4), channel_id=1, source_target_pairs={{0,1},{1,0},{2,3},{3,2},{4,5},{5,4},{6,7},{7,6},{8,9},{9,8},{10,11... | collective-permute-start | bytes 368648 | tf_op jit(solution)/shard_map/cond/branch_1_fun/ppermute | solution.py:643
  324.9 17.4 %collective-permute-start.12 = (bf16[2,40,768]{2,1,0:T(8,128)(2,1)S(1)}, bf16[2,40,768]{2,1,0:T(8,128)(2,1)S(1)}, u32[]{:S(2)}, u32[]{:S(2)}) collective-permute-start(bf16[2,40,768]{2,1,0:T(8,128)(2,1)S(1)} %pad_maximum_fusion.5), channel_id=1, source_target_pairs={{0,2},{1,3},{2,0},{3,1},{4,6},{5,7},{6,4},{7,5},{8,10},{9,11},{10,... | collective-permute-start | bytes 368648 | tf_op jit(solution)/shard_map/cond/branch_1_fun/ppermute | solution.py:643
  325.5 16.8 %collective-permute-start.13 = (bf16[2,40,768]{2,1,0:T(8,128)(2,1)S(1)}, bf16[2,40,768]{2,1,0:T(8,128)(2,1)S(1)}, u32[]{:S(2)}, u32[]{:S(2)}) collective-permute-start(bf16[2,40,768]{2,1,0:T(8,128)(2,1)S(1)} %pad_maximum_fusion.6), channel_id=1, source_target_pairs={{0,3},{1,2},{2,1},{3,0},{4,7},{5,6},{6,5},{7,4},{8,11},{9,10},{10,... | collective-permute-start | bytes 368648 | tf_op jit(solution)/shard_map/cond/branch_1_fun/ppermute | solution.py:643
  342.3 6.0 %collective-permute-start.14 = (bf16[2,40,768]{2,1,0:T(8,128)(2,1)S(1)}, bf16[2,40,768]{2,1,0:T(8,128)(2,1)S(1)}, u32[]{:S(2)}, u32[]{:S(2)}) collective-permute-start(bf16[2,40,768]{2,1,0:T(8,128)(2,1)S(1)} %add_convert_fusion), channel_id=1, source_target_pairs={{0,1},{1,0},{2,3},{3,2},{4,5},{5,4},{6,7},{7,6},{8,9},{9,8},{10,11... | collective-permute-start | bytes 368648 | tf_op jit(solution)/shard_map/cond/branch_1_fun/ppermute | solution.py:650
  344.6 12.9 %collective-permute-start.15 = (bf16[2,40,768]{2,1,0:T(8,128)(2,1)S(1)}, bf16[2,40,768]{2,1,0:T(8,128)(2,1)S(1)}, u32[]{:S(2)}, u32[]{:S(2)}) collective-permute-start(bf16[2,40,768]{2,1,0:T(8,128)(2,1)S(1)} %add_convert_fusion), channel_id=1, source_target_pairs={{0,2},{1,3},{2,0},{3,1},{4,6},{5,7},{6,4},{7,5},{8,10},{9,11},{10,... | collective-permute-start | bytes 368648 | tf_op jit(solution)/shard_map/cond/branch_1_fun/ppermute | solution.py:650
  344.6 12.9 %collective-permute-start.16 = (bf16[2,40,768]{2,1,0:T(8,128)(2,1)S(1)}, bf16[2,40,768]{2,1,0:T(8,128)(2,1)S(1)}, u32[]{:S(2)}, u32[]{:S(2)}) collective-permute-start(bf16[2,40,768]{2,1,0:T(8,128)(2,1)S(1)} %add_convert_fusion), channel_id=1, source_target_pairs={{0,3},{1,2},{2,1},{3,0},{4,7},{5,6},{6,5},{7,4},{8,11},{9,10},{10,... | collective-permute-start | bytes 368648 | tf_op jit(solution)/shard_map/cond/branch_1_fun/ppermute | solution.py:650
  357.6 6.3 %collective-permute-start.19 = (bf16[4,40,768]{2,1,0:T(8,128)(2,1)S(1)}, bf16[4,40,768]{2,1,0:T(8,128)(2,1)S(1)}, u32[]{:S(2)}, u32[]{:S(2)}) collective-permute-start(bf16[4,40,768]{2,1,0:T(8,128)(2,1)S(1)} %pad_maximum_fusion.3), channel_id=1, source_target_pairs={{0,8},{4,12},{8,0},{12,4},{16,24},{20,28},{24,16},{28,20},{1,9},{5... | collective-permute-start | bytes 737288 | tf_op jit(solution)/shard_map/cond/branch_1_fun/ppermute | solution.py:657
  359.0 8.4 %collective-permute-start.17 = (bf16[4,40,768]{2,1,0:T(8,128)(2,1)S(1)}, bf16[4,40,768]{2,1,0:T(8,128)(2,1)S(1)}, u32[]{:S(2)}, u32[]{:S(2)}) collective-permute-start(bf16[4,40,768]{2,1,0:T(8,128)(2,1)S(1)} %pad_maximum_fusion.2), channel_id=1, source_target_pairs={{0,16},{4,20},{8,24},{12,28},{16,0},{20,4},{24,8},{28,12},{1,17},{... | collective-permute-start | bytes 737288 | tf_op jit(solution)/shard_map/cond/branch_1_fun/ppermute | solution.py:657
  363.9 15.6 %collective-permute-start.20 = (bf16[8,40,768]{2,1,0:T(8,128)(2,1)S(1)}, bf16[8,40,768]{2,1,0:T(8,128)(2,1)S(1)}, u32[]{:S(2)}, u32[]{:S(2)}) collective-permute-start(bf16[8,40,768]{2,1,0:T(8,128)(2,1)S(1)} %get-tuple-element.224), channel_id=1, source_target_pairs={{0,16},{4,20},{8,24},{12,28},{16,0},{20,4},{24,8},{28,12},{1,17},{... | collective-permute-start | bytes 1474568 | tf_op jit(solution)/shard_map/cond/branch_1_fun/ppermute | solution.py:657
  367.4 12.2 %collective-permute-start.18 = (bf16[8,40,768]{2,1,0:T(8,128)(2,1)S(1)}, bf16[8,40,768]{2,1,0:T(8,128)(2,1)S(1)}, u32[]{:S(2)}, u32[]{:S(2)}) collective-permute-start(bf16[8,40,768]{2,1,0:T(8,128)(2,1)S(1)} %get-tuple-element.226), channel_id=1, source_target_pairs={{0,8},{4,12},{8,0},{12,4},{16,24},{20,28},{24,16},{28,20},{1,9},{5... | collective-permute-start | bytes 1474568 | tf_op jit(solution)/shard_map/cond/branch_1_fun/ppermute | solution.py:657
  379.5 2.8 collective-permute-start.22
  379.7 12.1 %copy-start.2 = (bf16[8,64,768]{2,1,0:T(8,128)(2,1)S(1)}, bf16[8,64,768]{2,1,0:T(8,128)(2,1)}, u32[]{:S(2)}) copy-start(bf16[8,64,768]{2,1,0:T(8,128)(2,1)} %copy-done.1) | copy-start | bytes 2359300 | tf_op jit(solution)/shard_map/cond
  379.7 4.2 collective-permute-start.21
  392.0 35.3 %copy-start = (f32[768,768]{1,0:T(8,128)}, f32[768,768]{1,0:T(8,128)S(1)}, u32[]{:S(2)}) copy-start(f32[768,768]{1,0:T(8,128)S(1)} %get-tuple-element.341.after_ref) | copy-start | bytes 7077892
  392.1 35.3 %copy-start.18 = (f32[33,12]{0,1:T(8,128)}, f32[33,12]{0,1:T(8,128)S(1)}, u32[]{:S(2)}) copy-start(f32[33,12]{0,1:T(8,128)S(1)} %get-tuple-element.353) | copy-start | bytes 4756
  392.1 35.3 %copy-start.19 = (f32[65,12]{0,1:T(8,128)}, f32[65,12]{0,1:T(8,128)S(1)}, u32[]{:S(2)}) copy-start(f32[65,12]{0,1:T(8,128)S(1)} %get-tuple-element.354) | copy-start | bytes 9364
  392.1 35.3 %copy-start.20 = (f32[65,12]{0,1:T(8,128)}, f32[65,12]{0,1:T(8,128)S(1)}, u32[]{:S(2)}) copy-start(f32[65,12]{0,1:T(8,128)S(1)} %get-tuple-element.355) | copy-start | bytes 9364
  392.1 35.3 %copy-start.29 = (f32[768]{0:T(1024)}, f32[768]{0:T(1024)S(1)}, u32[]{:S(2)}) copy-start(f32[768]{0:T(1024)S(1)} %get-tuple-element.339) | copy-start | bytes 9220
  392.1 35.3 %copy-start.30 = (f32[768]{0:T(1024)}, f32[768]{0:T(1024)S(1)}, u32[]{:S(2)}) copy-start(f32[768]{0:T(1024)S(1)} %get-tuple-element.342) | copy-start | bytes 9220
  (22 other events, 92.2 us)
Sparse Core Ops, SparseCore 0:
  153.6 258.2 all-reduce.10

commit v5 on v4

--- a/solution.py
+++ b/solution.py
@@ -155,10 +155,20 @@
     )(*pieces, q_weight, k_weight, v_weight, bias, hot, mask, hot_t, line, width, height)
 
 
+def by_distance(sums, turn):
+    if sums.shape[0] == sums.shape[1]:
+        sums = jnp.concatenate([sums, jnp.zeros_like(sums)], axis=1)
+    sums = pltpu.roll(sums, turn, 1, stride=1, stride_axis=0)
+    sums = jnp.sum(sums, axis=0, keepdims=True)
+    if sums.shape[1] < 256:
+        sums = jnp.concatenate([sums, jnp.zeros_like(sums)], axis=1)
+    return sums
+
+
 def attend_back_kernel(held, *refs):
     (
         exp_ref, ctxt_ref, inv_ref, v_ref, kt_ref, q_ref, dattn_ref, outw_ref, hot_ref, hott_ref,
-        dqkv_ref, gwidth_ref, gheight_ref, gline_ref, values, dctx, lefts, rights, ds, dattn,
+        dqkv_ref, spread_ref, values, dctx, lefts, rights, ds, dattn,
     ) = refs[:10] + refs[10 + held :]
     seq = v_ref.shape[0]
     lanes = q_ref.shape[0]
@@ -197,11 +207,15 @@
         ds[h] = (exp_ref[h].astype(F32) * d_scores).astype(BF)
         by_query = mm(lefts[h], ds[h])
         by_queries.append(by_query[0:64] * 0.125)
-        gwidth_ref[h] = mm(by_query[64:192].astype(BF), hot_ref[:, 64:192])
         by_key = mm(ds[h], rights[h])
+        width = mm(by_query[64:192].astype(BF), hot_ref[:, 64:192])
+        height = mm(hott_ref[192:320, 0:seq], by_key[:, 128:256].astype(BF))
         near = mm(hott_ref[0:64, 0:seq], by_key[:, 0:128].astype(BF))
-        gline_ref[h] = near[:, 64:128] if h == 0 else near[:, 0:64]
-        gheight_ref[h] = mm(hott_ref[192:320, 0:seq], by_key[:, 128:256].astype(BF))
+        spread_ref[h, 0:1, :] = by_distance(width, 0)
+        spread_ref[h, 1:2, :] = by_distance(height, 0)
+        line_lane = lax.broadcasted_iota(jnp.int32, near.shape, 1)
+        near = jnp.where((line_lane >= 64) if h == 0 else (line_lane < 64), near, 0.0)
+        spread_ref[h, 2:3, :] = by_distance(near, 64 if h == 0 else 0)
         results.append((by_key[:, 0:128], mm(exp_ref[h], d_rows)))
     dqkv_ref[0] = jnp.concatenate(by_queries, axis=0).T[0:seq].astype(BF)
     dqkv_ref[1] = jnp.where(lane < 64, results[0][0], results[1][0]).astype(BF)
@@ -243,15 +257,11 @@
         + [pl.BlockSpec(memory_space=pl.ANY)] * len(held),
         out_specs=[
             pl.BlockSpec((3, seq, 128), lambda p: (0, 0, p)),
-            pair(128, 128, start=0),
-            pair(128, 128, start=0),
-            pair(64, 64, start=0),
+            pair(3, 256, start=0),
         ],
         out_shape=[
             shape((3, seq, 128 * pairs), BF),
-            shape((2 * pairs, 128, 128), F32),
-            shape((2 * pairs, 128, 128), F32),
-            shape((2 * pairs, 64, 64), F32),
+            shape((2 * pairs, 3, 256), F32),
         ],
         scratch_shapes=[
             pltpu.VMEM((2, seq, 128), BF),
@@ -370,7 +380,7 @@
         out_ref[...] = mm(ctxt_ref[:, 0:seq], d_attns[...]).astype(BF)
 
 
-def rows_pass(room, pieces, x, ctx, ctx_t, out_w, up_w, down_w, bias, up_b):
+def rows_pass(pieces, x, ctx, ctx_t, out_w, up_w, down_w, bias, up_b):
     seq, dim = ctx.shape
     ff = up_w.shape[1]
     blocks = 4
@@ -409,7 +419,7 @@
             shape((seq, dim), BF),
             shape((dim, ff), BF),
             shape((ff, dim), BF),
-            shape((dim + room, dim), BF),
+            shape((dim, dim), BF),
             shape((8, dim), F32),
             shape((1, ff), F32),
         ],
@@ -430,58 +440,85 @@
     )(*pieces, x, ctx, ctx_t, out_w, up_w, down_w, bias, up_b)
 
 
-def last_kernel(count, held, *refs):
-    parts = refs[:count]
-    x_ref, weight_ref, dmid_ref = refs[count : count + 3]
-    grad_ref, drows_ref, sums_ref, x_t, total = refs[count + 3 + held :]
+def qkv_kernel(held, x_ref, dqkv_ref, out_ref, *refs):
+    grad_ref, sums_ref, x_t = refs[held:]
     step = pl.program_id(0)
-    d_qkv = jnp.concatenate([part[0] for part in parts], axis=1)
 
     @pl.when(step == 0)
     def _():
         x_t[...] = x_ref[...].astype(F32).T.astype(BF)
-        total[...] = dmid_ref[...]
-
-    grad_ref[...] = mm(x_t[...], d_qkv).astype(BF)
-    total[...] += against(d_qkv, weight_ref[0])
-    sums_ref[0] = jnp.broadcast_to(
-        jnp.sum(d_qkv.astype(F32), axis=0, keepdims=True), sums_ref.shape[1:]
-    )
-
-    @pl.when(step == 2)
-    def _():
-        drows_ref[...] = total[...].astype(BF)
-
-
-def last_products(rows, held, x, d_qkv, weights, d_mid):
-    seq, dim = d_mid.shape
+
+    @pl.when(step < 3)
+    def _():
+        grad_ref[...] = mm(x_t[...], dqkv_ref[0]).astype(BF)
+        sums_ref[0] = jnp.broadcast_to(total(dqkv_ref[0].astype(F32)), sums_ref.shape[1:])
+
+    @pl.when(step == 3)
+    def _():
+        grad_ref[...] = out_ref[...]
+
+
+def qkv_sums(room, held, x, d_qkv, out_low):
+    _, seq, dim = d_qkv.shape
 
     def whole(a):
         return pl.BlockSpec(a.shape, lambda p: (0,) * a.ndim, pipeline_mode=pl.Buffered(1))
 
     shape = jax.ShapeDtypeStruct
     return pl.pallas_call(
-        partial(last_kernel, len(d_qkv), len(held)),
-        grid=(3,),
-        in_specs=[pl.BlockSpec((1,) + a.shape[1:], lambda p: (p, 0, 0)) for a in d_qkv]
-        + [
+        partial(qkv_kernel, len(held)),
+        grid=(4,),
+        in_specs=[
             whole(x),
-            pl.BlockSpec((1, dim, dim), lambda p: (p, 0, 0)),
-            whole(d_mid),
+            pl.BlockSpec((1, seq, dim), lambda p: (jnp.minimum(p, 2), 0, 0)),
+            whole(out_low),
         ]
         + [pl.BlockSpec(memory_space=pl.ANY)] * len(held),
         out_specs=[
             pl.BlockSpec((dim, dim), lambda p: (p, 0)),
-            pl.BlockSpec((seq, dim), lambda p: (0, 0)),
-            pl.BlockSpec((1, 8, dim), lambda p: (p, 0, 0)),
-        ],
-        out_shape=[shape((rows, dim), BF), shape((seq, dim), BF), shape((3, 8, dim), F32)],
-        scratch_shapes=[pltpu.VMEM((dim, seq), BF), pltpu.VMEM((seq, dim), F32)],
+            pl.BlockSpec((1, 8, dim), lambda p: (jnp.minimum(p, 2), 0, 0)),
+        ],
+        out_shape=[shape((4 * dim + room, dim), BF), shape((3, 8, dim), F32)],
+        scratch_shapes=[pltpu.VMEM((dim, seq), BF)],
         compiler_params=pltpu.CompilerParams(vmem_limit_bytes=VMEM_BYTES),
         cost_estimate=pl.CostEstimate(
-            flops=12 * seq * dim * dim, bytes_accessed=32 * seq * dim, transcendentals=0
+            flops=8 * seq * dim * dim, bytes_accessed=24 * seq * dim, transcendentals=0
         ),
-    )(*d_qkv, x, weights, d_mid, *held)
+    )(x, d_qkv, out_low, *held)
+
+
+def rows_grad_kernel(dqkv_ref, weight_ref, dmid_ref, drows_ref, sum_ref):
+    step = pl.program_id(0)
+
+    @pl.when(step == 0)
+    def _():
+        sum_ref[...] = dmid_ref[...]
+
+    sum_ref[...] += against(dqkv_ref[0], weight_ref[0])
+
+    @pl.when(step == 2)
+    def _():
+        drows_ref[...] = sum_ref[...].astype(BF)
+
+
+def rows_grad(d_qkv, weights, d_mid):
+    _, seq, dim = d_qkv.shape
+    return pl.pallas_call(
+        rows_grad_kernel,
+        grid=(3,),
+        in_specs=[
+            pl.BlockSpec((1, seq, dim), lambda p: (p, 0, 0)),
+            pl.BlockSpec((1, dim, dim), lambda p: (p, 0, 0)),
+            pl.BlockSpec((seq, dim), lambda p: (0, 0), pipeline_mode=pl.Buffered(1)),
+        ],
+        out_specs=pl.BlockSpec((seq, dim), lambda p: (0, 0)),
+        out_shape=jax.ShapeDtypeStruct((seq, dim), BF),
+        scratch_shapes=[pltpu.VMEM((seq, dim), F32)],
+        compiler_params=pltpu.CompilerParams(vmem_limit_bytes=VMEM_BYTES),
+        cost_estimate=pl.CostEstimate(
+            flops=6 * seq * dim * dim, bytes_accessed=16 * seq * dim, transcendentals=0
+        ),
+    )(d_qkv, weights, d_mid)
 
 
 def bucket_select(table):
@@ -502,20 +539,17 @@
     return spread.astype(BF).reshape(HEADS, span, span)
 
 
-def gather_table(parts, table):
-    select = bucket_select(table).astype(F32).reshape(table.shape[0], -1)
-    return jnp.concatenate(
-        [
-            lax.dot_general(
-                select,
-                grads.reshape(grads.shape[0], -1),
-                (((1,), (1,)), ((), ())),
-                precision=lax.Precision.HIGHEST,
-                preferred_element_type=F32,
-            )
-            for grads in parts
-        ],
-        axis=1,
+def gather_table(spread, table):
+    reach = (table.shape[0] - 1) // 2
+    distance = jnp.arange(spread.shape[1], dtype=jnp.int32) - (4 * reach - 1)
+    bucket = jnp.clip(distance, -reach, reach) + reach
+    select = bucket[None, :] == jnp.arange(table.shape[0], dtype=jnp.int32)[:, None]
+    return lax.dot_general(
+        select.astype(F32),
+        spread,
+        (((1,), (1,)), ((), ())),
+        precision=lax.Precision.HIGHEST,
+        preferred_element_type=F32,
     )
 
 
@@ -562,12 +596,14 @@
 
 
 def patch_away(rows, size):
-    me = lax.axis_index("narrow")
     parts = rows.reshape(size, -1, rows.shape[1])
-    arrived = [parts[0]] + [
+    return [parts[0]] + [
         lax.ppermute(parts[k], "narrow", flip_pairs(size, k)) for k in range(1, size)
     ]
-    return from_flipped(jnp.stack(arrived), me)
+
+
+def patch_set(pieces, shape):
+    return from_flipped(jnp.stack(pieces), lax.axis_index("narrow")).reshape(shape)
 
 
 def add(*terms):
@@ -619,9 +655,9 @@
     return add_own(parts, me, arrived, held) if held else add(pick(parts, me), arrived)
 
 
-def cut(grad, ways):
-    part = grad.shape[0] // ways
-    return [grad[i * part : (i + 1) * part] for i in range(ways)]
+def cut(grad, parts):
+    first = -(-grad.shape[0] // (16 * parts)) * 8 * parts
+    return [grad[:first], grad[first:]]
 
 
 def wide_steps(shares, wide, i, held=()):
@@ -637,7 +673,7 @@
     parts = [a.reshape(narrow, -1, a.shape[1]) for a in shares]
 
     def picked(index):
-        return jnp.stack([pick(a, index) for a in parts])
+        return jnp.concatenate([pick(a, index) for a in parts], axis=0)
 
     arrived = [
         lax.ppermute(picked(me ^ k), "narrow", flip_pairs(narrow, k)) for k in range(1, narrow)
@@ -645,11 +681,12 @@
     return add(picked(me), *arrived)
 
 
-def gather_narrow(part, narrow):
+def gather_narrow(part, narrow, lengths):
     parts = [part] + [
         lax.ppermute(part, "narrow", flip_pairs(narrow, k)) for k in range(1, narrow)
     ]
-    return [jnp.stack([p[n] for p in parts]) for n in range(part.shape[0])]
+    parts = jnp.stack(parts)
+    return [parts[:, : lengths[0]], parts[:, lengths[0] :]]
 
 
 def gather_wide(shares, wide, i):
@@ -663,24 +700,20 @@
     return shares + [lax.ppermute(a, "wide", flip_pairs(wide, 1)) for a in shares]
 
 
-def convert_kernel(up_ref, down_ref, out_ref, after_ref, up_out, down_out, out_out):
+def convert_kernel(up_ref, down_ref, after_ref, up_out, down_out):
     step = pl.program_id(0)
-    parts = (pl.num_programs(0) - 1) // 2
+    parts = pl.num_programs(0) // 2
 
     @pl.when(step < parts)
     def _():
         up_out[...] = up_ref[...].astype(F32)
 
-    @pl.when((step >= parts) & (step < 2 * parts))
+    @pl.when(step >= parts)
     def _():
         down_out[...] = down_ref[...].astype(F32)
 
-    @pl.when(step == 2 * parts)
-    def _():
-        out_out[...] = out_ref[...].astype(F32)
-
-
-def convert(up_total, down_total, out_total, after):
+
+def convert(up_total, down_total, after):
     dim, ff = up_total.shape
     parts = ff // dim
 
@@ -688,37 +721,35 @@
         return pl.BlockSpec((dim, dim), index)
 
     up_block = block(lambda p: (0, jnp.minimum(p, parts - 1)))
-    down_block = block(lambda p: (jnp.clip(p - parts, 0, parts - 1), 0))
-    out_block = block(lambda p: (0, 0))
+    down_block = block(lambda p: (jnp.maximum(p - parts, 0), 0))
     shape = jax.ShapeDtypeStruct
     return pl.pallas_call(
         convert_kernel,
-        grid=(2 * parts + 1,),
-        in_specs=[up_block, down_block, out_block, pl.BlockSpec(memory_space=pl.ANY)],
-        out_specs=[up_block, down_block, out_block],
-        out_shape=[shape((dim, ff), F32), shape((ff, dim), F32), shape((dim, dim), F32)],
+        grid=(2 * parts,),
+        in_specs=[up_block, down_block, pl.BlockSpec(memory_space=pl.ANY)],
+        out_specs=[up_block, down_block],
+        out_shape=[shape((dim, ff), F32), shape((ff, dim), F32)],
         compiler_params=pltpu.CompilerParams(vmem_limit_bytes=VMEM_BYTES),
-        cost_estimate=pl.CostEstimate(flops=0, bytes_accessed=13 * dim * ff, transcendentals=0),
-    )(up_total, down_total, out_total, after)
+        cost_estimate=pl.CostEstimate(flops=0, bytes_accessed=12 * dim * ff, transcendentals=0),
+    )(up_total, down_total, after)
 
 
 def finish_kernel(places, ways, cuts, index_ref, *refs):
     pieces, outs = refs[: 2 * ways], refs[2 * ways :]
-    rows = pieces[0].shape[1]
+    at = 0
     for core in range(2):
         for way in range(ways):
+            rows = pieces[way].shape[1]
             for place in range(places):
-                at = ((core * ways + way) * places + place) * rows
-                if at >= cuts[-1][1]:
-                    continue
                 here = index_ref[way, place]
-                same = pieces[way][here].astype(F32)
-                other = pieces[ways + way][here].astype(F32)
-                block = jnp.where(index_ref[2, 0] == core, same, other)
                 for (start, stop), out in zip(cuts, outs):
                     low, high = max(at, start), min(at + rows, stop)
                     if low < high:
+                        same = pieces[way][here].astype(F32)
+                        other = pieces[ways + way][here].astype(F32)
+                        block = jnp.where(index_ref[2, 0] == core, same, other)
                         out[low - start : high - start, :] = block[low - at : high - at]
+                at += rows
 
 
 def finish(pieces, wide, narrow, lengths):
@@ -750,7 +781,7 @@
 
 
 def room_for(rows, wide, narrow):
-    return 16 + -(rows + 16) % (8 * wide * narrow)
+    return 32 + -(rows + 32) % (8 * wide * narrow)
 
 
 def pack(grads, columns, rows):
@@ -838,13 +869,16 @@
     height = spread_table(height_table)
     hots = []
     hots_t = []
+    hots_back = []
     for spots, table in ((line_spots, line_table), (x_spots, width_table), (y_spots, height_table)):
         span = jnp.arange(2 * (table.shape[0] - 1), dtype=jnp.int32)
         long = jnp.pad(spots, (0, lanes - seq), constant_values=-1)
         hots.append((long[:, None] == span[None, :]).astype(BF))
         hots_t.append((long[None, :] == span[:, None]).astype(BF))
+        hots_back.append((long[None, :] == span[::-1, None]).astype(BF))
     hot = jnp.concatenate(hots, axis=1)
     hot_t = jnp.concatenate(hots_t, axis=0)
+    hot_back = jnp.concatenate(hots_back, axis=0)
     column = jnp.arange(128, dtype=jnp.int32)
     mask = jnp.where((column[None, :] % 64 == 0) & ~valid[:, None], -1e30, 0.0).astype(BF)
 
@@ -864,47 +898,46 @@
     vectors = jnp.stack(
         [output_bias, norm_gain, norm_shift, down_bias, final_gain, final_shift] + [final_shift] * 2
     )
-    room = 16
     final_low, d_mid, d_attn, up_low, down_low, out_low, sums, up_sum = rows_pass(
-        room, cots, rows_in, ctx, ctx_t, output_weight, up_weight, down_weight, vectors, up_bias[None]
+        cots, rows_in, ctx, ctx_t, output_weight, up_weight, down_weight, vectors, up_bias[None]
     )
     early = (sums[0], sums[1], sums[2], up_sum, sums[3], sums[4], sums[5])
-    out_low = lax.dynamic_update_slice(out_low, pack(early, dim, room).astype(BF), (dim, 0))
-    down_total, up_total, out_total = lax.psum((down_low, up_low, out_low), ("wide", "narrow"))
+    down_total, up_total = lax.psum((down_low, up_low), ("wide", "narrow"))
     qkv_weight = jnp.stack([query_weight, key_weight, value_weight])
 
     def backward():
         text_out = swap_text(final_low[:TEXT].reshape(wide, -1, dim)).reshape(text_shape)
-        patch_out = patch_away(final_low[TEXT:], narrow).reshape(patch_shape)
+        out_pieces = patch_away(final_low[TEXT:], narrow)
         levels = wide.bit_length() - 2
-        d_qkv, g_width, g_height, g_line = attend_back(
-            0, HEADS // 2, [], exps, ctx_t, inverse, v, k_t, q, d_attn, output_weight, hot, hot_t
+        d_qkv, spread = attend_back(
+            0, HEADS // 2, [], exps, ctx_t, inverse, v, k_t, q, d_attn, output_weight, hot, hot_back
         )
-        late_room = room_for(3 * dim, wide, narrow)
-        tail, d_rows, qkv_sums = last_products(
-            3 * dim + late_room, [text_out, patch_out], rows_in, [d_qkv], qkv_weight, d_mid
+        room = room_for(4 * dim, wide, narrow)
+        tail, d_sums = qkv_sums(room, [text_out, *out_pieces[1:]], rows_in, d_qkv, out_low)
+        d_rows = rows_grad(d_qkv, qkv_weight, d_mid)
+        text_grad = swap_text(d_rows[:TEXT].reshape(wide, -1, dim)).reshape(text_shape)
+        grad_pieces = patch_away(d_rows[TEXT:], narrow)
+        late = (
+            d_sums[0, 0],
+            d_sums[2, 0],
+            gather_table(spread[:, 2], line_table),
+            gather_table(spread[:, 0], width_table),
+            gather_table(spread[:, 1], height_table),
         )
-        text_grad = swap_text(d_rows[:TEXT].reshape(wide, -1, dim)).reshape(text_shape)
-        patch_grad = patch_away(d_rows[TEXT:], narrow).reshape(patch_shape)
-        late = (
-            qkv_sums[0, 0],
-            qkv_sums[2, 0],
-            gather_table([g_line], line_table),
-            gather_table([g_width], width_table),
-            gather_table([g_height], height_table),
-        )
-        small = pack(late, dim, late_room).astype(BF)
-        tail = lax.dynamic_update_slice(tail, small, (3 * dim, 0))
-        halves = cut(wide_step(tail, wide, 0), 2)
+        small = pack(early + late, dim, room).astype(BF)
+        tail = lax.dynamic_update_slice(tail, small, (4 * dim, 0))
+        halves = cut(wide_step(tail, wide, 0), wide * narrow // 2)
         for i in range(levels):
-            moved = [text_grad, patch_grad] if i == levels - 1 else []
+            moved = [text_grad, *grad_pieces[1:]] if i == levels - 1 else []
             halves = wide_steps(halves, wide, i, moved)
-        halves = gather_narrow(narrow_step(halves, narrow), narrow)
+        lengths = [a.shape[0] // narrow for a in halves]
+        halves = gather_narrow(narrow_step(halves, narrow), narrow, lengths)
         for i in range(levels - 1, -1, -1):
             halves = gather_wide(halves, wide, i)
-        *large, late_small = finish(gather_core(halves, wide), wide, narrow, (dim,) * 3 + (16,))
+        *large, small = finish(gather_core(halves, wide), wide, narrow, (dim,) * 4 + (32,))
         return (
-            text_out, patch_out, text_grad, patch_grad, *large, *unpack(late_small, late),
+            text_out, patch_set(out_pieces, patch_shape), text_grad,
+            patch_set(grad_pieces, patch_shape), *large, *unpack(small, early + late),
         )
 
     def never():
@@ -912,21 +945,11 @@
 
     (
         text_out, patch_out, text_grad, patch_grad, query_weight_grad, key_weight_grad,
-        value_weight_grad, query_bias_grad, value_bias_grad, line_table_grad, width_table_grad,
-        height_table_grad,
+        value_weight_grad, output_weight_grad, output_bias_grad, norm_gain_grad, norm_shift_grad,
+        up_bias_grad, down_bias_grad, final_gain_grad, final_shift_grad, query_bias_grad,
+        value_bias_grad, line_table_grad, width_table_grad, height_table_grad,
     ) = lax.cond(text_len.reshape(()) >= 0, backward, never)
-    up_weight_grad, down_weight_grad, output_weight_grad = convert(
-        up_total, down_total, out_total, value_weight_grad
-    )
-    (
-        output_bias_grad,
-        norm_gain_grad,
-        norm_shift_grad,
-        up_bias_grad,
-        down_bias_grad,
-        final_gain_grad,
-        final_shift_grad,
-    ) = unpack(out_total[dim:].astype(F32), early)
+    up_weight_grad, down_weight_grad = convert(up_total, down_total, value_weight_grad)
     up_bias_grad = up_bias_grad.reshape(-1)
     return (
         text_out,

time: 443 us -> 427 us (0.964)
  waiting for transfers between devices: 94.3 us -> 77.6 us
  matrix products: 10.4 us -> 2.44 us
  local copies, waits for them, and re-layouts: 30 us -> 34.7 us
    psum x1, waiting for transfers between devices: 19.8 us -> 0.02 us  [body(): down_total, up_total = lax.psum((down_low, up_low), ('wide', 'narrow'))]
    ppermute x3, waiting for transfers between devices: 10.4 us -> 18.8 us  [gather_narrow(): lax.ppermute(part, 'narrow', flip_pairs(narrow, k))]
    ppermute x5, waiting for transfers between devices: 18.3 us -> 10.1 us  [wide_step(): lax.ppermute(pick(parts, 1 - me), 'wide', flip_pairs(wide, 1 << bit))]
    dot_general x3, matrix products: 8.29 us -> 0.37 us  [gather_table(): lax.dot_general(select.astype(F32), spread, (((1,), (1,)), ((), ())), pre...]
    concatenate x0 -> x8, other arithmetic: none -> 5.91 us  [the longest x4 4.95 us: gather_wide(): jnp.concatenate([a, lax.ppermute(a, 'wide', flip_pairs(wide, 1 << order[i...]
    ppermute x4, waiting for transfers between devices: 17 us -> 22.7 us  [gather_wide(): lax.ppermute(a, 'wide', flip_pairs(wide, 1 << order[i]))]
    pallas_call x2 -> x3, Pallas kernels: 29.7 us -> 31.5 us  [the longest x1 12.8 us: convert(): pl.pallas_call(convert_kernel, grid=(2 * parts,), in_specs=[up_block, dow...]
  transfers between devices with their start and end apart: 34 -> 34, of which waited for: 15 -> 10; matrix products, arithmetic and copies ran while one was open for 11% -> 13% of each run, Pallas kernels for 30% -> 32%
where the time goes in v5:
time: 427 us; the launch traced here: 421 us
  Pallas kernels  206 us (48%)
  waiting for transfers between devices  77.6 us (18%)
  starting transfers between devices  58.3 us (14%)
  local copies, waits for them, and re-layouts  34.7 us (8%)
  other arithmetic  24.7 us (6%)
  between operations  16.3 us (4%)
    pallas_call x1, Pallas kernels, attend_back(): pl.pallas_call(partial(attend_back_kernel, len(held)), grid=(pairs,), in_...  60.6 us
    pallas_call x1, Pallas kernels, rows_pass(): pl.pallas_call(partial(rows_kernel, len(pieces), blocks), grid=(blocks +...  59.7 us
    pallas_call x1, Pallas kernels, attend(): pl.pallas_call(partial(attend_kernel, len(pieces)), grid=(HEADS // 2,), i...  46.4 us
    ppermute x4, waiting for transfers between devices, gather_wide(): lax.ppermute(a, 'wide', flip_pairs(wide, 1 << order[i]))  22.7 us
    ppermute x3, waiting for transfers between devices, gather_narrow(): lax.ppermute(part, 'narrow', flip_pairs(narrow, k))  18.8 us
    all_to_all x4, starting transfers between devices, swap_text(): lax.all_to_all(parts, 'wide', split_axis=0, concat_axis=0, tiled=True)  17.3 us
    ppermute x3, waiting for transfers between devices, narrow_step(): lax.ppermute(picked(me ^ k), 'narrow', flip_pairs(narrow, k))  15.6 us
    pallas_call x1, Pallas kernels, convert(): pl.pallas_call(convert_kernel, grid=(2 * parts,), in_specs=[up_block, dow...  12.8 us
  transfers between devices with their start and end apart: 34, of which 10 were waited for; matrix products, arithmetic and copies ran while one was open for 13% of the time, Pallas kernels for 32%

profile of v5, /device:TPU:0, one launch (start us, length us, event | category | flops | bytes accessed | tf_op | source)
XLA Modules:
  0.0 420.6 jit_solution(16383225447861408821)
XLA Ops:
  7.3 5.3 %all-to-all-start.2 = ((bf16[8,64,768]{2,1,0:T(8,128)(2,1)}), bf16[8,64,768]{2,1,0:T(8,128)(2,1)S(1)}, u32[]{:S(2)}, u32[]{:S(2)}) async-start(bf16[8,64,768]{2,1,0:T(8,128)(2,1)} %bitcast.157), calls=%async_computation.2 | async-start | bytes 1572864 | tf_op jit(solution)/shard_map/all_to_all | solution.py:569
  12.6 2.1 dynamic-slice_bitcast_fusion.17
  14.8 3.6 collective-permute-start.25
  31.2 4.2 %all-to-all-start.3 = ((bf16[8,64,768]{2,1,0:T(8,128)(2,1)}), bf16[8,64,768]{2,1,0:T(8,128)(2,1)}, u32[]{:S(2)}, u32[]{:S(2)}) async-start(bf16[8,64,768]{2,1,0:T(8,128)(2,1)} %bitcast.50), calls=%async_computation.3 | async-start | bytes 1572864 | tf_op jit(solution)/shard_map/all_to_all | solution.py:569
  35.7 2.4 collective-permute-done.24.refs_3_
  38.9 2.5 collective-permute-start.28
  41.4 1.9 collective-permute-start.26
  43.3 46.4 %shard_map.426 = (bf16[12,1088,1152]{2,1,0:T(8,128)(2,1)}, bf16[768,1152]{1,0:T(8,128)(2,1)}, bf16[1088,768]{1,0:T(8,128)(2,1)}, f32[12,1,1152]{2,1,0:T(1,128)S(...) custom-call(bf16[512,768]{1,0:T(8,128)(2,1)} %bitcast.158, ...), custom_call_target="tpu_custom_call" | custom-call | flops 61605937152 | bytes 30081024 | tf_op jit(solution)/shard_map/pallas_call | solution.py:108
  90.5 59.7 %shard_map.427 = (bf16[1088,768]{1,0:T(8,128)(2,1)}, f32[1088,768]{1,0:T(8,128)}, bf16[1088,768]{1,0:T(8,128)(2,1)}, bf16[768,3072]{1,0:T(8,128)(2,1)}, bf16[307...) custom-call(bf16[512,768]{1,0:T(8,128)(2,1)} %bitcast.51.refs_0_, ...), custom_call_target="tpu_custom_call" | custom-call | flops 35936796672 | bytes 53477376 | tf_op jit(solution)/shard_map/pallas_call | solution.py:400
  151.8 3.2 pad_maximum_fusion.11
  155.9 241.6 %conditional.1 = (bf16[8,1,64,768]{3,2,1,0:T(8,128)(2,1)}, bf16[1,4,144,768]{3,2,1,0:T(8,128)(2,1)}, bf16[8,1,64,768]{3,2,1,0:T(8,128)(2,1)S(1)}, bf16[1,4,144,7...) conditional(s32[]{:T(128)} %convert_element_type.129, () %tuple.20, ...), branch_computations={%region_0.1_spmd, %region_1.2_spmd} | conditional | flops 70616072192 | bytes 232809920 | solution.py:951
  155.9 2.4 slice.131
  158.4 4.2 %all-to-all-start = ((bf16[8,64,768]{2,1,0:T(8,128)(2,1)}), bf16[8,64,768]{2,1,0:T(8,128)(2,1)}, u32[]{:S(2)}, u32[]{:S(2)}) async-start(bf16[8,64,768]{2,1,0:T(8,128)(2,1)} %bitcast), calls=%async_computation | async-start | bytes 1572864 | tf_op jit(solution)/shard_map/cond/branch_1_fun/all_to_all | solution.py:569
  163.4 2.3 collective-permute-start.2
  165.8 2.1 collective-permute-start
  167.9 60.6 %branch_1_fun.5 = (bf16[3,1088,768]{2,1,0:T(8,128)(2,1)}, f32[12,3,256]{2,1,0:T(4,128)}) custom-call(bf16[12,1088,1152]{2,1,0:T(8,128)(2,1)} %get-tuple-element.53.refs_0_, bf16[768,1152]{1,0:T(8,128)(2,1)} %get-tuple-element.54.refs_1_, f32[12,1,1152]{2,1,0:T(1,128)S(1)} %get-tuple-element.55.refs_2_, bf16[1088,768]{1,0:T(8,128)(2,1)} %get-tuple-element.56.refs_3_, ...), custom_call_target="tpu_custom_call" | custom-call | flops 61605937152 | bytes 30081024 | tf_op jit(solution)/shard_map/cond/branch_1_fun/pallas_call | solution.py:242
  231.6 9.5 %branch_1_fun.7 = (bf16[3328,768]{1,0:T(8,128)(2,1)}, f32[3,8,768]{2,1,0:T(8,128)}) custom-call(bf16[1088,768]{1,0:T(8,128)(2,1)} %get-tuple-element.66.x_ref, bf16[3,1088,768]{2,1,0:T(8,128)(2,1)} %get-tuple-element.63.dqkv_ref, bf16[768,768]{1,0:T(8,128)(2,1)S(1)} %copy-done.50, bf16[8,1,64,768]{3,2,1,0:T(8,128)(2,1)} %bitcast.1.refs_0_, ...), custom_call_target="tpu_custom_call" | custom-call | flops 5133828096 | bytes 20054016 | tf_op jit(solution)/shard_map/cond/branch_1_fun/pallas_call | solution.py:468
  243.0 3.4 dynamic-slice_bitcast_fusion
  246.5 5.0 %collective-permute-done.6 = bf16[1664,768]{1,0:T(8,128)(2,1)S(1)} collective-permute-done((bf16[1664,768]{1,0:T(8,128)(2,1)}, bf16[1664,768]{1,0:T(8,128)(2,1)S(1)}, u32[]{:S(2)}, u32[]{:S(2)}) %collective-permute-start.6) | collective-permute-done | bytes 2555936 | tf_op jit(solution)/shard_map/cond/branch_1_fun/ppermute | solution.py:654
  251.5 2.4 fusion
  255.1 1.9 collective-permute-start.9
  257.1 1.5 collective-permute-start.7
  258.6 9.2 %branch_1_fun.6 = bf16[1088,768]{1,0:T(8,128)(2,1)} custom-call(bf16[3,1088,768]{2,1,0:T(8,128)(2,1)} %get-tuple-element.63.dqkv_ref, bf16[3,768,768]{2,1,0:T(8,128)(2,1)} %get-tuple-element.64.weight_ref, f32[1088,768]{1,0:T(8,128)} %get-tuple-element.65.dmid_ref), custom_call_target="tpu_custom_call" | custom-call | flops 3850371072 | bytes 13369344 | tf_op jit(solution)/shard_map/cond/branch_1_fun/pallas_call | solution.py:506
  267.8 2.1 slice.188
  269.9 3.5 all-to-all-start.1
  273.4 2.2 slice_bitcast_fusion
  275.6 2.2 collective-permute-start.5
  277.9 2.1 collective-permute-start.3
  281.4 2.0 collective-permute-start.10
  284.8 1.6 collective-permute-start.8
  286.3 5.1 %collective-permute-done.10 = bf16[192,768]{1,0:T(8,128)(2,1)S(1)} collective-permute-done((bf16[192,768]{1,0:T(8,128)(2,1)S(1)}, bf16[192,768]{1,0:T(8,128)(2,1)S(1)}, u32[]{:S(2)}, u32[]{:S(2)}) %collective-permute-start.10) | collective-permute-done | bytes 294944 | tf_op jit(solution)/shard_map/cond/branch_1_fun/ppermute | solution.py:654
  291.5 7.8 %collective-permute-done.4.refs_2_ = bf16[144,768]{1,0:T(8,128)(2,1)} collective-permute-done((bf16[144,768]{1,0:T(8,128)(2,1)}, bf16[144,768]{1,0:T(8,128)(2,1)}, u32[]{:S(2)}, u32[]{:S(2)}) %collective-permute-start.4) | collective-permute-done | bytes 221216 | tf_op jit(solution)/shard_map/cond/branch_1_fun/ppermute | solution.py:601
  300.1 1.9 branch_1_fun.8
  303.1 2.6 collective-permute-start.12
  305.8 1.9 collective-permute-start.13
  307.7 9.6 %collective-permute-done.11 = bf16[104,768]{1,0:T(8,128)(2,1)S(1)} collective-permute-done((bf16[104,768]{1,0:T(8,128)(2,1)S(1)}, bf16[104,768]{1,0:T(8,128)(2,1)S(1)}, u32[]{:S(2)}, u32[]{:S(2)}) %collective-permute-start.11) | collective-permute-done | bytes 159776 | tf_op jit(solution)/shard_map/cond/branch_1_fun/ppermute | solution.py:679
  317.3 6.0 %collective-permute-done.12 = bf16[104,768]{1,0:T(8,128)(2,1)S(1)} collective-permute-done((bf16[104,768]{1,0:T(8,128)(2,1)S(1)}, bf16[104,768]{1,0:T(8,128)(2,1)S(1)}, u32[]{:S(2)}, u32[]{:S(2)}) %collective-permute-start.12) | collective-permute-done | bytes 159776 | tf_op jit(solution)/shard_map/cond/branch_1_fun/ppermute | solution.py:679
  324.8 3.4 collective-permute-start.15
  328.3 3.5 collective-permute-done.16
  331.7 15.4 %collective-permute-done.15 = bf16[104,768]{1,0:T(8,128)(2,1)S(1)} collective-permute-done((bf16[104,768]{1,0:T(8,128)(2,1)S(1)}, bf16[104,768]{1,0:T(8,128)(2,1)S(1)}, u32[]{:S(2)}, u32[]{:S(2)}) %collective-permute-start.15) | collective-permute-done | bytes 159776 | tf_op jit(solution)/shard_map/cond/branch_1_fun/ppermute | solution.py:686
  350.1 11.5 %collective-permute-done.17 = bf16[4,56,768]{2,1,0:T(8,128)(2,1)S(1)} collective-permute-done((bf16[4,56,768]{2,1,0:T(8,128)(2,1)S(1)}, bf16[4,56,768]{2,1,0:T(8,128)(2,1)S(1)}, u32[]{:S(2)}, u32[]{:S(2)}) %collective-permute-start.17) | collective-permute-done | bytes 344096 | tf_op jit(solution)/shard_map/cond/branch_1_fun/ppermute | solution.py:694
  361.6 2.3 collective-permute-start.18
  364.8 1.6 collective-permute-start.20
  366.4 11.2 %collective-permute-done.18 = bf16[8,56,768]{2,1,0:T(8,128)(2,1)} collective-permute-done((bf16[8,56,768]{2,1,0:T(8,128)(2,1)S(1)}, bf16[8,56,768]{2,1,0:T(8,128)(2,1)}, u32[]{:S(2)}, u32[]{:S(2)}) %collective-permute-start.18) | collective-permute-done | bytes 688160 | tf_op jit(solution)/shard_map/cond/branch_1_fun/ppermute | solution.py:694
  379.0 2.8 pad_maximum_fusion.1.refs_1_
  387.4 6.1 %branch_1_fun.9 = (f32[768,768]{1,0:T(8,128)}, f32[768,768]{1,0:T(8,128)}, f32[768,768]{1,0:T(8,128)S(1)}, f32[768,768]{1,0:T(8,128)}, f32[32,768]{1,0:T(8,128)}) custom-call(s32[3,16]{1,0:T(4,128)} %add_add_fusion.index_ref, bf16[16,56,768]{2,1,0:T(8,128)(2,1)} %copy-done.3, bf16[16,48,768]{2,1,0:T(8,128)(2,1)} %pad_maximum_fusion.1.refs_1_, ...), custom_call_target="tpu_custom_call" | custom-call | bytes 19070976 | tf_op jit(solution)/shard_map/cond/branch_1_fun/pallas_call | solution.py:770
  397.7 12.8 %shard_map.428 = (f32[768,3072]{1,0:T(8,128)}, f32[3072,768]{1,0:T(8,128)}) custom-call(bf16[768,3072]{1,0:T(8,128)(2,1)} %get-tuple-element.250.up_ref, bf16[3072,768]{1,0:T(8,128)(2,1)} %get-tuple-element.251.down_ref, f32[768,768]{1,0:T(8,128)S(1)} %get-tuple-element.374.after_ref), custom_call_target="tpu_custom_call" | custom-call | bytes 28311552 | tf_op jit(solution)/shard_map/pallas_call | solution.py:726
  410.6 2.1 copy.136
  (261 shorter events, 44.7 us)
Async XLA Ops:
  7.2 13.9 %copy-start.28 = (f32[768]{0:T(1024)S(1)}, f32[768]{0:T(1024)}, u32[]{:S(2)}) copy-start(f32[768]{0:T(1024)} %param.37) | copy-start | bytes 9220
  7.2 14.5 %copy-start.30 = (f32[768]{0:T(1024)S(1)}, f32[768]{0:T(1024)}, u32[]{:S(2)}) copy-start(f32[768]{0:T(1024)} %param.42) | copy-start | bytes 9220
  7.3 14.5 %copy-start.31 = (f32[768]{0:T(1024)S(1)}, f32[768]{0:T(1024)}, u32[]{:S(2)}) copy-start(f32[768]{0:T(1024)} %param.43) | copy-start | bytes 9220
  7.3 14.5 %copy-start.32 = (f32[768]{0:T(1024)S(1)}, f32[768]{0:T(1024)}, u32[]{:S(2)}) copy-start(f32[768]{0:T(1024)} %param.44) | copy-start | bytes 9220
  7.3 14.5 %copy-start.33 = (f32[768]{0:T(1024)S(1)}, f32[768]{0:T(1024)}, u32[]{:S(2)}) copy-start(f32[768]{0:T(1024)} %param.48) | copy-start | bytes 9220
  7.3 14.5 %copy-start.34 = (f32[768]{0:T(1024)S(1)}, f32[768]{0:T(1024)}, u32[]{:S(2)}) copy-start(f32[768]{0:T(1024)} %param.49) | copy-start | bytes 9220
  7.3 14.6 %copy-start.35 = (f32[768]{0:T(1024)S(1)}, f32[768]{0:T(1024)}, u32[]{:S(2)}) copy-start(f32[768]{0:T(1024)} %param.50) | copy-start | bytes 9220
  7.3 14.7 %copy-start.47 = (f32[33,12]{0,1:T(8,128)S(1)}, f32[33,12]{0,1:T(8,128)}, u32[]{:S(2)}) copy-start(f32[33,12]{0,1:T(8,128)} %param.51) | copy-start | bytes 4756
  7.3 16.5 %copy-start.48 = (f32[65,12]{0,1:T(8,128)S(1)}, f32[65,12]{0,1:T(8,128)}, u32[]{:S(2)}) copy-start(f32[65,12]{0,1:T(8,128)} %param.53) | copy-start | bytes 9364
  7.3 23.9 %all-to-all-start.2 = ((bf16[8,64,768]{2,1,0:T(8,128)(2,1)}), bf16[8,64,768]{2,1,0:T(8,128)(2,1)S(1)}, u32[]{:S(2)}, u32[]{:S(2)}) async-start(bf16[8,64,768]{2,1,0:T(8,128)(2,1)} %bitcast.157), calls=%async_computation.2 | async-start | bytes 1572864 | tf_op jit(solution)/shard_map/all_to_all | solution.py:569
  14.8 20.9 %collective-permute-start.25 = (bf16[144,768]{1,0:T(8,128)(2,1)}, bf16[144,768]{1,0:T(8,128)(2,1)}, u32[]{:S(2)}, u32[]{:S(2)}) collective-permute-start(bf16[144,768]{1,0:T(8,128)(2,1)} %get-tuple-element.285), channel_id=1, source_target_pairs={{0,3},{1,2},{2,1},{3,0},{4,7},{5,6},{6,5},{7,4},{8,11},{9,10},{10,... | collective-permute-start | bytes 663560 | tf_op jit(solution)/shard_map/ppermute | solution.py:581
  18.4 17.3 %collective-permute-start.23 = (bf16[144,768]{1,0:T(8,128)(2,1)}, bf16[144,768]{1,0:T(8,128)(2,1)}, u32[]{:S(2)}, u32[]{:S(2)}) collective-permute-start(bf16[144,768]{1,0:T(8,128)(2,1)} %get-tuple-element.286), channel_id=1, source_target_pairs={{0,1},{1,0},{2,3},{3,2},{4,5},{5,4},{6,7},{7,6},{8,9},{9,8},{10,11... | collective-permute-start | bytes 663560 | tf_op jit(solution)/shard_map/ppermute | solution.py:581
  18.4 19.8 %collective-permute-start.24 = (bf16[144,768]{1,0:T(8,128)(2,1)S(1)}, bf16[144,768]{1,0:T(8,128)(2,1)}, u32[]{:S(2)}, u32[]{:S(2)}) collective-permute-start(bf16[144,768]{1,0:T(8,128)(2,1)S(1)} %get-tuple-element.288), channel_id=1, source_target_pairs={{0,2},{1,3},{2,0},{3,1},{4,6},{5,7},{6,4},{7,5},{8,10},{9,11},{10,... | collective-permute-start | bytes 663560 | tf_op jit(solution)/shard_map/ppermute | solution.py:581
  29.4 60.3 %copy-start.13 = (bf16[1152,320]{1,0:T(8,128)(2,1)}, bf16[1152,320]{1,0:T(8,128)(2,1)S(1)}, u32[]{:S(2)}) copy-start(bf16[1152,320]{1,0:T(8,128)(2,1)S(1)} %add_convert_fusion.1.refs_9_) | copy-start | bytes 2211844
  31.2 58.6 %all-to-all-start.3 = ((bf16[8,64,768]{2,1,0:T(8,128)(2,1)}), bf16[8,64,768]{2,1,0:T(8,128)(2,1)}, u32[]{:S(2)}, u32[]{:S(2)}) async-start(bf16[8,64,768]{2,1,0:T(8,128)(2,1)} %bitcast.50), calls=%async_computation.3 | async-start | bytes 1572864 | tf_op jit(solution)/shard_map/all_to_all | solution.py:569
  35.4 362.2 %all-reduce.10.cloned.1.call-start = ((), (), s32[]{:S(2)}) async-start(), calls=%async_computation.4 | async-start | bytes 18874368 | tf_op jit(solution)/shard_map/psum | solution.py:905
  38.9 50.8 %collective-permute-start.28 = (bf16[144,768]{1,0:T(8,128)(2,1)S(1)}, bf16[144,768]{1,0:T(8,128)(2,1)S(1)}, u32[]{:S(2)}, u32[]{:S(2)}) collective-permute-start(bf16[144,768]{1,0:T(8,128)(2,1)S(1)} %get-tuple-element.281), channel_id=1, source_target_pairs={{0,3},{1,2},{2,1},{3,0},{4,7},{5,6},{6,5},{7,4},{8,11},{9,10},{10,... | collective-permute-start | bytes 663560 | tf_op jit(solution)/shard_map/ppermute | solution.py:581
  41.4 48.3 %collective-permute-start.27 = (bf16[144,768]{1,0:T(8,128)(2,1)S(1)}, bf16[144,768]{1,0:T(8,128)(2,1)S(1)}, u32[]{:S(2)}, u32[]{:S(2)}) collective-permute-start(bf16[144,768]{1,0:T(8,128)(2,1)S(1)} %get-tuple-element.282), channel_id=1, source_target_pairs={{0,2},{1,3},{2,0},{3,1},{4,6},{5,7},{6,4},{7,5},{8,10},{9,11},{10,... | collective-permute-start | bytes 663560 | tf_op jit(solution)/shard_map/ppermute | solution.py:581
  41.4 48.3 %collective-permute-start.26 = (bf16[144,768]{1,0:T(8,128)(2,1)S(1)}, bf16[144,768]{1,0:T(8,128)(2,1)S(1)}, u32[]{:S(2)}, u32[]{:S(2)}) collective-permute-start(bf16[144,768]{1,0:T(8,128)(2,1)S(1)} %get-tuple-element.283), channel_id=1, source_target_pairs={{0,1},{1,0},{2,3},{3,2},{4,5},{5,4},{6,7},{7,6},{8,9},{9,8},{10,11... | collective-permute-start | bytes 663560 | tf_op jit(solution)/shard_map/ppermute | solution.py:581
  158.4 72.4 %all-to-all-start = ((bf16[8,64,768]{2,1,0:T(8,128)(2,1)}), bf16[8,64,768]{2,1,0:T(8,128)(2,1)}, u32[]{:S(2)}, u32[]{:S(2)}) async-start(bf16[8,64,768]{2,1,0:T(8,128)(2,1)} %bitcast), calls=%async_computation | async-start | bytes 1572864 | tf_op jit(solution)/shard_map/cond/branch_1_fun/all_to_all | solution.py:569
  163.4 67.3 %collective-permute-start.2 = (bf16[144,768]{1,0:T(8,128)(2,1)}, bf16[144,768]{1,0:T(8,128)(2,1)S(1)}, u32[]{:S(2)}, u32[]{:S(2)}) collective-permute-start(bf16[144,768]{1,0:T(8,128)(2,1)} %get-tuple-element.257), channel_id=1, source_target_pairs={{0,3},{1,2},{2,1},{3,0},{4,7},{5,6},{6,5},{7,4},{8,11},{9,10},{10,... | collective-permute-start | bytes 663560 | tf_op jit(solution)/shard_map/cond/branch_1_fun/ppermute | solution.py:601
  165.8 65.0 %collective-permute-start.1 = (bf16[144,768]{1,0:T(8,128)(2,1)}, bf16[144,768]{1,0:T(8,128)(2,1)S(1)}, u32[]{:S(2)}, u32[]{:S(2)}) collective-permute-start(bf16[144,768]{1,0:T(8,128)(2,1)} %get-tuple-element.258), channel_id=1, source_target_pairs={{0,2},{1,3},{2,0},{3,1},{4,6},{5,7},{6,4},{7,5},{8,10},{9,11},{10,... | collective-permute-start | bytes 663560 | tf_op jit(solution)/shard_map/cond/branch_1_fun/ppermute | solution.py:601
  165.8 65.0 %collective-permute-start = (bf16[144,768]{1,0:T(8,128)(2,1)S(1)}, bf16[144,768]{1,0:T(8,128)(2,1)S(1)}, u32[]{:S(2)}, u32[]{:S(2)}) collective-permute-start(bf16[144,768]{1,0:T(8,128)(2,1)S(1)} %get-tuple-element.259), channel_id=1, source_target_pairs={{0,1},{1,0},{2,3},{3,2},{4,5},{5,4},{6,7},{7,6},{8,9},{9,8},{10,11... | collective-permute-start | bytes 663560 | tf_op jit(solution)/shard_map/cond/branch_1_fun/ppermute | solution.py:601
  167.9 63.8 %copy-start.50 = (bf16[768,768]{1,0:T(8,128)(2,1)S(1)}, bf16[768,768]{1,0:T(8,128)(2,1)}, u32[]{:S(2)}) copy-start(bf16[768,768]{1,0:T(8,128)(2,1)} %get-tuple-element.67.out_ref) | copy-start | bytes 3538948 | tf_op jit(solution)/shard_map/cond
  246.5 5.0 %collective-permute-start.6 = (bf16[1664,768]{1,0:T(8,128)(2,1)}, bf16[1664,768]{1,0:T(8,128)(2,1)S(1)}, u32[]{:S(2)}, u32[]{:S(2)}) collective-permute-start(bf16[1664,768]{1,0:T(8,128)(2,1)} %dynamic-slice_bitcast_fusion), channel_id=1, source_target_pairs={{0,4},{4,0},{8,12},{12,8},{16,20},{20,16},{24,28},{28,24},{1,5},{5... | collective-permute-start | bytes 7667720 | tf_op jit(solution)/shard_map/cond/branch_1_fun/ppermute | solution.py:654
  255.1 25.0 %collective-permute-start.9 = (bf16[384,768]{1,0:T(8,128)(2,1)}, bf16[384,768]{1,0:T(8,128)(2,1)}, u32[]{:S(2)}, u32[]{:S(2)}) collective-permute-start(bf16[384,768]{1,0:T(8,128)(2,1)} %dynamic-slice_bitcast_fusion.2), channel_id=1, source_target_pairs={{0,16},{4,20},{8,24},{12,28},{16,0},{20,4},{24,8},{28,12},{1,17},{... | collective-permute-start | bytes 1769480 | tf_op jit(solution)/shard_map/cond/branch_1_fun/ppermute | solution.py:654
  257.1 26.4 %collective-permute-start.7 = (bf16[448,768]{1,0:T(8,128)(2,1)S(1)}, bf16[448,768]{1,0:T(8,128)(2,1)}, u32[]{:S(2)}, u32[]{:S(2)}) collective-permute-start(bf16[448,768]{1,0:T(8,128)(2,1)S(1)} %dynamic-slice_bitcast_fusion.1), channel_id=1, source_target_pairs={{0,8},{4,12},{8,0},{12,4},{16,24},{20,28},{24,16},{28,20},{1,9},{5... | collective-permute-start | bytes 2064392 | tf_op jit(solution)/shard_map/cond/branch_1_fun/ppermute | solution.py:654
  269.9 29.4 %all-to-all-start.1 = ((bf16[8,64,768]{2,1,0:T(8,128)(2,1)}), bf16[8,64,768]{2,1,0:T(8,128)(2,1)S(1)}, u32[]{:S(2)}, u32[]{:S(2)}) async-start(bf16[8,64,768]{2,1,0:T(8,128)(2,1)} %bitcast.8), calls=%async_computation.1 | async-start | bytes 1572864 | tf_op jit(solution)/shard_map/cond/branch_1_fun/all_to_all | solution.py:569
  275.6 15.9 %collective-permute-start.5 = (bf16[144,768]{1,0:T(8,128)(2,1)}, bf16[144,768]{1,0:T(8,128)(2,1)S(1)}, u32[]{:S(2)}, u32[]{:S(2)}) collective-permute-start(bf16[144,768]{1,0:T(8,128)(2,1)} %get-tuple-element.253), channel_id=1, source_target_pairs={{0,3},{1,2},{2,1},{3,0},{4,7},{5,6},{6,5},{7,4},{8,11},{9,10},{10,... | collective-permute-start | bytes 663560 | tf_op jit(solution)/shard_map/cond/branch_1_fun/ppermute | solution.py:601
  277.9 21.4 %collective-permute-start.4 = (bf16[144,768]{1,0:T(8,128)(2,1)}, bf16[144,768]{1,0:T(8,128)(2,1)}, u32[]{:S(2)}, u32[]{:S(2)}) collective-permute-start(bf16[144,768]{1,0:T(8,128)(2,1)} %get-tuple-element.254), channel_id=1, source_target_pairs={{0,2},{1,3},{2,0},{3,1},{4,6},{5,7},{6,4},{7,5},{8,10},{9,11},{10,... | collective-permute-start | bytes 663560 | tf_op jit(solution)/shard_map/cond/branch_1_fun/ppermute | solution.py:601
  277.9 21.4 %collective-permute-start.3 = (bf16[144,768]{1,0:T(8,128)(2,1)}, bf16[144,768]{1,0:T(8,128)(2,1)}, u32[]{:S(2)}, u32[]{:S(2)}) collective-permute-start(bf16[144,768]{1,0:T(8,128)(2,1)} %get-tuple-element.255), channel_id=1, source_target_pairs={{0,1},{1,0},{2,3},{3,2},{4,5},{5,4},{6,7},{7,6},{8,9},{9,8},{10,11... | collective-permute-start | bytes 663560 | tf_op jit(solution)/shard_map/cond/branch_1_fun/ppermute | solution.py:601
  281.4 9.9 %collective-permute-start.10 = (bf16[192,768]{1,0:T(8,128)(2,1)S(1)}, bf16[192,768]{1,0:T(8,128)(2,1)S(1)}, u32[]{:S(2)}, u32[]{:S(2)}) collective-permute-start(bf16[192,768]{1,0:T(8,128)(2,1)S(1)} %dynamic-slice_bitcast_fusion.4), channel_id=1, source_target_pairs={{0,8},{4,12},{8,0},{12,4},{16,24},{20,28},{24,16},{28,20},{1,9},{5... | collective-permute-start | bytes 884744 | tf_op jit(solution)/shard_map/cond/branch_1_fun/ppermute | solution.py:654
  284.7 14.6 %copy-start.5 = (bf16[448,768]{1,0:T(8,128)(2,1)}, bf16[448,768]{1,0:T(8,128)(2,1)S(1)}, u32[]{:S(2)}) copy-start(bf16[448,768]{1,0:T(8,128)(2,1)S(1)} %fusion.1) | copy-start | bytes 2064388 | tf_op jit(solution)/shard_map/cond
  284.8 14.5 %collective-permute-start.8 = (bf16[224,768]{1,0:T(8,128)(2,1)S(1)}, bf16[224,768]{1,0:T(8,128)(2,1)S(1)}, u32[]{:S(2)}, u32[]{:S(2)}) collective-permute-start(bf16[224,768]{1,0:T(8,128)(2,1)S(1)} %dynamic-slice_bitcast_fusion.3), channel_id=1, source_target_pairs={{0,16},{4,20},{8,24},{12,28},{16,0},{20,4},{24,8},{28,12},{1,17},{... | collective-permute-start | bytes 1032200 | tf_op jit(solution)/shard_map/cond/branch_1_fun/ppermute | solution.py:654
  299.3 24.1 %copy-start.1 = (bf16[8,64,768]{2,1,0:T(8,128)(2,1)}, bf16[8,64,768]{2,1,0:T(8,128)(2,1)S(1)}, u32[]{:S(2)}) copy-start(bf16[8,64,768]{2,1,0:T(8,128)(2,1)S(1)} %all-to-all-done.1) | copy-start | bytes 2359300 | tf_op jit(solution)/shard_map/cond
  303.0 14.2 %collective-permute-start.11 = (bf16[104,768]{1,0:T(8,128)(2,1)S(1)}, bf16[104,768]{1,0:T(8,128)(2,1)S(1)}, u32[]{:S(2)}, u32[]{:S(2)}) collective-permute-start(bf16[104,768]{1,0:T(8,128)(2,1)S(1)} %pad_maximum_fusion.8), channel_id=1, source_target_pairs={{0,1},{1,0},{2,3},{3,2},{4,5},{5,4},{6,7},{7,6},{8,9},{9,8},{10,11... | collective-permute-start | bytes 479240 | tf_op jit(solution)/shard_map/cond/branch_1_fun/ppermute | solution.py:679
  303.1 20.1 %collective-permute-start.12 = (bf16[104,768]{1,0:T(8,128)(2,1)S(1)}, bf16[104,768]{1,0:T(8,128)(2,1)S(1)}, u32[]{:S(2)}, u32[]{:S(2)}) collective-permute-start(bf16[104,768]{1,0:T(8,128)(2,1)S(1)} %pad_maximum_fusion.9), channel_id=1, source_target_pairs={{0,2},{1,3},{2,0},{3,1},{4,6},{5,7},{6,4},{7,5},{8,10},{9,11},{10,... | collective-permute-start | bytes 479240 | tf_op jit(solution)/shard_map/cond/branch_1_fun/ppermute | solution.py:679
  305.8 17.5 %collective-permute-start.13 = (bf16[104,768]{1,0:T(8,128)(2,1)S(1)}, bf16[104,768]{1,0:T(8,128)(2,1)S(1)}, u32[]{:S(2)}, u32[]{:S(2)}) collective-permute-start(bf16[104,768]{1,0:T(8,128)(2,1)S(1)} %pad_maximum_fusion.10), channel_id=1, source_target_pairs={{0,3},{1,2},{2,1},{3,0},{4,7},{5,6},{6,5},{7,4},{8,11},{9,10},{10,... | collective-permute-start | bytes 479240 | tf_op jit(solution)/shard_map/cond/branch_1_fun/ppermute | solution.py:679
  323.4 8.3 %collective-permute-start.16 = (bf16[104,768]{1,0:T(8,128)(2,1)S(1)}, bf16[104,768]{1,0:T(8,128)(2,1)S(1)}, u32[]{:S(2)}, u32[]{:S(2)}) collective-permute-start(bf16[104,768]{1,0:T(8,128)(2,1)S(1)} %add_convert_fusion), channel_id=1, source_target_pairs={{0,3},{1,2},{2,1},{3,0},{4,7},{5,6},{6,5},{7,4},{8,11},{9,10},{10,... | collective-permute-start | bytes 479240 | tf_op jit(solution)/shard_map/cond/branch_1_fun/ppermute | solution.py:686
  324.8 22.3 %collective-permute-start.15 = (bf16[104,768]{1,0:T(8,128)(2,1)S(1)}, bf16[104,768]{1,0:T(8,128)(2,1)S(1)}, u32[]{:S(2)}, u32[]{:S(2)}) collective-permute-start(bf16[104,768]{1,0:T(8,128)(2,1)S(1)} %add_convert_fusion), channel_id=1, source_target_pairs={{0,2},{1,3},{2,0},{3,1},{4,6},{5,7},{6,4},{7,5},{8,10},{9,11},{10,... | collective-permute-start | bytes 479240 | tf_op jit(solution)/shard_map/cond/branch_1_fun/ppermute | solution.py:686
  328.2 18.8 %collective-permute-start.14 = (bf16[104,768]{1,0:T(8,128)(2,1)S(1)}, bf16[104,768]{1,0:T(8,128)(2,1)S(1)}, u32[]{:S(2)}, u32[]{:S(2)}) collective-permute-start(bf16[104,768]{1,0:T(8,128)(2,1)S(1)} %add_convert_fusion), channel_id=1, source_target_pairs={{0,1},{1,0},{2,3},{3,2},{4,5},{5,4},{6,7},{7,6},{8,9},{9,8},{10,11... | collective-permute-start | bytes 479240 | tf_op jit(solution)/shard_map/cond/branch_1_fun/ppermute | solution.py:686
  347.2 14.3 %collective-permute-start.17 = (bf16[4,56,768]{2,1,0:T(8,128)(2,1)S(1)}, bf16[4,56,768]{2,1,0:T(8,128)(2,1)S(1)}, u32[]{:S(2)}, u32[]{:S(2)}) collective-permute-start(bf16[4,56,768]{2,1,0:T(8,128)(2,1)S(1)} %slice.199), channel_id=1, source_target_pairs={{0,16},{4,20},{8,24},{12,28},{16,0},{20,4},{24,8},{28,12},{1,17},{... | collective-permute-start | bytes 1032200 | tf_op jit(solution)/shard_map/cond/branch_1_fun/ppermute | solution.py:694
  348.5 15.4 %collective-permute-start.19 = (bf16[4,48,768]{2,1,0:T(8,128)(2,1)S(1)}, bf16[4,48,768]{2,1,0:T(8,128)(2,1)S(1)}, u32[]{:S(2)}, u32[]{:S(2)}) collective-permute-start(bf16[4,48,768]{2,1,0:T(8,128)(2,1)S(1)} %pad_maximum_fusion.7), channel_id=1, source_target_pairs={{0,8},{4,12},{8,0},{12,4},{16,24},{20,28},{24,16},{28,20},{1,9},{5... | collective-permute-start | bytes 884744 | tf_op jit(solution)/shard_map/cond/branch_1_fun/ppermute | solution.py:694
  361.6 16.1 %collective-permute-start.18 = (bf16[8,56,768]{2,1,0:T(8,128)(2,1)S(1)}, bf16[8,56,768]{2,1,0:T(8,128)(2,1)}, u32[]{:S(2)}, u32[]{:S(2)}) collective-permute-start(bf16[8,56,768]{2,1,0:T(8,128)(2,1)S(1)} %pad_maximum_fusion.4), channel_id=1, source_target_pairs={{0,8},{4,12},{8,0},{12,4},{16,24},{20,28},{24,16},{28,20},{1,9},{5... | collective-permute-start | bytes 2064392 | tf_op jit(solution)/shard_map/cond/branch_1_fun/ppermute | solution.py:694
  364.8 14.2 %collective-permute-start.20 = (bf16[8,48,768]{2,1,0:T(8,128)(2,1)}, bf16[8,48,768]{2,1,0:T(8,128)(2,1)}, u32[]{:S(2)}, u32[]{:S(2)}) collective-permute-start(bf16[8,48,768]{2,1,0:T(8,128)(2,1)} %pad_maximum_fusion.6), channel_id=1, source_target_pairs={{0,16},{4,20},{8,24},{12,28},{16,0},{20,4},{24,8},{28,12},{1,17},{... | collective-permute-start | bytes 1769480 | tf_op jit(solution)/shard_map/cond/branch_1_fun/ppermute | solution.py:694
  366.4 16.0 %copy-start.10 = (bf16[144,768]{1,0:T(8,128)(2,1)S(1)}, bf16[144,768]{1,0:T(8,128)(2,1)}, u32[]{:S(2)}) copy-start(bf16[144,768]{1,0:T(8,128)(2,1)} %copy-done.9) | copy-start | bytes 663556 | tf_op jit(solution)/shard_map/cond
  378.9 8.5 %collective-permute-start.21 = (bf16[16,56,768]{2,1,0:T(8,128)(2,1)S(1)}, bf16[16,56,768]{2,1,0:T(8,128)(2,1)}, u32[]{:S(2)}, u32[]{:S(2)}) collective-permute-start(bf16[16,56,768]{2,1,0:T(8,128)(2,1)S(1)} %pad_maximum_fusion.refs_0_), channel_id=1, source_target_pairs={{0,4},{4,0},{8,12},{12,8},{16,20},{20,16},{24,28},{28,24},{1,5},{5... | collective-permute-start | bytes 4128776 | tf_op jit(solution)/shard_map/cond/branch_1_fun/ppermute | solution.py:700
  381.8 5.6 %collective-permute-start.22 = (bf16[16,48,768]{2,1,0:T(8,128)(2,1)}, bf16[16,48,768]{2,1,0:T(8,128)(2,1)}, u32[]{:S(2)}, u32[]{:S(2)}) collective-permute-start(bf16[16,48,768]{2,1,0:T(8,128)(2,1)} %pad_maximum_fusion.1.refs_1_), channel_id=1, source_target_pairs={{0,4},{4,0},{8,12},{12,8},{16,20},{20,16},{24,28},{28,24},{1,5},{5... | collective-permute-start | bytes 3538952 | tf_op jit(solution)/shard_map/cond/branch_1_fun/ppermute | solution.py:700
  (37 other events, 319.2 us)
Sparse Core Ops, SparseCore 0:
  150.4 232.7 all-reduce.9

commit v6 on v5

--- a/solution.py
+++ b/solution.py
@@ -700,42 +700,18 @@
     return shares + [lax.ppermute(a, "wide", flip_pairs(wide, 1)) for a in shares]
 
 
-def convert_kernel(up_ref, down_ref, after_ref, up_out, down_out):
-    step = pl.program_id(0)
-    parts = pl.num_programs(0) // 2
-
-    @pl.when(step < parts)
-    def _():
-        up_out[...] = up_ref[...].astype(F32)
-
-    @pl.when(step >= parts)
-    def _():
-        down_out[...] = down_ref[...].astype(F32)
-
-
-def convert(up_total, down_total, after):
-    dim, ff = up_total.shape
-    parts = ff // dim
-
-    def block(index):
-        return pl.BlockSpec((dim, dim), index)
-
-    up_block = block(lambda p: (0, jnp.minimum(p, parts - 1)))
-    down_block = block(lambda p: (jnp.maximum(p - parts, 0), 0))
-    shape = jax.ShapeDtypeStruct
-    return pl.pallas_call(
-        convert_kernel,
-        grid=(2 * parts,),
-        in_specs=[up_block, down_block, pl.BlockSpec(memory_space=pl.ANY)],
-        out_specs=[up_block, down_block],
-        out_shape=[shape((dim, ff), F32), shape((ff, dim), F32)],
-        compiler_params=pltpu.CompilerParams(vmem_limit_bytes=VMEM_BYTES),
-        cost_estimate=pl.CostEstimate(flops=0, bytes_accessed=12 * dim * ff, transcendentals=0),
-    )(up_total, down_total, after)
-
-
-def finish_kernel(places, ways, cuts, index_ref, *refs):
+def finish_kernel(places, ways, cuts, index_ref, up_ref, down_ref, *refs):
     pieces, outs = refs[: 2 * ways], refs[2 * ways :]
+    *outs, up_out, down_out = outs
+    up_out[...] = up_ref[...].astype(F32)
+    down_out[...] = down_ref[...].astype(F32)
+
+    @pl.when(pl.program_id(0) == 0)
+    def _():
+        put_pieces(places, ways, cuts, index_ref, pieces, outs)
+
+
+def put_pieces(places, ways, cuts, index_ref, pieces, outs):
     at = 0
     for core in range(2):
         for way in range(ways):
@@ -752,7 +728,7 @@
                 at += rows
 
 
-def finish(pieces, wide, narrow, lengths):
+def finish(totals, pieces, wide, narrow, lengths):
     places, _, columns = pieces[0].shape
     ways = len(pieces) // 2
     index = []
@@ -767,17 +743,27 @@
     for length in lengths:
         start = cuts[-1][1] if cuts else 0
         cuts.append((start, start + length))
+    blocks = [pl.BlockSpec((a.shape[0] // 2, a.shape[1]), lambda p: (p, 0)) for a in totals]
+
+    def whole(shape):
+        return pl.BlockSpec(shape, lambda p: (0,) * len(shape), pipeline_mode=pl.Buffered(1))
+
     return pl.pallas_call(
         partial(finish_kernel, places, ways, cuts),
+        grid=(2,),
         in_specs=[pl.BlockSpec(memory_space=pltpu.SMEM)]
-        + [pl.BlockSpec(memory_space=pltpu.VMEM)] * len(pieces),
-        out_specs=[pl.BlockSpec(memory_space=pltpu.VMEM)] * len(lengths),
-        out_shape=[jax.ShapeDtypeStruct((length, columns), F32) for length in lengths],
+        + blocks
+        + [whole(a.shape) for a in pieces],
+        out_specs=[whole((length, columns)) for length in lengths] + blocks,
+        out_shape=[jax.ShapeDtypeStruct((length, columns), F32) for length in lengths]
+        + [jax.ShapeDtypeStruct(a.shape, F32) for a in totals],
         compiler_params=pltpu.CompilerParams(vmem_limit_bytes=VMEM_BYTES),
         cost_estimate=pl.CostEstimate(
-            flops=0, bytes_accessed=8 * sum(lengths) * columns, transcendentals=0
+            flops=0,
+            bytes_accessed=8 * sum(lengths) * columns + 6 * sum(a.size for a in totals),
+            transcendentals=0,
         ),
-    )(jnp.stack(index), *pieces)
+    )(jnp.stack(index), *totals, *pieces)
 
 
 def room_for(rows, wide, narrow):
@@ -934,22 +920,27 @@
         halves = gather_narrow(narrow_step(halves, narrow), narrow, lengths)
         for i in range(levels - 1, -1, -1):
             halves = gather_wide(halves, wide, i)
-        *large, small = finish(gather_core(halves, wide), wide, narrow, (dim,) * 4 + (32,))
         return (
             text_out, patch_set(out_pieces, patch_shape), text_grad,
-            patch_set(grad_pieces, patch_shape), *large, *unpack(small, early + late),
+            patch_set(grad_pieces, patch_shape), *gather_core(halves, wide),
         )
 
     def never():
         return jax.tree.map(lambda a: jnp.zeros(a.shape, a.dtype), jax.eval_shape(backward))
 
+    text_out, patch_out, text_grad, patch_grad, *pieces = lax.cond(
+        text_len.reshape(()) >= 0, backward, never
+    )
     (
-        text_out, patch_out, text_grad, patch_grad, query_weight_grad, key_weight_grad,
-        value_weight_grad, output_weight_grad, output_bias_grad, norm_gain_grad, norm_shift_grad,
-        up_bias_grad, down_bias_grad, final_gain_grad, final_shift_grad, query_bias_grad,
-        value_bias_grad, line_table_grad, width_table_grad, height_table_grad,
-    ) = lax.cond(text_len.reshape(()) >= 0, backward, never)
-    up_weight_grad, down_weight_grad = convert(up_total, down_total, value_weight_grad)
+        query_weight_grad, key_weight_grad, value_weight_grad, output_weight_grad, small,
+        up_weight_grad, down_weight_grad,
+    ) = finish((up_total, down_total), pieces, wide, narrow, (dim,) * 4 + (32,))
+    late = (query_bias, value_bias, line_table, width_table, height_table)
+    (
+        output_bias_grad, norm_gain_grad, norm_shift_grad, up_bias_grad, down_bias_grad,
+        final_gain_grad, final_shift_grad, query_bias_grad, value_bias_grad, line_table_grad,
+        width_table_grad, height_table_grad,
+    ) = unpack(small, early + late)
     up_bias_grad = up_bias_grad.reshape(-1)
     return (
         text_out,

time: 427 us -> 423 us (level)
  other arithmetic: 24.7 us -> 20.3 us
    ppermute x6, waiting for transfers between devices: 7.76 us -> 0.02 us  [patch_away(): lax.ppermute(parts[k], 'narrow', flip_pairs(size, k))]
    ppermute x5, waiting for transfers between devices: 10.1 us -> 17.7 us  [wide_step(): lax.ppermute(pick(parts, 1 - me), 'wide', flip_pairs(wide, 1 << bit))]
    ppermute x3, waiting for transfers between devices: 15.6 us -> 20.3 us  [narrow_step(): lax.ppermute(picked(me ^ k), 'narrow', flip_pairs(narrow, k))]
    pallas_call x2 -> x1, Pallas kernels: 18.9 us -> 14.4 us  [finish(): pl.pallas_call(partial(finish_kernel, places, ways, cuts), grid=(2,), in_...]
  transfers between devices with their start and end apart: 34 -> 34, of which waited for: 10 -> 11; matrix products, arithmetic and copies ran while one was open for 13% -> 11% of each run, Pallas kernels for 32% -> 31%
where the time goes in v6:
time: 423 us; the launch traced here: 417 us
  Pallas kernels  202 us (48%)
  waiting for transfers between devices  79.3 us (19%)
  starting transfers between devices  59.9 us (14%)
  local copies, waits for them, and re-layouts  36.8 us (9%)
  other arithmetic  20.3 us (5%)
  between operations  16.2 us (4%)
    pallas_call x1, Pallas kernels, attend_back(): pl.pallas_call(partial(attend_back_kernel, len(held)), grid=(pairs,), in_...  60.4 us
    pallas_call x1, Pallas kernels, rows_pass(): pl.pallas_call(partial(rows_kernel, len(pieces), blocks), grid=(blocks +...  59.7 us
    pallas_call x1, Pallas kernels, attend(): pl.pallas_call(partial(attend_kernel, len(pieces)), grid=(HEADS // 2,), i...  46.4 us
    ppermute x4, waiting for transfers between devices, gather_wide(): lax.ppermute(a, 'wide', flip_pairs(wide, 1 << order[i]))  24 us
    ppermute x3, waiting for transfers between devices, narrow_step(): lax.ppermute(picked(me ^ k), 'narrow', flip_pairs(narrow, k))  20.3 us
    ppermute x5, waiting for transfers between devices, wide_step(): lax.ppermute(pick(parts, 1 - me), 'wide', flip_pairs(wide, 1 << bit))  17.7 us
    all_to_all x4, starting transfers between devices, swap_text(): lax.all_to_all(parts, 'wide', split_axis=0, concat_axis=0, tiled=True)  17.4 us
    ppermute x3, waiting for transfers between devices, gather_narrow(): lax.ppermute(part, 'narrow', flip_pairs(narrow, k))  15.6 us
  transfers between devices with their start and end apart: 34, of which 11 were waited for; matrix products, arithmetic and copies ran while one was open for 11% of the time, Pallas kernels for 31%

profile of v6, /device:TPU:0, one launch (start us, length us, event | category | flops | bytes accessed | tf_op | source)
XLA Modules:
  0.0 417.4 jit_solution(349572070444335418)
XLA Ops:
  7.3 5.3 %all-to-all-start.2 = ((bf16[8,64,768]{2,1,0:T(8,128)(2,1)}), bf16[8,64,768]{2,1,0:T(8,128)(2,1)S(1)}, u32[]{:S(2)}, u32[]{:S(2)}) async-start(bf16[8,64,768]{2,1,0:T(8,128)(2,1)} %bitcast.157), calls=%async_computation.2 | async-start | bytes 1572864 | tf_op jit(solution)/shard_map/all_to_all | solution.py:569
  13.5 1.6 collective-permute-start.23
  15.1 2.6 collective-permute-start.24
  31.3 4.2 %all-to-all-start.3 = ((bf16[8,64,768]{2,1,0:T(8,128)(2,1)}), bf16[8,64,768]{2,1,0:T(8,128)(2,1)S(1)}, u32[]{:S(2)}, u32[]{:S(2)}) async-start(bf16[8,64,768]{2,1,0:T(8,128)(2,1)} %bitcast.50), calls=%async_computation.3 | async-start | bytes 1572864 | tf_op jit(solution)/shard_map/all_to_all | solution.py:569
  36.6 2.9 collective-permute-start.26
  42.0 46.4 %shard_map.426 = (bf16[12,1088,1152]{2,1,0:T(8,128)(2,1)}, bf16[768,1152]{1,0:T(8,128)(2,1)}, bf16[1088,768]{1,0:T(8,128)(2,1)}, f32[12,1,1152]{2,1,0:T(1,128)},...) custom-call(bf16[512,768]{1,0:T(8,128)(2,1)} %bitcast.158, ...), custom_call_target="tpu_custom_call" | custom-call | flops 61605937152 | bytes 30081024 | tf_op jit(solution)/shard_map/pallas_call | solution.py:108
  89.5 59.7 %shard_map.427 = (bf16[1088,768]{1,0:T(8,128)(2,1)}, f32[1088,768]{1,0:T(8,128)}, bf16[1088,768]{1,0:T(8,128)(2,1)}, bf16[768,3072]{1,0:T(8,128)(2,1)}, bf16[307...) custom-call(bf16[512,768]{1,0:T(8,128)(2,1)} %bitcast.159, ...), custom_call_target="tpu_custom_call" | custom-call | flops 35936796672 | bytes 53477376 | tf_op jit(solution)/shard_map/pallas_call | solution.py:400
  151.2 2.1 pad_maximum_fusion.11
  153.4 231.0 %conditional.1 = (bf16[8,1,64,768]{3,2,1,0:T(8,128)(2,1)}, bf16[1,4,144,768]{3,2,1,0:T(8,128)(2,1)}, bf16[8,1,64,768]{3,2,1,0:T(8,128)(2,1)S(1)}, bf16[1,4,144,7...) conditional(s32[]{:T(128)} %convert_element_type.129, () %tuple.18, ...), branch_computations={%region_0.1_spmd, %region_1.2_spmd} | conditional | flops 70616072192 | bytes 209943680 | solution.py:931
  153.4 2.2 slice.131
  155.6 4.3 %all-to-all-start = ((bf16[8,64,768]{2,1,0:T(8,128)(2,1)}), bf16[8,64,768]{2,1,0:T(8,128)(2,1)}, u32[]{:S(2)}, u32[]{:S(2)}) async-start(bf16[8,64,768]{2,1,0:T(8,128)(2,1)} %bitcast), calls=%async_computation | async-start | bytes 1572864 | tf_op jit(solution)/shard_map/cond/branch_1_fun/all_to_all | solution.py:569
  160.9 2.6 collective-permute-start.2
  163.5 1.8 collective-permute-start
  165.3 60.4 %branch_1_fun.4 = (bf16[3,1088,768]{2,1,0:T(8,128)(2,1)}, f32[12,3,256]{2,1,0:T(4,128)}) custom-call(bf16[12,1088,1152]{2,1,0:T(8,128)(2,1)} %get-tuple-element.52.refs_0_, bf16[768,1152]{1,0:T(8,128)(2,1)} %get-tuple-element.53.refs_1_, f32[12,1,1152]{2,1,0:T(1,128)S(1)} %copy-done.44, bf16[1088,768]{1,0:T(8,128)(2,1)} %get-tuple-element.55.refs_3_, ...), custom_call_target="tpu_custom_call" | custom-call | flops 61605937152 | bytes 30081024 | tf_op jit(solution)/shard_map/cond/branch_1_fun/pallas_call | solution.py:242
  228.9 9.8 %branch_1_fun.6 = (bf16[3328,768]{1,0:T(8,128)(2,1)}, f32[3,8,768]{2,1,0:T(8,128)}) custom-call(bf16[1088,768]{1,0:T(8,128)(2,1)} %get-tuple-element.65.x_ref, bf16[3,1088,768]{2,1,0:T(8,128)(2,1)} %get-tuple-element.62.dqkv_ref, bf16[768,768]{1,0:T(8,128)(2,1)} %get-tuple-element.66.out_ref, bf16[8,1,64,768]{3,2,1,0:T(8,128)(2,1)} %bitcast.1.refs_0_, ...), custom_call_target="tpu_custom_call" | custom-call | flops 5133828096 | bytes 20054016 | tf_op jit(solution)/shard_map/cond/branch_1_fun/pallas_call | solution.py:468
  240.6 3.5 dynamic-slice_bitcast_fusion
  244.1 5.0 %collective-permute-done.6 = bf16[1664,768]{1,0:T(8,128)(2,1)S(1)} collective-permute-done((bf16[1664,768]{1,0:T(8,128)(2,1)}, bf16[1664,768]{1,0:T(8,128)(2,1)S(1)}, u32[]{:S(2)}, u32[]{:S(2)}) %collective-permute-start.6) | collective-permute-done | bytes 2555936 | tf_op jit(solution)/shard_map/cond/branch_1_fun/ppermute | solution.py:654
  249.1 2.4 fusion
  252.5 1.9 collective-permute-start.9
  255.3 1.4 collective-permute-start.7
  256.7 9.2 %branch_1_fun.5 = bf16[1088,768]{1,0:T(8,128)(2,1)} custom-call(bf16[3,1088,768]{2,1,0:T(8,128)(2,1)} %get-tuple-element.62.dqkv_ref, bf16[3,768,768]{2,1,0:T(8,128)(2,1)} %get-tuple-element.63.weight_ref, f32[1088,768]{1,0:T(8,128)} %get-tuple-element.64.dmid_ref), custom_call_target="tpu_custom_call" | custom-call | flops 3850371072 | bytes 13369344 | tf_op jit(solution)/shard_map/cond/branch_1_fun/pallas_call | solution.py:506
  265.9 2.2 slice_bitcast_fusion
  268.1 2.8 collective-permute-start.5
  270.9 1.6 collective-permute-start.3
  272.5 2.1 slice.204
  274.6 3.5 all-to-all-start.1
  279.4 2.0 collective-permute-start.10
  282.7 1.6 collective-permute-start.8
  284.2 11.9 %collective-permute-done.10 = bf16[192,768]{1,0:T(8,128)(2,1)S(1)} collective-permute-done((bf16[192,768]{1,0:T(8,128)(2,1)S(1)}, bf16[192,768]{1,0:T(8,128)(2,1)S(1)}, u32[]{:S(2)}, u32[]{:S(2)}) %collective-permute-start.10) | collective-permute-done | bytes 294944 | tf_op jit(solution)/shard_map/cond/branch_1_fun/ppermute | solution.py:654
  297.8 1.9 branch_1_fun.7
  300.9 2.8 collective-permute-start.13
  303.8 1.7 collective-permute-start.11
  305.5 7.5 %collective-permute-done.13 = bf16[104,768]{1,0:T(8,128)(2,1)S(1)} collective-permute-done((bf16[104,768]{1,0:T(8,128)(2,1)S(1)}, bf16[104,768]{1,0:T(8,128)(2,1)S(1)}, u32[]{:S(2)}, u32[]{:S(2)}) %collective-permute-start.13) | collective-permute-done | bytes 159776 | tf_op jit(solution)/shard_map/cond/branch_1_fun/ppermute | solution.py:679
  313.0 12.9 %collective-permute-done.12 = bf16[104,768]{1,0:T(8,128)(2,1)S(1)} collective-permute-done((bf16[104,768]{1,0:T(8,128)(2,1)S(1)}, bf16[104,768]{1,0:T(8,128)(2,1)S(1)}, u32[]{:S(2)}, u32[]{:S(2)}) %collective-permute-start.12) | collective-permute-done | bytes 159776 | tf_op jit(solution)/shard_map/cond/branch_1_fun/ppermute | solution.py:679
  327.1 3.3 collective-permute-start.14
  330.4 5.4 %collective-permute-done.16 = bf16[104,768]{1,0:T(8,128)(2,1)S(1)} collective-permute-done((bf16[104,768]{1,0:T(8,128)(2,1)S(1)}, bf16[104,768]{1,0:T(8,128)(2,1)S(1)}, u32[]{:S(2)}, u32[]{:S(2)}) %collective-permute-start.16) | collective-permute-done | bytes 159776 | tf_op jit(solution)/shard_map/cond/branch_1_fun/ppermute | solution.py:686
  335.7 8.2 %collective-permute-done.15 = bf16[104,768]{1,0:T(8,128)(2,1)S(1)} collective-permute-done((bf16[104,768]{1,0:T(8,128)(2,1)S(1)}, bf16[104,768]{1,0:T(8,128)(2,1)S(1)}, u32[]{:S(2)}, u32[]{:S(2)}) %collective-permute-start.15) | collective-permute-done | bytes 159776 | tf_op jit(solution)/shard_map/cond/branch_1_fun/ppermute | solution.py:686
  343.9 2.0 collective-permute-done.14
  346.1 1.5 collective-permute-start.17
  347.5 1.5 collective-permute-start.19
  349.1 6.8 %collective-permute-done.17 = bf16[4,56,768]{2,1,0:T(8,128)(2,1)S(1)} collective-permute-done((bf16[4,56,768]{2,1,0:T(8,128)(2,1)S(1)}, bf16[4,56,768]{2,1,0:T(8,128)(2,1)S(1)}, u32[]{:S(2)}, u32[]{:S(2)}) %collective-permute-start.17) | collective-permute-done | bytes 344096 | tf_op jit(solution)/shard_map/cond/branch_1_fun/ppermute | solution.py:694
  356.0 2.5 collective-permute-start.18
  358.6 1.8 collective-permute-start.20
  360.3 17.2 %collective-permute-done.18 = bf16[8,56,768]{2,1,0:T(8,128)(2,1)S(1)} collective-permute-done((bf16[8,56,768]{2,1,0:T(8,128)(2,1)S(1)}, bf16[8,56,768]{2,1,0:T(8,128)(2,1)S(1)}, u32[]{:S(2)}, u32[]{:S(2)}) %collective-permute-start.18) | collective-permute-done | bytes 688160 | tf_op jit(solution)/shard_map/cond/branch_1_fun/ppermute | solution.py:694
  384.4 1.6 all-reduce.10.cloned.1.call-done
  386.1 14.4 %shard_map.428 = (f32[768,768]{1,0:T(8,128)}, f32[768,768]{1,0:T(8,128)}, f32[768,768]{1,0:T(8,128)}, f32[768,768]{1,0:T(8,128)}, f32[32,768]{1,0:T(8,128)}, /*index=5*/f32[768,3072]{1,0:T(8,128)}, f32[3072,768]{1,0:T(8,128)}) custom-call(s32[3,16]{1,0:T(4,128)} %add_add_fusion.index_ref, bf16[768,3072]{1,0:T(8,128)(2,1)} %get-tuple-element.227.up_ref, ...), custom_call_target="tpu_custom_call" | custom-call | bytes 47382528 | tf_op jit(solution)/shard_map/pallas_call | solution.py:751
  400.5 1.6 slice_reduce_fusion.3
  407.4 2.1 copy.106
  (248 shorter events, 47.2 us)
Async XLA Ops:
  7.2 5.4 %copy-start.11 = (bf16[1,4,144,768]{3,2,1,0:T(8,128)(2,1)S(1)}, bf16[1,4,144,768]{3,2,1,0:T(8,128)(2,1)}, u32[]{:S(2)}) copy-start(bf16[1,4,144,768]{3,2,1,0:T(8,128)(2,1)} %param.30) | copy-start | bytes 2654212
  7.2 12.0 %copy-start.27 = (s32[1,1,1088]{2,1,0:T(1,128)S(1)}, s32[1,1,1088]{2,1,0:T(1,128)}, u32[]{:S(2)}) copy-start(s32[1,1,1088]{2,1,0:T(1,128)} %param.35) | copy-start | bytes 13060
  7.2 12.0 %copy-start.28 = (s32[1,1,1088]{2,1,0:T(1,128)S(1)}, s32[1,1,1088]{2,1,0:T(1,128)}, u32[]{:S(2)}) copy-start(s32[1,1,1088]{2,1,0:T(1,128)} %param.34) | copy-start | bytes 13060
  7.2 12.0 %copy-start.29 = (s32[1,1,1088]{2,1,0:T(1,128)S(1)}, s32[1,1,1088]{2,1,0:T(1,128)}, u32[]{:S(2)}) copy-start(s32[1,1,1088]{2,1,0:T(1,128)} %param.33) | copy-start | bytes 13060
  7.2 12.5 %copy-start.30 = (f32[768]{0:T(1024)S(1)}, f32[768]{0:T(1024)}, u32[]{:S(2)}) copy-start(f32[768]{0:T(1024)} %param.40) | copy-start | bytes 9220
  7.2 12.5 %copy-start.31 = (f32[768]{0:T(1024)S(1)}, f32[768]{0:T(1024)}, u32[]{:S(2)}) copy-start(f32[768]{0:T(1024)} %param.37) | copy-start | bytes 9220
  7.3 24.0 %all-to-all-start.2 = ((bf16[8,64,768]{2,1,0:T(8,128)(2,1)}), bf16[8,64,768]{2,1,0:T(8,128)(2,1)S(1)}, u32[]{:S(2)}, u32[]{:S(2)}) async-start(bf16[8,64,768]{2,1,0:T(8,128)(2,1)} %bitcast.157), calls=%async_computation.2 | async-start | bytes 1572864 | tf_op jit(solution)/shard_map/all_to_all | solution.py:569
  12.6 9.8 %copy-start.41 = (f32[33,12]{0,1:T(8,128)S(1)}, f32[33,12]{0,1:T(8,128)}, u32[]{:S(2)}) copy-start(f32[33,12]{0,1:T(8,128)} %param.51) | copy-start | bytes 4756
  12.6 10.9 %copy-start.42 = (f32[65,12]{0,1:T(8,128)S(1)}, f32[65,12]{0,1:T(8,128)}, u32[]{:S(2)}) copy-start(f32[65,12]{0,1:T(8,128)} %param.52) | copy-start | bytes 9364
  13.5 22.2 %collective-permute-start.23 = (bf16[144,768]{1,0:T(8,128)(2,1)}, bf16[144,768]{1,0:T(8,128)(2,1)}, u32[]{:S(2)}, u32[]{:S(2)}) collective-permute-start(bf16[144,768]{1,0:T(8,128)(2,1)} %get-tuple-element.259), channel_id=1, source_target_pairs={{0,1},{1,0},{2,3},{3,2},{4,5},{5,4},{6,7},{7,6},{8,9},{9,8},{10,11... | collective-permute-start | bytes 663560 | tf_op jit(solution)/shard_map/ppermute | solution.py:581
  15.1 20.6 %collective-permute-start.24 = (bf16[144,768]{1,0:T(8,128)(2,1)}, bf16[144,768]{1,0:T(8,128)(2,1)}, u32[]{:S(2)}, u32[]{:S(2)}) collective-permute-start(bf16[144,768]{1,0:T(8,128)(2,1)} %get-tuple-element.261), channel_id=1, source_target_pairs={{0,2},{1,3},{2,0},{3,1},{4,6},{5,7},{6,4},{7,5},{8,10},{9,11},{10,... | collective-permute-start | bytes 663560 | tf_op jit(solution)/shard_map/ppermute | solution.py:581
  17.7 18.1 %collective-permute-start.25 = (bf16[144,768]{1,0:T(8,128)(2,1)}, bf16[144,768]{1,0:T(8,128)(2,1)}, u32[]{:S(2)}, u32[]{:S(2)}) collective-permute-start(bf16[144,768]{1,0:T(8,128)(2,1)} %get-tuple-element.258), channel_id=1, source_target_pairs={{0,3},{1,2},{2,1},{3,0},{4,7},{5,6},{6,5},{7,4},{8,11},{9,10},{10,... | collective-permute-start | bytes 663560 | tf_op jit(solution)/shard_map/ppermute | solution.py:581
  28.9 13.1 %copy-start.13 = (bf16[1152,320]{1,0:T(8,128)(2,1)}, bf16[1152,320]{1,0:T(8,128)(2,1)S(1)}, u32[]{:S(2)}) copy-start(bf16[1152,320]{1,0:T(8,128)(2,1)S(1)} %add_convert_fusion.1.refs_9_) | copy-start | bytes 2211844
  28.9 6.8 %copy-start.12 = (bf16[1,4,144,768]{3,2,1,0:T(8,128)(2,1)S(1)}, bf16[1,4,144,768]{3,2,1,0:T(8,128)(2,1)}, u32[]{:S(2)}) copy-start(bf16[1,4,144,768]{3,2,1,0:T(8,128)(2,1)} %param.55) | copy-start | bytes 2654212
  31.3 57.2 %all-to-all-start.3 = ((bf16[8,64,768]{2,1,0:T(8,128)(2,1)}), bf16[8,64,768]{2,1,0:T(8,128)(2,1)S(1)}, u32[]{:S(2)}, u32[]{:S(2)}) async-start(bf16[8,64,768]{2,1,0:T(8,128)(2,1)} %bitcast.50), calls=%async_computation.3 | async-start | bytes 1572864 | tf_op jit(solution)/shard_map/all_to_all | solution.py:569
  35.5 350.6 %all-reduce.10.cloned.1.call-start = ((), (), s32[]{:S(2)}) async-start(), calls=%async_computation.4 | async-start | bytes 18874368 | tf_op jit(solution)/shard_map/psum | solution.py:891
  36.6 51.8 %collective-permute-start.26 = (bf16[144,768]{1,0:T(8,128)(2,1)}, bf16[144,768]{1,0:T(8,128)(2,1)S(1)}, u32[]{:S(2)}, u32[]{:S(2)}) collective-permute-start(bf16[144,768]{1,0:T(8,128)(2,1)} %get-tuple-element.256), channel_id=1, source_target_pairs={{0,1},{1,0},{2,3},{3,2},{4,5},{5,4},{6,7},{7,6},{8,9},{9,8},{10,11... | collective-permute-start | bytes 663560 | tf_op jit(solution)/shard_map/ppermute | solution.py:581
  39.5 48.9 %collective-permute-start.27 = (bf16[144,768]{1,0:T(8,128)(2,1)S(1)}, bf16[144,768]{1,0:T(8,128)(2,1)S(1)}, u32[]{:S(2)}, u32[]{:S(2)}) collective-permute-start(bf16[144,768]{1,0:T(8,128)(2,1)S(1)} %get-tuple-element.255), channel_id=1, source_target_pairs={{0,2},{1,3},{2,0},{3,1},{4,6},{5,7},{6,4},{7,5},{8,10},{9,11},{10,... | collective-permute-start | bytes 663560 | tf_op jit(solution)/shard_map/ppermute | solution.py:581
  40.8 47.7 %collective-permute-start.28 = (bf16[144,768]{1,0:T(8,128)(2,1)S(1)}, bf16[144,768]{1,0:T(8,128)(2,1)S(1)}, u32[]{:S(2)}, u32[]{:S(2)}) collective-permute-start(bf16[144,768]{1,0:T(8,128)(2,1)S(1)} %get-tuple-element.254), channel_id=1, source_target_pairs={{0,3},{1,2},{2,1},{3,0},{4,7},{5,6},{6,5},{7,4},{8,11},{9,10},{10,... | collective-permute-start | bytes 663560 | tf_op jit(solution)/shard_map/ppermute | solution.py:581
  153.4 6.6 %copy-start.5 = (bf16[1088,768]{1,0:T(8,128)(2,1)S(1)}, bf16[1088,768]{1,0:T(8,128)(2,1)}, u32[]{:S(2)}) copy-start(bf16[1088,768]{1,0:T(8,128)(2,1)} %get-tuple-element.51) | copy-start | bytes 5013508 | tf_op jit(solution)/shard_map/cond
  155.6 9.7 %copy-start.14 = (bf16[1152,320]{1,0:T(8,128)(2,1)S(1)}, bf16[1152,320]{1,0:T(8,128)(2,1)}, u32[]{:S(2)}) copy-start(bf16[1152,320]{1,0:T(8,128)(2,1)} %get-tuple-element.60.refs_8_) | copy-start | bytes 2211844 | tf_op jit(solution)/shard_map/cond
  155.6 72.4 %all-to-all-start = ((bf16[8,64,768]{2,1,0:T(8,128)(2,1)}), bf16[8,64,768]{2,1,0:T(8,128)(2,1)}, u32[]{:S(2)}, u32[]{:S(2)}) async-start(bf16[8,64,768]{2,1,0:T(8,128)(2,1)} %bitcast), calls=%async_computation | async-start | bytes 1572864 | tf_op jit(solution)/shard_map/cond/branch_1_fun/all_to_all | solution.py:569
  160.9 67.2 %collective-permute-start.2 = (bf16[144,768]{1,0:T(8,128)(2,1)}, bf16[144,768]{1,0:T(8,128)(2,1)S(1)}, u32[]{:S(2)}, u32[]{:S(2)}) collective-permute-start(bf16[144,768]{1,0:T(8,128)(2,1)} %get-tuple-element.234), channel_id=1, source_target_pairs={{0,3},{1,2},{2,1},{3,0},{4,7},{5,6},{6,5},{7,4},{8,11},{9,10},{10,... | collective-permute-start | bytes 663560 | tf_op jit(solution)/shard_map/cond/branch_1_fun/ppermute | solution.py:601
  163.5 64.6 %collective-permute-start.1 = (bf16[144,768]{1,0:T(8,128)(2,1)}, bf16[144,768]{1,0:T(8,128)(2,1)S(1)}, u32[]{:S(2)}, u32[]{:S(2)}) collective-permute-start(bf16[144,768]{1,0:T(8,128)(2,1)} %get-tuple-element.235), channel_id=1, source_target_pairs={{0,2},{1,3},{2,0},{3,1},{4,6},{5,7},{6,4},{7,5},{8,10},{9,11},{10,... | collective-permute-start | bytes 663560 | tf_op jit(solution)/shard_map/cond/branch_1_fun/ppermute | solution.py:601
  163.5 64.6 %collective-permute-start = (bf16[144,768]{1,0:T(8,128)(2,1)S(1)}, bf16[144,768]{1,0:T(8,128)(2,1)S(1)}, u32[]{:S(2)}, u32[]{:S(2)}) collective-permute-start(bf16[144,768]{1,0:T(8,128)(2,1)S(1)} %get-tuple-element.236), channel_id=1, source_target_pairs={{0,1},{1,0},{2,3},{3,2},{4,5},{5,4},{6,7},{7,6},{8,9},{9,8},{10,11... | collective-permute-start | bytes 663560 | tf_op jit(solution)/shard_map/cond/branch_1_fun/ppermute | solution.py:601
  165.3 61.5 %copy-start.26 = (f32[8,768]{1,0:T(8,128)S(1)}, f32[8,768]{1,0:T(8,128)}, u32[]{:S(2)}) copy-start(f32[8,768]{1,0:T(8,128)} %get-tuple-element.68) | copy-start | bytes 73732 | tf_op jit(solution)/shard_map/cond
  244.1 5.0 %collective-permute-start.6 = (bf16[1664,768]{1,0:T(8,128)(2,1)}, bf16[1664,768]{1,0:T(8,128)(2,1)S(1)}, u32[]{:S(2)}, u32[]{:S(2)}) collective-permute-start(bf16[1664,768]{1,0:T(8,128)(2,1)} %dynamic-slice_bitcast_fusion), channel_id=1, source_target_pairs={{0,4},{4,0},{8,12},{12,8},{16,20},{20,16},{24,28},{28,24},{1,5},{5... | collective-permute-start | bytes 7667720 | tf_op jit(solution)/shard_map/cond/branch_1_fun/ppermute | solution.py:654
  252.5 25.6 %collective-permute-start.9 = (bf16[384,768]{1,0:T(8,128)(2,1)}, bf16[384,768]{1,0:T(8,128)(2,1)}, u32[]{:S(2)}, u32[]{:S(2)}) collective-permute-start(bf16[384,768]{1,0:T(8,128)(2,1)} %dynamic-slice_bitcast_fusion.2), channel_id=1, source_target_pairs={{0,16},{4,20},{8,24},{12,28},{16,0},{20,4},{24,8},{28,12},{1,17},{... | collective-permute-start | bytes 1769480 | tf_op jit(solution)/shard_map/cond/branch_1_fun/ppermute | solution.py:654
  255.3 26.1 %collective-permute-start.7 = (bf16[448,768]{1,0:T(8,128)(2,1)}, bf16[448,768]{1,0:T(8,128)(2,1)}, u32[]{:S(2)}, u32[]{:S(2)}) collective-permute-start(bf16[448,768]{1,0:T(8,128)(2,1)} %dynamic-slice_bitcast_fusion.1), channel_id=1, source_target_pairs={{0,8},{4,12},{8,0},{12,4},{16,24},{20,28},{24,16},{28,20},{1,9},{5... | collective-permute-start | bytes 2064392 | tf_op jit(solution)/shard_map/cond/branch_1_fun/ppermute | solution.py:654
  268.1 28.1 %collective-permute-start.5 = (bf16[144,768]{1,0:T(8,128)(2,1)}, bf16[144,768]{1,0:T(8,128)(2,1)}, u32[]{:S(2)}, u32[]{:S(2)}) collective-permute-start(bf16[144,768]{1,0:T(8,128)(2,1)} %get-tuple-element.230), channel_id=1, source_target_pairs={{0,3},{1,2},{2,1},{3,0},{4,7},{5,6},{6,5},{7,4},{8,11},{9,10},{10,... | collective-permute-start | bytes 663560 | tf_op jit(solution)/shard_map/cond/branch_1_fun/ppermute | solution.py:601
  270.9 25.3 %collective-permute-start.4 = (bf16[144,768]{1,0:T(8,128)(2,1)}, bf16[144,768]{1,0:T(8,128)(2,1)}, u32[]{:S(2)}, u32[]{:S(2)}) collective-permute-start(bf16[144,768]{1,0:T(8,128)(2,1)} %get-tuple-element.231), channel_id=1, source_target_pairs={{0,2},{1,3},{2,0},{3,1},{4,6},{5,7},{6,4},{7,5},{8,10},{9,11},{10,... | collective-permute-start | bytes 663560 | tf_op jit(solution)/shard_map/cond/branch_1_fun/ppermute | solution.py:601
  270.9 25.3 %collective-permute-start.3 = (bf16[144,768]{1,0:T(8,128)(2,1)}, bf16[144,768]{1,0:T(8,128)(2,1)}, u32[]{:S(2)}, u32[]{:S(2)}) collective-permute-start(bf16[144,768]{1,0:T(8,128)(2,1)} %get-tuple-element.232), channel_id=1, source_target_pairs={{0,1},{1,0},{2,3},{3,2},{4,5},{5,4},{6,7},{7,6},{8,9},{9,8},{10,11... | collective-permute-start | bytes 663560 | tf_op jit(solution)/shard_map/cond/branch_1_fun/ppermute | solution.py:601
  274.6 21.7 %all-to-all-start.1 = ((bf16[8,64,768]{2,1,0:T(8,128)(2,1)}), bf16[8,64,768]{2,1,0:T(8,128)(2,1)S(1)}, u32[]{:S(2)}, u32[]{:S(2)}) async-start(bf16[8,64,768]{2,1,0:T(8,128)(2,1)} %bitcast.145), calls=%async_computation.1 | async-start | bytes 1572864 | tf_op jit(solution)/shard_map/cond/branch_1_fun/all_to_all | solution.py:569
  279.4 16.7 %collective-permute-start.10 = (bf16[192,768]{1,0:T(8,128)(2,1)S(1)}, bf16[192,768]{1,0:T(8,128)(2,1)S(1)}, u32[]{:S(2)}, u32[]{:S(2)}) collective-permute-start(bf16[192,768]{1,0:T(8,128)(2,1)S(1)} %dynamic-slice_bitcast_fusion.4), channel_id=1, source_target_pairs={{0,8},{4,12},{8,0},{12,4},{16,24},{20,28},{24,16},{28,20},{1,9},{5... | collective-permute-start | bytes 884744 | tf_op jit(solution)/shard_map/cond/branch_1_fun/ppermute | solution.py:654
  282.6 14.4 %copy-start.4 = (bf16[448,768]{1,0:T(8,128)(2,1)}, bf16[448,768]{1,0:T(8,128)(2,1)S(1)}, u32[]{:S(2)}) copy-start(bf16[448,768]{1,0:T(8,128)(2,1)S(1)} %fusion.1) | copy-start | bytes 2064388 | tf_op jit(solution)/shard_map/cond
  282.7 14.4 %collective-permute-start.8 = (bf16[224,768]{1,0:T(8,128)(2,1)S(1)}, bf16[224,768]{1,0:T(8,128)(2,1)S(1)}, u32[]{:S(2)}, u32[]{:S(2)}) collective-permute-start(bf16[224,768]{1,0:T(8,128)(2,1)S(1)} %dynamic-slice_bitcast_fusion.3), channel_id=1, source_target_pairs={{0,16},{4,20},{8,24},{12,28},{16,0},{20,4},{24,8},{28,12},{1,17},{... | collective-permute-start | bytes 1032200 | tf_op jit(solution)/shard_map/cond/branch_1_fun/ppermute | solution.py:654
  300.9 12.1 %collective-permute-start.13 = (bf16[104,768]{1,0:T(8,128)(2,1)S(1)}, bf16[104,768]{1,0:T(8,128)(2,1)S(1)}, u32[]{:S(2)}, u32[]{:S(2)}) collective-permute-start(bf16[104,768]{1,0:T(8,128)(2,1)S(1)} %pad_maximum_fusion.10), channel_id=1, source_target_pairs={{0,3},{1,2},{2,1},{3,0},{4,7},{5,6},{6,5},{7,4},{8,11},{9,10},{10,... | collective-permute-start | bytes 479240 | tf_op jit(solution)/shard_map/cond/branch_1_fun/ppermute | solution.py:679
  303.7 22.1 %collective-permute-start.12 = (bf16[104,768]{1,0:T(8,128)(2,1)S(1)}, bf16[104,768]{1,0:T(8,128)(2,1)S(1)}, u32[]{:S(2)}, u32[]{:S(2)}) collective-permute-start(bf16[104,768]{1,0:T(8,128)(2,1)S(1)} %pad_maximum_fusion.9), channel_id=1, source_target_pairs={{0,2},{1,3},{2,0},{3,1},{4,6},{5,7},{6,4},{7,5},{8,10},{9,11},{10,... | collective-permute-start | bytes 479240 | tf_op jit(solution)/shard_map/cond/branch_1_fun/ppermute | solution.py:679
  303.8 22.0 %collective-permute-start.11 = (bf16[104,768]{1,0:T(8,128)(2,1)S(1)}, bf16[104,768]{1,0:T(8,128)(2,1)S(1)}, u32[]{:S(2)}, u32[]{:S(2)}) collective-permute-start(bf16[104,768]{1,0:T(8,128)(2,1)S(1)} %pad_maximum_fusion.8), channel_id=1, source_target_pairs={{0,1},{1,0},{2,3},{3,2},{4,5},{5,4},{6,7},{7,6},{8,9},{9,8},{10,11... | collective-permute-start | bytes 479240 | tf_op jit(solution)/shard_map/cond/branch_1_fun/ppermute | solution.py:679
  325.9 9.8 %collective-permute-start.16 = (bf16[104,768]{1,0:T(8,128)(2,1)S(1)}, bf16[104,768]{1,0:T(8,128)(2,1)S(1)}, u32[]{:S(2)}, u32[]{:S(2)}) collective-permute-start(bf16[104,768]{1,0:T(8,128)(2,1)S(1)} %add_convert_fusion), channel_id=1, source_target_pairs={{0,3},{1,2},{2,1},{3,0},{4,7},{5,6},{6,5},{7,4},{8,11},{9,10},{10,... | collective-permute-start | bytes 479240 | tf_op jit(solution)/shard_map/cond/branch_1_fun/ppermute | solution.py:686
  327.1 16.8 %collective-permute-start.15 = (bf16[104,768]{1,0:T(8,128)(2,1)S(1)}, bf16[104,768]{1,0:T(8,128)(2,1)S(1)}, u32[]{:S(2)}, u32[]{:S(2)}) collective-permute-start(bf16[104,768]{1,0:T(8,128)(2,1)S(1)} %add_convert_fusion), channel_id=1, source_target_pairs={{0,2},{1,3},{2,0},{3,1},{4,6},{5,7},{6,4},{7,5},{8,10},{9,11},{10,... | collective-permute-start | bytes 479240 | tf_op jit(solution)/shard_map/cond/branch_1_fun/ppermute | solution.py:686
  327.1 18.9 %collective-permute-start.14 = (bf16[104,768]{1,0:T(8,128)(2,1)S(1)}, bf16[104,768]{1,0:T(8,128)(2,1)S(1)}, u32[]{:S(2)}, u32[]{:S(2)}) collective-permute-start(bf16[104,768]{1,0:T(8,128)(2,1)S(1)} %add_convert_fusion), channel_id=1, source_target_pairs={{0,1},{1,0},{2,3},{3,2},{4,5},{5,4},{6,7},{7,6},{8,9},{9,8},{10,11... | collective-permute-start | bytes 479240 | tf_op jit(solution)/shard_map/cond/branch_1_fun/ppermute | solution.py:686
  346.1 9.8 %collective-permute-start.17 = (bf16[4,56,768]{2,1,0:T(8,128)(2,1)S(1)}, bf16[4,56,768]{2,1,0:T(8,128)(2,1)S(1)}, u32[]{:S(2)}, u32[]{:S(2)}) collective-permute-start(bf16[4,56,768]{2,1,0:T(8,128)(2,1)S(1)} %slice.215), channel_id=1, source_target_pairs={{0,16},{4,20},{8,24},{12,28},{16,0},{20,4},{24,8},{28,12},{1,17},{... | collective-permute-start | bytes 1032200 | tf_op jit(solution)/shard_map/cond/branch_1_fun/ppermute | solution.py:694
  347.5 10.9 %collective-permute-start.19 = (bf16[4,48,768]{2,1,0:T(8,128)(2,1)S(1)}, bf16[4,48,768]{2,1,0:T(8,128)(2,1)S(1)}, u32[]{:S(2)}, u32[]{:S(2)}) collective-permute-start(bf16[4,48,768]{2,1,0:T(8,128)(2,1)S(1)} %pad_maximum_fusion.7), channel_id=1, source_target_pairs={{0,8},{4,12},{8,0},{12,4},{16,24},{20,28},{24,16},{28,20},{1,9},{5... | collective-permute-start | bytes 884744 | tf_op jit(solution)/shard_map/cond/branch_1_fun/ppermute | solution.py:694
  356.0 21.6 %collective-permute-start.18 = (bf16[8,56,768]{2,1,0:T(8,128)(2,1)S(1)}, bf16[8,56,768]{2,1,0:T(8,128)(2,1)S(1)}, u32[]{:S(2)}, u32[]{:S(2)}) collective-permute-start(bf16[8,56,768]{2,1,0:T(8,128)(2,1)S(1)} %pad_maximum_fusion.4), channel_id=1, source_target_pairs={{0,8},{4,12},{8,0},{12,4},{16,24},{20,28},{24,16},{28,20},{1,9},{5... | collective-permute-start | bytes 2064392 | tf_op jit(solution)/shard_map/cond/branch_1_fun/ppermute | solution.py:694
  358.6 19.3 %collective-permute-start.20 = (bf16[8,48,768]{2,1,0:T(8,128)(2,1)S(1)}, bf16[8,48,768]{2,1,0:T(8,128)(2,1)S(1)}, u32[]{:S(2)}, u32[]{:S(2)}) collective-permute-start(bf16[8,48,768]{2,1,0:T(8,128)(2,1)S(1)} %pad_maximum_fusion.6), channel_id=1, source_target_pairs={{0,16},{4,20},{8,24},{12,28},{16,0},{20,4},{24,8},{28,12},{1,17},{... | collective-permute-start | bytes 1769480 | tf_op jit(solution)/shard_map/cond/branch_1_fun/ppermute | solution.py:694
  377.8 6.7 %collective-permute-start.21 = (bf16[16,56,768]{2,1,0:T(8,128)(2,1)S(1)}, bf16[16,56,768]{2,1,0:T(8,128)(2,1)}, u32[]{:S(2)}, u32[]{:S(2)}) collective-permute-start(bf16[16,56,768]{2,1,0:T(8,128)(2,1)S(1)} %pad_maximum_fusion), channel_id=1, source_target_pairs={{0,4},{4,0},{8,12},{12,8},{16,20},{20,16},{24,28},{28,24},{1,5},{5... | collective-permute-start | bytes 4128776 | tf_op jit(solution)/shard_map/cond/branch_1_fun/ppermute | solution.py:700
  379.0 5.4 %collective-permute-start.22 = (bf16[16,48,768]{2,1,0:T(8,128)(2,1)}, bf16[16,48,768]{2,1,0:T(8,128)(2,1)}, u32[]{:S(2)}, u32[]{:S(2)}) collective-permute-start(bf16[16,48,768]{2,1,0:T(8,128)(2,1)} %pad_maximum_fusion.1), channel_id=1, source_target_pairs={{0,4},{4,0},{8,12},{12,8},{16,20},{20,16},{24,28},{28,24},{1,5},{5... | collective-permute-start | bytes 3538952 | tf_op jit(solution)/shard_map/cond/branch_1_fun/ppermute | solution.py:700
  (31 other events, 65.1 us)
Sparse Core Ops, SparseCore 0:
  149.4 236.6 all-reduce.9

commit v7 on v6

--- a/solution.py
+++ b/solution.py
@@ -487,30 +487,33 @@
     )(x, d_qkv, out_low, *held)
 
 
-def rows_grad_kernel(dqkv_ref, weight_ref, dmid_ref, drows_ref, sum_ref):
+def rows_grad_kernel(dqkv_ref, q_ref, k_ref, v_ref, dmid_ref, drows_ref, sum_ref):
     step = pl.program_id(0)
 
     @pl.when(step == 0)
     def _():
-        sum_ref[...] = dmid_ref[...]
-
-    sum_ref[...] += against(dqkv_ref[0], weight_ref[0])
+        sum_ref[...] = dmid_ref[...] + against(dqkv_ref[0], q_ref[...])
+
+    @pl.when(step == 1)
+    def _():
+        sum_ref[...] += against(dqkv_ref[0], k_ref[...])
 
     @pl.when(step == 2)
     def _():
-        drows_ref[...] = sum_ref[...].astype(BF)
-
-
-def rows_grad(d_qkv, weights, d_mid):
+        drows_ref[...] = (sum_ref[...] + against(dqkv_ref[0], v_ref[...])).astype(BF)
+
+
+def rows_grad(d_qkv, q_weight, k_weight, v_weight, d_mid):
     _, seq, dim = d_qkv.shape
+
+    def whole(a):
+        return pl.BlockSpec(a.shape, lambda p: (0,) * a.ndim, pipeline_mode=pl.Buffered(1))
+
     return pl.pallas_call(
         rows_grad_kernel,
         grid=(3,),
-        in_specs=[
-            pl.BlockSpec((1, seq, dim), lambda p: (p, 0, 0)),
-            pl.BlockSpec((1, dim, dim), lambda p: (p, 0, 0)),
-            pl.BlockSpec((seq, dim), lambda p: (0, 0), pipeline_mode=pl.Buffered(1)),
-        ],
+        in_specs=[pl.BlockSpec((1, seq, dim), lambda p: (p, 0, 0))]
+        + [whole(a) for a in (q_weight, k_weight, v_weight, d_mid)],
         out_specs=pl.BlockSpec((seq, dim), lambda p: (0, 0)),
         out_shape=jax.ShapeDtypeStruct((seq, dim), BF),
         scratch_shapes=[pltpu.VMEM((seq, dim), F32)],
@@ -518,7 +521,7 @@
         cost_estimate=pl.CostEstimate(
             flops=6 * seq * dim * dim, bytes_accessed=16 * seq * dim, transcendentals=0
         ),
-    )(d_qkv, weights, d_mid)
+    )(d_qkv, q_weight, k_weight, v_weight, d_mid)
 
 
 def bucket_select(table):
@@ -889,7 +892,6 @@
     )
     early = (sums[0], sums[1], sums[2], up_sum, sums[3], sums[4], sums[5])
     down_total, up_total = lax.psum((down_low, up_low), ("wide", "narrow"))
-    qkv_weight = jnp.stack([query_weight, key_weight, value_weight])
 
     def backward():
         text_out = swap_text(final_low[:TEXT].reshape(wide, -1, dim)).reshape(text_shape)
@@ -900,7 +902,7 @@
         )
         room = room_for(4 * dim, wide, narrow)
         tail, d_sums = qkv_sums(room, [text_out, *out_pieces[1:]], rows_in, d_qkv, out_low)
-        d_rows = rows_grad(d_qkv, qkv_weight, d_mid)
+        d_rows = rows_grad(d_qkv, query_weight, key_weight, value_weight, d_mid)
         text_grad = swap_text(d_rows[:TEXT].reshape(wide, -1, dim)).reshape(text_shape)
         grad_pieces = patch_away(d_rows[TEXT:], narrow)
         late = (

time: 423 us -> 419 us (level)
  transfers between devices with their start and end apart: 34 -> 34, of which waited for: 11 -> 11; matrix products, arithmetic and copies ran while one was open for 11% -> 10% of each run, Pallas kernels for 31% -> 31%
where the time goes in v7:
time: 419 us; the launch traced here: 413 us
  Pallas kernels  203 us (48%)
  waiting for transfers between devices  79 us (19%)
  starting transfers between devices  59.6 us (14%)
  local copies, waits for them, and re-layouts  35.1 us (8%)
  other arithmetic  17.7 us (4%)
  between operations  16.1 us (4%)
    pallas_call x1, Pallas kernels, attend_back(): pl.pallas_call(partial(attend_back_kernel, len(held)), grid=(pairs,), in_...  60.6 us
    pallas_call x1, Pallas kernels, rows_pass(): pl.pallas_call(partial(rows_kernel, len(pieces), blocks), grid=(blocks +...  59.9 us
    pallas_call x1, Pallas kernels, attend(): pl.pallas_call(partial(attend_kernel, len(pieces)), grid=(HEADS // 2,), i...  46.5 us
    ppermute x4, waiting for transfers between devices, gather_wide(): lax.ppermute(a, 'wide', flip_pairs(wide, 1 << order[i]))  25.6 us
    ppermute x3, waiting for transfers between devices, narrow_step(): lax.ppermute(picked(me ^ k), 'narrow', flip_pairs(narrow, k))  19.1 us
    ppermute x5, waiting for transfers between devices, wide_step(): lax.ppermute(pick(parts, 1 - me), 'wide', flip_pairs(wide, 1 << bit))  17.7 us
    all_to_all x4, starting transfers between devices, swap_text(): lax.all_to_all(parts, 'wide', split_axis=0, concat_axis=0, tiled=True)  17.3 us
    ppermute x3, waiting for transfers between devices, gather_narrow(): lax.ppermute(part, 'narrow', flip_pairs(narrow, k))  15.1 us
  transfers between devices with their start and end apart: 34, of which 11 were waited for; matrix products, arithmetic and copies ran while one was open for 10% of the time, Pallas kernels for 31%

profile of v7, /device:TPU:0, one launch (start us, length us, event | category | flops | bytes accessed | tf_op | source)
XLA Modules:
  0.0 413.0 jit_solution(5310806946040432694)
XLA Ops:
  7.3 5.3 %all-to-all-start.2 = ((bf16[8,64,768]{2,1,0:T(8,128)(2,1)}), bf16[8,64,768]{2,1,0:T(8,128)(2,1)S(1)}, u32[]{:S(2)}, u32[]{:S(2)}) async-start(bf16[8,64,768]{2,1,0:T(8,128)(2,1)} %bitcast.151), calls=%async_computation.2 | async-start | bytes 1572864 | tf_op jit(solution)/shard_map/all_to_all | solution.py:572
  13.5 1.6 collective-permute-start.23
  15.0 2.6 collective-permute-start.24
  29.9 4.2 %all-to-all-start.3 = ((bf16[8,64,768]{2,1,0:T(8,128)(2,1)}), bf16[8,64,768]{2,1,0:T(8,128)(2,1)}, u32[]{:S(2)}, u32[]{:S(2)}) async-start(bf16[8,64,768]{2,1,0:T(8,128)(2,1)} %bitcast.50), calls=%async_computation.3 | async-start | bytes 1572864 | tf_op jit(solution)/shard_map/all_to_all | solution.py:572
  35.2 4.2 %collective-permute-start.26 = (bf16[144,768]{1,0:T(8,128)(2,1)S(1)}, bf16[144,768]{1,0:T(8,128)(2,1)S(1)}, u32[]{:S(2)}, u32[]{:S(2)}) collective-permute-start(bf16[144,768]{1,0:T(8,128)(2,1)S(1)} %get-tuple-element.262), channel_id=1, source_target_pairs={{0,1},{1,0},{2,3},{3,2},{4,5},{5,4},{6,7},{7,6},{8,9},{9,8},{10,11... | collective-permute-start | bytes 663560 | tf_op jit(solution)/shard_map/ppermute | solution.py:584
  40.4 1.5 collective-permute-start.28
  41.8 46.5 %shard_map.426 = (bf16[12,1088,1152]{2,1,0:T(8,128)(2,1)}, bf16[768,1152]{1,0:T(8,128)(2,1)}, bf16[1088,768]{1,0:T(8,128)(2,1)}, f32[12,1,1152]{2,1,0:T(1,128)},...) custom-call(bf16[512,768]{1,0:T(8,128)(2,1)} %bitcast.152, ...), custom_call_target="tpu_custom_call" | custom-call | flops 61605937152 | bytes 30081024 | tf_op jit(solution)/shard_map/pallas_call | solution.py:108
  89.2 59.9 %shard_map.427 = (bf16[1088,768]{1,0:T(8,128)(2,1)}, f32[1088,768]{1,0:T(8,128)}, bf16[1088,768]{1,0:T(8,128)(2,1)}, bf16[768,3072]{1,0:T(8,128)(2,1)}, bf16[307...) custom-call(bf16[512,768]{1,0:T(8,128)(2,1)} %bitcast.51.refs_0_, ...), custom_call_target="tpu_custom_call" | custom-call | flops 35936796672 | bytes 53477376 | tf_op jit(solution)/shard_map/pallas_call | solution.py:400
  150.7 229.4 %conditional.1 = (bf16[8,1,64,768]{3,2,1,0:T(8,128)(2,1)}, bf16[1,4,144,768]{3,2,1,0:T(8,128)(2,1)}, bf16[8,1,64,768]{3,2,1,0:T(8,128)(2,1)S(1)}, bf16[1,4,144,7...) conditional(s32[]{:T(128)} %convert_element_type.129, () %tuple.18, ...), branch_computations={%region_0.1_spmd, %region_1.2_spmd} | conditional | flops 70616072192 | bytes 206675008 | solution.py:933
  150.7 2.2 slice.131
  152.9 4.3 %all-to-all-start = ((bf16[8,64,768]{2,1,0:T(8,128)(2,1)}), bf16[8,64,768]{2,1,0:T(8,128)(2,1)}, u32[]{:S(2)}, u32[]{:S(2)}) async-start(bf16[8,64,768]{2,1,0:T(8,128)(2,1)} %bitcast), calls=%async_computation | async-start | bytes 1572864 | tf_op jit(solution)/shard_map/cond/branch_1_fun/all_to_all | solution.py:572
  158.0 2.3 collective-permute-start.2
  160.5 1.9 collective-permute-start
  162.4 60.6 %branch_1_fun.4 = (bf16[3,1088,768]{2,1,0:T(8,128)(2,1)}, f32[12,3,256]{2,1,0:T(4,128)}) custom-call(bf16[12,1088,1152]{2,1,0:T(8,128)(2,1)} %get-tuple-element.56.refs_0_, bf16[768,1152]{1,0:T(8,128)(2,1)} %get-tuple-element.57.refs_1_, f32[12,1,1152]{2,1,0:T(1,128)S(1)} %get-tuple-element.58.refs_2_, bf16[1088,768]{1,0:T(8,128)(2,1)} %get-tuple-element.59.refs_3_, ...), custom_call_target="tpu_custom_call" | custom-call | flops 61605937152 | bytes 30081024 | tf_op jit(solution)/shard_map/cond/branch_1_fun/pallas_call | solution.py:242
  226.2 9.8 %branch_1_fun.6 = (bf16[3328,768]{1,0:T(8,128)(2,1)}, f32[3,8,768]{2,1,0:T(8,128)}) custom-call(bf16[1088,768]{1,0:T(8,128)(2,1)} %get-tuple-element.71.x_ref, bf16[3,1088,768]{2,1,0:T(8,128)(2,1)} %get-tuple-element.66.dqkv_ref, bf16[768,768]{1,0:T(8,128)(2,1)} %get-tuple-element.72.out_ref, bf16[8,1,64,768]{3,2,1,0:T(8,128)(2,1)} %bitcast.1.refs_0_, ...), custom_call_target="tpu_custom_call" | custom-call | flops 5133828096 | bytes 20054016 | tf_op jit(solution)/shard_map/cond/branch_1_fun/pallas_call | solution.py:468
  238.0 3.5 dynamic-slice_bitcast_fusion
  241.4 5.0 %collective-permute-done.6 = bf16[1664,768]{1,0:T(8,128)(2,1)S(1)} collective-permute-done((bf16[1664,768]{1,0:T(8,128)(2,1)}, bf16[1664,768]{1,0:T(8,128)(2,1)S(1)}, u32[]{:S(2)}, u32[]{:S(2)}) %collective-permute-start.6) | collective-permute-done | bytes 2555936 | tf_op jit(solution)/shard_map/cond/branch_1_fun/ppermute | solution.py:657
  246.5 2.4 fusion
  249.9 1.8 collective-permute-start.9
  252.6 1.3 collective-permute-start.7
  253.9 9.3 %branch_1_fun.5 = bf16[1088,768]{1,0:T(8,128)(2,1)} custom-call(bf16[3,1088,768]{2,1,0:T(8,128)(2,1)} %get-tuple-element.66.dqkv_ref, bf16[768,768]{1,0:T(8,128)(2,1)} %get-tuple-element.67.q_ref, bf16[768,768]{1,0:T(8,128)(2,1)} %get-tuple-element.68.k_ref, bf16[768,768]{1,0:T(8,128)(2,1)} %get-tuple-element.69.v_ref, f32[1088,768]{1,0:T(8,128)} %get-tuple-element.70.dmid_ref), custom_call_target="tpu_custom_call" | custom-call | flops 3850371072 | bytes 13369344 | tf_op jit(solution)/shard_map/cond/branch_1_fun/pallas_call | solution.py:512
  263.2 2.2 slice_bitcast_fusion
  265.4 2.9 collective-permute-start.5
  268.3 1.5 collective-permute-start.3
  269.8 2.1 slice.204
  271.9 3.5 all-to-all-start.1
  276.7 2.0 collective-permute-start.10
  280.0 1.6 collective-permute-start.8
  281.6 11.9 %collective-permute-done.10 = bf16[192,768]{1,0:T(8,128)(2,1)S(1)} collective-permute-done((bf16[192,768]{1,0:T(8,128)(2,1)S(1)}, bf16[192,768]{1,0:T(8,128)(2,1)S(1)}, u32[]{:S(2)}, u32[]{:S(2)}) %collective-permute-start.10) | collective-permute-done | bytes 294944 | tf_op jit(solution)/shard_map/cond/branch_1_fun/ppermute | solution.py:657
  295.1 2.0 branch_1_fun.7
  298.2 3.0 collective-permute-start.13
  301.3 1.5 collective-permute-start.11
  302.8 7.2 %collective-permute-done.13 = bf16[104,768]{1,0:T(8,128)(2,1)S(1)} collective-permute-done((bf16[104,768]{1,0:T(8,128)(2,1)S(1)}, bf16[104,768]{1,0:T(8,128)(2,1)S(1)}, u32[]{:S(2)}, u32[]{:S(2)}) %collective-permute-start.13) | collective-permute-done | bytes 159776 | tf_op jit(solution)/shard_map/cond/branch_1_fun/ppermute | solution.py:682
  310.1 11.8 %collective-permute-done.12 = bf16[104,768]{1,0:T(8,128)(2,1)S(1)} collective-permute-done((bf16[104,768]{1,0:T(8,128)(2,1)S(1)}, bf16[104,768]{1,0:T(8,128)(2,1)S(1)}, u32[]{:S(2)}, u32[]{:S(2)}) %collective-permute-start.12) | collective-permute-done | bytes 159776 | tf_op jit(solution)/shard_map/cond/branch_1_fun/ppermute | solution.py:682
  323.0 3.5 collective-permute-start.14
  326.5 5.8 %collective-permute-done.16 = bf16[104,768]{1,0:T(8,128)(2,1)S(1)} collective-permute-done((bf16[104,768]{1,0:T(8,128)(2,1)S(1)}, bf16[104,768]{1,0:T(8,128)(2,1)S(1)}, u32[]{:S(2)}, u32[]{:S(2)}) %collective-permute-start.16) | collective-permute-done | bytes 159776 | tf_op jit(solution)/shard_map/cond/branch_1_fun/ppermute | solution.py:689
  332.2 7.3 %collective-permute-done.15 = bf16[104,768]{1,0:T(8,128)(2,1)S(1)} collective-permute-done((bf16[104,768]{1,0:T(8,128)(2,1)S(1)}, bf16[104,768]{1,0:T(8,128)(2,1)S(1)}, u32[]{:S(2)}, u32[]{:S(2)}) %collective-permute-start.15) | collective-permute-done | bytes 159776 | tf_op jit(solution)/shard_map/cond/branch_1_fun/ppermute | solution.py:689
  339.5 2.1 collective-permute-done.14
  341.7 1.8 collective-permute-start.17
  343.6 1.8 collective-permute-start.19
  345.4 8.3 %collective-permute-done.17 = bf16[4,56,768]{2,1,0:T(8,128)(2,1)S(1)} collective-permute-done((bf16[4,56,768]{2,1,0:T(8,128)(2,1)S(1)}, bf16[4,56,768]{2,1,0:T(8,128)(2,1)S(1)}, u32[]{:S(2)}, u32[]{:S(2)}) %collective-permute-start.17) | collective-permute-done | bytes 344096 | tf_op jit(solution)/shard_map/cond/branch_1_fun/ppermute | solution.py:697
  353.7 1.6 collective-permute-start.18
  356.1 17.2 %collective-permute-done.18 = bf16[8,56,768]{2,1,0:T(8,128)(2,1)S(1)} collective-permute-done((bf16[8,56,768]{2,1,0:T(8,128)(2,1)S(1)}, bf16[8,56,768]{2,1,0:T(8,128)(2,1)S(1)}, u32[]{:S(2)}, u32[]{:S(2)}) %collective-permute-start.18) | collective-permute-done | bytes 688160 | tf_op jit(solution)/shard_map/cond/branch_1_fun/ppermute | solution.py:697
  375.3 1.3 pad_maximum_fusion.3
  380.2 1.5 all-reduce.10.cloned.1.call-done
  381.7 14.4 %shard_map.428 = (f32[768,768]{1,0:T(8,128)}, f32[768,768]{1,0:T(8,128)}, f32[768,768]{1,0:T(8,128)}, f32[768,768]{1,0:T(8,128)}, f32[32,768]{1,0:T(8,128)}, /*index=5*/f32[768,3072]{1,0:T(8,128)}, f32[3072,768]{1,0:T(8,128)}) custom-call(s32[3,16]{1,0:T(4,128)} %add_add_fusion.index_ref, bf16[768,3072]{1,0:T(8,128)(2,1)} %get-tuple-element.233.up_ref, ...), custom_call_target="tpu_custom_call" | custom-call | bytes 47382528 | tf_op jit(solution)/shard_map/pallas_call | solution.py:754
  396.1 1.6 slice_reduce_fusion.3
  403.0 2.1 copy.106
  (227 shorter events, 42.8 us)
Async XLA Ops:
  7.2 5.4 %copy-start.8 = (bf16[1,4,144,768]{3,2,1,0:T(8,128)(2,1)S(1)}, bf16[1,4,144,768]{3,2,1,0:T(8,128)(2,1)}, u32[]{:S(2)}) copy-start(bf16[1,4,144,768]{3,2,1,0:T(8,128)(2,1)} %param.30) | copy-start | bytes 2654212
  7.2 12.0 %copy-start.17 = (s32[1,1,1088]{2,1,0:T(1,128)S(1)}, s32[1,1,1088]{2,1,0:T(1,128)}, u32[]{:S(2)}) copy-start(s32[1,1,1088]{2,1,0:T(1,128)} %param.35) | copy-start | bytes 13060
  7.2 12.0 %copy-start.18 = (s32[1,1,1088]{2,1,0:T(1,128)S(1)}, s32[1,1,1088]{2,1,0:T(1,128)}, u32[]{:S(2)}) copy-start(s32[1,1,1088]{2,1,0:T(1,128)} %param.34) | copy-start | bytes 13060
  7.2 12.0 %copy-start.19 = (s32[1,1,1088]{2,1,0:T(1,128)S(1)}, s32[1,1,1088]{2,1,0:T(1,128)}, u32[]{:S(2)}) copy-start(s32[1,1,1088]{2,1,0:T(1,128)} %param.33) | copy-start | bytes 13060
  7.2 12.4 %copy-start.20 = (f32[768]{0:T(1024)S(1)}, f32[768]{0:T(1024)}, u32[]{:S(2)}) copy-start(f32[768]{0:T(1024)} %param.40) | copy-start | bytes 9220
  7.2 12.4 %copy-start.21 = (f32[768]{0:T(1024)S(1)}, f32[768]{0:T(1024)}, u32[]{:S(2)}) copy-start(f32[768]{0:T(1024)} %param.37) | copy-start | bytes 9220
  7.3 22.6 %all-to-all-start.2 = ((bf16[8,64,768]{2,1,0:T(8,128)(2,1)}), bf16[8,64,768]{2,1,0:T(8,128)(2,1)S(1)}, u32[]{:S(2)}, u32[]{:S(2)}) async-start(bf16[8,64,768]{2,1,0:T(8,128)(2,1)} %bitcast.151), calls=%async_computation.2 | async-start | bytes 1572864 | tf_op jit(solution)/shard_map/all_to_all | solution.py:572
  12.6 9.0 %copy-start.31 = (f32[33,12]{0,1:T(8,128)S(1)}, f32[33,12]{0,1:T(8,128)}, u32[]{:S(2)}) copy-start(f32[33,12]{0,1:T(8,128)} %param.51) | copy-start | bytes 4756
  12.6 10.1 %copy-start.32 = (f32[65,12]{0,1:T(8,128)S(1)}, f32[65,12]{0,1:T(8,128)}, u32[]{:S(2)}) copy-start(f32[65,12]{0,1:T(8,128)} %param.52) | copy-start | bytes 9364
  13.5 20.9 %collective-permute-start.23 = (bf16[144,768]{1,0:T(8,128)(2,1)}, bf16[144,768]{1,0:T(8,128)(2,1)}, u32[]{:S(2)}, u32[]{:S(2)}) collective-permute-start(bf16[144,768]{1,0:T(8,128)(2,1)} %get-tuple-element.265), channel_id=1, source_target_pairs={{0,1},{1,0},{2,3},{3,2},{4,5},{5,4},{6,7},{7,6},{8,9},{9,8},{10,11... | collective-permute-start | bytes 663560 | tf_op jit(solution)/shard_map/ppermute | solution.py:584
  15.0 19.3 %collective-permute-start.24 = (bf16[144,768]{1,0:T(8,128)(2,1)}, bf16[144,768]{1,0:T(8,128)(2,1)}, u32[]{:S(2)}, u32[]{:S(2)}) collective-permute-start(bf16[144,768]{1,0:T(8,128)(2,1)} %get-tuple-element.267), channel_id=1, source_target_pairs={{0,2},{1,3},{2,0},{3,1},{4,6},{5,7},{6,4},{7,5},{8,10},{9,11},{10,... | collective-permute-start | bytes 663560 | tf_op jit(solution)/shard_map/ppermute | solution.py:584
  17.6 16.8 %collective-permute-start.25 = (bf16[144,768]{1,0:T(8,128)(2,1)S(1)}, bf16[144,768]{1,0:T(8,128)(2,1)}, u32[]{:S(2)}, u32[]{:S(2)}) collective-permute-start(bf16[144,768]{1,0:T(8,128)(2,1)S(1)} %get-tuple-element.264), channel_id=1, source_target_pairs={{0,3},{1,2},{2,1},{3,0},{4,7},{5,6},{6,5},{7,4},{8,11},{9,10},{10,... | collective-permute-start | bytes 663560 | tf_op jit(solution)/shard_map/ppermute | solution.py:584
  28.1 6.2 %copy-start.9 = (bf16[1,4,144,768]{3,2,1,0:T(8,128)(2,1)S(1)}, bf16[1,4,144,768]{3,2,1,0:T(8,128)(2,1)}, u32[]{:S(2)}) copy-start(bf16[1,4,144,768]{3,2,1,0:T(8,128)(2,1)} %param.55) | copy-start | bytes 2654212
  29.9 5.3 %copy-start.10 = (bf16[8,64,768]{2,1,0:T(8,128)(2,1)}, bf16[8,64,768]{2,1,0:T(8,128)(2,1)S(1)}, u32[]{:S(2)}) copy-start(bf16[8,64,768]{2,1,0:T(8,128)(2,1)S(1)} %all-to-all-done.2) | copy-start | bytes 2359300
  29.9 58.5 %all-to-all-start.3 = ((bf16[8,64,768]{2,1,0:T(8,128)(2,1)}), bf16[8,64,768]{2,1,0:T(8,128)(2,1)}, u32[]{:S(2)}, u32[]{:S(2)}) async-start(bf16[8,64,768]{2,1,0:T(8,128)(2,1)} %bitcast.50), calls=%async_computation.3 | async-start | bytes 1572864 | tf_op jit(solution)/shard_map/all_to_all | solution.py:572
  34.1 347.6 %all-reduce.10.cloned.1.call-start = ((), (), s32[]{:S(2)}) async-start(), calls=%async_computation.4 | async-start | bytes 18874368 | tf_op jit(solution)/shard_map/psum | solution.py:894
  35.2 53.2 %collective-permute-start.26 = (bf16[144,768]{1,0:T(8,128)(2,1)S(1)}, bf16[144,768]{1,0:T(8,128)(2,1)S(1)}, u32[]{:S(2)}, u32[]{:S(2)}) collective-permute-start(bf16[144,768]{1,0:T(8,128)(2,1)S(1)} %get-tuple-element.262), channel_id=1, source_target_pairs={{0,1},{1,0},{2,3},{3,2},{4,5},{5,4},{6,7},{7,6},{8,9},{9,8},{10,11... | collective-permute-start | bytes 663560 | tf_op jit(solution)/shard_map/ppermute | solution.py:584
  39.4 49.0 %collective-permute-start.27 = (bf16[144,768]{1,0:T(8,128)(2,1)S(1)}, bf16[144,768]{1,0:T(8,128)(2,1)S(1)}, u32[]{:S(2)}, u32[]{:S(2)}) collective-permute-start(bf16[144,768]{1,0:T(8,128)(2,1)S(1)} %get-tuple-element.261), channel_id=1, source_target_pairs={{0,2},{1,3},{2,0},{3,1},{4,6},{5,7},{6,4},{7,5},{8,10},{9,11},{10,... | collective-permute-start | bytes 663560 | tf_op jit(solution)/shard_map/ppermute | solution.py:584
  40.4 48.0 %collective-permute-start.28 = (bf16[144,768]{1,0:T(8,128)(2,1)S(1)}, bf16[144,768]{1,0:T(8,128)(2,1)S(1)}, u32[]{:S(2)}, u32[]{:S(2)}) collective-permute-start(bf16[144,768]{1,0:T(8,128)(2,1)S(1)} %get-tuple-element.260), channel_id=1, source_target_pairs={{0,3},{1,2},{2,1},{3,0},{4,7},{5,6},{6,5},{7,4},{8,11},{9,10},{10,... | collective-permute-start | bytes 663560 | tf_op jit(solution)/shard_map/ppermute | solution.py:584
  150.7 6.5 %copy-start.5 = (bf16[1088,768]{1,0:T(8,128)(2,1)S(1)}, bf16[1088,768]{1,0:T(8,128)(2,1)}, u32[]{:S(2)}) copy-start(bf16[1088,768]{1,0:T(8,128)(2,1)} %get-tuple-element.55) | copy-start | bytes 5013508 | tf_op jit(solution)/shard_map/cond
  152.9 72.5 %all-to-all-start = ((bf16[8,64,768]{2,1,0:T(8,128)(2,1)}), bf16[8,64,768]{2,1,0:T(8,128)(2,1)}, u32[]{:S(2)}, u32[]{:S(2)}) async-start(bf16[8,64,768]{2,1,0:T(8,128)(2,1)} %bitcast), calls=%async_computation | async-start | bytes 1572864 | tf_op jit(solution)/shard_map/cond/branch_1_fun/all_to_all | solution.py:572
  158.0 67.4 %collective-permute-start.2 = (bf16[144,768]{1,0:T(8,128)(2,1)S(1)}, bf16[144,768]{1,0:T(8,128)(2,1)S(1)}, u32[]{:S(2)}, u32[]{:S(2)}) collective-permute-start(bf16[144,768]{1,0:T(8,128)(2,1)S(1)} %get-tuple-element.240), channel_id=1, source_target_pairs={{0,3},{1,2},{2,1},{3,0},{4,7},{5,6},{6,5},{7,4},{8,11},{9,10},{10,... | collective-permute-start | bytes 663560 | tf_op jit(solution)/shard_map/cond/branch_1_fun/ppermute | solution.py:604
  160.3 65.1 %collective-permute-start.1 = (bf16[144,768]{1,0:T(8,128)(2,1)S(1)}, bf16[144,768]{1,0:T(8,128)(2,1)S(1)}, u32[]{:S(2)}, u32[]{:S(2)}) collective-permute-start(bf16[144,768]{1,0:T(8,128)(2,1)S(1)} %get-tuple-element.241), channel_id=1, source_target_pairs={{0,2},{1,3},{2,0},{3,1},{4,6},{5,7},{6,4},{7,5},{8,10},{9,11},{10,... | collective-permute-start | bytes 663560 | tf_op jit(solution)/shard_map/cond/branch_1_fun/ppermute | solution.py:604
  160.5 64.9 %collective-permute-start = (bf16[144,768]{1,0:T(8,128)(2,1)S(1)}, bf16[144,768]{1,0:T(8,128)(2,1)S(1)}, u32[]{:S(2)}, u32[]{:S(2)}) collective-permute-start(bf16[144,768]{1,0:T(8,128)(2,1)S(1)} %get-tuple-element.242), channel_id=1, source_target_pairs={{0,1},{1,0},{2,3},{3,2},{4,5},{5,4},{6,7},{7,6},{8,9},{9,8},{10,11... | collective-permute-start | bytes 663560 | tf_op jit(solution)/shard_map/cond/branch_1_fun/ppermute | solution.py:604
  241.4 5.0 %collective-permute-start.6 = (bf16[1664,768]{1,0:T(8,128)(2,1)}, bf16[1664,768]{1,0:T(8,128)(2,1)S(1)}, u32[]{:S(2)}, u32[]{:S(2)}) collective-permute-start(bf16[1664,768]{1,0:T(8,128)(2,1)} %dynamic-slice_bitcast_fusion), channel_id=1, source_target_pairs={{0,4},{4,0},{8,12},{12,8},{16,20},{20,16},{24,28},{28,24},{1,5},{5... | collective-permute-start | bytes 7667720 | tf_op jit(solution)/shard_map/cond/branch_1_fun/ppermute | solution.py:657
  249.9 25.6 %collective-permute-start.9 = (bf16[384,768]{1,0:T(8,128)(2,1)}, bf16[384,768]{1,0:T(8,128)(2,1)}, u32[]{:S(2)}, u32[]{:S(2)}) collective-permute-start(bf16[384,768]{1,0:T(8,128)(2,1)} %dynamic-slice_bitcast_fusion.2), channel_id=1, source_target_pairs={{0,16},{4,20},{8,24},{12,28},{16,0},{20,4},{24,8},{28,12},{1,17},{... | collective-permute-start | bytes 1769480 | tf_op jit(solution)/shard_map/cond/branch_1_fun/ppermute | solution.py:657
  252.6 26.1 %collective-permute-start.7 = (bf16[448,768]{1,0:T(8,128)(2,1)}, bf16[448,768]{1,0:T(8,128)(2,1)}, u32[]{:S(2)}, u32[]{:S(2)}) collective-permute-start(bf16[448,768]{1,0:T(8,128)(2,1)} %dynamic-slice_bitcast_fusion.1), channel_id=1, source_target_pairs={{0,8},{4,12},{8,0},{12,4},{16,24},{20,28},{24,16},{28,20},{1,9},{5... | collective-permute-start | bytes 2064392 | tf_op jit(solution)/shard_map/cond/branch_1_fun/ppermute | solution.py:657
  265.4 28.1 %collective-permute-start.5 = (bf16[144,768]{1,0:T(8,128)(2,1)}, bf16[144,768]{1,0:T(8,128)(2,1)}, u32[]{:S(2)}, u32[]{:S(2)}) collective-permute-start(bf16[144,768]{1,0:T(8,128)(2,1)} %get-tuple-element.236), channel_id=1, source_target_pairs={{0,3},{1,2},{2,1},{3,0},{4,7},{5,6},{6,5},{7,4},{8,11},{9,10},{10,... | collective-permute-start | bytes 663560 | tf_op jit(solution)/shard_map/cond/branch_1_fun/ppermute | solution.py:604
  268.3 25.2 %collective-permute-start.4 = (bf16[144,768]{1,0:T(8,128)(2,1)}, bf16[144,768]{1,0:T(8,128)(2,1)}, u32[]{:S(2)}, u32[]{:S(2)}) collective-permute-start(bf16[144,768]{1,0:T(8,128)(2,1)} %get-tuple-element.237), channel_id=1, source_target_pairs={{0,2},{1,3},{2,0},{3,1},{4,6},{5,7},{6,4},{7,5},{8,10},{9,11},{10,... | collective-permute-start | bytes 663560 | tf_op jit(solution)/shard_map/cond/branch_1_fun/ppermute | solution.py:604
  268.3 25.2 %collective-permute-start.3 = (bf16[144,768]{1,0:T(8,128)(2,1)}, bf16[144,768]{1,0:T(8,128)(2,1)}, u32[]{:S(2)}, u32[]{:S(2)}) collective-permute-start(bf16[144,768]{1,0:T(8,128)(2,1)} %get-tuple-element.238), channel_id=1, source_target_pairs={{0,1},{1,0},{2,3},{3,2},{4,5},{5,4},{6,7},{7,6},{8,9},{9,8},{10,11... | collective-permute-start | bytes 663560 | tf_op jit(solution)/shard_map/cond/branch_1_fun/ppermute | solution.py:604
  271.9 21.7 %all-to-all-start.1 = ((bf16[8,64,768]{2,1,0:T(8,128)(2,1)}), bf16[8,64,768]{2,1,0:T(8,128)(2,1)S(1)}, u32[]{:S(2)}, u32[]{:S(2)}) async-start(bf16[8,64,768]{2,1,0:T(8,128)(2,1)} %bitcast.142), calls=%async_computation.1 | async-start | bytes 1572864 | tf_op jit(solution)/shard_map/cond/branch_1_fun/all_to_all | solution.py:572
  276.7 16.7 %collective-permute-start.10 = (bf16[192,768]{1,0:T(8,128)(2,1)S(1)}, bf16[192,768]{1,0:T(8,128)(2,1)S(1)}, u32[]{:S(2)}, u32[]{:S(2)}) collective-permute-start(bf16[192,768]{1,0:T(8,128)(2,1)S(1)} %dynamic-slice_bitcast_fusion.4), channel_id=1, source_target_pairs={{0,8},{4,12},{8,0},{12,4},{16,24},{20,28},{24,16},{28,20},{1,9},{5... | collective-permute-start | bytes 884744 | tf_op jit(solution)/shard_map/cond/branch_1_fun/ppermute | solution.py:657
  279.9 14.4 %copy-start.4 = (bf16[448,768]{1,0:T(8,128)(2,1)}, bf16[448,768]{1,0:T(8,128)(2,1)S(1)}, u32[]{:S(2)}) copy-start(bf16[448,768]{1,0:T(8,128)(2,1)S(1)} %fusion.1) | copy-start | bytes 2064388 | tf_op jit(solution)/shard_map/cond
  280.0 14.4 %collective-permute-start.8 = (bf16[224,768]{1,0:T(8,128)(2,1)S(1)}, bf16[224,768]{1,0:T(8,128)(2,1)S(1)}, u32[]{:S(2)}, u32[]{:S(2)}) collective-permute-start(bf16[224,768]{1,0:T(8,128)(2,1)S(1)} %dynamic-slice_bitcast_fusion.3), channel_id=1, source_target_pairs={{0,16},{4,20},{8,24},{12,28},{16,0},{20,4},{24,8},{28,12},{1,17},{... | collective-permute-start | bytes 1032200 | tf_op jit(solution)/shard_map/cond/branch_1_fun/ppermute | solution.py:657
  293.6 4.6 %copy-start = (bf16[8,64,768]{2,1,0:T(8,128)(2,1)}, bf16[8,64,768]{2,1,0:T(8,128)(2,1)S(1)}, u32[]{:S(2)}) copy-start(bf16[8,64,768]{2,1,0:T(8,128)(2,1)S(1)} %all-to-all-done.1) | copy-start | bytes 2359300 | tf_op jit(solution)/shard_map/cond
  298.2 11.9 %collective-permute-start.13 = (bf16[104,768]{1,0:T(8,128)(2,1)S(1)}, bf16[104,768]{1,0:T(8,128)(2,1)S(1)}, u32[]{:S(2)}, u32[]{:S(2)}) collective-permute-start(bf16[104,768]{1,0:T(8,128)(2,1)S(1)} %pad_maximum_fusion.10), channel_id=1, source_target_pairs={{0,3},{1,2},{2,1},{3,0},{4,7},{5,6},{6,5},{7,4},{8,11},{9,10},{10,... | collective-permute-start | bytes 479240 | tf_op jit(solution)/shard_map/cond/branch_1_fun/ppermute | solution.py:682
  301.2 20.7 %collective-permute-start.12 = (bf16[104,768]{1,0:T(8,128)(2,1)S(1)}, bf16[104,768]{1,0:T(8,128)(2,1)S(1)}, u32[]{:S(2)}, u32[]{:S(2)}) collective-permute-start(bf16[104,768]{1,0:T(8,128)(2,1)S(1)} %pad_maximum_fusion.9), channel_id=1, source_target_pairs={{0,2},{1,3},{2,0},{3,1},{4,6},{5,7},{6,4},{7,5},{8,10},{9,11},{10,... | collective-permute-start | bytes 479240 | tf_op jit(solution)/shard_map/cond/branch_1_fun/ppermute | solution.py:682
  301.3 20.6 %collective-permute-start.11 = (bf16[104,768]{1,0:T(8,128)(2,1)S(1)}, bf16[104,768]{1,0:T(8,128)(2,1)S(1)}, u32[]{:S(2)}, u32[]{:S(2)}) collective-permute-start(bf16[104,768]{1,0:T(8,128)(2,1)S(1)} %pad_maximum_fusion.8), channel_id=1, source_target_pairs={{0,1},{1,0},{2,3},{3,2},{4,5},{5,4},{6,7},{7,6},{8,9},{9,8},{10,11... | collective-permute-start | bytes 479240 | tf_op jit(solution)/shard_map/cond/branch_1_fun/ppermute | solution.py:682
  322.0 10.2 %collective-permute-start.16 = (bf16[104,768]{1,0:T(8,128)(2,1)S(1)}, bf16[104,768]{1,0:T(8,128)(2,1)S(1)}, u32[]{:S(2)}, u32[]{:S(2)}) collective-permute-start(bf16[104,768]{1,0:T(8,128)(2,1)S(1)} %add_convert_fusion), channel_id=1, source_target_pairs={{0,3},{1,2},{2,1},{3,0},{4,7},{5,6},{6,5},{7,4},{8,11},{9,10},{10,... | collective-permute-start | bytes 479240 | tf_op jit(solution)/shard_map/cond/branch_1_fun/ppermute | solution.py:689
  323.0 16.5 %collective-permute-start.15 = (bf16[104,768]{1,0:T(8,128)(2,1)S(1)}, bf16[104,768]{1,0:T(8,128)(2,1)S(1)}, u32[]{:S(2)}, u32[]{:S(2)}) collective-permute-start(bf16[104,768]{1,0:T(8,128)(2,1)S(1)} %add_convert_fusion), channel_id=1, source_target_pairs={{0,2},{1,3},{2,0},{3,1},{4,6},{5,7},{6,4},{7,5},{8,10},{9,11},{10,... | collective-permute-start | bytes 479240 | tf_op jit(solution)/shard_map/cond/branch_1_fun/ppermute | solution.py:689
  323.0 18.6 %collective-permute-start.14 = (bf16[104,768]{1,0:T(8,128)(2,1)S(1)}, bf16[104,768]{1,0:T(8,128)(2,1)S(1)}, u32[]{:S(2)}, u32[]{:S(2)}) collective-permute-start(bf16[104,768]{1,0:T(8,128)(2,1)S(1)} %add_convert_fusion), channel_id=1, source_target_pairs={{0,1},{1,0},{2,3},{3,2},{4,5},{5,4},{6,7},{7,6},{8,9},{9,8},{10,11... | collective-permute-start | bytes 479240 | tf_op jit(solution)/shard_map/cond/branch_1_fun/ppermute | solution.py:689
  341.7 12.0 %collective-permute-start.17 = (bf16[4,56,768]{2,1,0:T(8,128)(2,1)S(1)}, bf16[4,56,768]{2,1,0:T(8,128)(2,1)S(1)}, u32[]{:S(2)}, u32[]{:S(2)}) collective-permute-start(bf16[4,56,768]{2,1,0:T(8,128)(2,1)S(1)} %slice.215), channel_id=1, source_target_pairs={{0,16},{4,20},{8,24},{12,28},{16,0},{20,4},{24,8},{28,12},{1,17},{... | collective-permute-start | bytes 1032200 | tf_op jit(solution)/shard_map/cond/branch_1_fun/ppermute | solution.py:697
  343.6 11.8 %collective-permute-start.19 = (bf16[4,48,768]{2,1,0:T(8,128)(2,1)S(1)}, bf16[4,48,768]{2,1,0:T(8,128)(2,1)S(1)}, u32[]{:S(2)}, u32[]{:S(2)}) collective-permute-start(bf16[4,48,768]{2,1,0:T(8,128)(2,1)S(1)} %pad_maximum_fusion.7), channel_id=1, source_target_pairs={{0,8},{4,12},{8,0},{12,4},{16,24},{20,28},{24,16},{28,20},{1,9},{5... | collective-permute-start | bytes 884744 | tf_op jit(solution)/shard_map/cond/branch_1_fun/ppermute | solution.py:697
  353.7 19.6 %collective-permute-start.18 = (bf16[8,56,768]{2,1,0:T(8,128)(2,1)S(1)}, bf16[8,56,768]{2,1,0:T(8,128)(2,1)S(1)}, u32[]{:S(2)}, u32[]{:S(2)}) collective-permute-start(bf16[8,56,768]{2,1,0:T(8,128)(2,1)S(1)} %pad_maximum_fusion.4), channel_id=1, source_target_pairs={{0,8},{4,12},{8,0},{12,4},{16,24},{20,28},{24,16},{28,20},{1,9},{5... | collective-permute-start | bytes 2064392 | tf_op jit(solution)/shard_map/cond/branch_1_fun/ppermute | solution.py:697
  355.4 18.2 %collective-permute-start.20 = (bf16[8,48,768]{2,1,0:T(8,128)(2,1)S(1)}, bf16[8,48,768]{2,1,0:T(8,128)(2,1)S(1)}, u32[]{:S(2)}, u32[]{:S(2)}) collective-permute-start(bf16[8,48,768]{2,1,0:T(8,128)(2,1)S(1)} %pad_maximum_fusion.6), channel_id=1, source_target_pairs={{0,16},{4,20},{8,24},{12,28},{16,0},{20,4},{24,8},{28,12},{1,17},{... | collective-permute-start | bytes 1769480 | tf_op jit(solution)/shard_map/cond/branch_1_fun/ppermute | solution.py:697
  373.5 3.0 copy-start.2
  373.5 6.6 %collective-permute-start.21 = (bf16[16,56,768]{2,1,0:T(8,128)(2,1)S(1)}, bf16[16,56,768]{2,1,0:T(8,128)(2,1)}, u32[]{:S(2)}, u32[]{:S(2)}) collective-permute-start(bf16[16,56,768]{2,1,0:T(8,128)(2,1)S(1)} %pad_maximum_fusion), channel_id=1, source_target_pairs={{0,4},{4,0},{8,12},{12,8},{16,20},{20,16},{24,28},{28,24},{1,5},{5... | collective-permute-start | bytes 4128776 | tf_op jit(solution)/shard_map/cond/branch_1_fun/ppermute | solution.py:703
  374.8 5.4 %collective-permute-start.22 = (bf16[16,48,768]{2,1,0:T(8,128)(2,1)}, bf16[16,48,768]{2,1,0:T(8,128)(2,1)}, u32[]{:S(2)}, u32[]{:S(2)}) collective-permute-start(bf16[16,48,768]{2,1,0:T(8,128)(2,1)} %pad_maximum_fusion.1), channel_id=1, source_target_pairs={{0,4},{4,0},{8,12},{12,8},{16,20},{20,16},{24,28},{28,24},{1,5},{5... | collective-permute-start | bytes 3538952 | tf_op jit(solution)/shard_map/cond/branch_1_fun/ppermute | solution.py:703
  (21 other events, 36.1 us)
Sparse Core Ops, SparseCore 0:
  149.2 232.4 all-reduce.9
